TPU v7x, 32 devices: a whole 2x2x4 slice. The times are simulated.
32 devices in a mesh: ind: 8 (over y, x, core), bin: 4 (over z).
Axes of the slice: x: 2, y: 2, z: 4, core: 2. Of those that a mesh axis runs over, the one named last changes fastest.
Arguments:
- genotype: int32 [2048, 102400], P('ind', 'bin'), may hold values from 0 to 2
- snp_mean: float32 [102400], P('bin'), may hold values from 0.9 to 1.1
- snp_scale: float32 [102400], P('bin'), may hold values from 0.75 to 0.9
- snp_label: int32 [102400], P('bin'), may hold values from 0 to 23, as said below
- probe_bits: int32 [10, 2048], P(None, 'ind'), may hold values from 0 to 1
- phenotype: bfloat16 [2048], P('ind'), may hold values from -6 to 6
Outputs:
- field: bfloat16 [24, 10, 2048], P('bin', None, 'ind')
- pair: float32 [24, 24], P('bin')
- trace: float32 [24], P('bin')
- quadratic: float32 [24], P('bin')
Inputs may be any that keep to these rules, and one draw needn't show every extreme that they name: `snp_label`: the label of SNP m lies from (m // 25600) * 6 to (m // 25600) * 6 + 5, and every bin holds at least one SNP.
All inputs are finite; a program needn't handle non-finite values.
Results may differ from a plain program's by a relative error of at most 0.0053.
Values may be sent and summed in bfloat16 or wider, within the bound.
No kernel may reach another device: no remote copies, remote signals or barrier semaphores. Data moves between devices by JAX's collectives and lax.ppermute only.
A program may use at most 128 MiB of HBM per device.

v0:
```python
import jax
import jax.numpy as jnp
from jax import lax
from jax.sharding import PartitionSpec as P

BINS = 24
PROBES = 10


def shards(genotype, snp_mean, snp_scale, snp_label, probe_bits, phenotype):
    ind_count = lax.axis_size("ind")
    bin_count = lax.axis_size("bin")
    own_bins = BINS // bin_count
    first_bin = lax.axis_index("bin") * own_bins
    rows = genotype.shape[0]
    snps = genotype.shape[1]
    total_rows = rows * ind_count
    stand = ((genotype.astype(jnp.float32) - snp_mean[None, :]) / snp_scale[None, :]).astype(
        jnp.bfloat16
    )
    probes = (2 * probe_bits - 1).astype(jnp.bfloat16)
    left = jnp.concatenate([probes, phenotype[None, :]], axis=0)
    partial_value = jnp.dot(left, stand, preferred_element_type=jnp.float32)
    local_label = snp_label - first_bin
    bin_ids = jnp.arange(own_bins, dtype=jnp.int32)[:, None]
    member = local_label[None, :] == bin_ids
    count = jnp.sum(member.astype(jnp.float32), axis=1)
    squares = jnp.sum(jnp.square(stand.astype(jnp.float32)), axis=0)
    trace_part = jnp.sum(jnp.where(member, squares[None, :], 0.0), axis=1)
    totals = lax.psum(partial_value, "ind")
    trait = totals[PROBES]
    quad_whole = jnp.sum(jnp.where(member, (trait * trait)[None, :], 0.0), axis=1)
    weights = totals[:PROBES].astype(jnp.bfloat16)
    expanded = jnp.where(member[:, None, :], weights[None, :, :], jnp.zeros((), jnp.bfloat16))
    expanded = expanded.reshape(own_bins * PROBES, snps)
    hidden = lax.dot_general(
        expanded, stand, (((1,), (1,)), ((), ())), preferred_element_type=jnp.float32
    )
    field = (hidden.reshape(own_bins, PROBES, rows) / count[:, None, None]).astype(jnp.bfloat16)
    own_flat = field.reshape(own_bins, PROBES * rows)
    piece = lax.all_gather(field, "bin", axis=0, tiled=True)
    other = piece.reshape(piece.shape[0], PROBES * rows)
    pair_part = lax.dot_general(
        own_flat, other, (((1,), (1,)), ((), ())), preferred_element_type=jnp.float32
    )
    pair_total, trace_total = lax.psum((pair_part, trace_part), "ind")
    pair = pair_total / (PROBES * total_rows)
    trace = trace_total / (count * total_rows)
    quadratic = quad_whole / (count * total_rows)
    return (field, pair, trace, quadratic)


def solution(mesh):
    placed = (P("ind", "bin"), P("bin"), P("bin"), P("bin"), P(None, "ind"), P("ind"))
    return jax.shard_map(
        shards,
        mesh=mesh,
        in_specs=placed,
        out_specs=(P("bin", None, "ind"), P("bin", None), P("bin"), P("bin")),
        check_vma=False,
    )
```

profile of v0, /device:TPU:0, one launch (start us, length us, event | category | flops | bytes accessed | tf_op | source)
XLA Modules:
  0.0 136.8 jit_solution(2616185120043475101)
XLA Ops:
  7.2 0.0 all-reduce.3.cloned.1.call-start
  7.2 0.7 add_convert_fusion
  7.9 0.7 broadcast_in_dim.53
  8.6 12.0 %multiply_reduce_fusion = (f32[25600]{0:T(1024)S(1)}, bf16[256,25600]{1,0:T(8,128)(2,1)S(1)}) fusion(f32[25600]{0:T(1024)} %param.8, f32[25600]{0:T(1024)} %param.7, s32[256,25600]{1,0:T(8,128)} %param.6), kind=kLoop, calls=%fused_computation | loop fusion | flops 45849600 | bytes 39628800 | tf_op jit(solution)/shard_map/reduce_sum | solution.py:28
  20.6 0.0 copy-start
  20.6 0.0 copy-start.2
  20.6 4.6 %copy-done = bf16[256,25600]{1,0:T(8,128)(2,1)} copy-done((bf16[256,25600]{1,0:T(8,128)(2,1)}, bf16[256,25600]{1,0:T(8,128)(2,1)S(1)}, u32[]{:S(2)}) %copy-start) | copy-done | bytes 13107224
  25.3 3.0 %fusion.17 = f32[11,25600]{1,0:T(8,128)} fusion(bf16[256,25600]{1,0:T(8,128)(2,1)S(1)} %get-tuple-element.18, bf16[1,256]{1,0:T(2,128)(2,1)S(1)} %broadcast_in_dim.53, bf16[10,256]{1,0:T(8,128)(2,1)S(1)} %add_convert_fusion), kind=kOutput, calls=%fused_computation.20 | convolution fusion | flops 144190464 | bytes 14239232 | tf_op jit(solution)/shard_map/dot_general | solution.py:23
  28.3 0.0 all-reduce.3.cloned.1.call-update
  28.3 0.0 copy-done.2
  28.3 0.1 iota_compare_fusion
  28.4 62.0 %all-reduce.3.cloned.1.call-done = f32[11,25600]{1,0:T(8,128)} async-done(((f32[11,25600]{1,0:T(8,128)}), f32[11,25600]{1,0:T(8,128)}) %all-reduce.3.cloned.1.call-update) | async-done | bytes 1126416 | tf_op jit(solution)/shard_map/psum | solution.py:30
  90.5 1.2 slice_multiply_fusion
  91.7 0.5 select_reduce_fusion
  92.2 1.5 %slice.13 = bf16[10,25600]{1,0:T(8,128)(2,1)S(1)} slice(f32[11,25600]{1,0:T(8,128)} %all-reduce.3.cloned.1.call-done), slice={[0:10], [0:25600]} | slice | bytes 1024000 | tf_op jit(solution)/shard_map/slice | solution.py:33
  93.8 9.0 %fusion.11 = bf16[6,10,256]{2,1,0:T(8,128)(2,1)S(1)} fusion(bf16[256,25600]{1,0:T(8,128)(2,1)} %copy-done, pred[6,25600]{1,0:T(8,128)(4,1)S(1)} %iota_compare_fusion, bf16[10,25600]{1,0:T(8,128)(2,1)S(1)} %slice.13, f32[6]{0:T(128)S(1)} %get-tuple-element.14), kind=kOutput, calls=%fused_computation.11 | convolution fusion | flops 787998720 | bytes 13803544 | tf_op jit(solution)/shard_map/dot_general | solution.py:36
  102.7 0.0 copy-start.1
  102.8 13.8 %all_gather.3 = bf16[24,10,256]{2,1,0:T(8,128)(2,1)S(1)} all-gather(bf16[6,10,256]{2,1,0:T(8,128)(2,1)S(1)} %fusion.11), channel_id=1, replica_groups=mesh['ind'=8,'bin'=4] {'bin'}, dimensions={0}, use_global_device_ids=true | all-gather | bytes 153600 | tf_op jit(solution)/shard_map/all_gather | solution.py:41
  116.6 0.2 convolution_bitcast_fusion
  116.7 12.1 %all-reduce = (f32[6,24]{1,0:T(8,128)S(1)}, f32[6]{0:T(128)S(1)}) all-reduce(f32[6,24]{1,0:T(8,128)S(1)} %convolution_bitcast_fusion, f32[6]{0:T(128)S(1)} %get-tuple-element.13), channel_id=1, replica_groups=mesh['ind'=8,'bin'=4] {'ind'}, use_global_device_ids=true, to_apply=%region_2.3 | all-reduce | flops 150 | bytes 1200 | tf_op jit(solution)/shard_map/psum | solution.py:46
  128.8 0.6 broadcast_multiply_fusion
  129.4 0.5 multiply_divide_fusion
  130.0 0.0 copy-done.1
  (2 shorter events, 0.0 us)
Async XLA Ops:
  7.2 83.3 %all-reduce.3.cloned.1.call-start = ((), (), s32[]{:S(2)}) async-start(), calls=%async_computation | async-start | bytes 3276800 | tf_op jit(solution)/shard_map/psum | solution.py:30
  20.6 4.7 %copy-start = (bf16[256,25600]{1,0:T(8,128)(2,1)}, bf16[256,25600]{1,0:T(8,128)(2,1)S(1)}, u32[]{:S(2)}) copy-start(bf16[256,25600]{1,0:T(8,128)(2,1)S(1)} %get-tuple-element.18) | copy-start | bytes 39321604
  20.6 7.7 %copy-start.2 = (s32[25600]{0:T(1024)S(1)}, s32[25600]{0:T(1024)}, u32[]{:S(2)}) copy-start(s32[25600]{0:T(1024)} %param.9) | copy-start | bytes 307204
  102.7 27.2 %copy-start.1 = (bf16[6,10,256]{2,0,1:T(8,128)(2,1)}, bf16[6,10,256]{2,0,1:T(8,128)(2,1)S(1)}, u32[]{:S(2)}) copy-start(bf16[6,10,256]{2,0,1:T(8,128)(2,1)S(1)} %copy.15) | copy-start | bytes 92164
Sparse Core Ops, SparseCore 0:
  28.4 62.0 all-reduce.2
where the time goes:
time: 137 us
  waiting for transfers between devices  62 us (45%)
  blocking collectives  25.9 us (19%)
  other arithmetic  15.7 us (11%)
  between operations  14.1 us (10%)
  matrix products  12.1 us (9%)
  local copies, waits for them, and re-layouts  6.84 us (5%)
    psum x1, waiting for transfers between devices, shards(): totals = lax.psum(partial_value, 'ind')  62 us
    all_gather x1, blocking collectives, shards(): piece = lax.all_gather(field, 'bin', axis=0, tiled=True)  13.8 us
    psum x1, blocking collectives, shards(): pair_total, trace_total = lax.psum((pair_part, trace_part), 'ind')  12.1 us
    reduce_sum x1, other arithmetic, shards(): squares = jnp.sum(jnp.square(stand.astype(jnp.float32)), axis=0)  12 us
    dot_general x1, matrix products, shards(): lax.dot_general(expanded, stand, (((1,), (1,)), ((), ())), preferred_elem...  8.96 us
    unnamed x7, local copies, waits for them, and re-layouts  4.67 us
    dot_general x1, matrix products, shards(): partial_value = jnp.dot(left, stand, preferred_element_type=jnp.float32)  3 us
  transfers between devices with their start and end apart: 1, of which 1 were waited for; matrix products, arithmetic and copies ran while one was open for 0% of the time, Pallas kernels for 0%

commit v1 on v0

v1 whole, which is shorter than its diff:
```python
import functools

import jax
import jax.numpy as jnp
from jax import lax
from jax.experimental import pallas as pl
from jax.experimental.pallas import tpu as pltpu
from jax.sharding import PartitionSpec as P

BINS = 24
PROBES = 10
LANES = 128
SUBLANES = 8
ROWS = 16
TRAIT, ONES = PROBES, PROBES + 1
TRACE_LANE, QUAD_LANE = LANES - 2, LANES - 1
PIECE = 640
DOT_PIECE = 768
F32 = jnp.float32
BF16 = jnp.bfloat16
VMEM = pltpu.VMEM
MIB = 1 << 20


def core():
    return lax.rem(lax.axis_index("ind"), 2)


def fold_lanes(value):
    return tree_sum([value[:, at : at + LANES] for at in range(0, value.shape[1], LANES)])


def rows_iota(count, width=1):
    return lax.broadcasted_iota(jnp.int32, (count, width), 0)


def tree_sum(terms):
    terms = list(terms)
    while len(terms) > 1:
        pairs = [a + b for a, b in zip(terms[::2], terms[1::2])]
        terms = pairs + terms[len(pairs) * 2 :]
    return terms[0]


def pack_sums(value):
    half = value.shape[1] // 2
    low = value[SUBLANES:]
    turned = pltpu.roll(low[:, half:], 4, 0)
    low = jnp.where(rows_iota(SUBLANES) < 4, low[:, :half], turned)
    return value[:SUBLANES], low


def unpack_sums(value):
    span = value.shape[1] * 2 // 3
    low = value[:, span:]
    return value[:, :span], jnp.concatenate([low, pltpu.roll(low, 4, 0)], axis=1)


def moments_kernel(snps, distances, opening, taken, given, geno_ref, *rest):
    rest = list(rest)
    if opening:
        bits_ref, trait_ref, kept_ref, sums_ref, local_ref, left_ref = rest[:6]
        rest = rest[6:]
    else:
        raw_in = rest.pop(0) if taken else None
        left_ref, kept_ref, sums_ref, local_ref = rest[:4]
        rest = rest[4:]
    raw_out = rest.pop(0) if given is not None else None
    slots, rows, block = kept_ref.shape
    fetched = slots - taken
    devices = -(-snps // block)
    tail = snps - (devices - 1) * block
    span = sums_ref.shape[2] * 2 // 3

    def copy(distance, target, semaphore, width):
        start = pl.multiple_of((lax.axis_index("ind") ^ distance) * block, LANES)
        return pltpu.make_async_copy(
            geno_ref.at[:, pl.ds(start, width)], target.at[:, pl.ds(0, width)], semaphore
        )

    def whole_or_tail(distance, target, semaphore, act):
        if tail == block:
            act(copy(distance, target, semaphore, block))
        else:
            last = (lax.axis_index("ind") ^ distance) == devices - 1
            pl.when(last)(lambda: act(copy(distance, target, semaphore, tail)))
            pl.when(jnp.logical_not(last))(lambda: act(copy(distance, target, semaphore, block)))

    if fetched:
        buffer, arrived = rest[:2]
        rest = rest[2:]

        def fetch(index, act):
            distance = distances[0] - 2 * (index + taken)
            whole_or_tail(distance, buffer.at[index], arrived.at[index], act)

    if raw_out is not None:
        raw_arrived = rest.pop(0)

    if opening:
        bits, trait, small = rest[:3]
        bits_copy = pltpu.make_async_copy(bits_ref, bits, small.at[0])
        trait_copy = pltpu.make_async_copy(trait_ref, trait, small.at[1])
        bits_copy.start()
        trait_copy.start()
    if fetched:
        pl.loop(0, fetched)(lambda index: fetch(index, lambda c: c.start()))
    if raw_out is not None:
        whole_or_tail(given, raw_out, raw_arrived, lambda c: c.start())
    if opening:
        bits_copy.wait()
        trait_copy.wait()
        left_ref[...] = jnp.zeros_like(left_ref)
        left_ref[0:PROBES] = (2 * bits[...] - 1).astype(F32)
        left_ref[TRAIT : TRAIT + 1] = trait[...].astype(F32).reshape(1, rows)
        left_ref[ONES : ONES + 1] = jnp.ones((1, rows), F32)
    left = left_ref[...]
    base = jnp.sum(left, axis=1, keepdims=True)
    left = left.astype(BF16)
    row = rows_iota(ROWS)

    def with_low(value):
        high = value[TRAIT : TRAIT + 1]
        return jnp.where(row == TRAIT + 1, high - high.astype(BF16).astype(F32), value)

    ends = jnp.broadcast_to(with_low(base), (ROWS, span - block))

    def work(slot, source):
        squares = []
        for at in range(0, block, PIECE):
            lanes = slice(at, min(at + PIECE, block))
            square = 0.0
            for r in range(0, rows, 16):
                dose = source[r : r + 16, lanes].astype(F32)
                kept_ref[slot, r : r + 16, lanes] = dose.astype(BF16)
                dose = dose * dose
                square = square + (dose[:8] + dose[8:])
            squares.append(jnp.sum(square, axis=0, keepdims=True))
        total = jnp.dot(left, kept_ref[slot], preferred_element_type=F32) - base
        ones = total[ONES : ONES + 1]
        local_ref[slot, 0:1] = ones
        local_ref[slot, 1:2] = jnp.concatenate(squares, axis=1) - 2.0 * ones - rows
        high, low = pack_sums(jnp.concatenate([with_low(total), ends], axis=1))
        sums_ref[slot, :, :span] = high.astype(BF16)
        sums_ref[slot, :, span:] = low.astype(BF16)

    if taken:
        work(0, raw_in)
    if fetched:

        @pl.loop(0, fetched)
        def _(index):
            fetch(index, lambda c: c.wait())
            work(index + taken, buffer.at[index])

    if raw_out is not None:
        whole_or_tail(given, raw_out, raw_arrived, lambda c: c.wait())


def cores_kernel(left_ref, here_ref, away_ref, *outs):
    outs, left_out = outs[:-1], outs[-1]
    left_out[...] = left_ref[...]
    for index, out in enumerate(outs):
        out[...] = (here_ref[index].astype(F32) + away_ref[index].astype(F32)).astype(BF16)


def relay_kernel(token_ref, value_ref, out_ref):
    out_ref[...] = value_ref[...]


def weights_kernel(mean_ref, scale_ref, own_ref, near_ref, *refs):
    parts, (u_ref, trait_ref) = refs[:-2], refs[-2:]
    block = trait_ref.shape[1]
    width = u_ref.shape[1] - block
    here = pl.ds(pl.multiple_of(lax.axis_index("ind") * block, LANES), block)
    parts = [own_ref[0], near_ref[0]] + [part[...] for part in parts]
    total = tree_sum([part.astype(F32) for part in parts])
    shift = mean_ref[:, here] - 1.0
    inverse = 1.0 / scale_ref[:, here]
    high, low = [
        (part[:, :block] - part[:, block : block + 1] * shift) * inverse
        for part in unpack_sums(total)
    ]
    trait_ref[...] = low[2:3] + low[3:4]
    high, low = [part.astype(BF16).astype(F32) * inverse for part in (high, low)]
    low = jnp.concatenate([low, jnp.zeros((SUBLANES, 4 * width - block), F32)], axis=1)
    folded = low[:, :width]
    for j in range(1, 4):
        turned = pltpu.roll(low[:, j * width : (j + 1) * width], 2 * j, 0)
        folded = jnp.where(rows_iota(SUBLANES) < 2 * j, folded, turned)
    u_ref[:, :block] = high.astype(BF16)
    u_ref[:, block:] = folded.astype(BF16)


def stats_kernel(own_bins, order, flat_ref, mean_ref, scale_ref, label_ref, trait_ref, *rest):
    locals_, (out_ref, field_ref) = rest[:-2], rest[-2:]
    block = trait_ref.shape[1]
    rows = order[0]
    bins = rows_iota(SUBLANES)

    def member_of(owner):
        here = pl.ds(pl.multiple_of(owner * block, LANES), block)
        member = label_ref[:, here] - lax.axis_index("bin") * own_bins == bins
        return here, member & (bins < own_bins)

    trace = jnp.zeros((SUBLANES, 1), F32)
    for ref, distances in zip(locals_, order[1]):
        for slot, distance in enumerate(distances):
            here, member = member_of(lax.axis_index("ind") ^ distance)
            shift = mean_ref[:, here] - 1.0
            inverse = 1.0 / scale_ref[:, here]
            square = ref[slot, 1:2] - 2.0 * shift * ref[slot, 0:1] + rows * shift * shift
            square = square * (inverse * inverse)
            trace += jnp.sum(jnp.where(member, square, 0.0), axis=1, keepdims=True)
    _, member = member_of(lax.axis_index("ind"))
    trait = trait_ref[...]
    quad = jnp.sum(jnp.where(member, trait * trait, 0.0), axis=1, keepdims=True)
    lane = lax.broadcasted_iota(jnp.int32, (SUBLANES, LANES), 1)
    out_ref[...] = jnp.where(lane == TRACE_LANE, trace, jnp.where(lane == QUAD_LANE, quad, 0.0))
    flat = flat_ref[...].astype(F32)
    for b in range(PROBES):
        field_ref[b] = flat[:own_bins, b * rows : (b + 1) * rows].astype(BF16)


def field_kernel(own_bins, blocks, sources, started, last, *refs):
    refs = list(refs)
    mean_ref, label_ref = refs[:2]
    kept_refs, refs = refs[2 : 2 + sources], refs[2 + sources :]
    u_refs, refs = refs[: len(blocks)], refs[len(blocks) :]
    rows, block = kept_refs[0].shape[1:]
    bins = rows_iota(SUBLANES)
    if started:
        acc, offset, number = [ref[...] for ref in refs[:3]]
        refs = refs[3:]
    else:
        acc = jnp.zeros((rows, PROBES * SUBLANES), F32)
        offset = jnp.zeros((PROBES * SUBLANES, LANES), F32)
        number = jnp.zeros((SUBLANES, LANES), F32)
    for index, (slot, distance) in enumerate(blocks):
        start = (lax.axis_index("ind") ^ distance) * block
        u = u_refs[index][...].astype(F32)
        lines = [u[b : b + 1, :block] for b in range(SUBLANES)]
        for b in range(PROBES - SUBLANES):
            line = [u[2 * j + b : 2 * j + b + 1, block:] for j in range(4)]
            lines.append(jnp.concatenate(line, axis=1)[:, :block])
        for at in range(0, block, DOT_PIECE):
            width = min(DOT_PIECE, block - at)
            here = pl.ds(pl.multiple_of(start + at, LANES), width)
            member = label_ref[:, here] - lax.axis_index("bin") * own_bins == bins
            member = member & (bins < own_bins)
            mean = mean_ref[:, here]
            spread = [jnp.where(member, line[:, at : at + width], 0.0) for line in lines]
            offset += jnp.concatenate([fold_lanes(value * mean) for value in spread], axis=0)
            number += fold_lanes(jnp.where(member, 1.0, 0.0))
            acc += lax.dot_general(
                kept_refs[index if sources > 1 else 0][slot, :, at : at + width],
                jnp.concatenate(spread, axis=0).astype(BF16),
                (((1,), (1,)), ((), ())),
                preferred_element_type=F32,
            )
    if not last:
        for ref, value in zip(refs, (acc, offset, number)):
            ref[...] = value
        return
    flat_ref, count_ref = refs
    acc = jnp.concatenate([acc, jnp.zeros((rows, LANES - acc.shape[1]), F32)], axis=1)
    acc = jnp.transpose(acc)[: PROBES * SUBLANES] - jnp.sum(offset, axis=1, keepdims=True)
    number = jnp.sum(number, axis=1, keepdims=True)
    count_ref[...] = jnp.broadcast_to(number, count_ref.shape)
    inverse = 1.0 / jnp.maximum(number, 1.0)
    flat = [acc[b * SUBLANES : (b + 1) * SUBLANES] * inverse for b in range(PROBES)]
    flat_ref[...] = jnp.concatenate(flat, axis=1).astype(BF16)


def pair_kernel(stats_ref, *rest):
    flats, out_ref = rest[:-1], rest[-1]
    everyone = [flat[...].astype(F32) for flat in flats]
    everyone += [jnp.zeros_like(everyone[0])] * (LANES // SUBLANES - len(flats))
    out_ref[...] = stats_ref[...] + lax.dot_general(
        flats[0][...],
        jnp.concatenate(everyone, axis=0).astype(BF16),
        (((1,), (1,)), ((), ())),
        preferred_element_type=F32,
    )


def final_kernel(own_bins, n_bin, pairs, total_rows, count_ref, own_ref, common_ref, *rest):
    mine, theirs, outs = rest[:pairs], rest[pairs : 2 * pairs + 1], rest[2 * pairs + 1 :]
    pair_ref, trace_ref, quad_ref = outs
    terms = [own_ref[...]]
    even = core() == 0
    for ref, other in zip(mine, theirs):
        terms.append(jnp.where(even, ref[...], other[...]))
        terms.append(jnp.where(even, other[...], ref[...]))
    terms.append(common_ref[...] + theirs[pairs][...])
    total = tree_sum(terms)
    row = lax.broadcasted_iota(jnp.int32, (SUBLANES, LANES), 0)
    lane = lax.broadcasted_iota(jnp.int32, (SUBLANES, LANES), 1)
    pair = jnp.zeros_like(total)
    for slot in range(n_bin):
        start = slot * SUBLANES
        part = jnp.where((lane >= start) & (lane < start + own_bins), total, 0.0)
        shift = (lax.axis_index("bin") ^ slot) * own_bins - start + LANES
        pair = pair + pltpu.roll(part, lax.rem(shift, LANES), 1)
    pair_ref[...] = pair[:own_bins, :BINS] / (PROBES * total_rows)
    scaled = total / (count_ref[...] * total_rows)
    for ref, column in ((trace_ref, TRACE_LANE), (quad_ref, QUAD_LANE)):
        turned = jnp.where(row == lane, scaled[:, column : column + 1], 0.0)
        ref[...] = jnp.sum(turned, axis=0, keepdims=True)[:, :own_bins]


def swap(value, axis, size, distance):
    return lax.ppermute(value, axis, [(i, i ^ distance) for i in range(size)])


def swap_mixed(value, size, pair):
    return lax.ppermute(value, "ind", [(i, i ^ pair[i % 2]) for i in range(size)])


def chosen_pairs(distances):
    return list(zip(distances[:-1:2], distances[1:-1:2])), distances[-1]


def in_vmem():
    return pl.BlockSpec(memory_space=VMEM)


def in_hbm():
    return pl.BlockSpec(memory_space=pltpu.HBM)


def params(mib):
    return pltpu.CompilerParams(vmem_limit_bytes=mib * MIB)


def cost(flops, moved):
    return pl.CostEstimate(flops=flops, bytes_accessed=moved, transcendentals=0)


def shards(genotype, snp_mean, snp_scale, snp_label, probe_bits, phenotype):
    n = lax.axis_size("ind")
    n_bin = lax.axis_size("bin")
    chips = n // 2
    own_bins = BINS // n_bin
    rows, snps = genotype.shape
    tiles = -(-snps // LANES)
    block_tiles = -(-tiles // n)
    block = block_tiles * LANES
    span = block + LANES * (2 - block_tiles % 2)
    folded = block + -(-block_tiles // 4) * LANES
    whole = n * block
    mean, scale, label = snp_mean, snp_scale, snp_label
    if whole != snps:
        mean = jnp.pad(mean, (0, whole - snps), constant_values=1.0)
        scale = jnp.pad(scale, (0, whole - snps), constant_values=1.0)
        label = jnp.pad(label, (0, whole - snps), constant_values=-1)
    mean, scale, label = mean[None, :], scale[None, :], label[None, :]
    genotype, probe_bits, phenotype = [
        pltpu.with_memory_space_constraint(value, pltpu.HBM)
        for value in (genotype, probe_bits, phenotype)
    ]

    def moments(distances, given, extra, name):
        slots = len(distances)
        opening = extra[0] is probe_bits
        taken = int(not opening and extra[0] is not None)
        extra = [value for value in extra if value is not None]
        fetched = slots - taken
        out_shape = [
            jax.ShapeDtypeStruct((slots, rows, block), BF16),
            jax.ShapeDtypeStruct((slots, SUBLANES, span * 3 // 2), BF16),
            jax.ShapeDtypeStruct((slots, 2, block), F32),
        ]
        if opening:
            out_shape.append(jax.ShapeDtypeStruct((ROWS, rows), F32))
        if given is not None:
            out_shape.append(jax.ShapeDtypeStruct((rows, block), jnp.int32))
        scratch = []
        if fetched:
            scratch += [VMEM((fetched, rows, block), jnp.int32), pltpu.SemaphoreType.DMA((fetched,))]
        if given is not None:
            scratch.append(pltpu.SemaphoreType.DMA)
        if opening:
            scratch += [
                VMEM(probe_bits.shape, jnp.int32),
                VMEM((rows,), BF16),
                pltpu.SemaphoreType.DMA((2,)),
            ]
        return pl.pallas_call(
            functools.partial(moments_kernel, snps, distances, opening, taken, given),
            in_specs=[in_hbm()] + [in_hbm() if opening else in_vmem()] * len(extra),
            out_specs=[in_vmem()] * len(out_shape),
            scratch_shapes=scratch,
            out_shape=out_shape,
            cost_estimate=cost(1, 4 * rows * block * slots if slots > 1 else 1),
            compiler_params=params(20),
            name=name,
        )(genotype, *extra)

    here_order = list(range(n - 2, 0, -2))
    away_order = [d + 1 for d in here_order]

    def plain(kernel, operands, out_shape, name, **options):
        return pl.pallas_call(
            kernel,
            in_specs=[in_vmem()] * len(operands),
            out_specs=[in_vmem()] * len(out_shape),
            out_shape=out_shape,
            compiler_params=params(20),
            name=name,
            **options,
        )(*operands)

    kept_away, away, local_away, left, raw = moments(
        away_order, here_order[0], (probe_bits, phenotype), "moments_away"
    )
    away = swap(away, "ind", n, 1)
    kept_here, here, local_here = moments(here_order, None, (raw, left), "moments_here")
    packed = jax.ShapeDtypeStruct((SUBLANES, span * 3 // 2), BF16)
    *sums, left = plain(
        cores_kernel,
        (left, here, away),
        [packed] * (chips - 1) + [jax.ShapeDtypeStruct(left.shape, F32)],
        "cores",
    )
    sums = [swap(value, "ind", n, d) for value, d in zip(sums, here_order)]
    kept_near, near, local_near, raw = moments([1], 0, (None, left), "moments_near")
    near = swap(near, "ind", n, 1)
    kept_own, own, local_own = moments([0], None, (raw, left), "moments_own")

    u, trait = plain(
        weights_kernel,
        (mean, scale, own, near, *sums),
        [
            jax.ShapeDtypeStruct((SUBLANES, folded), BF16),
            jax.ShapeDtypeStruct((1, block), F32),
        ],
        "weights",
    )

    number_shape = jax.ShapeDtypeStruct((SUBLANES, LANES), F32)
    term_shape = [
        jax.ShapeDtypeStruct((rows, PROBES * SUBLANES), F32),
        jax.ShapeDtypeStruct((PROBES * SUBLANES, LANES), F32),
        number_shape,
    ]
    end_shape = [jax.ShapeDtypeStruct((SUBLANES, PROBES * rows), BF16), number_shape]

    def fields(kept, blocks, us, terms, last=False):
        return plain(
            functools.partial(field_kernel, own_bins, blocks, len(kept), bool(terms), last),
            (mean, label, *kept, *us, *terms),
            end_shape if last else term_shape,
            "field",
            cost_estimate=cost(1, 1),
        )

    u_near = swap(u, "ind", n, 1)
    u_here = [swap(u, "ind", n, d) for d in here_order]
    terms = fields([kept_own, kept_near], [(0, 0), (0, 1)], [u, u_near], [])
    u_away = []
    for slot, (distance, value) in enumerate(zip(here_order, u_here)):
        shape = [jax.ShapeDtypeStruct(value.shape, value.dtype)]
        (value,) = plain(relay_kernel, (terms[2], value), shape, "relay")
        u_away.append(swap(value, "ind", n, 1))
        terms = fields([kept_here], [(slot, distance)], [value], terms)
    blocks = list(enumerate(away_order))
    middle = (chips - 1) // 2
    terms = fields([kept_away], blocks[:middle], u_away[:middle], terms)
    flat, number = fields([kept_away], blocks[middle:], u_away[middle:], terms, last=True)

    flats = [flat] + [swap(flat, "bin", n_bin, d) for d in range(1, n_bin)]
    order = (rows, (away_order, here_order, [1], [0]))
    stats, field = plain(
        functools.partial(stats_kernel, own_bins, order),
        (flat, mean, scale, label, trait, local_away, local_here, local_near, local_own),
        [number_shape, jax.ShapeDtypeStruct((PROBES, own_bins, rows), BF16)],
        "stats",
    )
    (part,) = plain(pair_kernel, (stats, *flats), [number_shape], "pair")
    pairs, common = chosen_pairs(list(range(2, n, 2)))
    part_common = swap(part, "ind", n, common)
    part = part + swap(part, "ind", n, 1)
    mine = [swap_mixed(part, n, pair) for pair in pairs]
    theirs = [swap(value, "ind", n, 1) for value in mine + [part_common]]
    pair, trace, quad = plain(
        functools.partial(final_kernel, own_bins, n_bin, len(pairs), rows * n),
        (number, part, part_common, *mine, *theirs),
        [
            jax.ShapeDtypeStruct((own_bins, BINS), F32),
            jax.ShapeDtypeStruct((1, own_bins), F32),
            jax.ShapeDtypeStruct((1, own_bins), F32),
        ],
        "final",
    )
    return jnp.transpose(field, (1, 0, 2)), pair, trace[0], quad[0]


def solution(mesh):
    placed = (P("ind", "bin"), P("bin"), P("bin"), P("bin"), P(None, "ind"), P("ind"))
    return jax.shard_map(
        shards,
        mesh=mesh,
        in_specs=placed,
        out_specs=(P("bin", None, "ind"), P("bin", None), P("bin"), P("bin")),
        check_vma=False,
    )
```

time: 137 us -> 46.3 us (0.34)
  waiting for transfers between devices: 62 us -> 9.98 us
  blocking collectives: 25.9 us -> 0 us
  Pallas kernels: 0 us -> 18.7 us
  starting transfers between devices: 0.04 us -> 16.5 us
  other arithmetic: 15.7 us -> 0.01 us
  between operations: 14.1 us -> 0.84 us
  matrix products: 12.1 us -> 0 us
  local copies, waits for them, and re-layouts: 6.84 us -> 0.02 us
    psum x1 -> x0, waiting for transfers between devices: 62 us -> none  [shards(): totals = lax.psum(partial_value, 'ind')]
    pallas_call x0 -> x18, Pallas kernels: none -> 18.7 us  [the longest x4 12.1 us: moments(): pl.pallas_call(functools.partial(moments_kernel, snps, distances, opening...]
    ppermute x0 -> x20, starting transfers between devices: none -> 16.5 us  [the longest x19 15.9 us: swap(): return lax.ppermute(value, axis, [(i, i ^ distance) for i in range(size)])]
    all_gather x1 -> x0, blocking collectives: 13.8 us -> none  [shards(): piece = lax.all_gather(field, 'bin', axis=0, tiled=True)]
    reduce_sum x2 -> x0, other arithmetic: 12.5 us -> none  [the longest x1 12 us: shards(): squares = jnp.sum(jnp.square(stand.astype(jnp.float32)), axis=0)]
    dot_general x3 -> x0, matrix products: 12.1 us -> none  [the longest x1 8.96 us: shards(): lax.dot_general(expanded, stand, (((1,), (1,)), ((), ())), preferred_elem...]
    psum x1 -> x0, blocking collectives: 12.1 us -> none  [shards(): pair_total, trace_total = lax.psum((pair_part, trace_part), 'ind')]
    ppermute x0 -> x20, waiting for transfers between devices: none -> 9.98 us  [the longest x19 8.6 us: swap(): return lax.ppermute(value, axis, [(i, i ^ distance) for i in range(size)])]
  transfers between devices with their start and end apart: 1 -> 20, of which waited for: 1 -> 9; matrix products, arithmetic and copies ran while one was open for 0% -> 0% of each run, Pallas kernels for 0% -> 25%
where the time goes in v1:
time: 46.3 us; the launch traced here: 46 us
  Pallas kernels  18.7 us (40%)
  starting transfers between devices  16.5 us (36%)
  waiting for transfers between devices  9.98 us (22%)
  between operations  0.84 us (2%)
    ppermute x19, starting transfers between devices, swap(): return lax.ppermute(value, axis, [(i, i ^ distance) for i in range(size)])  15.9 us
    pallas_call x4, Pallas kernels, moments(): pl.pallas_call(functools.partial(moments_kernel, snps, distances, opening...  12.1 us
    ppermute x19, waiting for transfers between devices, swap(): return lax.ppermute(value, axis, [(i, i ^ distance) for i in range(size)])  8.6 us
    pallas_call x14, Pallas kernels, plain(): pl.pallas_call(kernel, in_specs=[in_vmem()] * len(operands), out_specs=[i...  6.6 us
    ppermute x1, waiting for transfers between devices, swap_mixed(): lax.ppermute(value, 'ind', [(i, i ^ pair[i % 2]) for i in range(size)])  1.38 us
  transfers between devices with their start and end apart: 20, of which 9 were waited for; matrix products, arithmetic and copies ran while one was open for 0% of the time, Pallas kernels for 25%

profile of v1, /device:TPU:0, one launch (start us, length us, event | category | flops | bytes accessed | tf_op | source)
XLA Modules:
  0.0 46.0 jit_solution(1146878922100485859)
XLA Ops:
  0.6 4.9 %moments_away.1 = (bf16[3,256,3200]{2,1,0:T(8,128)(2,1)S(1)}, bf16[3,8,4992]{2,1,0:T(8,128)(2,1)S(1)}, f32[3,2,3200]{2,1,0:T(2,128)S(1)}, f32[16,256]{1,0:T(8,128)S(1)}, s32[256,3200]{1,0:T(8,128)S(1)}) custom-call(s32[256,25600]{1,0:T(8,128)} %geno_ref.7, s32[10,256]{1,0:T(8,128)} %rest_0_.1, bf16[256]{0:T(256)(128)(2,1)} %rest_1_.1), custom_call_target="tpu_custom_call" | custom-call | flops 1 | bytes 9830400 | tf_op jit(solution)/shard_map/moments_away/pallas_call | solution.py:389
  6.0 3.6 %moments_here.1 = (bf16[3,256,3200]{2,1,0:T(8,128)(2,1)S(1)}, bf16[3,8,4992]{2,1,0:T(8,128)(2,1)S(1)}, f32[3,2,3200]{2,1,0:T(2,128)S(1)}) custom-call(s32[256,25600]{1,0:T(8,128)} %geno_ref.7, s32[256,3200]{1,0:T(8,128)S(1)} %get-tuple-element.48.rest_0_, f32[16,256]{1,0:T(8,128)S(1)} %get-tuple-element.49.rest_1_.left_ref), custom_call_target="tpu_custom_call" | custom-call | flops 1 | bytes 9830400 | tf_op jit(solution)/shard_map/moments_here/pallas_call | solution.py:389
  9.8 3.5 %collective-permute-start.2 = (bf16[8,4992]{1,0:T(8,128)(2,1)S(1)}, bf16[8,4992]{1,0:T(8,128)(2,1)S(1)}, u32[]{:S(2)}, u32[]{:S(2)}) collective-permute-start(bf16[8,4992]{1,0:T(8,128)(2,1)S(1)} %get-tuple-element.59), channel_id=1, source_target_pairs={{0,24},{4,28},{8,16},{12,20},{16,8},{20,12},{24,0},{28,4},{1,25},{... | collective-permute-start | bytes 239624 | tf_op jit(solution)/shard_map/ppermute | solution.py:313
  13.9 2.9 %moments_near.1 = (bf16[1,256,3200]{2,1,0:T(8,128)(2,1)S(1)}, bf16[1,8,4992]{2,1,0:T(8,128)(2,1)S(1)}, f32[1,2,3200]{2,1,0:T(2,128)S(1)}, s32[256,3200]{1,0:T(8,128)S(1)}) custom-call(s32[256,25600]{1,0:T(8,128)} %geno_ref.7, f32[16,256]{1,0:T(8,128)S(1)} %get-tuple-element.53.rest_0_.rest_1_), custom_call_target="tpu_custom_call" | custom-call | flops 1 | bytes 1 | tf_op jit(solution)/shard_map/moments_near/pallas_call | solution.py:389
  17.0 0.7 %moments_own.1 = (bf16[1,256,3200]{2,1,0:T(8,128)(2,1)S(1)}, bf16[1,8,4992]{2,1,0:T(8,128)(2,1)S(1)}, f32[1,2,3200]{2,1,0:T(2,128)S(1)}) custom-call(s32[256,25600]{1,0:T(8,128)} %geno_ref.7, s32[256,3200]{1,0:T(8,128)S(1)} %get-tuple-element.54.rest_0_, f32[16,256]{1,0:T(8,128)S(1)} %get-tuple-element.53.rest_0_.rest_1_), custom_call_target="tpu_custom_call" | custom-call | flops 1 | bytes 1 | tf_op jit(solution)/shard_map/moments_own/pallas_call | solution.py:389
  18.6 2.8 %collective-permute-start.6 = (bf16[8,4096]{1,0:T(8,128)(2,1)S(1)}, bf16[8,4096]{1,0:T(8,128)(2,1)S(1)}, u32[]{:S(2)}, u32[]{:S(2)}) collective-permute-start(bf16[8,4096]{1,0:T(8,128)(2,1)S(1)} %get-tuple-element.62.refs_4_), channel_id=1, source_target_pairs={{0,24},{4,28},{8,16},{12,20},{16,8},{20,12},{24,0},{28,4},{1,25},{... | collective-permute-start | bytes 196616 | tf_op jit(solution)/shard_map/ppermute | solution.py:313
  22.1 1.1 %field.6 = (f32[256,80]{1,0:T(8,128)S(1)}, f32[80,128]{1,0:T(8,128)S(1)}, f32[8,128]{1,0:T(8,128)S(1)}) custom-call(f32[1,25600]{1,0:T(1,128)S(1)} %bitcast.7, s32[1,25600]{1,0:T(1,128)S(1)} %bitcast.14, bf16[1,256,3200]{2,1,0:T(8,128)(2,1)S(1)} %get-tuple-element.55.refs_2_, bf16[1,256,3200]{2,1,0:T(8,128)(2,1)S(1)} %get-tuple-element.56.refs_3_, ...), custom_call_target="tpu_custom_call" | custom-call | flops 1 | bytes 1 | tf_op jit(solution)/shard_map/field/pallas_call | solution.py:404
  23.2 0.9 %collective-permute-done.6.value_ref = bf16[8,4096]{1,0:T(8,128)(2,1)S(1)} collective-permute-done((bf16[8,4096]{1,0:T(8,128)(2,1)S(1)}, bf16[8,4096]{1,0:T(8,128)(2,1)S(1)}, u32[]{:S(2)}, u32[]{:S(2)}) %collective-permute-start.6) | collective-permute-done | bytes 65568 | tf_op jit(solution)/shard_map/ppermute | solution.py:313
  24.1 0.6 %field.7 = (f32[256,80]{1,0:T(8,128)S(1)}, f32[80,128]{1,0:T(8,128)S(1)}, f32[8,128]{1,0:T(8,128)S(1)}) custom-call(f32[1,25600]{1,0:T(1,128)S(1)} %bitcast.8, s32[1,25600]{1,0:T(1,128)S(1)} %bitcast.15, bf16[3,256,3200]{2,1,0:T(8,128)(2,1)S(1)} %get-tuple-element.50.refs_2_, bf16[8,4096]{1,0:T(8,128)(2,1)S(1)} %relay.3.refs_3_, ...), custom_call_target="tpu_custom_call" | custom-call | flops 1 | bytes 1 | tf_op jit(solution)/shard_map/field/pallas_call | solution.py:404
  24.7 1.0 %collective-permute-done.7.value_ref = bf16[8,4096]{1,0:T(8,128)(2,1)S(1)} collective-permute-done((bf16[8,4096]{1,0:T(8,128)(2,1)S(1)}, bf16[8,4096]{1,0:T(8,128)(2,1)S(1)}, u32[]{:S(2)}, u32[]{:S(2)}) %collective-permute-start.7) | collective-permute-done | bytes 65568 | tf_op jit(solution)/shard_map/ppermute | solution.py:313
  25.8 0.6 %field.8 = (f32[256,80]{1,0:T(8,128)S(1)}, f32[80,128]{1,0:T(8,128)S(1)}, f32[8,128]{1,0:T(8,128)S(1)}) custom-call(f32[1,25600]{1,0:T(1,128)S(1)} %bitcast.9, s32[1,25600]{1,0:T(1,128)S(1)} %bitcast.16, bf16[3,256,3200]{2,1,0:T(8,128)(2,1)S(1)} %get-tuple-element.50.refs_2_, bf16[8,4096]{1,0:T(8,128)(2,1)S(1)} %relay.4.refs_3_, ...), custom_call_target="tpu_custom_call" | custom-call | flops 1 | bytes 1 | tf_op jit(solution)/shard_map/field/pallas_call | solution.py:404
  27.6 0.6 %field.10 = (f32[256,80]{1,0:T(8,128)S(1)}, f32[80,128]{1,0:T(8,128)S(1)}, f32[8,128]{1,0:T(8,128)S(1)}) custom-call(f32[1,25600]{1,0:T(1,128)S(1)} %bitcast.11, s32[1,25600]{1,0:T(1,128)S(1)} %bitcast.18, bf16[3,256,3200]{2,1,0:T(8,128)(2,1)S(1)} %get-tuple-element.47.refs_2_, bf16[8,4096]{1,0:T(8,128)(2,1)S(1)} %collective-permute-done.11.refs_3_, ...), custom_call_target="tpu_custom_call" | custom-call | flops 1 | bytes 1 | tf_op jit(solution)/shard_map/field/pallas_call | solution.py:404
  28.2 1.2 %field.11 = (bf16[8,2560]{1,0:T(8,128)(2,1)S(1)}, f32[8,128]{1,0:T(8,128)S(1)}) custom-call(f32[1,25600]{1,0:T(1,128)S(1)} %bitcast.12, s32[1,25600]{1,0:T(1,128)S(1)} %bitcast.19, bf16[3,256,3200]{2,1,0:T(8,128)(2,1)S(1)} %get-tuple-element.47.refs_2_, bf16[8,4096]{1,0:T(8,128)(2,1)S(1)} %collective-permute-done.8.refs_3_, ...), custom_call_target="tpu_custom_call" | custom-call | flops 1 | bytes 1 | tf_op jit(solution)/shard_map/field/pallas_call | solution.py:404
  29.4 3.7 %collective-permute-start.14 = (bf16[8,2560]{1,0:T(8,128)(2,1)S(1)}, bf16[8,2560]{1,0:T(8,128)(2,1)S(1)}, u32[]{:S(2)}, u32[]{:S(2)}) collective-permute-start(bf16[8,2560]{1,0:T(8,128)(2,1)S(1)} %get-tuple-element.78.flat_ref.rest_0_), channel_id=1, source_target_pairs={{0,3},{1,2},{2,1},{3,0},{4,7},{5,6},{6,5},{7,4},{8,11},{9,10},{10,... | collective-permute-start | bytes 122888 | tf_op jit(solution)/shard_map/ppermute | solution.py:313
  33.1 0.8 %collective-permute-start.12 = (bf16[8,2560]{1,0:T(8,128)(2,1)S(1)}, bf16[8,2560]{1,0:T(8,128)(2,1)S(1)}, u32[]{:S(2)}, u32[]{:S(2)}) collective-permute-start(bf16[8,2560]{1,0:T(8,128)(2,1)S(1)} %get-tuple-element.78.flat_ref.rest_0_), channel_id=1, source_target_pairs={{0,1},{1,0},{2,3},{3,2},{4,5},{5,4},{6,7},{7,6},{8,9},{9,8},{10,11... | collective-permute-start | bytes 122888 | tf_op jit(solution)/shard_map/ppermute | solution.py:313
  33.9 0.8 %stats.1 = (f32[8,128]{1,0:T(8,128)S(1)}, bf16[10,6,256]{2,1,0:T(8,128)(2,1)}) custom-call(bf16[8,2560]{1,0:T(8,128)(2,1)S(1)} %get-tuple-element.78.flat_ref.rest_0_, f32[1,25600]{1,0:T(1,128)S(1)} %bitcast.13, f32[1,25600]{1,0:T(1,128)S(1)} %bitcast.22, s32[1,25600]{1,0:T(1,128)S(1)} %bitcast.20, f32[1,3200]{1,0:T(1,128)S(1)} %get-tuple-element.79.trait_ref, ...), custom_call_target="tpu_custom_call" | custom-call | tf_op jit(solution)/shard_map/stats/pallas_call | solution.py:404
  34.7 0.6 %collective-permute-done.14.rest_3_ = bf16[8,2560]{1,0:T(8,128)(2,1)S(1)} collective-permute-done((bf16[8,2560]{1,0:T(8,128)(2,1)S(1)}, bf16[8,2560]{1,0:T(8,128)(2,1)S(1)}, u32[]{:S(2)}, u32[]{:S(2)}) %collective-permute-start.14) | collective-permute-done | bytes 40992 | tf_op jit(solution)/shard_map/ppermute | solution.py:313
  35.4 2.7 %collective-permute-done.13.rest_2_ = bf16[8,2560]{1,0:T(8,128)(2,1)S(1)} collective-permute-done((bf16[8,2560]{1,0:T(8,128)(2,1)S(1)}, bf16[8,2560]{1,0:T(8,128)(2,1)S(1)}, u32[]{:S(2)}, u32[]{:S(2)}) %collective-permute-start.13) | collective-permute-done | bytes 40992 | tf_op jit(solution)/shard_map/ppermute | solution.py:313
  38.2 2.3 %collective-permute-start.16 = (f32[8,128]{1,0:T(8,128)S(1)}, f32[8,128]{1,0:T(8,128)S(1)}, u32[]{:S(2)}, u32[]{:S(2)}) collective-permute-start(f32[8,128]{1,0:T(8,128)S(1)} %pair.1), channel_id=1, source_target_pairs={{0,24},{4,28},{8,16},{12,20},{16,8},{20,12},{24,0},{28,4},{1,25},{... | collective-permute-start | bytes 12296 | tf_op jit(solution)/shard_map/ppermute | solution.py:313
  40.6 0.6 %collective-permute-start.17 = (f32[8,128]{1,0:T(8,128)S(1)}, f32[8,128]{1,0:T(8,128)S(1)}, u32[]{:S(2)}, u32[]{:S(2)}) collective-permute-start(f32[8,128]{1,0:T(8,128)S(1)} %add.3.own_ref), channel_id=1, source_target_pairs={{0,8},{4,20},{8,0},{12,28},{16,24},{20,4},{24,16},{28,12},{1,9},{5... | collective-permute-start | bytes 12296 | tf_op jit(solution)/shard_map/ppermute | solution.py:317
  41.2 1.6 %collective-permute-done.16.common_ref = f32[8,128]{1,0:T(8,128)S(1)} collective-permute-done((f32[8,128]{1,0:T(8,128)S(1)}, f32[8,128]{1,0:T(8,128)S(1)}, u32[]{:S(2)}, u32[]{:S(2)}) %collective-permute-start.16) | collective-permute-done | bytes 4128 | tf_op jit(solution)/shard_map/ppermute | solution.py:313
  42.8 1.4 %collective-permute-done.17.rest_0_ = f32[8,128]{1,0:T(8,128)S(1)} collective-permute-done((f32[8,128]{1,0:T(8,128)S(1)}, f32[8,128]{1,0:T(8,128)S(1)}, u32[]{:S(2)}, u32[]{:S(2)}) %collective-permute-start.17) | collective-permute-done | bytes 4128 | tf_op jit(solution)/shard_map/ppermute | solution.py:317
  44.2 1.2 %collective-permute-done.18.rest_1_ = f32[8,128]{1,0:T(8,128)S(1)} collective-permute-done((f32[8,128]{1,0:T(8,128)S(1)}, f32[8,128]{1,0:T(8,128)S(1)}, u32[]{:S(2)}, u32[]{:S(2)}) %collective-permute-start.18) | collective-permute-done | bytes 4128 | tf_op jit(solution)/shard_map/ppermute | solution.py:313
  45.4 0.7 %final.1 = (f32[6,24]{1,0:T(8,128)}, f32[1,6]{1,0:T(1,128)}, f32[1,6]{1,0:T(1,128)}) custom-call(f32[8,128]{1,0:T(8,128)S(1)} %get-tuple-element.85.count_ref, f32[8,128]{1,0:T(8,128)S(1)} %add.3.own_ref, f32[8,128]{1,0:T(8,128)S(1)} %collective-permute-done.16.common_ref, f32[8,128]{1,0:T(8,128)S(1)} %collective-permute-done.17.rest_0_, ...), custom_call_target="tpu_custom_call" | custom-call | tf_op jit(solution)/shard_map/final/pallas_call | solution.py:404
  (41 shorter events, 4.4 us)
Async XLA Ops:
  5.5 4.1 %collective-permute-start = (bf16[3,8,4992]{2,1,0:T(8,128)(2,1)S(1)}, bf16[3,8,4992]{2,1,0:T(8,128)(2,1)S(1)}, u32[]{:S(2)}, u32[]{:S(2)}) collective-permute-start(bf16[3,8,4992]{2,1,0:T(8,128)(2,1)S(1)} %get-tuple-element.52), channel_id=1, source_target_pairs={{0,4},{4,0},{8,12},{12,8},{16,20},{20,16},{24,28},{28,24},{1,5},{5... | collective-permute-start | bytes 718856 | tf_op jit(solution)/shard_map/ppermute | solution.py:313
  9.8 7.9 %collective-permute-start.2 = (bf16[8,4992]{1,0:T(8,128)(2,1)S(1)}, bf16[8,4992]{1,0:T(8,128)(2,1)S(1)}, u32[]{:S(2)}, u32[]{:S(2)}) collective-permute-start(bf16[8,4992]{1,0:T(8,128)(2,1)S(1)} %get-tuple-element.59), channel_id=1, source_target_pairs={{0,24},{4,28},{8,16},{12,20},{16,8},{20,12},{24,0},{28,4},{1,25},{... | collective-permute-start | bytes 239624 | tf_op jit(solution)/shard_map/ppermute | solution.py:313
  13.3 4.8 %collective-permute-start.3 = (bf16[8,4992]{1,0:T(8,128)(2,1)S(1)}, bf16[8,4992]{1,0:T(8,128)(2,1)S(1)}, u32[]{:S(2)}, u32[]{:S(2)}) collective-permute-start(bf16[8,4992]{1,0:T(8,128)(2,1)S(1)} %get-tuple-element.60), channel_id=1, source_target_pairs={{0,16},{4,20},{8,24},{12,28},{16,0},{20,4},{24,8},{28,12},{1,17},{... | collective-permute-start | bytes 239624 | tf_op jit(solution)/shard_map/ppermute | solution.py:313
  13.8 4.5 %collective-permute-start.4 = (bf16[8,4992]{1,0:T(8,128)(2,1)S(1)}, bf16[8,4992]{1,0:T(8,128)(2,1)S(1)}, u32[]{:S(2)}, u32[]{:S(2)}) collective-permute-start(bf16[8,4992]{1,0:T(8,128)(2,1)S(1)} %get-tuple-element.61), channel_id=1, source_target_pairs={{0,8},{4,12},{8,0},{12,4},{16,24},{20,28},{24,16},{28,20},{1,9},{5... | collective-permute-start | bytes 239624 | tf_op jit(solution)/shard_map/ppermute | solution.py:313
  16.9 1.4 %collective-permute-start.1 = (bf16[1,8,4992]{2,1,0:T(8,128)(2,1)S(1)}, bf16[1,8,4992]{2,1,0:T(8,128)(2,1)S(1)}, u32[]{:S(2)}, u32[]{:S(2)}) collective-permute-start(bf16[1,8,4992]{2,1,0:T(8,128)(2,1)S(1)} %get-tuple-element.58), channel_id=1, source_target_pairs={{0,4},{4,0},{8,12},{12,8},{16,20},{20,16},{24,28},{28,24},{1,5},{5... | collective-permute-start | bytes 239624 | tf_op jit(solution)/shard_map/ppermute | solution.py:313
  17.0 1.3 %copy-start = (f32[25600]{0:T(1024)S(1)}, f32[25600]{0:T(1024)}, u32[]{:S(2)}) copy-start(f32[25600]{0:T(1024)} %param.7) | copy-start | bytes 307204
  17.0 1.3 %copy-start.2 = (f32[25600]{0:T(1024)S(1)}, f32[25600]{0:T(1024)}, u32[]{:S(2)}) copy-start(f32[25600]{0:T(1024)} %param.8) | copy-start | bytes 307204
  17.0 5.1 %copy-start.1 = (s32[25600]{0:T(1024)S(1)}, s32[25600]{0:T(1024)}, u32[]{:S(2)}) copy-start(s32[25600]{0:T(1024)} %param.9) | copy-start | bytes 307204
  18.5 3.7 %collective-permute-start.5 = (bf16[8,4096]{1,0:T(8,128)(2,1)S(1)}, bf16[8,4096]{1,0:T(8,128)(2,1)S(1)}, u32[]{:S(2)}, u32[]{:S(2)}) collective-permute-start(bf16[8,4096]{1,0:T(8,128)(2,1)S(1)} %get-tuple-element.62.refs_4_), channel_id=1, source_target_pairs={{0,4},{4,0},{8,12},{12,8},{16,20},{20,16},{24,28},{28,24},{1,5},{5... | collective-permute-start | bytes 196616 | tf_op jit(solution)/shard_map/ppermute | solution.py:313
  18.6 5.4 %collective-permute-start.6 = (bf16[8,4096]{1,0:T(8,128)(2,1)S(1)}, bf16[8,4096]{1,0:T(8,128)(2,1)S(1)}, u32[]{:S(2)}, u32[]{:S(2)}) collective-permute-start(bf16[8,4096]{1,0:T(8,128)(2,1)S(1)} %get-tuple-element.62.refs_4_), channel_id=1, source_target_pairs={{0,24},{4,28},{8,16},{12,20},{16,8},{20,12},{24,0},{28,4},{1,25},{... | collective-permute-start | bytes 196616 | tf_op jit(solution)/shard_map/ppermute | solution.py:313
  21.5 4.3 %collective-permute-start.7 = (bf16[8,4096]{1,0:T(8,128)(2,1)S(1)}, bf16[8,4096]{1,0:T(8,128)(2,1)S(1)}, u32[]{:S(2)}, u32[]{:S(2)}) collective-permute-start(bf16[8,4096]{1,0:T(8,128)(2,1)S(1)} %get-tuple-element.62.refs_4_), channel_id=1, source_target_pairs={{0,16},{4,20},{8,24},{12,28},{16,0},{20,4},{24,8},{28,12},{1,17},{... | collective-permute-start | bytes 196616 | tf_op jit(solution)/shard_map/ppermute | solution.py:313
  22.0 4.4 %collective-permute-start.9 = (bf16[8,4096]{1,0:T(8,128)(2,1)S(1)}, bf16[8,4096]{1,0:T(8,128)(2,1)S(1)}, u32[]{:S(2)}, u32[]{:S(2)}) collective-permute-start(bf16[8,4096]{1,0:T(8,128)(2,1)S(1)} %get-tuple-element.62.refs_4_), channel_id=1, source_target_pairs={{0,8},{4,12},{8,0},{12,4},{16,24},{20,28},{24,16},{28,20},{1,9},{5... | collective-permute-start | bytes 196616 | tf_op jit(solution)/shard_map/ppermute | solution.py:313
  24.1 3.5 %collective-permute-start.11 = (bf16[8,4096]{1,0:T(8,128)(2,1)S(1)}, bf16[8,4096]{1,0:T(8,128)(2,1)S(1)}, u32[]{:S(2)}, u32[]{:S(2)}) collective-permute-start(bf16[8,4096]{1,0:T(8,128)(2,1)S(1)} %relay.3.refs_3_), channel_id=1, source_target_pairs={{0,4},{4,0},{8,12},{12,8},{16,20},{20,16},{24,28},{28,24},{1,5},{5... | collective-permute-start | bytes 196616 | tf_op jit(solution)/shard_map/ppermute | solution.py:313
  26.4 1.8 %collective-permute-start.10 = (bf16[8,4096]{1,0:T(8,128)(2,1)S(1)}, bf16[8,4096]{1,0:T(8,128)(2,1)S(1)}, u32[]{:S(2)}, u32[]{:S(2)}) collective-permute-start(bf16[8,4096]{1,0:T(8,128)(2,1)S(1)} %relay.5.refs_3_), channel_id=1, source_target_pairs={{0,4},{4,0},{8,12},{12,8},{16,20},{20,16},{24,28},{28,24},{1,5},{5... | collective-permute-start | bytes 196616 | tf_op jit(solution)/shard_map/ppermute | solution.py:313
  26.5 1.8 %collective-permute-start.8 = (bf16[8,4096]{1,0:T(8,128)(2,1)S(1)}, bf16[8,4096]{1,0:T(8,128)(2,1)S(1)}, u32[]{:S(2)}, u32[]{:S(2)}) collective-permute-start(bf16[8,4096]{1,0:T(8,128)(2,1)S(1)} %relay.4.refs_3_), channel_id=1, source_target_pairs={{0,4},{4,0},{8,12},{12,8},{16,20},{20,16},{24,28},{28,24},{1,5},{5... | collective-permute-start | bytes 196616 | tf_op jit(solution)/shard_map/ppermute | solution.py:313
  29.4 5.9 %collective-permute-start.14 = (bf16[8,2560]{1,0:T(8,128)(2,1)S(1)}, bf16[8,2560]{1,0:T(8,128)(2,1)S(1)}, u32[]{:S(2)}, u32[]{:S(2)}) collective-permute-start(bf16[8,2560]{1,0:T(8,128)(2,1)S(1)} %get-tuple-element.78.flat_ref.rest_0_), channel_id=1, source_target_pairs={{0,3},{1,2},{2,1},{3,0},{4,7},{5,6},{6,5},{7,4},{8,11},{9,10},{10,... | collective-permute-start | bytes 122888 | tf_op jit(solution)/shard_map/ppermute | solution.py:313
  33.1 4.9 %collective-permute-start.13 = (bf16[8,2560]{1,0:T(8,128)(2,1)S(1)}, bf16[8,2560]{1,0:T(8,128)(2,1)S(1)}, u32[]{:S(2)}, u32[]{:S(2)}) collective-permute-start(bf16[8,2560]{1,0:T(8,128)(2,1)S(1)} %get-tuple-element.78.flat_ref.rest_0_), channel_id=1, source_target_pairs={{0,2},{1,3},{2,0},{3,1},{4,6},{5,7},{6,4},{7,5},{8,10},{9,11},{10,... | collective-permute-start | bytes 122888 | tf_op jit(solution)/shard_map/ppermute | solution.py:313
  33.1 4.9 %collective-permute-start.12 = (bf16[8,2560]{1,0:T(8,128)(2,1)S(1)}, bf16[8,2560]{1,0:T(8,128)(2,1)S(1)}, u32[]{:S(2)}, u32[]{:S(2)}) collective-permute-start(bf16[8,2560]{1,0:T(8,128)(2,1)S(1)} %get-tuple-element.78.flat_ref.rest_0_), channel_id=1, source_target_pairs={{0,1},{1,0},{2,3},{3,2},{4,5},{5,4},{6,7},{7,6},{8,9},{9,8},{10,11... | collective-permute-start | bytes 122888 | tf_op jit(solution)/shard_map/ppermute | solution.py:313
  38.2 2.4 %collective-permute-start.15 = (f32[8,128]{1,0:T(8,128)S(1)}, f32[8,128]{1,0:T(8,128)S(1)}, u32[]{:S(2)}, u32[]{:S(2)}) collective-permute-start(f32[8,128]{1,0:T(8,128)S(1)} %pair.1), channel_id=1, source_target_pairs={{0,4},{4,0},{8,12},{12,8},{16,20},{20,16},{24,28},{28,24},{1,5},{5... | collective-permute-start | bytes 12296 | tf_op jit(solution)/shard_map/ppermute | solution.py:313
  38.2 4.6 %collective-permute-start.16 = (f32[8,128]{1,0:T(8,128)S(1)}, f32[8,128]{1,0:T(8,128)S(1)}, u32[]{:S(2)}, u32[]{:S(2)}) collective-permute-start(f32[8,128]{1,0:T(8,128)S(1)} %pair.1), channel_id=1, source_target_pairs={{0,24},{4,28},{8,16},{12,20},{16,8},{20,12},{24,0},{28,4},{1,25},{... | collective-permute-start | bytes 12296 | tf_op jit(solution)/shard_map/ppermute | solution.py:313
  40.6 3.6 %collective-permute-start.17 = (f32[8,128]{1,0:T(8,128)S(1)}, f32[8,128]{1,0:T(8,128)S(1)}, u32[]{:S(2)}, u32[]{:S(2)}) collective-permute-start(f32[8,128]{1,0:T(8,128)S(1)} %add.3.own_ref), channel_id=1, source_target_pairs={{0,8},{4,20},{8,0},{12,28},{16,24},{20,4},{24,16},{28,12},{1,9},{5... | collective-permute-start | bytes 12296 | tf_op jit(solution)/shard_map/ppermute | solution.py:317
  42.8 1.4 %collective-permute-start.19 = (f32[8,128]{1,0:T(8,128)S(1)}, f32[8,128]{1,0:T(8,128)S(1)}, u32[]{:S(2)}, u32[]{:S(2)}) collective-permute-start(f32[8,128]{1,0:T(8,128)S(1)} %collective-permute-done.16.common_ref), channel_id=1, source_target_pairs={{0,4},{4,0},{8,12},{12,8},{16,20},{20,16},{24,28},{28,24},{1,5},{5... | collective-permute-start | bytes 12296 | tf_op jit(solution)/shard_map/ppermute | solution.py:313
  44.2 1.2 %collective-permute-start.18 = (f32[8,128]{1,0:T(8,128)S(1)}, f32[8,128]{1,0:T(8,128)S(1)}, u32[]{:S(2)}, u32[]{:S(2)}) collective-permute-start(f32[8,128]{1,0:T(8,128)S(1)} %collective-permute-done.17.rest_0_), channel_id=1, source_target_pairs={{0,4},{4,0},{8,12},{12,8},{16,20},{20,16},{24,28},{28,24},{1,5},{5... | collective-permute-start | bytes 12296 | tf_op jit(solution)/shard_map/ppermute | solution.py:313

commit v2 on v1

--- a/solution.py
+++ b/solution.py
@@ -50,6 +50,11 @@
     return value[:SUBLANES], low
 
 
+def halves_of(block):
+    first = -(-block // (2 * LANES)) * LANES
+    return (0, first), (first, block - first)
+
+
 def unpack_sums(value):
     span = value.shape[1] * 2 // 3
     low = value[:, span:]
@@ -65,37 +70,47 @@
         raw_in = rest.pop(0) if taken else None
         left_ref, kept_ref, sums_ref, local_ref = rest[:4]
         rest = rest[4:]
-    raw_out = rest.pop(0) if given is not None else None
+    raw_out = rest.pop(0) if given else None
+    buffer, arrived, total_ref = rest[:3]
+    rest = rest[3:]
+    raw_arrived = rest.pop(0) if given else None
     slots, rows, block = kept_ref.shape
-    fetched = slots - taken
     devices = -(-snps // block)
     tail = snps - (devices - 1) * block
-    span = sums_ref.shape[2] * 2 // 3
-
-    def copy(distance, target, semaphore, width):
-        start = pl.multiple_of((lax.axis_index("ind") ^ distance) * block, LANES)
-        return pltpu.make_async_copy(
-            geno_ref.at[:, pl.ds(start, width)], target.at[:, pl.ds(0, width)], semaphore
-        )
-
-    def whole_or_tail(distance, target, semaphore, act):
+    span = total_ref.shape[1]
+    halves = halves_of(block)
+
+    def move(distance, target, semaphore, half, act):
+        first, width = halves[half]
+        owner = lax.axis_index("ind") ^ distance
+
+        def copy(size):
+            start = pl.multiple_of(owner * block + first, LANES)
+            act(
+                pltpu.make_async_copy(
+                    geno_ref.at[:, pl.ds(start, size)],
+                    target.at[:, pl.ds(first, size)],
+                    semaphore.at[half],
+                )
+            )
+
         if tail == block:
-            act(copy(distance, target, semaphore, block))
+            copy(width)
         else:
-            last = (lax.axis_index("ind") ^ distance) == devices - 1
-            pl.when(last)(lambda: act(copy(distance, target, semaphore, tail)))
-            pl.when(jnp.logical_not(last))(lambda: act(copy(distance, target, semaphore, block)))
-
-    if fetched:
-        buffer, arrived = rest[:2]
-        rest = rest[2:]
-
-        def fetch(index, act):
-            distance = distances[0] - 2 * (index + taken)
-            whole_or_tail(distance, buffer.at[index], arrived.at[index], act)
-
-    if raw_out is not None:
-        raw_arrived = rest.pop(0)
+            last = owner == devices - 1
+            short = min(max(tail - first, 0), width)
+            pl.when(jnp.logical_not(last))(lambda: copy(width))
+            if short:
+                pl.when(last)(lambda: copy(short))
+
+    def fetch(slot, half, act):
+        move(distances[0] - 2 * slot, buffer.at[slot], arrived.at[slot], half, act)
+
+    def start(copy):
+        copy.start()
+
+    def wait(copy):
+        copy.wait()
 
     if opening:
         bits, trait, small = rest[:3]
@@ -103,10 +118,14 @@
         trait_copy = pltpu.make_async_copy(trait_ref, trait, small.at[1])
         bits_copy.start()
         trait_copy.start()
-    if fetched:
-        pl.loop(0, fetched)(lambda index: fetch(index, lambda c: c.start()))
-    if raw_out is not None:
-        whole_or_tail(given, raw_out, raw_arrived, lambda c: c.start())
+    for half in range(taken, 2):
+        fetch(0, half, start)
+    for slot in range(1, slots):
+        fetch(slot, 0, start)
+        fetch(slot, 1, start)
+    if given:
+        for half in range(given[1]):
+            move(given[0], raw_out, raw_arrived, half, start)
     if opening:
         bits_copy.wait()
         trait_copy.wait()
@@ -123,38 +142,49 @@
         high = value[TRAIT : TRAIT + 1]
         return jnp.where(row == TRAIT + 1, high - high.astype(BF16).astype(F32), value)
 
-    ends = jnp.broadcast_to(with_low(base), (ROWS, span - block))
-
-    def work(slot, source):
+    total_ref[:, block:] = jnp.broadcast_to(with_low(base), (ROWS, span - block))
+
+    def work(slot, half, source):
+        first, width = halves[half]
+        lanes = slice(first, first + width)
         squares = []
-        for at in range(0, block, PIECE):
-            lanes = slice(at, min(at + PIECE, block))
+        for at in range(first, first + width, PIECE):
+            piece = slice(at, min(at + PIECE, first + width))
             square = 0.0
             for r in range(0, rows, 16):
-                dose = source[r : r + 16, lanes].astype(F32)
-                kept_ref[slot, r : r + 16, lanes] = dose.astype(BF16)
+                dose = source[r : r + 16, piece].astype(F32)
+                kept_ref[slot, r : r + 16, piece] = dose.astype(BF16)
                 dose = dose * dose
                 square = square + (dose[:8] + dose[8:])
             squares.append(jnp.sum(square, axis=0, keepdims=True))
-        total = jnp.dot(left, kept_ref[slot], preferred_element_type=F32) - base
+        total = jnp.dot(left, kept_ref[slot, :, lanes], preferred_element_type=F32) - base
         ones = total[ONES : ONES + 1]
-        local_ref[slot, 0:1] = ones
-        local_ref[slot, 1:2] = jnp.concatenate(squares, axis=1) - 2.0 * ones - rows
-        high, low = pack_sums(jnp.concatenate([with_low(total), ends], axis=1))
+        local_ref[slot, 0:1, lanes] = ones
+        local_ref[slot, 1:2, lanes] = jnp.concatenate(squares, axis=1) - 2.0 * ones - rows
+        total_ref[:, lanes] = with_low(total)
+
+    def close(slot):
+        high, low = pack_sums(total_ref[...])
         sums_ref[slot, :, :span] = high.astype(BF16)
         sums_ref[slot, :, span:] = low.astype(BF16)
 
-    if taken:
-        work(0, raw_in)
-    if fetched:
-
-        @pl.loop(0, fetched)
-        def _(index):
-            fetch(index, lambda c: c.wait())
-            work(index + taken, buffer.at[index])
-
-    if raw_out is not None:
-        whole_or_tail(given, raw_out, raw_arrived, lambda c: c.wait())
+    for half in range(2):
+        if half >= taken:
+            fetch(0, half, wait)
+        work(0, half, raw_in if half < taken else buffer.at[0])
+    close(0)
+    if slots > 1:
+
+        @pl.loop(1, slots)
+        def _(slot):
+            for half in range(2):
+                fetch(slot, half, wait)
+                work(slot, half, buffer.at[slot])
+            close(slot)
+
+    if given:
+        for half in range(given[1]):
+            move(given[0], raw_out, raw_arrived, half, wait)
 
 
 def cores_kernel(left_ref, here_ref, away_ref, *outs):
@@ -168,8 +198,8 @@
     out_ref[...] = value_ref[...]
 
 
-def weights_kernel(mean_ref, scale_ref, own_ref, near_ref, *refs):
-    parts, (u_ref, trait_ref) = refs[:-2], refs[-2:]
+def weights_kernel(mean_ref, scale_ref, own_ref, *refs):
+    parts, (near_ref, u_ref, trait_ref) = refs[:-3], refs[-3:]
     block = trait_ref.shape[1]
     width = u_ref.shape[1] - block
     here = pl.ds(pl.multiple_of(lax.axis_index("ind") * block, LANES), block)
@@ -222,20 +252,29 @@
         field_ref[b] = flat[:own_bins, b * rows : (b + 1) * rows].astype(BF16)
 
 
+def labels_kernel(own_bins, token_ref, mean_ref, label_ref, split_ref, count_ref):
+    mean = mean_ref[...]
+    high = mean.astype(BF16).astype(F32)
+    middle = (mean - high).astype(BF16).astype(F32)
+    row = rows_iota(ROWS)
+    split = jnp.where(row == 0, high, jnp.where(row == 1, middle, mean - high - middle))
+    split_ref[...] = jnp.where(row < 3, split, 0.0).astype(BF16)
+    member = label_ref[...] - lax.axis_index("bin") * own_bins == rows_iota(SUBLANES)
+    number = jnp.sum(jnp.where(member, 1.0, 0.0), axis=1, keepdims=True)
+    count_ref[...] = jnp.broadcast_to(number, count_ref.shape)
+
+
 def field_kernel(own_bins, blocks, sources, started, last, *refs):
     refs = list(refs)
-    mean_ref, label_ref = refs[:2]
+    split_ref, label_ref = refs[:2]
     kept_refs, refs = refs[2 : 2 + sources], refs[2 + sources :]
     u_refs, refs = refs[: len(blocks)], refs[len(blocks) :]
     rows, block = kept_refs[0].shape[1:]
     bins = rows_iota(SUBLANES)
     if started:
-        acc, offset, number = [ref[...] for ref in refs[:3]]
-        refs = refs[3:]
+        acc, refs = refs[0][...], refs[1:]
     else:
-        acc = jnp.zeros((rows, PROBES * SUBLANES), F32)
-        offset = jnp.zeros((PROBES * SUBLANES, LANES), F32)
-        number = jnp.zeros((SUBLANES, LANES), F32)
+        acc = jnp.zeros((rows + ROWS, PROBES * SUBLANES), F32)
     for index, (slot, distance) in enumerate(blocks):
         start = (lax.axis_index("ind") ^ distance) * block
         u = u_refs[index][...].astype(F32)
@@ -248,32 +287,28 @@
             here = pl.ds(pl.multiple_of(start + at, LANES), width)
             member = label_ref[:, here] - lax.axis_index("bin") * own_bins == bins
             member = member & (bins < own_bins)
-            mean = mean_ref[:, here]
             spread = [jnp.where(member, line[:, at : at + width], 0.0) for line in lines]
-            offset += jnp.concatenate([fold_lanes(value * mean) for value in spread], axis=0)
-            number += fold_lanes(jnp.where(member, 1.0, 0.0))
+            kept = kept_refs[index if sources > 1 else 0][slot, :, at : at + width]
             acc += lax.dot_general(
-                kept_refs[index if sources > 1 else 0][slot, :, at : at + width],
+                jnp.concatenate([kept, split_ref[:, here]], axis=0),
                 jnp.concatenate(spread, axis=0).astype(BF16),
                 (((1,), (1,)), ((), ())),
                 preferred_element_type=F32,
             )
     if not last:
-        for ref, value in zip(refs, (acc, offset, number)):
-            ref[...] = value
+        refs[0][...] = acc
         return
-    flat_ref, count_ref = refs
+    count_ref, flat_ref = refs
+    acc = acc[:rows] - jnp.sum(acc[rows:], axis=0, keepdims=True)
     acc = jnp.concatenate([acc, jnp.zeros((rows, LANES - acc.shape[1]), F32)], axis=1)
-    acc = jnp.transpose(acc)[: PROBES * SUBLANES] - jnp.sum(offset, axis=1, keepdims=True)
-    number = jnp.sum(number, axis=1, keepdims=True)
-    count_ref[...] = jnp.broadcast_to(number, count_ref.shape)
-    inverse = 1.0 / jnp.maximum(number, 1.0)
+    acc = jnp.transpose(acc)
+    inverse = 1.0 / jnp.maximum(count_ref[:, :1], 1.0)
     flat = [acc[b * SUBLANES : (b + 1) * SUBLANES] * inverse for b in range(PROBES)]
     flat_ref[...] = jnp.concatenate(flat, axis=1).astype(BF16)
 
 
 def pair_kernel(stats_ref, *rest):
-    flats, out_ref = rest[:-1], rest[-1]
+    flats, out_ref = rest[-2::-1], rest[-1]
     everyone = [flat[...].astype(F32) for flat in flats]
     everyone += [jnp.zeros_like(everyone[0])] * (LANES // SUBLANES - len(flats))
     out_ref[...] = stats_ref[...] + lax.dot_general(
@@ -360,12 +395,10 @@
         for value in (genotype, probe_bits, phenotype)
     ]
 
-    def moments(distances, given, extra, name):
+    def moments(distances, taken, given, extra, name):
         slots = len(distances)
         opening = extra[0] is probe_bits
-        taken = int(not opening and extra[0] is not None)
         extra = [value for value in extra if value is not None]
-        fetched = slots - taken
         out_shape = [
             jax.ShapeDtypeStruct((slots, rows, block), BF16),
             jax.ShapeDtypeStruct((slots, SUBLANES, span * 3 // 2), BF16),
@@ -373,13 +406,15 @@
         ]
         if opening:
             out_shape.append(jax.ShapeDtypeStruct((ROWS, rows), F32))
-        if given is not None:
+        if given:
             out_shape.append(jax.ShapeDtypeStruct((rows, block), jnp.int32))
-        scratch = []
-        if fetched:
-            scratch += [VMEM((fetched, rows, block), jnp.int32), pltpu.SemaphoreType.DMA((fetched,))]
-        if given is not None:
-            scratch.append(pltpu.SemaphoreType.DMA)
+        scratch = [
+            VMEM((slots, rows, block), jnp.int32),
+            pltpu.SemaphoreType.DMA((slots, 2)),
+            VMEM((ROWS, span), F32),
+        ]
+        if given:
+            scratch.append(pltpu.SemaphoreType.DMA((2,)))
         if opening:
             scratch += [
                 VMEM(probe_bits.shape, jnp.int32),
@@ -412,10 +447,10 @@
         )(*operands)
 
     kept_away, away, local_away, left, raw = moments(
-        away_order, here_order[0], (probe_bits, phenotype), "moments_away"
+        away_order, 0, (here_order[0], 2), (probe_bits, phenotype), "moments_away"
     )
     away = swap(away, "ind", n, 1)
-    kept_here, here, local_here = moments(here_order, None, (raw, left), "moments_here")
+    kept_here, here, local_here = moments(here_order, 2, None, (raw, left), "moments_here")
     packed = jax.ShapeDtypeStruct((SUBLANES, span * 3 // 2), BF16)
     *sums, left = plain(
         cores_kernel,
@@ -424,13 +459,13 @@
         "cores",
     )
     sums = [swap(value, "ind", n, d) for value, d in zip(sums, here_order)]
-    kept_near, near, local_near, raw = moments([1], 0, (None, left), "moments_near")
+    kept_near, near, local_near, raw = moments([1], 0, (0, 1), (None, left), "moments_near")
     near = swap(near, "ind", n, 1)
-    kept_own, own, local_own = moments([0], None, (raw, left), "moments_own")
+    kept_own, own, local_own = moments([0], 1, None, (raw, left), "moments_own")
 
     u, trait = plain(
         weights_kernel,
-        (mean, scale, own, near, *sums),
+        (mean, scale, own, *sums, near),
         [
             jax.ShapeDtypeStruct((SUBLANES, folded), BF16),
             jax.ShapeDtypeStruct((1, block), F32),
@@ -439,37 +474,42 @@
     )
 
     number_shape = jax.ShapeDtypeStruct((SUBLANES, LANES), F32)
-    term_shape = [
-        jax.ShapeDtypeStruct((rows, PROBES * SUBLANES), F32),
-        jax.ShapeDtypeStruct((PROBES * SUBLANES, LANES), F32),
-        number_shape,
-    ]
-    end_shape = [jax.ShapeDtypeStruct((SUBLANES, PROBES * rows), BF16), number_shape]
+    term_shape = jax.ShapeDtypeStruct((rows + ROWS, PROBES * SUBLANES), F32)
+    flat_shape = jax.ShapeDtypeStruct((SUBLANES, PROBES * rows), BF16)
+    split, number = plain(
+        functools.partial(labels_kernel, own_bins),
+        (trait, mean, label),
+        [jax.ShapeDtypeStruct((ROWS, whole), BF16), number_shape],
+        "labels",
+    )
 
     def fields(kept, blocks, us, terms, last=False):
+        terms = ([terms] if terms is not None else []) + ([number] if last else [])
+        started = len(terms) > last
         return plain(
-            functools.partial(field_kernel, own_bins, blocks, len(kept), bool(terms), last),
-            (mean, label, *kept, *us, *terms),
-            end_shape if last else term_shape,
+            functools.partial(field_kernel, own_bins, blocks, len(kept), started, last),
+            (split, label, *kept, *us, *terms),
+            [flat_shape if last else term_shape],
             "field",
-            cost_estimate=cost(1, 1),
-        )
+            cost_estimate=cost(1, 2 * MIB),
+        )[0]
 
     u_near = swap(u, "ind", n, 1)
     u_here = [swap(u, "ind", n, d) for d in here_order]
-    terms = fields([kept_own, kept_near], [(0, 0), (0, 1)], [u, u_near], [])
+    terms = fields([kept_own, kept_near], [(0, 0), (0, 1)], [u, u_near], None)
     u_away = []
     for slot, (distance, value) in enumerate(zip(here_order, u_here)):
         shape = [jax.ShapeDtypeStruct(value.shape, value.dtype)]
-        (value,) = plain(relay_kernel, (terms[2], value), shape, "relay")
+        (value,) = plain(relay_kernel, (terms, value), shape, "relay")
         u_away.append(swap(value, "ind", n, 1))
         terms = fields([kept_here], [(slot, distance)], [value], terms)
     blocks = list(enumerate(away_order))
     middle = (chips - 1) // 2
     terms = fields([kept_away], blocks[:middle], u_away[:middle], terms)
-    flat, number = fields([kept_away], blocks[middle:], u_away[middle:], terms, last=True)
-
-    flats = [flat] + [swap(flat, "bin", n_bin, d) for d in range(1, n_bin)]
+    flat = fields([kept_away], blocks[middle:], u_away[middle:], terms, last=True)
+
+    flats = [swap(flat, "bin", n_bin, d) for d in range(n_bin - 1, 0, -1)]
+    flats = [flat] + flats[::-1]
     order = (rows, (away_order, here_order, [1], [0]))
     stats, field = plain(
         functools.partial(stats_kernel, own_bins, order),
@@ -477,7 +517,7 @@
         [number_shape, jax.ShapeDtypeStruct((PROBES, own_bins, rows), BF16)],
         "stats",
     )
-    (part,) = plain(pair_kernel, (stats, *flats), [number_shape], "pair")
+    (part,) = plain(pair_kernel, (stats, *flats[::-1]), [number_shape], "pair")
     pairs, common = chosen_pairs(list(range(2, n, 2)))
     part_common = swap(part, "ind", n, common)
     part = part + swap(part, "ind", n, 1)

time: 46.3 us -> 49.7 us (1.073)
  Pallas kernels: 18.7 us -> 22 us
    pallas_call x4, Pallas kernels: 12.1 us -> 14.2 us  [moments(): pl.pallas_call(functools.partial(moments_kernel, snps, distances, opening...]
    pallas_call x14 -> x15, Pallas kernels: 6.6 us -> 7.74 us  [plain(): pl.pallas_call(kernel, in_specs=[in_vmem()] * len(operands), out_specs=[i...]
  transfers between devices with their start and end apart: 20 -> 20, of which waited for: 9 -> 6; matrix products, arithmetic and copies ran while one was open for 0% -> 0% of each run, Pallas kernels for 25% -> 28%
where the time goes in v2:
time: 49.7 us; the launch traced here: 49.4 us
  Pallas kernels  22 us (44%)
  starting transfers between devices  16.7 us (34%)
  waiting for transfers between devices  9.86 us (20%)
  between operations  0.89 us (2%)
    ppermute x19, starting transfers between devices, swap(): return lax.ppermute(value, axis, [(i, i ^ distance) for i in range(size)])  16.2 us
    pallas_call x4, Pallas kernels, moments(): pl.pallas_call(functools.partial(moments_kernel, snps, distances, opening...  14.2 us
    ppermute x19, waiting for transfers between devices, swap(): return lax.ppermute(value, axis, [(i, i ^ distance) for i in range(size)])  8.61 us
    pallas_call x15, Pallas kernels, plain(): pl.pallas_call(kernel, in_specs=[in_vmem()] * len(operands), out_specs=[i...  7.74 us
    ppermute x1, waiting for transfers between devices, swap_mixed(): lax.ppermute(value, 'ind', [(i, i ^ pair[i % 2]) for i in range(size)])  1.25 us
  transfers between devices with their start and end apart: 20, of which 6 were waited for; matrix products, arithmetic and copies ran while one was open for 0% of the time, Pallas kernels for 28%

profile of v2, /device:TPU:0, one launch (start us, length us, event | category | flops | bytes accessed | tf_op | source)
XLA Modules:
  0.0 49.4 jit_solution(16515161187318101031)
XLA Ops:
  0.6 5.9 %moments_away.1 = (bf16[3,256,3200]{2,1,0:T(8,128)(2,1)S(1)}, bf16[3,8,4992]{2,1,0:T(8,128)(2,1)S(1)}, f32[3,2,3200]{2,1,0:T(2,128)S(1)}, f32[16,256]{1,0:T(8,128)S(1)}, s32[256,3200]{1,0:T(8,128)S(1)}) custom-call(s32[256,25600]{1,0:T(8,128)} %geno_ref.7, s32[10,256]{1,0:T(8,128)} %rest_0_.1, bf16[256]{0:T(256)(128)(2,1)} %rest_1_.1), custom_call_target="tpu_custom_call" | custom-call | flops 1 | bytes 9830400 | tf_op jit(solution)/shard_map/moments_away/pallas_call | solution.py:424
  7.1 3.8 %moments_here.1 = (bf16[3,256,3200]{2,1,0:T(8,128)(2,1)S(1)}, bf16[3,8,4992]{2,1,0:T(8,128)(2,1)S(1)}, f32[3,2,3200]{2,1,0:T(2,128)S(1)}) custom-call(s32[256,25600]{1,0:T(8,128)} %geno_ref.7, s32[256,3200]{1,0:T(8,128)S(1)} %get-tuple-element.33.rest_0_, f32[16,256]{1,0:T(8,128)S(1)} %get-tuple-element.32.rest_1_.left_ref), custom_call_target="tpu_custom_call" | custom-call | flops 1 | bytes 9830400 | tf_op jit(solution)/shard_map/moments_here/pallas_call | solution.py:424
  11.0 3.5 %collective-permute-start.1 = (bf16[8,4992]{1,0:T(8,128)(2,1)S(1)}, bf16[8,4992]{1,0:T(8,128)(2,1)S(1)}, u32[]{:S(2)}, u32[]{:S(2)}) collective-permute-start(bf16[8,4992]{1,0:T(8,128)(2,1)S(1)} %get-tuple-element.39), channel_id=1, source_target_pairs={{0,24},{4,28},{8,16},{12,20},{16,8},{20,12},{24,0},{28,4},{1,25},{... | collective-permute-start | bytes 239624 | tf_op jit(solution)/shard_map/ppermute | solution.py:348
  15.2 2.5 %moments_near.1 = (bf16[1,256,3200]{2,1,0:T(8,128)(2,1)S(1)}, bf16[1,8,4992]{2,1,0:T(8,128)(2,1)S(1)}, f32[1,2,3200]{2,1,0:T(2,128)S(1)}, s32[256,3200]{1,0:T(8,128)S(1)}) custom-call(s32[256,25600]{1,0:T(8,128)} %geno_ref.7, f32[16,256]{1,0:T(8,128)S(1)} %get-tuple-element.36.rest_0_.rest_1_), custom_call_target="tpu_custom_call" | custom-call | flops 1 | bytes 1 | tf_op jit(solution)/shard_map/moments_near/pallas_call | solution.py:424
  17.8 2.0 %moments_own.1 = (bf16[1,256,3200]{2,1,0:T(8,128)(2,1)S(1)}, bf16[1,8,4992]{2,1,0:T(8,128)(2,1)S(1)}, f32[1,2,3200]{2,1,0:T(2,128)S(1)}) custom-call(s32[256,25600]{1,0:T(8,128)} %geno_ref.7, s32[256,3200]{1,0:T(8,128)S(1)} %get-tuple-element.37.rest_0_, f32[16,256]{1,0:T(8,128)S(1)} %get-tuple-element.36.rest_0_.rest_1_), custom_call_target="tpu_custom_call" | custom-call | flops 1 | bytes 1 | tf_op jit(solution)/shard_map/moments_own/pallas_call | solution.py:424
  20.5 2.8 %collective-permute-start.6 = (bf16[8,4096]{1,0:T(8,128)(2,1)S(1)}, bf16[8,4096]{1,0:T(8,128)(2,1)S(1)}, u32[]{:S(2)}, u32[]{:S(2)}) collective-permute-start(bf16[8,4096]{1,0:T(8,128)(2,1)S(1)} %get-tuple-element.49.refs_4_), channel_id=1, source_target_pairs={{0,24},{4,28},{8,16},{12,20},{16,8},{20,12},{24,0},{28,4},{1,25},{... | collective-permute-start | bytes 196616 | tf_op jit(solution)/shard_map/ppermute | solution.py:348
  24.0 1.0 %labels.1 = (bf16[16,25600]{1,0:T(8,128)(2,1)S(1)}, f32[8,128]{1,0:T(8,128)S(1)}) custom-call(f32[1,3200]{1,0:T(1,128)S(1)} %get-tuple-element.43.token_ref.trait_ref, f32[1,25600]{1,0:T(1,128)S(1)} %bitcast.15, s32[1,25600]{1,0:T(1,128)S(1)} %bitcast.6), custom_call_target="tpu_custom_call" | custom-call | tf_op jit(solution)/shard_map/labels/pallas_call | solution.py:439
  25.0 1.1 %field.6.token_ref.refs_4_ = f32[272,80]{1,0:T(8,128)S(1)} custom-call(bf16[16,25600]{1,0:T(8,128)(2,1)S(1)} %get-tuple-element.44.refs_0_, s32[1,25600]{1,0:T(1,128)S(1)} %bitcast.7, bf16[1,256,3200]{2,1,0:T(8,128)(2,1)S(1)} %get-tuple-element.47.refs_2_, bf16[1,256,3200]{2,1,0:T(8,128)(2,1)S(1)} %get-tuple-element.48.refs_3_, ...), custom_call_target="tpu_custom_call" | custom-call | flops 1 | bytes 2097152 | tf_op jit(solution)/shard_map/field/pallas_call | solution.py:439
  26.2 0.6 %field.7.token_ref.refs_4_ = f32[272,80]{1,0:T(8,128)S(1)} custom-call(bf16[16,25600]{1,0:T(8,128)(2,1)S(1)} %get-tuple-element.44.refs_0_, s32[1,25600]{1,0:T(1,128)S(1)} %bitcast.8, bf16[3,256,3200]{2,1,0:T(8,128)(2,1)S(1)} %get-tuple-element.46.refs_2_, bf16[8,4096]{1,0:T(8,128)(2,1)S(1)} %relay.3.refs_3_, f32[272,80]{1,0:T(8,128)S(1)} %field.6.token_ref.refs_4_), custom_call_target="tpu_custom_call" | custom-call | flops 1 | bytes 2097152 | tf_op jit(solution)/shard_map/field/pallas_call | solution.py:439
  26.8 0.8 %collective-permute-done.7.value_ref = bf16[8,4096]{1,0:T(8,128)(2,1)S(1)} collective-permute-done((bf16[8,4096]{1,0:T(8,128)(2,1)S(1)}, bf16[8,4096]{1,0:T(8,128)(2,1)S(1)}, u32[]{:S(2)}, u32[]{:S(2)}) %collective-permute-start.7) | collective-permute-done | bytes 65568 | tf_op jit(solution)/shard_map/ppermute | solution.py:348
  27.7 0.6 %field.8.token_ref.refs_4_ = f32[272,80]{1,0:T(8,128)S(1)} custom-call(bf16[16,25600]{1,0:T(8,128)(2,1)S(1)} %get-tuple-element.44.refs_0_, s32[1,25600]{1,0:T(1,128)S(1)} %bitcast.9, bf16[3,256,3200]{2,1,0:T(8,128)(2,1)S(1)} %get-tuple-element.46.refs_2_, bf16[8,4096]{1,0:T(8,128)(2,1)S(1)} %relay.4.refs_3_, f32[272,80]{1,0:T(8,128)S(1)} %field.7.token_ref.refs_4_), custom_call_target="tpu_custom_call" | custom-call | flops 1 | bytes 2097152 | tf_op jit(solution)/shard_map/field/pallas_call | solution.py:439
  29.0 0.6 %field.9.refs_4_ = f32[272,80]{1,0:T(8,128)S(1)} custom-call(bf16[16,25600]{1,0:T(8,128)(2,1)S(1)} %get-tuple-element.44.refs_0_, s32[1,25600]{1,0:T(1,128)S(1)} %bitcast.10, bf16[3,256,3200]{2,1,0:T(8,128)(2,1)S(1)} %get-tuple-element.46.refs_2_, bf16[8,4096]{1,0:T(8,128)(2,1)S(1)} %relay.5.refs_3_, f32[272,80]{1,0:T(8,128)S(1)} %field.8.token_ref.refs_4_), custom_call_target="tpu_custom_call" | custom-call | flops 1 | bytes 2097152 | tf_op jit(solution)/shard_map/field/pallas_call | solution.py:439
  29.6 0.6 %field.10.refs_5_ = f32[272,80]{1,0:T(8,128)S(1)} custom-call(bf16[16,25600]{1,0:T(8,128)(2,1)S(1)} %get-tuple-element.44.refs_0_, s32[1,25600]{1,0:T(1,128)S(1)} %bitcast.11, bf16[3,256,3200]{2,1,0:T(8,128)(2,1)S(1)} %get-tuple-element.45.refs_2_, bf16[8,4096]{1,0:T(8,128)(2,1)S(1)} %collective-permute-done.11.refs_3_, f32[272,80]{1,0:T(8,128)S(1)} %field.9.refs_4_), custom_call_target="tpu_custom_call" | custom-call | flops 1 | bytes 2097152 | tf_op jit(solution)/shard_map/field/pallas_call | solution.py:439
  30.3 1.2 %field.11.flat_ref.rest_3_ = bf16[8,2560]{1,0:T(8,128)(2,1)S(1)} custom-call(bf16[16,25600]{1,0:T(8,128)(2,1)S(1)} %get-tuple-element.44.refs_0_, s32[1,25600]{1,0:T(1,128)S(1)} %bitcast.12, bf16[3,256,3200]{2,1,0:T(8,128)(2,1)S(1)} %get-tuple-element.45.refs_2_, bf16[8,4096]{1,0:T(8,128)(2,1)S(1)} %collective-permute-done.8.refs_3_, ...), custom_call_target="tpu_custom_call" | custom-call | flops 1 | bytes 2097152 | tf_op jit(solution)/shard_map/field/pallas_call | solution.py:439
  31.5 1.6 %collective-permute-start.14 = (bf16[8,2560]{1,0:T(8,128)(2,1)S(1)}, bf16[8,2560]{1,0:T(8,128)(2,1)S(1)}, u32[]{:S(2)}, u32[]{:S(2)}) collective-permute-start(bf16[8,2560]{1,0:T(8,128)(2,1)S(1)} %field.11.flat_ref.rest_3_), channel_id=1, source_target_pairs={{0,1},{1,0},{2,3},{3,2},{4,5},{5,4},{6,7},{7,6},{8,9},{9,8},{10,11... | collective-permute-start | bytes 122888 | tf_op jit(solution)/shard_map/ppermute | solution.py:348
  33.1 2.6 %collective-permute-start.13 = (bf16[8,2560]{1,0:T(8,128)(2,1)S(1)}, bf16[8,2560]{1,0:T(8,128)(2,1)S(1)}, u32[]{:S(2)}, u32[]{:S(2)}) collective-permute-start(bf16[8,2560]{1,0:T(8,128)(2,1)S(1)} %field.11.flat_ref.rest_3_), channel_id=1, source_target_pairs={{0,2},{1,3},{2,0},{3,1},{4,6},{5,7},{6,4},{7,5},{8,10},{9,11},{10,... | collective-permute-start | bytes 122888 | tf_op jit(solution)/shard_map/ppermute | solution.py:348
  35.9 0.8 %stats.1 = (f32[8,128]{1,0:T(8,128)S(1)}, bf16[10,6,256]{2,1,0:T(8,128)(2,1)}) custom-call(bf16[8,2560]{1,0:T(8,128)(2,1)S(1)} %field.11.flat_ref.rest_3_, f32[1,25600]{1,0:T(1,128)S(1)} %bitcast.16, f32[1,25600]{1,0:T(1,128)S(1)} %bitcast.18, s32[1,25600]{1,0:T(1,128)S(1)} %bitcast.13, f32[1,3200]{1,0:T(1,128)S(1)} %get-tuple-element.43.token_ref.trait_ref, ...), custom_call_target="tpu_custom_call" | custom-call | tf_op jit(solution)/shard_map/stats/pallas_call | solution.py:439
  36.8 2.1 %collective-permute-done.13.rest_1_ = bf16[8,2560]{1,0:T(8,128)(2,1)S(1)} collective-permute-done((bf16[8,2560]{1,0:T(8,128)(2,1)S(1)}, bf16[8,2560]{1,0:T(8,128)(2,1)S(1)}, u32[]{:S(2)}, u32[]{:S(2)}) %collective-permute-start.13) | collective-permute-done | bytes 40992 | tf_op jit(solution)/shard_map/ppermute | solution.py:348
  38.9 2.6 %collective-permute-done.12.rest_0_ = bf16[8,2560]{1,0:T(8,128)(2,1)S(1)} collective-permute-done((bf16[8,2560]{1,0:T(8,128)(2,1)S(1)}, bf16[8,2560]{1,0:T(8,128)(2,1)S(1)}, u32[]{:S(2)}, u32[]{:S(2)}) %collective-permute-start.12) | collective-permute-done | bytes 40992 | tf_op jit(solution)/shard_map/ppermute | solution.py:348
  41.7 2.2 %collective-permute-start.16 = (f32[8,128]{1,0:T(8,128)S(1)}, f32[8,128]{1,0:T(8,128)S(1)}, u32[]{:S(2)}, u32[]{:S(2)}) collective-permute-start(f32[8,128]{1,0:T(8,128)S(1)} %pair.1), channel_id=1, source_target_pairs={{0,24},{4,28},{8,16},{12,20},{16,8},{20,12},{24,0},{28,4},{1,25},{... | collective-permute-start | bytes 12296 | tf_op jit(solution)/shard_map/ppermute | solution.py:348
  44.5 1.8 %collective-permute-done.16.common_ref = f32[8,128]{1,0:T(8,128)S(1)} collective-permute-done((f32[8,128]{1,0:T(8,128)S(1)}, f32[8,128]{1,0:T(8,128)S(1)}, u32[]{:S(2)}, u32[]{:S(2)}) %collective-permute-start.16) | collective-permute-done | bytes 4128 | tf_op jit(solution)/shard_map/ppermute | solution.py:348
  46.3 1.3 %collective-permute-done.17.rest_0_ = f32[8,128]{1,0:T(8,128)S(1)} collective-permute-done((f32[8,128]{1,0:T(8,128)S(1)}, f32[8,128]{1,0:T(8,128)S(1)}, u32[]{:S(2)}, u32[]{:S(2)}) %collective-permute-start.17) | collective-permute-done | bytes 4128 | tf_op jit(solution)/shard_map/ppermute | solution.py:352
  47.6 1.2 %collective-permute-done.18.rest_1_ = f32[8,128]{1,0:T(8,128)S(1)} collective-permute-done((f32[8,128]{1,0:T(8,128)S(1)}, f32[8,128]{1,0:T(8,128)S(1)}, u32[]{:S(2)}, u32[]{:S(2)}) %collective-permute-start.18) | collective-permute-done | bytes 4128 | tf_op jit(solution)/shard_map/ppermute | solution.py:348
  48.7 0.7 %final.1 = (f32[6,24]{1,0:T(8,128)}, f32[1,6]{1,0:T(1,128)}, f32[1,6]{1,0:T(1,128)}) custom-call(f32[8,128]{1,0:T(8,128)S(1)} %get-tuple-element.50.refs_6_.count_ref, f32[8,128]{1,0:T(8,128)S(1)} %add.3.own_ref, f32[8,128]{1,0:T(8,128)S(1)} %collective-permute-done.16.common_ref, f32[8,128]{1,0:T(8,128)S(1)} %collective-permute-done.17.rest_0_, ...), custom_call_target="tpu_custom_call" | custom-call | tf_op jit(solution)/shard_map/final/pallas_call | solution.py:439
  (42 shorter events, 4.3 us)
Async XLA Ops:
  6.6 4.4 %collective-permute-start = (bf16[3,8,4992]{2,1,0:T(8,128)(2,1)S(1)}, bf16[3,8,4992]{2,1,0:T(8,128)(2,1)S(1)}, u32[]{:S(2)}, u32[]{:S(2)}) collective-permute-start(bf16[3,8,4992]{2,1,0:T(8,128)(2,1)S(1)} %get-tuple-element.35), channel_id=1, source_target_pairs={{0,4},{4,0},{8,12},{12,8},{16,20},{20,16},{24,28},{28,24},{1,5},{5... | collective-permute-start | bytes 718856 | tf_op jit(solution)/shard_map/ppermute | solution.py:348
  11.0 8.8 %collective-permute-start.1 = (bf16[8,4992]{1,0:T(8,128)(2,1)S(1)}, bf16[8,4992]{1,0:T(8,128)(2,1)S(1)}, u32[]{:S(2)}, u32[]{:S(2)}) collective-permute-start(bf16[8,4992]{1,0:T(8,128)(2,1)S(1)} %get-tuple-element.39), channel_id=1, source_target_pairs={{0,24},{4,28},{8,16},{12,20},{16,8},{20,12},{24,0},{28,4},{1,25},{... | collective-permute-start | bytes 239624 | tf_op jit(solution)/shard_map/ppermute | solution.py:348
  14.5 5.2 %collective-permute-start.2 = (bf16[8,4992]{1,0:T(8,128)(2,1)S(1)}, bf16[8,4992]{1,0:T(8,128)(2,1)S(1)}, u32[]{:S(2)}, u32[]{:S(2)}) collective-permute-start(bf16[8,4992]{1,0:T(8,128)(2,1)S(1)} %get-tuple-element.40), channel_id=1, source_target_pairs={{0,16},{4,20},{8,24},{12,28},{16,0},{20,4},{24,8},{28,12},{1,17},{... | collective-permute-start | bytes 239624 | tf_op jit(solution)/shard_map/ppermute | solution.py:348
  15.1 4.8 %collective-permute-start.3 = (bf16[8,4992]{1,0:T(8,128)(2,1)S(1)}, bf16[8,4992]{1,0:T(8,128)(2,1)S(1)}, u32[]{:S(2)}, u32[]{:S(2)}) collective-permute-start(bf16[8,4992]{1,0:T(8,128)(2,1)S(1)} %get-tuple-element.41), channel_id=1, source_target_pairs={{0,8},{4,12},{8,0},{12,4},{16,24},{20,28},{24,16},{28,20},{1,9},{5... | collective-permute-start | bytes 239624 | tf_op jit(solution)/shard_map/ppermute | solution.py:348
  17.7 2.1 %collective-permute-start.4 = (bf16[1,8,4992]{2,1,0:T(8,128)(2,1)S(1)}, bf16[1,8,4992]{2,1,0:T(8,128)(2,1)S(1)}, u32[]{:S(2)}, u32[]{:S(2)}) collective-permute-start(bf16[1,8,4992]{2,1,0:T(8,128)(2,1)S(1)} %get-tuple-element.42), channel_id=1, source_target_pairs={{0,4},{4,0},{8,12},{12,8},{16,20},{20,16},{24,28},{28,24},{1,5},{5... | collective-permute-start | bytes 239624 | tf_op jit(solution)/shard_map/ppermute | solution.py:348
  17.8 2.1 %copy-start.1 = (f32[25600]{0:T(1024)S(1)}, f32[25600]{0:T(1024)}, u32[]{:S(2)}) copy-start(f32[25600]{0:T(1024)} %param.7) | copy-start | bytes 307204
  17.8 2.1 %copy-start.2 = (f32[25600]{0:T(1024)S(1)}, f32[25600]{0:T(1024)}, u32[]{:S(2)}) copy-start(f32[25600]{0:T(1024)} %param.8) | copy-start | bytes 307204
  17.8 6.2 %copy-start = (s32[25600]{0:T(1024)S(1)}, s32[25600]{0:T(1024)}, u32[]{:S(2)}) copy-start(s32[25600]{0:T(1024)} %param.9) | copy-start | bytes 307204
  20.0 5.0 %collective-permute-start.5 = (bf16[8,4096]{1,0:T(8,128)(2,1)S(1)}, bf16[8,4096]{1,0:T(8,128)(2,1)S(1)}, u32[]{:S(2)}, u32[]{:S(2)}) collective-permute-start(bf16[8,4096]{1,0:T(8,128)(2,1)S(1)} %get-tuple-element.49.refs_4_), channel_id=1, source_target_pairs={{0,4},{4,0},{8,12},{12,8},{16,20},{20,16},{24,28},{28,24},{1,5},{5... | collective-permute-start | bytes 196616 | tf_op jit(solution)/shard_map/ppermute | solution.py:348
  20.5 5.6 %collective-permute-start.6 = (bf16[8,4096]{1,0:T(8,128)(2,1)S(1)}, bf16[8,4096]{1,0:T(8,128)(2,1)S(1)}, u32[]{:S(2)}, u32[]{:S(2)}) collective-permute-start(bf16[8,4096]{1,0:T(8,128)(2,1)S(1)} %get-tuple-element.49.refs_4_), channel_id=1, source_target_pairs={{0,24},{4,28},{8,16},{12,20},{16,8},{20,12},{24,0},{28,4},{1,25},{... | collective-permute-start | bytes 196616 | tf_op jit(solution)/shard_map/ppermute | solution.py:348
  23.4 4.3 %collective-permute-start.7 = (bf16[8,4096]{1,0:T(8,128)(2,1)S(1)}, bf16[8,4096]{1,0:T(8,128)(2,1)S(1)}, u32[]{:S(2)}, u32[]{:S(2)}) collective-permute-start(bf16[8,4096]{1,0:T(8,128)(2,1)S(1)} %get-tuple-element.49.refs_4_), channel_id=1, source_target_pairs={{0,16},{4,20},{8,24},{12,28},{16,0},{20,4},{24,8},{28,12},{1,17},{... | collective-permute-start | bytes 196616 | tf_op jit(solution)/shard_map/ppermute | solution.py:348
  23.9 4.4 %collective-permute-start.9 = (bf16[8,4096]{1,0:T(8,128)(2,1)S(1)}, bf16[8,4096]{1,0:T(8,128)(2,1)S(1)}, u32[]{:S(2)}, u32[]{:S(2)}) collective-permute-start(bf16[8,4096]{1,0:T(8,128)(2,1)S(1)} %get-tuple-element.49.refs_4_), channel_id=1, source_target_pairs={{0,8},{4,12},{8,0},{12,4},{16,24},{20,28},{24,16},{28,20},{1,9},{5... | collective-permute-start | bytes 196616 | tf_op jit(solution)/shard_map/ppermute | solution.py:348
  27.7 2.0 %collective-permute-start.11 = (bf16[8,4096]{1,0:T(8,128)(2,1)S(1)}, bf16[8,4096]{1,0:T(8,128)(2,1)S(1)}, u32[]{:S(2)}, u32[]{:S(2)}) collective-permute-start(bf16[8,4096]{1,0:T(8,128)(2,1)S(1)} %relay.3.refs_3_), channel_id=1, source_target_pairs={{0,4},{4,0},{8,12},{12,8},{16,20},{20,16},{24,28},{28,24},{1,5},{5... | collective-permute-start | bytes 196616 | tf_op jit(solution)/shard_map/ppermute | solution.py:348
  28.3 1.9 %collective-permute-start.10 = (bf16[8,4096]{1,0:T(8,128)(2,1)S(1)}, bf16[8,4096]{1,0:T(8,128)(2,1)S(1)}, u32[]{:S(2)}, u32[]{:S(2)}) collective-permute-start(bf16[8,4096]{1,0:T(8,128)(2,1)S(1)} %relay.5.refs_3_), channel_id=1, source_target_pairs={{0,4},{4,0},{8,12},{12,8},{16,20},{20,16},{24,28},{28,24},{1,5},{5... | collective-permute-start | bytes 196616 | tf_op jit(solution)/shard_map/ppermute | solution.py:348
  28.9 1.4 %collective-permute-start.8 = (bf16[8,4096]{1,0:T(8,128)(2,1)S(1)}, bf16[8,4096]{1,0:T(8,128)(2,1)S(1)}, u32[]{:S(2)}, u32[]{:S(2)}) collective-permute-start(bf16[8,4096]{1,0:T(8,128)(2,1)S(1)} %relay.4.refs_3_), channel_id=1, source_target_pairs={{0,4},{4,0},{8,12},{12,8},{16,20},{20,16},{24,28},{28,24},{1,5},{5... | collective-permute-start | bytes 196616 | tf_op jit(solution)/shard_map/ppermute | solution.py:348
  31.5 5.3 %collective-permute-start.14 = (bf16[8,2560]{1,0:T(8,128)(2,1)S(1)}, bf16[8,2560]{1,0:T(8,128)(2,1)S(1)}, u32[]{:S(2)}, u32[]{:S(2)}) collective-permute-start(bf16[8,2560]{1,0:T(8,128)(2,1)S(1)} %field.11.flat_ref.rest_3_), channel_id=1, source_target_pairs={{0,1},{1,0},{2,3},{3,2},{4,5},{5,4},{6,7},{7,6},{8,9},{9,8},{10,11... | collective-permute-start | bytes 122888 | tf_op jit(solution)/shard_map/ppermute | solution.py:348
  33.1 5.8 %collective-permute-start.13 = (bf16[8,2560]{1,0:T(8,128)(2,1)S(1)}, bf16[8,2560]{1,0:T(8,128)(2,1)S(1)}, u32[]{:S(2)}, u32[]{:S(2)}) collective-permute-start(bf16[8,2560]{1,0:T(8,128)(2,1)S(1)} %field.11.flat_ref.rest_3_), channel_id=1, source_target_pairs={{0,2},{1,3},{2,0},{3,1},{4,6},{5,7},{6,4},{7,5},{8,10},{9,11},{10,... | collective-permute-start | bytes 122888 | tf_op jit(solution)/shard_map/ppermute | solution.py:348
  35.7 5.8 %collective-permute-start.12 = (bf16[8,2560]{1,0:T(8,128)(2,1)S(1)}, bf16[8,2560]{1,0:T(8,128)(2,1)S(1)}, u32[]{:S(2)}, u32[]{:S(2)}) collective-permute-start(bf16[8,2560]{1,0:T(8,128)(2,1)S(1)} %field.11.flat_ref.rest_3_), channel_id=1, source_target_pairs={{0,3},{1,2},{2,1},{3,0},{4,7},{5,6},{6,5},{7,4},{8,11},{9,10},{10,... | collective-permute-start | bytes 122888 | tf_op jit(solution)/shard_map/ppermute | solution.py:348
  41.7 2.3 %collective-permute-start.15 = (f32[8,128]{1,0:T(8,128)S(1)}, f32[8,128]{1,0:T(8,128)S(1)}, u32[]{:S(2)}, u32[]{:S(2)}) collective-permute-start(f32[8,128]{1,0:T(8,128)S(1)} %pair.1), channel_id=1, source_target_pairs={{0,4},{4,0},{8,12},{12,8},{16,20},{20,16},{24,28},{28,24},{1,5},{5... | collective-permute-start | bytes 12296 | tf_op jit(solution)/shard_map/ppermute | solution.py:348
  41.7 4.6 %collective-permute-start.16 = (f32[8,128]{1,0:T(8,128)S(1)}, f32[8,128]{1,0:T(8,128)S(1)}, u32[]{:S(2)}, u32[]{:S(2)}) collective-permute-start(f32[8,128]{1,0:T(8,128)S(1)} %pair.1), channel_id=1, source_target_pairs={{0,24},{4,28},{8,16},{12,20},{16,8},{20,12},{24,0},{28,4},{1,25},{... | collective-permute-start | bytes 12296 | tf_op jit(solution)/shard_map/ppermute | solution.py:348
  44.0 3.6 %collective-permute-start.17 = (f32[8,128]{1,0:T(8,128)S(1)}, f32[8,128]{1,0:T(8,128)S(1)}, u32[]{:S(2)}, u32[]{:S(2)}) collective-permute-start(f32[8,128]{1,0:T(8,128)S(1)} %add.3.own_ref), channel_id=1, source_target_pairs={{0,8},{4,20},{8,0},{12,28},{16,24},{20,4},{24,16},{28,12},{1,9},{5... | collective-permute-start | bytes 12296 | tf_op jit(solution)/shard_map/ppermute | solution.py:352
  46.3 1.3 %collective-permute-start.19 = (f32[8,128]{1,0:T(8,128)S(1)}, f32[8,128]{1,0:T(8,128)S(1)}, u32[]{:S(2)}, u32[]{:S(2)}) collective-permute-start(f32[8,128]{1,0:T(8,128)S(1)} %collective-permute-done.16.common_ref), channel_id=1, source_target_pairs={{0,4},{4,0},{8,12},{12,8},{16,20},{20,16},{24,28},{28,24},{1,5},{5... | collective-permute-start | bytes 12296 | tf_op jit(solution)/shard_map/ppermute | solution.py:348
  47.6 1.2 %collective-permute-start.18 = (f32[8,128]{1,0:T(8,128)S(1)}, f32[8,128]{1,0:T(8,128)S(1)}, u32[]{:S(2)}, u32[]{:S(2)}) collective-permute-start(f32[8,128]{1,0:T(8,128)S(1)} %collective-permute-done.17.rest_0_), channel_id=1, source_target_pairs={{0,4},{4,0},{8,12},{12,8},{16,20},{20,16},{24,28},{28,24},{1,5},{5... | collective-permute-start | bytes 12296 | tf_op jit(solution)/shard_map/ppermute | solution.py:348

commit v3 on v1

--- a/solution.py
+++ b/solution.py
@@ -26,6 +26,17 @@
     return lax.rem(lax.axis_index("ind"), 2)
 
 
+def pick(pair):
+    return pair[0] if pair[0] == pair[1] else jnp.where(core() == 0, pair[0], pair[1])
+
+
+def turns(distances):
+    pairs = [(distances[0], distances[0])]
+    for a, b in zip(distances[1::2], distances[2::2]):
+        pairs += [(a, b), (b, a)]
+    return pairs
+
+
 def fold_lanes(value):
     return tree_sum([value[:, at : at + LANES] for at in range(0, value.shape[1], LANES)])
 
@@ -58,14 +69,15 @@
 
 def moments_kernel(snps, distances, opening, taken, given, geno_ref, *rest):
     rest = list(rest)
+    raw_ins = []
     if opening:
         bits_ref, trait_ref, kept_ref, sums_ref, local_ref, left_ref = rest[:6]
         rest = rest[6:]
     else:
-        raw_in = rest.pop(0) if taken else None
+        raw_ins, rest = rest[:taken], rest[taken:]
         left_ref, kept_ref, sums_ref, local_ref = rest[:4]
         rest = rest[4:]
-    raw_out = rest.pop(0) if given is not None else None
+    raw_outs, rest = rest[: len(given)], rest[len(given) :]
     slots, rows, block = kept_ref.shape
     fetched = slots - taken
     devices = -(-snps // block)
@@ -91,11 +103,17 @@
         rest = rest[2:]
 
         def fetch(index, act):
-            distance = distances[0] - 2 * (index + taken)
+            distance = pick(distances[taken])
+            for slot in range(taken + 1, slots):
+                distance = jnp.where(index + taken == slot, pick(distances[slot]), distance)
             whole_or_tail(distance, buffer.at[index], arrived.at[index], act)
 
-    if raw_out is not None:
+    if given:
         raw_arrived = rest.pop(0)
+
+    def hand_over(act):
+        for index, (distance, out) in enumerate(zip(given, raw_outs)):
+            whole_or_tail(pick(distance), out, raw_arrived.at[index], act)
 
     if opening:
         bits, trait, small = rest[:3]
@@ -105,8 +123,7 @@
         trait_copy.start()
     if fetched:
         pl.loop(0, fetched)(lambda index: fetch(index, lambda c: c.start()))
-    if raw_out is not None:
-        whole_or_tail(given, raw_out, raw_arrived, lambda c: c.start())
+    hand_over(lambda c: c.start())
     if opening:
         bits_copy.wait()
         trait_copy.wait()
@@ -144,8 +161,8 @@
         sums_ref[slot, :, :span] = high.astype(BF16)
         sums_ref[slot, :, span:] = low.astype(BF16)
 
-    if taken:
-        work(0, raw_in)
+    for slot, raw_in in enumerate(raw_ins):
+        work(slot, raw_in)
     if fetched:
 
         @pl.loop(0, fetched)
@@ -153,8 +170,7 @@
             fetch(index, lambda c: c.wait())
             work(index + taken, buffer.at[index])
 
-    if raw_out is not None:
-        whole_or_tail(given, raw_out, raw_arrived, lambda c: c.wait())
+    hand_over(lambda c: c.wait())
 
 
 def cores_kernel(left_ref, here_ref, away_ref, *outs):
@@ -206,7 +222,7 @@
     trace = jnp.zeros((SUBLANES, 1), F32)
     for ref, distances in zip(locals_, order[1]):
         for slot, distance in enumerate(distances):
-            here, member = member_of(lax.axis_index("ind") ^ distance)
+            here, member = member_of(lax.axis_index("ind") ^ pick(distance))
             shift = mean_ref[:, here] - 1.0
             inverse = 1.0 / scale_ref[:, here]
             square = ref[slot, 1:2] - 2.0 * shift * ref[slot, 0:1] + rows * shift * shift
@@ -237,7 +253,7 @@
         offset = jnp.zeros((PROBES * SUBLANES, LANES), F32)
         number = jnp.zeros((SUBLANES, LANES), F32)
     for index, (slot, distance) in enumerate(blocks):
-        start = (lax.axis_index("ind") ^ distance) * block
+        start = (lax.axis_index("ind") ^ pick(distance)) * block
         u = u_refs[index][...].astype(F32)
         lines = [u[b : b + 1, :block] for b in range(SUBLANES)]
         for b in range(PROBES - SUBLANES):
@@ -274,7 +290,12 @@
 
 def pair_kernel(stats_ref, *rest):
     flats, out_ref = rest[:-1], rest[-1]
-    everyone = [flat[...].astype(F32) for flat in flats]
+    slots = [flat[...].astype(F32) for flat in flats]
+    everyone = slots[:1]
+    for low, high in zip(slots[1:-1:2], slots[2:-1:2]):
+        everyone.append(jnp.where(core() == 0, low, high))
+        everyone.append(jnp.where(core() == 0, high, low))
+    everyone.append(slots[-1])
     everyone += [jnp.zeros_like(everyone[0])] * (LANES // SUBLANES - len(flats))
     out_ref[...] = stats_ref[...] + lax.dot_general(
         flats[0][...],
@@ -313,8 +334,13 @@
     return lax.ppermute(value, axis, [(i, i ^ distance) for i in range(size)])
 
 
-def swap_mixed(value, size, pair):
-    return lax.ppermute(value, "ind", [(i, i ^ pair[i % 2]) for i in range(size)])
+def swap_mixed(value, axis, sizes, pair):
+    moves = []
+    for i in range(sizes[0]):
+        for j in range(sizes[1]):
+            k, m = (i ^ pair[i % 2], j) if axis == "ind" else (i, j ^ pair[i % 2])
+            moves.append((i * sizes[1] + j, k * sizes[1] + m))
+    return lax.ppermute(value, ("ind", "bin"), moves)
 
 
 def chosen_pairs(distances):
@@ -363,8 +389,7 @@
     def moments(distances, given, extra, name):
         slots = len(distances)
         opening = extra[0] is probe_bits
-        taken = int(not opening and extra[0] is not None)
-        extra = [value for value in extra if value is not None]
+        taken = 0 if opening else len(extra) - 1
         fetched = slots - taken
         out_shape = [
             jax.ShapeDtypeStruct((slots, rows, block), BF16),
@@ -373,13 +398,12 @@
         ]
         if opening:
             out_shape.append(jax.ShapeDtypeStruct((ROWS, rows), F32))
-        if given is not None:
-            out_shape.append(jax.ShapeDtypeStruct((rows, block), jnp.int32))
+        out_shape += [jax.ShapeDtypeStruct((rows, block), jnp.int32)] * len(given)
         scratch = []
         if fetched:
             scratch += [VMEM((fetched, rows, block), jnp.int32), pltpu.SemaphoreType.DMA((fetched,))]
-        if given is not None:
-            scratch.append(pltpu.SemaphoreType.DMA)
+        if given:
+            scratch.append(pltpu.SemaphoreType.DMA((len(given),)))
         if opening:
             scratch += [
                 VMEM(probe_bits.shape, jnp.int32),
@@ -397,8 +421,9 @@
             name=name,
         )(genotype, *extra)
 
-    here_order = list(range(n - 2, 0, -2))
-    away_order = [d + 1 for d in here_order]
+    sizes = (n, n_bin)
+    here_order = turns(list(range(n - 2, 0, -2)))
+    away_order = [(b + 1, a + 1) for a, b in here_order]
 
     def plain(kernel, operands, out_shape, name, **options):
         return pl.pallas_call(
@@ -411,11 +436,11 @@
             **options,
         )(*operands)
 
-    kept_away, away, local_away, left, raw = moments(
-        away_order, here_order[0], (probe_bits, phenotype), "moments_away"
+    kept_away, away, local_away, left, *raws = moments(
+        away_order, here_order[:2], (probe_bits, phenotype), "moments_away"
     )
     away = swap(away, "ind", n, 1)
-    kept_here, here, local_here = moments(here_order, None, (raw, left), "moments_here")
+    kept_here, here, local_here = moments(here_order, [], (*raws, left), "moments_here")
     packed = jax.ShapeDtypeStruct((SUBLANES, span * 3 // 2), BF16)
     *sums, left = plain(
         cores_kernel,
@@ -423,10 +448,10 @@
         [packed] * (chips - 1) + [jax.ShapeDtypeStruct(left.shape, F32)],
         "cores",
     )
-    sums = [swap(value, "ind", n, d) for value, d in zip(sums, here_order)]
-    kept_near, near, local_near, raw = moments([1], 0, (None, left), "moments_near")
+    sums = [swap_mixed(value, "ind", sizes, d) for value, d in zip(sums, here_order)]
+    kept_near, near, local_near, raw = moments([(1, 1)], [(0, 0)], (left,), "moments_near")
     near = swap(near, "ind", n, 1)
-    kept_own, own, local_own = moments([0], None, (raw, left), "moments_own")
+    kept_own, own, local_own = moments([(0, 0)], [], (raw, left), "moments_own")
 
     u, trait = plain(
         weights_kernel,
@@ -456,8 +481,8 @@
         )
 
     u_near = swap(u, "ind", n, 1)
-    u_here = [swap(u, "ind", n, d) for d in here_order]
-    terms = fields([kept_own, kept_near], [(0, 0), (0, 1)], [u, u_near], [])
+    u_here = [swap_mixed(u, "ind", sizes, d) for d in here_order]
+    terms = fields([kept_own, kept_near], [(0, (0, 0)), (0, (1, 1))], [u, u_near], [])
     u_away = []
     for slot, (distance, value) in enumerate(zip(here_order, u_here)):
         shape = [jax.ShapeDtypeStruct(value.shape, value.dtype)]
@@ -469,8 +494,9 @@
     terms = fields([kept_away], blocks[:middle], u_away[:middle], terms)
     flat, number = fields([kept_away], blocks[middle:], u_away[middle:], terms, last=True)
 
-    flats = [flat] + [swap(flat, "bin", n_bin, d) for d in range(1, n_bin)]
-    order = (rows, (away_order, here_order, [1], [0]))
+    bin_order = turns(list(range(n_bin - 1, 0, -1)))
+    flats = [flat] + [swap_mixed(flat, "bin", sizes, d) for d in bin_order[::-1]]
+    order = (rows, (away_order, here_order, [(1, 1)], [(0, 0)]))
     stats, field = plain(
         functools.partial(stats_kernel, own_bins, order),
         (flat, mean, scale, label, trait, local_away, local_here, local_near, local_own),
@@ -481,7 +507,7 @@
     pairs, common = chosen_pairs(list(range(2, n, 2)))
     part_common = swap(part, "ind", n, common)
     part = part + swap(part, "ind", n, 1)
-    mine = [swap_mixed(part, n, pair) for pair in pairs]
+    mine = [swap_mixed(part, "ind", sizes, pair) for pair in pairs]
     theirs = [swap(value, "ind", n, 1) for value in mine + [part_common]]
     pair, trace, quad = plain(
         functools.partial(final_kernel, own_bins, n_bin, len(pairs), rows * n),

time: 46.3 us -> 47.3 us (1.022)
  waiting for transfers between devices: 9.98 us -> 10.6 us
  Pallas kernels: 18.7 us -> 19.2 us
    ppermute x19 -> x10, starting transfers between devices: 15.9 us -> 3.69 us  [swap(): return lax.ppermute(value, axis, [(i, i ^ distance) for i in range(size)])]
    ppermute x1 -> x10, starting transfers between devices: 0.64 us -> 12.7 us  [swap_mixed(): return lax.ppermute(value, ('ind', 'bin'), moves)]
    ppermute x1 -> x10, waiting for transfers between devices: 1.38 us -> 7.74 us  [swap_mixed(): return lax.ppermute(value, ('ind', 'bin'), moves)]
    ppermute x19 -> x10, waiting for transfers between devices: 8.6 us -> 2.86 us  [swap(): return lax.ppermute(value, axis, [(i, i ^ distance) for i in range(size)])]
  transfers between devices with their start and end apart: 20 -> 20, of which waited for: 9 -> 9; matrix products, arithmetic and copies ran while one was open for 0% -> 0% of each run, Pallas kernels for 25% -> 24%
where the time goes in v3:
time: 47.3 us; the launch traced here: 47 us
  Pallas kernels  19.2 us (41%)
  starting transfers between devices  16.4 us (35%)
  waiting for transfers between devices  10.6 us (22%)
  between operations  0.84 us (2%)
    ppermute x10, starting transfers between devices, swap_mixed(): return lax.ppermute(value, ('ind', 'bin'), moves)  12.7 us
    pallas_call x4, Pallas kernels, moments(): pl.pallas_call(functools.partial(moments_kernel, snps, distances, opening...  12.6 us
    ppermute x10, waiting for transfers between devices, swap_mixed(): return lax.ppermute(value, ('ind', 'bin'), moves)  7.74 us
    pallas_call x14, Pallas kernels, plain(): pl.pallas_call(kernel, in_specs=[in_vmem()] * len(operands), out_specs=[i...  6.61 us
    ppermute x10, starting transfers between devices, swap(): return lax.ppermute(value, axis, [(i, i ^ distance) for i in range(size)])  3.69 us
    ppermute x10, waiting for transfers between devices, swap(): return lax.ppermute(value, axis, [(i, i ^ distance) for i in range(size)])  2.86 us
  transfers between devices with their start and end apart: 20, of which 9 were waited for; matrix products, arithmetic and copies ran while one was open for 0% of the time, Pallas kernels for 24%

profile of v3, /device:TPU:0, one launch (start us, length us, event | category | flops | bytes accessed | tf_op | source)
XLA Modules:
  0.0 47.0 jit_solution(14907796748438114921)
XLA Ops:
  0.6 5.8 %moments_away.1 = (bf16[3,256,3200]{2,1,0:T(8,128)(2,1)S(1)}, bf16[3,8,4992]{2,1,0:T(8,128)(2,1)S(1)}, f32[3,2,3200]{2,1,0:T(2,128)S(1)}, f32[16,256]{1,0:T(8,12...) custom-call(s32[256,25600]{1,0:T(8,128)} %geno_ref.7, s32[10,256]{1,0:T(8,128)} %rest_0_.1, bf16[256]{0:T(256)(128)(2,1)} %rest_1_.1), custom_call_target="tpu_custom_call" | custom-call | flops 1 | bytes 9830400 | tf_op jit(solution)/shard_map/moments_away/pallas_call | solution.py:413
  7.0 3.1 %moments_here.1 = (bf16[3,256,3200]{2,1,0:T(8,128)(2,1)S(1)}, bf16[3,8,4992]{2,1,0:T(8,128)(2,1)S(1)}, f32[3,2,3200]{2,1,0:T(2,128)S(1)}) custom-call(s32[256,25600]{1,0:T(8,128)} %geno_ref.7, s32[256,3200]{1,0:T(8,128)S(1)} %get-tuple-element.49.rest_0_, s32[256,3200]{1,0:T(8,128)S(1)} %get-tuple-element.50.rest_1_, ...), custom_call_target="tpu_custom_call" | custom-call | flops 1 | bytes 9830400 | tf_op jit(solution)/shard_map/moments_here/pallas_call | solution.py:413
  10.2 3.5 %collective-permute-start.2 = (bf16[8,4992]{1,0:T(8,128)(2,1)S(1)}, bf16[8,4992]{1,0:T(8,128)(2,1)S(1)}, u32[]{:S(2)}, u32[]{:S(2)}) collective-permute-start(bf16[8,4992]{1,0:T(8,128)(2,1)S(1)} %get-tuple-element.61), channel_id=1, source_target_pairs={{0,24},{1,25},{2,26},{3,27},{4,28},{5,29},{6,30},{7,31},{8,16},{9,... | collective-permute-start | bytes 239624 | tf_op jit(solution)/shard_map/ppermute | solution.py:343
  14.4 2.9 %moments_near.1 = (bf16[1,256,3200]{2,1,0:T(8,128)(2,1)S(1)}, bf16[1,8,4992]{2,1,0:T(8,128)(2,1)S(1)}, f32[1,2,3200]{2,1,0:T(2,128)S(1)}, s32[256,3200]{1,0:T(8,128)S(1)}) custom-call(s32[256,25600]{1,0:T(8,128)} %geno_ref.7, f32[16,256]{1,0:T(8,128)S(1)} %get-tuple-element.55.rest_0_.rest_1_), custom_call_target="tpu_custom_call" | custom-call | flops 1 | bytes 1 | tf_op jit(solution)/shard_map/moments_near/pallas_call | solution.py:413
  17.5 0.7 %moments_own.1 = (bf16[1,256,3200]{2,1,0:T(8,128)(2,1)S(1)}, bf16[1,8,4992]{2,1,0:T(8,128)(2,1)S(1)}, f32[1,2,3200]{2,1,0:T(2,128)S(1)}) custom-call(s32[256,25600]{1,0:T(8,128)} %geno_ref.7, s32[256,3200]{1,0:T(8,128)S(1)} %get-tuple-element.56.rest_0_, f32[16,256]{1,0:T(8,128)S(1)} %get-tuple-element.55.rest_0_.rest_1_), custom_call_target="tpu_custom_call" | custom-call | flops 1 | bytes 1 | tf_op jit(solution)/shard_map/moments_own/pallas_call | solution.py:413
  19.1 2.8 %collective-permute-start.6 = (bf16[8,4096]{1,0:T(8,128)(2,1)S(1)}, bf16[8,4096]{1,0:T(8,128)(2,1)S(1)}, u32[]{:S(2)}, u32[]{:S(2)}) collective-permute-start(bf16[8,4096]{1,0:T(8,128)(2,1)S(1)} %get-tuple-element.64.refs_4_), channel_id=1, source_target_pairs={{0,24},{1,25},{2,26},{3,27},{4,28},{5,29},{6,30},{7,31},{8,16},{9,... | collective-permute-start | bytes 196616 | tf_op jit(solution)/shard_map/ppermute | solution.py:343
  22.6 1.1 %field.6 = (f32[256,80]{1,0:T(8,128)S(1)}, f32[80,128]{1,0:T(8,128)S(1)}, f32[8,128]{1,0:T(8,128)S(1)}) custom-call(f32[1,25600]{1,0:T(1,128)S(1)} %bitcast.7, s32[1,25600]{1,0:T(1,128)S(1)} %bitcast.14, bf16[1,256,3200]{2,1,0:T(8,128)(2,1)S(1)} %get-tuple-element.57.refs_2_, bf16[1,256,3200]{2,1,0:T(8,128)(2,1)S(1)} %get-tuple-element.58.refs_3_, ...), custom_call_target="tpu_custom_call" | custom-call | flops 1 | bytes 1 | tf_op jit(solution)/shard_map/field/pallas_call | solution.py:429
  23.6 0.9 %collective-permute-done.6.value_ref = bf16[8,4096]{1,0:T(8,128)(2,1)S(1)} collective-permute-done((bf16[8,4096]{1,0:T(8,128)(2,1)S(1)}, bf16[8,4096]{1,0:T(8,128)(2,1)S(1)}, u32[]{:S(2)}, u32[]{:S(2)}) %collective-permute-start.6) | collective-permute-done | bytes 65568 | tf_op jit(solution)/shard_map/ppermute | solution.py:343
  24.5 0.6 %field.7 = (f32[256,80]{1,0:T(8,128)S(1)}, f32[80,128]{1,0:T(8,128)S(1)}, f32[8,128]{1,0:T(8,128)S(1)}) custom-call(f32[1,25600]{1,0:T(1,128)S(1)} %bitcast.8, s32[1,25600]{1,0:T(1,128)S(1)} %bitcast.15, bf16[3,256,3200]{2,1,0:T(8,128)(2,1)S(1)} %get-tuple-element.52.refs_2_, bf16[8,4096]{1,0:T(8,128)(2,1)S(1)} %relay.3.refs_3_, ...), custom_call_target="tpu_custom_call" | custom-call | flops 1 | bytes 1 | tf_op jit(solution)/shard_map/field/pallas_call | solution.py:429
  25.2 1.1 %collective-permute-done.7.value_ref = bf16[8,4096]{1,0:T(8,128)(2,1)S(1)} collective-permute-done((bf16[8,4096]{1,0:T(8,128)(2,1)S(1)}, bf16[8,4096]{1,0:T(8,128)(2,1)S(1)}, u32[]{:S(2)}, u32[]{:S(2)}) %collective-permute-start.7) | collective-permute-done | bytes 65568 | tf_op jit(solution)/shard_map/ppermute | solution.py:343
  26.2 0.6 %field.8 = (f32[256,80]{1,0:T(8,128)S(1)}, f32[80,128]{1,0:T(8,128)S(1)}, f32[8,128]{1,0:T(8,128)S(1)}) custom-call(f32[1,25600]{1,0:T(1,128)S(1)} %bitcast.9, s32[1,25600]{1,0:T(1,128)S(1)} %bitcast.16, bf16[3,256,3200]{2,1,0:T(8,128)(2,1)S(1)} %get-tuple-element.52.refs_2_, bf16[8,4096]{1,0:T(8,128)(2,1)S(1)} %relay.4.refs_3_, ...), custom_call_target="tpu_custom_call" | custom-call | flops 1 | bytes 1 | tf_op jit(solution)/shard_map/field/pallas_call | solution.py:429
  27.5 0.6 %field.9 = (f32[256,80]{1,0:T(8,128)S(1)}, f32[80,128]{1,0:T(8,128)S(1)}, f32[8,128]{1,0:T(8,128)S(1)}) custom-call(f32[1,25600]{1,0:T(1,128)S(1)} %bitcast.10, s32[1,25600]{1,0:T(1,128)S(1)} %bitcast.17, bf16[3,256,3200]{2,1,0:T(8,128)(2,1)S(1)} %get-tuple-element.52.refs_2_, bf16[8,4096]{1,0:T(8,128)(2,1)S(1)} %relay.5.refs_3_, ...), custom_call_target="tpu_custom_call" | custom-call | flops 1 | bytes 1 | tf_op jit(solution)/shard_map/field/pallas_call | solution.py:429
  28.1 0.6 %field.10 = (f32[256,80]{1,0:T(8,128)S(1)}, f32[80,128]{1,0:T(8,128)S(1)}, f32[8,128]{1,0:T(8,128)S(1)}) custom-call(f32[1,25600]{1,0:T(1,128)S(1)} %bitcast.11, s32[1,25600]{1,0:T(1,128)S(1)} %bitcast.18, bf16[3,256,3200]{2,1,0:T(8,128)(2,1)S(1)} %get-tuple-element.48.refs_2_, bf16[8,4096]{1,0:T(8,128)(2,1)S(1)} %collective-permute-done.11.refs_3_, ...), custom_call_target="tpu_custom_call" | custom-call | flops 1 | bytes 1 | tf_op jit(solution)/shard_map/field/pallas_call | solution.py:429
  28.7 1.2 %field.11 = (bf16[8,2560]{1,0:T(8,128)(2,1)S(1)}, f32[8,128]{1,0:T(8,128)S(1)}) custom-call(f32[1,25600]{1,0:T(1,128)S(1)} %bitcast.12, s32[1,25600]{1,0:T(1,128)S(1)} %bitcast.19, bf16[3,256,3200]{2,1,0:T(8,128)(2,1)S(1)} %get-tuple-element.48.refs_2_, bf16[8,4096]{1,0:T(8,128)(2,1)S(1)} %collective-permute-done.8.refs_3_, ...), custom_call_target="tpu_custom_call" | custom-call | flops 1 | bytes 1 | tf_op jit(solution)/shard_map/field/pallas_call | solution.py:429
  29.9 3.7 %collective-permute-start.14 = (bf16[8,2560]{1,0:T(8,128)(2,1)S(1)}, bf16[8,2560]{1,0:T(8,128)(2,1)S(1)}, u32[]{:S(2)}, u32[]{:S(2)}) collective-permute-start(bf16[8,2560]{1,0:T(8,128)(2,1)S(1)} %get-tuple-element.80.flat_ref.rest_0_), channel_id=1, source_target_pairs={{0,3},{1,2},{2,1},{3,0},{4,7},{5,6},{6,5},{7,4},{8,11},{9,10},{10,... | collective-permute-start | bytes 122888 | tf_op jit(solution)/shard_map/ppermute | solution.py:343
  33.7 0.7 %collective-permute-start.12 = (bf16[8,2560]{1,0:T(8,128)(2,1)S(1)}, bf16[8,2560]{1,0:T(8,128)(2,1)S(1)}, u32[]{:S(2)}, u32[]{:S(2)}) collective-permute-start(bf16[8,2560]{1,0:T(8,128)(2,1)S(1)} %get-tuple-element.80.flat_ref.rest_0_), channel_id=1, source_target_pairs={{0,1},{1,0},{2,3},{3,2},{4,6},{5,7},{6,4},{7,5},{8,9},{9,8},{10,11... | collective-permute-start | bytes 122888 | tf_op jit(solution)/shard_map/ppermute | solution.py:343
  34.4 0.8 %stats.1 = (f32[8,128]{1,0:T(8,128)S(1)}, bf16[10,6,256]{2,1,0:T(8,128)(2,1)}) custom-call(bf16[8,2560]{1,0:T(8,128)(2,1)S(1)} %get-tuple-element.80.flat_ref.rest_0_, f32[1,25600]{1,0:T(1,128)S(1)} %bitcast.13, f32[1,25600]{1,0:T(1,128)S(1)} %bitcast.22, s32[1,25600]{1,0:T(1,128)S(1)} %bitcast.20, f32[1,3200]{1,0:T(1,128)S(1)} %get-tuple-element.81.trait_ref, ...), custom_call_target="tpu_custom_call" | custom-call | tf_op jit(solution)/shard_map/stats/pallas_call | solution.py:429
  35.2 0.7 %collective-permute-done.14.rest_3_ = bf16[8,2560]{1,0:T(8,128)(2,1)S(1)} collective-permute-done((bf16[8,2560]{1,0:T(8,128)(2,1)S(1)}, bf16[8,2560]{1,0:T(8,128)(2,1)S(1)}, u32[]{:S(2)}, u32[]{:S(2)}) %collective-permute-start.14) | collective-permute-done | bytes 40992 | tf_op jit(solution)/shard_map/ppermute | solution.py:343
  35.9 3.1 %collective-permute-done.13.rest_2_ = bf16[8,2560]{1,0:T(8,128)(2,1)S(1)} collective-permute-done((bf16[8,2560]{1,0:T(8,128)(2,1)S(1)}, bf16[8,2560]{1,0:T(8,128)(2,1)S(1)}, u32[]{:S(2)}, u32[]{:S(2)}) %collective-permute-start.13) | collective-permute-done | bytes 40992 | tf_op jit(solution)/shard_map/ppermute | solution.py:343
  39.2 2.3 %collective-permute-start.16 = (f32[8,128]{1,0:T(8,128)S(1)}, f32[8,128]{1,0:T(8,128)S(1)}, u32[]{:S(2)}, u32[]{:S(2)}) collective-permute-start(f32[8,128]{1,0:T(8,128)S(1)} %pair.1), channel_id=1, source_target_pairs={{0,24},{4,28},{8,16},{12,20},{16,8},{20,12},{24,0},{28,4},{1,25},{... | collective-permute-start | bytes 12296 | tf_op jit(solution)/shard_map/ppermute | solution.py:334
  42.1 1.7 %collective-permute-done.16.common_ref = f32[8,128]{1,0:T(8,128)S(1)} collective-permute-done((f32[8,128]{1,0:T(8,128)S(1)}, f32[8,128]{1,0:T(8,128)S(1)}, u32[]{:S(2)}, u32[]{:S(2)}) %collective-permute-start.16) | collective-permute-done | bytes 4128 | tf_op jit(solution)/shard_map/ppermute | solution.py:334
  43.8 1.4 %collective-permute-done.17.rest_0_ = f32[8,128]{1,0:T(8,128)S(1)} collective-permute-done((f32[8,128]{1,0:T(8,128)S(1)}, f32[8,128]{1,0:T(8,128)S(1)}, u32[]{:S(2)}, u32[]{:S(2)}) %collective-permute-start.17) | collective-permute-done | bytes 4128 | tf_op jit(solution)/shard_map/ppermute | solution.py:343
  45.2 1.2 %collective-permute-done.18.rest_1_ = f32[8,128]{1,0:T(8,128)S(1)} collective-permute-done((f32[8,128]{1,0:T(8,128)S(1)}, f32[8,128]{1,0:T(8,128)S(1)}, u32[]{:S(2)}, u32[]{:S(2)}) %collective-permute-start.18) | collective-permute-done | bytes 4128 | tf_op jit(solution)/shard_map/ppermute | solution.py:334
  46.3 0.7 %final.1 = (f32[6,24]{1,0:T(8,128)}, f32[1,6]{1,0:T(1,128)}, f32[1,6]{1,0:T(1,128)}) custom-call(f32[8,128]{1,0:T(8,128)S(1)} %get-tuple-element.87.count_ref, f32[8,128]{1,0:T(8,128)S(1)} %add.3.own_ref, f32[8,128]{1,0:T(8,128)S(1)} %collective-permute-done.16.common_ref, f32[8,128]{1,0:T(8,128)S(1)} %collective-permute-done.17.rest_0_, ...), custom_call_target="tpu_custom_call" | custom-call | tf_op jit(solution)/shard_map/final/pallas_call | solution.py:429
  (41 shorter events, 4.3 us)
Async XLA Ops:
  6.5 3.7 %collective-permute-start = (bf16[3,8,4992]{2,1,0:T(8,128)(2,1)S(1)}, bf16[3,8,4992]{2,1,0:T(8,128)(2,1)S(1)}, u32[]{:S(2)}, u32[]{:S(2)}) collective-permute-start(bf16[3,8,4992]{2,1,0:T(8,128)(2,1)S(1)} %get-tuple-element.54), channel_id=1, source_target_pairs={{0,4},{4,0},{8,12},{12,8},{16,20},{20,16},{24,28},{28,24},{1,5},{5... | collective-permute-start | bytes 718856 | tf_op jit(solution)/shard_map/ppermute | solution.py:334
  10.2 7.9 %collective-permute-start.2 = (bf16[8,4992]{1,0:T(8,128)(2,1)S(1)}, bf16[8,4992]{1,0:T(8,128)(2,1)S(1)}, u32[]{:S(2)}, u32[]{:S(2)}) collective-permute-start(bf16[8,4992]{1,0:T(8,128)(2,1)S(1)} %get-tuple-element.61), channel_id=1, source_target_pairs={{0,24},{1,25},{2,26},{3,27},{4,28},{5,29},{6,30},{7,31},{8,16},{9,... | collective-permute-start | bytes 239624 | tf_op jit(solution)/shard_map/ppermute | solution.py:343
  13.7 4.9 %collective-permute-start.3 = (bf16[8,4992]{1,0:T(8,128)(2,1)S(1)}, bf16[8,4992]{1,0:T(8,128)(2,1)S(1)}, u32[]{:S(2)}, u32[]{:S(2)}) collective-permute-start(bf16[8,4992]{1,0:T(8,128)(2,1)S(1)} %get-tuple-element.62), channel_id=1, source_target_pairs={{0,16},{1,17},{2,18},{3,19},{4,12},{5,13},{6,14},{7,15},{8,24},{9,... | collective-permute-start | bytes 239624 | tf_op jit(solution)/shard_map/ppermute | solution.py:343
  14.3 4.5 %collective-permute-start.4 = (bf16[8,4992]{1,0:T(8,128)(2,1)S(1)}, bf16[8,4992]{1,0:T(8,128)(2,1)S(1)}, u32[]{:S(2)}, u32[]{:S(2)}) collective-permute-start(bf16[8,4992]{1,0:T(8,128)(2,1)S(1)} %get-tuple-element.63), channel_id=1, source_target_pairs={{0,8},{1,9},{2,10},{3,11},{4,20},{5,21},{6,22},{7,23},{8,0},{9,1},... | collective-permute-start | bytes 239624 | tf_op jit(solution)/shard_map/ppermute | solution.py:343
  17.3 1.4 %collective-permute-start.1 = (bf16[1,8,4992]{2,1,0:T(8,128)(2,1)S(1)}, bf16[1,8,4992]{2,1,0:T(8,128)(2,1)S(1)}, u32[]{:S(2)}, u32[]{:S(2)}) collective-permute-start(bf16[1,8,4992]{2,1,0:T(8,128)(2,1)S(1)} %get-tuple-element.60), channel_id=1, source_target_pairs={{0,4},{4,0},{8,12},{12,8},{16,20},{20,16},{24,28},{28,24},{1,5},{5... | collective-permute-start | bytes 239624 | tf_op jit(solution)/shard_map/ppermute | solution.py:334
  17.4 1.4 %copy-start = (f32[25600]{0:T(1024)S(1)}, f32[25600]{0:T(1024)}, u32[]{:S(2)}) copy-start(f32[25600]{0:T(1024)} %param.7) | copy-start | bytes 307204
  17.4 1.3 %copy-start.2 = (f32[25600]{0:T(1024)S(1)}, f32[25600]{0:T(1024)}, u32[]{:S(2)}) copy-start(f32[25600]{0:T(1024)} %param.8) | copy-start | bytes 307204
  17.4 5.1 %copy-start.1 = (s32[25600]{0:T(1024)S(1)}, s32[25600]{0:T(1024)}, u32[]{:S(2)}) copy-start(s32[25600]{0:T(1024)} %param.9) | copy-start | bytes 307204
  18.9 3.6 %collective-permute-start.5 = (bf16[8,4096]{1,0:T(8,128)(2,1)S(1)}, bf16[8,4096]{1,0:T(8,128)(2,1)S(1)}, u32[]{:S(2)}, u32[]{:S(2)}) collective-permute-start(bf16[8,4096]{1,0:T(8,128)(2,1)S(1)} %get-tuple-element.64.refs_4_), channel_id=1, source_target_pairs={{0,4},{4,0},{8,12},{12,8},{16,20},{20,16},{24,28},{28,24},{1,5},{5... | collective-permute-start | bytes 196616 | tf_op jit(solution)/shard_map/ppermute | solution.py:334
  19.1 5.4 %collective-permute-start.6 = (bf16[8,4096]{1,0:T(8,128)(2,1)S(1)}, bf16[8,4096]{1,0:T(8,128)(2,1)S(1)}, u32[]{:S(2)}, u32[]{:S(2)}) collective-permute-start(bf16[8,4096]{1,0:T(8,128)(2,1)S(1)} %get-tuple-element.64.refs_4_), channel_id=1, source_target_pairs={{0,24},{1,25},{2,26},{3,27},{4,28},{5,29},{6,30},{7,31},{8,16},{9,... | collective-permute-start | bytes 196616 | tf_op jit(solution)/shard_map/ppermute | solution.py:343
  21.9 4.3 %collective-permute-start.7 = (bf16[8,4096]{1,0:T(8,128)(2,1)S(1)}, bf16[8,4096]{1,0:T(8,128)(2,1)S(1)}, u32[]{:S(2)}, u32[]{:S(2)}) collective-permute-start(bf16[8,4096]{1,0:T(8,128)(2,1)S(1)} %get-tuple-element.64.refs_4_), channel_id=1, source_target_pairs={{0,16},{1,17},{2,18},{3,19},{4,12},{5,13},{6,14},{7,15},{8,24},{9,... | collective-permute-start | bytes 196616 | tf_op jit(solution)/shard_map/ppermute | solution.py:343
  22.4 4.4 %collective-permute-start.9 = (bf16[8,4096]{1,0:T(8,128)(2,1)S(1)}, bf16[8,4096]{1,0:T(8,128)(2,1)S(1)}, u32[]{:S(2)}, u32[]{:S(2)}) collective-permute-start(bf16[8,4096]{1,0:T(8,128)(2,1)S(1)} %get-tuple-element.64.refs_4_), channel_id=1, source_target_pairs={{0,8},{1,9},{2,10},{3,11},{4,20},{5,21},{6,22},{7,23},{8,0},{9,1},... | collective-permute-start | bytes 196616 | tf_op jit(solution)/shard_map/ppermute | solution.py:343
  24.5 3.6 %collective-permute-start.11 = (bf16[8,4096]{1,0:T(8,128)(2,1)S(1)}, bf16[8,4096]{1,0:T(8,128)(2,1)S(1)}, u32[]{:S(2)}, u32[]{:S(2)}) collective-permute-start(bf16[8,4096]{1,0:T(8,128)(2,1)S(1)} %relay.3.refs_3_), channel_id=1, source_target_pairs={{0,4},{4,0},{8,12},{12,8},{16,20},{20,16},{24,28},{28,24},{1,5},{5... | collective-permute-start | bytes 196616 | tf_op jit(solution)/shard_map/ppermute | solution.py:334
  26.9 1.8 %collective-permute-start.10 = (bf16[8,4096]{1,0:T(8,128)(2,1)S(1)}, bf16[8,4096]{1,0:T(8,128)(2,1)S(1)}, u32[]{:S(2)}, u32[]{:S(2)}) collective-permute-start(bf16[8,4096]{1,0:T(8,128)(2,1)S(1)} %relay.5.refs_3_), channel_id=1, source_target_pairs={{0,4},{4,0},{8,12},{12,8},{16,20},{20,16},{24,28},{28,24},{1,5},{5... | collective-permute-start | bytes 196616 | tf_op jit(solution)/shard_map/ppermute | solution.py:334
  27.0 1.8 %collective-permute-start.8 = (bf16[8,4096]{1,0:T(8,128)(2,1)S(1)}, bf16[8,4096]{1,0:T(8,128)(2,1)S(1)}, u32[]{:S(2)}, u32[]{:S(2)}) collective-permute-start(bf16[8,4096]{1,0:T(8,128)(2,1)S(1)} %relay.4.refs_3_), channel_id=1, source_target_pairs={{0,4},{4,0},{8,12},{12,8},{16,20},{20,16},{24,28},{28,24},{1,5},{5... | collective-permute-start | bytes 196616 | tf_op jit(solution)/shard_map/ppermute | solution.py:334
  29.9 6.0 %collective-permute-start.14 = (bf16[8,2560]{1,0:T(8,128)(2,1)S(1)}, bf16[8,2560]{1,0:T(8,128)(2,1)S(1)}, u32[]{:S(2)}, u32[]{:S(2)}) collective-permute-start(bf16[8,2560]{1,0:T(8,128)(2,1)S(1)} %get-tuple-element.80.flat_ref.rest_0_), channel_id=1, source_target_pairs={{0,3},{1,2},{2,1},{3,0},{4,7},{5,6},{6,5},{7,4},{8,11},{9,10},{10,... | collective-permute-start | bytes 122888 | tf_op jit(solution)/shard_map/ppermute | solution.py:343
  33.7 5.3 %collective-permute-start.13 = (bf16[8,2560]{1,0:T(8,128)(2,1)S(1)}, bf16[8,2560]{1,0:T(8,128)(2,1)S(1)}, u32[]{:S(2)}, u32[]{:S(2)}) collective-permute-start(bf16[8,2560]{1,0:T(8,128)(2,1)S(1)} %get-tuple-element.80.flat_ref.rest_0_), channel_id=1, source_target_pairs={{0,2},{1,3},{2,0},{3,1},{4,5},{5,4},{6,7},{7,6},{8,10},{9,11},{10,... | collective-permute-start | bytes 122888 | tf_op jit(solution)/shard_map/ppermute | solution.py:343
  33.7 5.3 %collective-permute-start.12 = (bf16[8,2560]{1,0:T(8,128)(2,1)S(1)}, bf16[8,2560]{1,0:T(8,128)(2,1)S(1)}, u32[]{:S(2)}, u32[]{:S(2)}) collective-permute-start(bf16[8,2560]{1,0:T(8,128)(2,1)S(1)} %get-tuple-element.80.flat_ref.rest_0_), channel_id=1, source_target_pairs={{0,1},{1,0},{2,3},{3,2},{4,6},{5,7},{6,4},{7,5},{8,9},{9,8},{10,11... | collective-permute-start | bytes 122888 | tf_op jit(solution)/shard_map/ppermute | solution.py:343
  39.2 2.4 %collective-permute-start.15 = (f32[8,128]{1,0:T(8,128)S(1)}, f32[8,128]{1,0:T(8,128)S(1)}, u32[]{:S(2)}, u32[]{:S(2)}) collective-permute-start(f32[8,128]{1,0:T(8,128)S(1)} %pair.1), channel_id=1, source_target_pairs={{0,4},{4,0},{8,12},{12,8},{16,20},{20,16},{24,28},{28,24},{1,5},{5... | collective-permute-start | bytes 12296 | tf_op jit(solution)/shard_map/ppermute | solution.py:334
  39.2 4.6 %collective-permute-start.16 = (f32[8,128]{1,0:T(8,128)S(1)}, f32[8,128]{1,0:T(8,128)S(1)}, u32[]{:S(2)}, u32[]{:S(2)}) collective-permute-start(f32[8,128]{1,0:T(8,128)S(1)} %pair.1), channel_id=1, source_target_pairs={{0,24},{4,28},{8,16},{12,20},{16,8},{20,12},{24,0},{28,4},{1,25},{... | collective-permute-start | bytes 12296 | tf_op jit(solution)/shard_map/ppermute | solution.py:334
  41.6 3.6 %collective-permute-start.17 = (f32[8,128]{1,0:T(8,128)S(1)}, f32[8,128]{1,0:T(8,128)S(1)}, u32[]{:S(2)}, u32[]{:S(2)}) collective-permute-start(f32[8,128]{1,0:T(8,128)S(1)} %add.3.own_ref), channel_id=1, source_target_pairs={{0,8},{1,9},{2,10},{3,11},{4,20},{5,21},{6,22},{7,23},{8,0},{9,1},... | collective-permute-start | bytes 12296 | tf_op jit(solution)/shard_map/ppermute | solution.py:343
  43.8 1.4 %collective-permute-start.19 = (f32[8,128]{1,0:T(8,128)S(1)}, f32[8,128]{1,0:T(8,128)S(1)}, u32[]{:S(2)}, u32[]{:S(2)}) collective-permute-start(f32[8,128]{1,0:T(8,128)S(1)} %collective-permute-done.16.common_ref), channel_id=1, source_target_pairs={{0,4},{4,0},{8,12},{12,8},{16,20},{20,16},{24,28},{28,24},{1,5},{5... | collective-permute-start | bytes 12296 | tf_op jit(solution)/shard_map/ppermute | solution.py:334
  45.2 1.2 %collective-permute-start.18 = (f32[8,128]{1,0:T(8,128)S(1)}, f32[8,128]{1,0:T(8,128)S(1)}, u32[]{:S(2)}, u32[]{:S(2)}) collective-permute-start(f32[8,128]{1,0:T(8,128)S(1)} %collective-permute-done.17.rest_0_), channel_id=1, source_target_pairs={{0,4},{4,0},{8,12},{12,8},{16,20},{20,16},{24,28},{28,24},{1,5},{5... | collective-permute-start | bytes 12296 | tf_op jit(solution)/shard_map/ppermute | solution.py:334

commit v4 on v1

--- a/solution.py
+++ b/solution.py
@@ -56,7 +56,11 @@
     return value[:, :span], jnp.concatenate([low, pltpu.roll(low, 4, 0)], axis=1)
 
 
-def moments_kernel(snps, distances, opening, taken, given, geno_ref, *rest):
+def owner_of(chip, keep):
+    return 2 * chip + (core() if keep else 1 - core())
+
+
+def moments_kernel(snps, chip, keep, opening, taken, given, geno_ref, *rest):
     rest = list(rest)
     if opening:
         bits_ref, trait_ref, kept_ref, sums_ref, local_ref, left_ref = rest[:6]
@@ -72,27 +76,27 @@
     tail = snps - (devices - 1) * block
     span = sums_ref.shape[2] * 2 // 3
 
-    def copy(distance, target, semaphore, width):
-        start = pl.multiple_of((lax.axis_index("ind") ^ distance) * block, LANES)
+    def copy(owner, target, semaphore, width):
+        start = pl.multiple_of(owner * block, LANES)
         return pltpu.make_async_copy(
             geno_ref.at[:, pl.ds(start, width)], target.at[:, pl.ds(0, width)], semaphore
         )
 
-    def whole_or_tail(distance, target, semaphore, act):
+    def whole_or_tail(owner, target, semaphore, act):
         if tail == block:
-            act(copy(distance, target, semaphore, block))
+            act(copy(owner, target, semaphore, block))
         else:
-            last = (lax.axis_index("ind") ^ distance) == devices - 1
-            pl.when(last)(lambda: act(copy(distance, target, semaphore, tail)))
-            pl.when(jnp.logical_not(last))(lambda: act(copy(distance, target, semaphore, block)))
+            last = owner == devices - 1
+            pl.when(last)(lambda: act(copy(owner, target, semaphore, tail)))
+            pl.when(jnp.logical_not(last))(lambda: act(copy(owner, target, semaphore, block)))
 
     if fetched:
         buffer, arrived = rest[:2]
         rest = rest[2:]
 
         def fetch(index, act):
-            distance = distances[0] - 2 * (index + taken)
-            whole_or_tail(distance, buffer.at[index], arrived.at[index], act)
+            owner = owner_of(chip + index + taken, keep)
+            whole_or_tail(owner, buffer.at[index], arrived.at[index], act)
 
     if raw_out is not None:
         raw_arrived = rest.pop(0)
@@ -106,7 +110,7 @@
     if fetched:
         pl.loop(0, fetched)(lambda index: fetch(index, lambda c: c.start()))
     if raw_out is not None:
-        whole_or_tail(given, raw_out, raw_arrived, lambda c: c.start())
+        whole_or_tail(owner_of(*given), raw_out, raw_arrived, lambda c: c.start())
     if opening:
         bits_copy.wait()
         trait_copy.wait()
@@ -154,67 +158,65 @@
             work(index + taken, buffer.at[index])
 
     if raw_out is not None:
-        whole_or_tail(given, raw_out, raw_arrived, lambda c: c.wait())
-
-
-def cores_kernel(left_ref, here_ref, away_ref, *outs):
-    outs, left_out = outs[:-1], outs[-1]
+        whole_or_tail(owner_of(*given), raw_out, raw_arrived, lambda c: c.wait())
+
+
+def cores_kernel(left_ref, here_ref, away_ref, out_ref, left_out):
     left_out[...] = left_ref[...]
-    for index, out in enumerate(outs):
-        out[...] = (here_ref[index].astype(F32) + away_ref[index].astype(F32)).astype(BF16)
-
-
-def relay_kernel(token_ref, value_ref, out_ref):
-    out_ref[...] = value_ref[...]
-
-
-def weights_kernel(mean_ref, scale_ref, own_ref, near_ref, *refs):
+    for slot in range(out_ref.shape[0]):
+        total = here_ref[slot].astype(F32) + away_ref[slot].astype(F32)
+        out_ref[slot] = total.astype(BF16)
+
+
+def weights_kernel(chip, token_ref, mean_ref, scale_ref, *refs):
     parts, (u_ref, trait_ref) = refs[:-2], refs[-2:]
-    block = trait_ref.shape[1]
-    width = u_ref.shape[1] - block
-    here = pl.ds(pl.multiple_of(lax.axis_index("ind") * block, LANES), block)
-    parts = [own_ref[0], near_ref[0]] + [part[...] for part in parts]
-    total = tree_sum([part.astype(F32) for part in parts])
-    shift = mean_ref[:, here] - 1.0
-    inverse = 1.0 / scale_ref[:, here]
-    high, low = [
-        (part[:, :block] - part[:, block : block + 1] * shift) * inverse
-        for part in unpack_sums(total)
-    ]
-    trait_ref[...] = low[2:3] + low[3:4]
-    high, low = [part.astype(BF16).astype(F32) * inverse for part in (high, low)]
-    low = jnp.concatenate([low, jnp.zeros((SUBLANES, 4 * width - block), F32)], axis=1)
-    folded = low[:, :width]
-    for j in range(1, 4):
-        turned = pltpu.roll(low[:, j * width : (j + 1) * width], 2 * j, 0)
-        folded = jnp.where(rows_iota(SUBLANES) < 2 * j, folded, turned)
-    u_ref[:, :block] = high.astype(BF16)
-    u_ref[:, block:] = folded.astype(BF16)
-
-
-def stats_kernel(own_bins, order, flat_ref, mean_ref, scale_ref, label_ref, trait_ref, *rest):
-    locals_, (out_ref, field_ref) = rest[:-2], rest[-2:]
-    block = trait_ref.shape[1]
-    rows = order[0]
+    slots, _, block = trait_ref.shape
+    width = u_ref.shape[2] - block
+    for slot in range(slots):
+        here = pl.ds(pl.multiple_of(owner_of(chip + slot, True) * block, LANES), block)
+        total = [part[slot].astype(F32) for part in parts]
+        total = tree_sum(total[:1] + total[:0:-1])
+        shift = mean_ref[:, here] - 1.0
+        inverse = 1.0 / scale_ref[:, here]
+        high, low = [
+            (part[:, :block] - part[:, block : block + 1] * shift) * inverse
+            for part in unpack_sums(total)
+        ]
+        trait_ref[slot] = low[2:3] + low[3:4]
+        high, low = [part.astype(BF16).astype(F32) * inverse for part in (high, low)]
+        low = jnp.concatenate([low, jnp.zeros((SUBLANES, 4 * width - block), F32)], axis=1)
+        folded = low[:, :width]
+        for j in range(1, 4):
+            turned = pltpu.roll(low[:, j * width : (j + 1) * width], 2 * j, 0)
+            folded = jnp.where(rows_iota(SUBLANES) < 2 * j, folded, turned)
+        u_ref[slot, :, :block] = high.astype(BF16)
+        u_ref[slot, :, block:] = folded.astype(BF16)
+
+
+def stats_kernel(own_bins, groups, flat_ref, mean_ref, scale_ref, label_ref, *rest):
+    rest, (out_ref, field_ref) = list(rest[:-2]), rest[-2:]
+    rows = flat_ref.shape[1] // PROBES
     bins = rows_iota(SUBLANES)
-
-    def member_of(owner):
-        here = pl.ds(pl.multiple_of(owner * block, LANES), block)
-        member = label_ref[:, here] - lax.axis_index("bin") * own_bins == bins
-        return here, member & (bins < own_bins)
-
     trace = jnp.zeros((SUBLANES, 1), F32)
-    for ref, distances in zip(locals_, order[1]):
-        for slot, distance in enumerate(distances):
-            here, member = member_of(lax.axis_index("ind") ^ distance)
+    quad = jnp.zeros((SUBLANES, 1), F32)
+    for chip, keep in groups:
+        local_ref = rest.pop(0)
+        trait_ref = rest.pop(0) if keep else None
+        slots, _, block = local_ref.shape
+        for slot in range(slots):
+            owner = owner_of(chip + slot, keep)
+            here = pl.ds(pl.multiple_of(owner * block, LANES), block)
+            member = label_ref[:, here] - lax.axis_index("bin") * own_bins == bins
+            member = member & (bins < own_bins)
             shift = mean_ref[:, here] - 1.0
             inverse = 1.0 / scale_ref[:, here]
-            square = ref[slot, 1:2] - 2.0 * shift * ref[slot, 0:1] + rows * shift * shift
+            square = local_ref[slot, 1:2] - 2.0 * shift * local_ref[slot, 0:1] + rows * shift * shift
             square = square * (inverse * inverse)
             trace += jnp.sum(jnp.where(member, square, 0.0), axis=1, keepdims=True)
-    _, member = member_of(lax.axis_index("ind"))
-    trait = trait_ref[...]
-    quad = jnp.sum(jnp.where(member, trait * trait, 0.0), axis=1, keepdims=True)
+            if keep:
+                mine = member & (owner == lax.axis_index("ind"))
+                trait = trait_ref[slot]
+                quad += jnp.sum(jnp.where(mine, trait * trait, 0.0), axis=1, keepdims=True)
     lane = lax.broadcasted_iota(jnp.int32, (SUBLANES, LANES), 1)
     out_ref[...] = jnp.where(lane == TRACE_LANE, trace, jnp.where(lane == QUAD_LANE, quad, 0.0))
     flat = flat_ref[...].astype(F32)
@@ -226,7 +228,7 @@
     refs = list(refs)
     mean_ref, label_ref = refs[:2]
     kept_refs, refs = refs[2 : 2 + sources], refs[2 + sources :]
-    u_refs, refs = refs[: len(blocks)], refs[len(blocks) :]
+    u_refs, refs = refs[:sources], refs[sources:]
     rows, block = kept_refs[0].shape[1:]
     bins = rows_iota(SUBLANES)
     if started:
@@ -236,9 +238,9 @@
         acc = jnp.zeros((rows, PROBES * SUBLANES), F32)
         offset = jnp.zeros((PROBES * SUBLANES, LANES), F32)
         number = jnp.zeros((SUBLANES, LANES), F32)
-    for index, (slot, distance) in enumerate(blocks):
-        start = (lax.axis_index("ind") ^ distance) * block
-        u = u_refs[index][...].astype(F32)
+    for chip, keep, source, slot in blocks:
+        start = owner_of(chip, keep) * block
+        u = u_refs[source][slot].astype(F32)
         lines = [u[b : b + 1, :block] for b in range(SUBLANES)]
         for b in range(PROBES - SUBLANES):
             line = [u[2 * j + b : 2 * j + b + 1, block:] for j in range(4)]
@@ -253,7 +255,7 @@
             offset += jnp.concatenate([fold_lanes(value * mean) for value in spread], axis=0)
             number += fold_lanes(jnp.where(member, 1.0, 0.0))
             acc += lax.dot_general(
-                kept_refs[index if sources > 1 else 0][slot, :, at : at + width],
+                kept_refs[source][slot, :, at : at + width],
                 jnp.concatenate(spread, axis=0).astype(BF16),
                 (((1,), (1,)), ((), ())),
                 preferred_element_type=F32,
@@ -272,8 +274,19 @@
     flat_ref[...] = jnp.concatenate(flat, axis=1).astype(BF16)
 
 
+def relay_kernel(token_ref, value_ref, out_ref):
+    out_ref[...] = value_ref[...]
+
+
+def weights_field_kernel(own_bins, chip, count, token_ref, mean_ref, scale_ref, label_ref, kept_ref, *refs):
+    parts, (u_ref, trait_ref), terms = refs[:-5], refs[-5:-3], refs[-3:]
+    weights_kernel(chip, token_ref, mean_ref, scale_ref, *parts, u_ref, trait_ref)
+    blocks = [(chip + slot, True, 0, slot) for slot in range(count)]
+    field_kernel(own_bins, blocks, 1, False, False, mean_ref, label_ref, kept_ref, u_ref, *terms)
+
+
 def pair_kernel(stats_ref, *rest):
-    flats, out_ref = rest[:-1], rest[-1]
+    flats, out_ref = rest[-2::-1], rest[-1]
     everyone = [flat[...].astype(F32) for flat in flats]
     everyone += [jnp.zeros_like(everyone[0])] * (LANES // SUBLANES - len(flats))
     out_ref[...] = stats_ref[...] + lax.dot_general(
@@ -360,8 +373,7 @@
         for value in (genotype, probe_bits, phenotype)
     ]
 
-    def moments(distances, given, extra, name):
-        slots = len(distances)
+    def moments(chip, slots, keep, given, extra, name):
         opening = extra[0] is probe_bits
         taken = int(not opening and extra[0] is not None)
         extra = [value for value in extra if value is not None]
@@ -387,7 +399,7 @@
                 pltpu.SemaphoreType.DMA((2,)),
             ]
         return pl.pallas_call(
-            functools.partial(moments_kernel, snps, distances, opening, taken, given),
+            functools.partial(moments_kernel, snps, chip, keep, opening, taken, given),
             in_specs=[in_hbm()] + [in_hbm() if opening else in_vmem()] * len(extra),
             out_specs=[in_vmem()] * len(out_shape),
             scratch_shapes=scratch,
@@ -397,8 +409,8 @@
             name=name,
         )(genotype, *extra)
 
-    here_order = list(range(n - 2, 0, -2))
-    away_order = [d + 1 for d in here_order]
+    others = list(range(n - 2, 0, -2))
+    split = max(chips * 3 // 4, 1)
 
     def plain(kernel, operands, out_shape, name, **options):
         return pl.pallas_call(
@@ -411,33 +423,36 @@
             **options,
         )(*operands)
 
-    kept_away, away, local_away, left, raw = moments(
-        away_order, here_order[0], (probe_bits, phenotype), "moments_away"
-    )
-    away = swap(away, "ind", n, 1)
-    kept_here, here, local_here = moments(here_order, None, (raw, left), "moments_here")
-    packed = jax.ShapeDtypeStruct((SUBLANES, span * 3 // 2), BF16)
-    *sums, left = plain(
-        cores_kernel,
-        (left, here, away),
-        [packed] * (chips - 1) + [jax.ShapeDtypeStruct(left.shape, F32)],
-        "cores",
-    )
-    sums = [swap(value, "ind", n, d) for value, d in zip(sums, here_order)]
-    kept_near, near, local_near, raw = moments([1], 0, (None, left), "moments_near")
-    near = swap(near, "ind", n, 1)
-    kept_own, own, local_own = moments([0], None, (raw, left), "moments_own")
-
-    u, trait = plain(
-        weights_kernel,
-        (mean, scale, own, near, *sums),
-        [
-            jax.ShapeDtypeStruct((SUBLANES, folded), BF16),
-            jax.ShapeDtypeStruct((1, block), F32),
-        ],
-        "weights",
-    )
-
+    def cores(left, here, away):
+        return plain(
+            cores_kernel,
+            (left, here, away),
+            [jax.ShapeDtypeStruct(here.shape, BF16), jax.ShapeDtypeStruct(left.shape, F32)],
+            "cores",
+        )
+
+    def spread(value):
+        return [value] + [swap(value, "ind", n, d) for d in others]
+
+    late = chips - split
+    kept_a_give, give, local_a_give, left, raw = moments(
+        0, split, False, (0, True), (probe_bits, phenotype), "moments_a_give"
+    )
+    give = swap(give, "ind", n, 1)
+    kept_a_keep, keep, local_a_keep, raw = moments(
+        0, split, True, (split, False), (raw, left), "moments_a_keep"
+    )
+    sum_a, left = cores(left, keep, give)
+    parts_a = spread(sum_a)
+    kept_b_give, give, local_b_give, raw = moments(
+        split, late, False, (split, True), (raw, left), "moments_b_give"
+    )
+    give = swap(give, "ind", n, 1)
+    kept_b_keep, keep, local_b_keep = moments(
+        split, late, True, None, (raw, left), "moments_b_keep"
+    )
+    sum_b, token = cores(left, keep, give)
+    parts_b = spread(sum_b)
     number_shape = jax.ShapeDtypeStruct((SUBLANES, LANES), F32)
     term_shape = [
         jax.ShapeDtypeStruct((rows, PROBES * SUBLANES), F32),
@@ -452,32 +467,54 @@
             (mean, label, *kept, *us, *terms),
             end_shape if last else term_shape,
             "field",
-            cost_estimate=cost(1, 1),
+            cost_estimate=cost(0, 0),
         )
 
-    u_near = swap(u, "ind", n, 1)
-    u_here = [swap(u, "ind", n, d) for d in here_order]
-    terms = fields([kept_own, kept_near], [(0, 0), (0, 1)], [u, u_near], [])
-    u_away = []
-    for slot, (distance, value) in enumerate(zip(here_order, u_here)):
-        shape = [jax.ShapeDtypeStruct(value.shape, value.dtype)]
-        (value,) = plain(relay_kernel, (terms[2], value), shape, "relay")
-        u_away.append(swap(value, "ind", n, 1))
-        terms = fields([kept_here], [(slot, distance)], [value], terms)
-    blocks = list(enumerate(away_order))
-    middle = (chips - 1) // 2
-    terms = fields([kept_away], blocks[:middle], u_away[:middle], terms)
-    flat, number = fields([kept_away], blocks[middle:], u_away[middle:], terms, last=True)
+    def listed(chip, slots, keep, source):
+        return [(chip + slot, keep, source, slot) for slot in range(slots)]
+
+    def weights_shape(slots):
+        return [
+            jax.ShapeDtypeStruct((slots, SUBLANES, folded), BF16),
+            jax.ShapeDtypeStruct((slots, 1, block), F32),
+        ]
+
+    u_a, trait_a, *terms = plain(
+        functools.partial(weights_field_kernel, own_bins, 0, split - 1),
+        (token, mean, scale, label, kept_a_keep, *parts_a),
+        weights_shape(split) + term_shape,
+        "weights_field",
+    )
+    u_b, trait_b = plain(
+        functools.partial(weights_kernel, split),
+        (terms[2], mean, scale, *parts_b),
+        weights_shape(late),
+        "weights",
+    )
+    u_b_other = swap(u_b, "ind", n, 1)
+    (u_a,) = plain(
+        relay_kernel, (trait_b, u_a), [jax.ShapeDtypeStruct(u_a.shape, u_a.dtype)], "relay"
+    )
+    u_a_other = swap(u_a, "ind", n, 1)
+    blocks = [(split - 1, True, 0, split - 1)] + listed(split, late, True, 1)
+    terms = fields([kept_a_keep, kept_b_keep], blocks, [u_a, u_b], terms)
+    terms = fields([kept_a_give], listed(0, split, False, 0), [u_a_other], terms)
+    flat, number = fields(
+        [kept_b_give], listed(split, late, False, 0), [u_b_other], terms, last=True
+    )
 
     flats = [flat] + [swap(flat, "bin", n_bin, d) for d in range(1, n_bin)]
-    order = (rows, (away_order, here_order, [1], [0]))
+    groups = [(0, False), (0, True), (split, False), (split, True)]
     stats, field = plain(
-        functools.partial(stats_kernel, own_bins, order),
-        (flat, mean, scale, label, trait, local_away, local_here, local_near, local_own),
+        functools.partial(stats_kernel, own_bins, groups),
+        (
+            flat, mean, scale, label,
+            local_a_give, local_a_keep, trait_a, local_b_give, local_b_keep, trait_b,
+        ),
         [number_shape, jax.ShapeDtypeStruct((PROBES, own_bins, rows), BF16)],
         "stats",
     )
-    (part,) = plain(pair_kernel, (stats, *flats), [number_shape], "pair")
+    (part,) = plain(pair_kernel, (stats, *flats[::-1]), [number_shape], "pair")
     pairs, common = chosen_pairs(list(range(2, n, 2)))
     part_common = swap(part, "ind", n, common)
     part = part + swap(part, "ind", n, 1)

time: 46.3 us -> 49.3 us (1.065)
  waiting for transfers between devices: 9.98 us -> 12.6 us
    ppermute x19 -> x17, waiting for transfers between devices: 8.6 us -> 11.8 us  [swap(): return lax.ppermute(value, axis, [(i, i ^ distance) for i in range(size)])]
    ppermute x1, waiting for transfers between devices: 1.38 us -> 0.76 us  [swap_mixed(): lax.ppermute(value, 'ind', [(i, i ^ pair[i % 2]) for i in range(size)])]
    ppermute x1, starting transfers between devices: 0.64 us -> 1.24 us  [swap_mixed(): lax.ppermute(value, 'ind', [(i, i ^ pair[i % 2]) for i in range(size)])]
    ppermute x19 -> x17, starting transfers between devices: 15.9 us -> 15.7 us  [swap(): return lax.ppermute(value, axis, [(i, i ^ distance) for i in range(size)])]
    pallas_call x14 -> x11, Pallas kernels: 6.6 us -> 6.67 us  [plain(): pl.pallas_call(kernel, in_specs=[in_vmem()] * len(operands), out_specs=[i...]
  transfers between devices with their start and end apart: 20 -> 18, of which waited for: 9 -> 11; matrix products, arithmetic and copies ran while one was open for 0% -> 0% of each run, Pallas kernels for 25% -> 25%
where the time goes in v4:
time: 49.3 us; the launch traced here: 49.1 us
  Pallas kernels  18.7 us (38%)
  starting transfers between devices  16.9 us (34%)
  waiting for transfers between devices  12.6 us (26%)
  between operations  0.8 us (2%)
    ppermute x17, starting transfers between devices, swap(): return lax.ppermute(value, axis, [(i, i ^ distance) for i in range(size)])  15.7 us
    pallas_call x4, Pallas kernels, moments(): pl.pallas_call(functools.partial(moments_kernel, snps, chip, keep, openin...  12 us
    ppermute x17, waiting for transfers between devices, swap(): return lax.ppermute(value, axis, [(i, i ^ distance) for i in range(size)])  11.8 us
    pallas_call x11, Pallas kernels, plain(): pl.pallas_call(kernel, in_specs=[in_vmem()] * len(operands), out_specs=[i...  6.67 us
    ppermute x1, starting transfers between devices, swap_mixed(): lax.ppermute(value, 'ind', [(i, i ^ pair[i % 2]) for i in range(size)])  1.24 us
  transfers between devices with their start and end apart: 18, of which 11 were waited for; matrix products, arithmetic and copies ran while one was open for 0% of the time, Pallas kernels for 25%

profile of v4, /device:TPU:0, one launch (start us, length us, event | category | flops | bytes accessed | tf_op | source)
XLA Modules:
  0.0 49.1 jit_solution(17931130696653118403)
XLA Ops:
  0.6 4.9 %moments_a_give.1 = (bf16[3,256,3200]{2,1,0:T(8,128)(2,1)S(1)}, bf16[3,8,4992]{2,1,0:T(8,128)(2,1)S(1)}, f32[3,2,3200]{2,1,0:T(2,128)S(1)}, f32[16,256]{1,0:T(8,128)S(1)}, s32[256,3200]{1,0:T(8,128)S(1)}) custom-call(s32[256,25600]{1,0:T(8,128)} %geno_ref.7, s32[10,256]{1,0:T(8,128)} %rest_0_.1, bf16[256]{0:T(256)(128)(2,1)} %rest_1_.1), custom_call_target="tpu_custom_call" | custom-call | flops 1 | bytes 9830400 | tf_op jit(solution)/shard_map/moments_a_give/pallas_call | solution.py:401
  6.0 4.0 %moments_a_keep.1 = (bf16[3,256,3200]{2,1,0:T(8,128)(2,1)S(1)}, bf16[3,8,4992]{2,1,0:T(8,128)(2,1)S(1)}, f32[3,2,3200]{2,1,0:T(2,128)S(1)}, s32[256,3200]{1,0:T(8,128)S(1)}) custom-call(s32[256,25600]{1,0:T(8,128)} %geno_ref.7, s32[256,3200]{1,0:T(8,128)S(1)} %get-tuple-element.44.rest_0_, f32[16,256]{1,0:T(8,128)S(1)} %get-tuple-element.45.rest_1_.left_ref), custom_call_target="tpu_custom_call" | custom-call | flops 1 | bytes 9830400 | tf_op jit(solution)/shard_map/moments_a_keep/pallas_call | solution.py:401
  10.2 3.5 %collective-permute-start.2 = (bf16[3,8,4992]{2,1,0:T(8,128)(2,1)S(1)}, bf16[3,8,4992]{2,1,0:T(8,128)(2,1)S(1)}, u32[]{:S(2)}, u32[]{:S(2)}) collective-permute-start(bf16[3,8,4992]{2,1,0:T(8,128)(2,1)S(1)} %get-tuple-element.56.refs_0_), channel_id=1, source_target_pairs={{0,24},{4,28},{8,16},{12,20},{16,8},{20,12},{24,0},{28,4},{1,25},{... | collective-permute-start | bytes 718856 | tf_op jit(solution)/shard_map/ppermute | solution.py:326
  14.3 2.5 %moments_b_give.1 = (bf16[1,256,3200]{2,1,0:T(8,128)(2,1)S(1)}, bf16[1,8,4992]{2,1,0:T(8,128)(2,1)S(1)}, f32[1,2,3200]{2,1,0:T(2,128)S(1)}, s32[256,3200]{1,0:T(8,128)S(1)}) custom-call(s32[256,25600]{1,0:T(8,128)} %geno_ref.7, s32[256,3200]{1,0:T(8,128)S(1)} %get-tuple-element.46.rest_0_, f32[16,256]{1,0:T(8,128)S(1)} %get-tuple-element.49.rest_1_.left_ref), custom_call_target="tpu_custom_call" | custom-call | flops 1 | bytes 1 | tf_op jit(solution)/shard_map/moments_b_give/pallas_call | solution.py:401
  16.9 0.7 %moments_b_keep.1 = (bf16[1,256,3200]{2,1,0:T(8,128)(2,1)S(1)}, bf16[1,8,4992]{2,1,0:T(8,128)(2,1)S(1)}, f32[1,2,3200]{2,1,0:T(2,128)S(1)}) custom-call(s32[256,25600]{1,0:T(8,128)} %geno_ref.7, s32[256,3200]{1,0:T(8,128)S(1)} %get-tuple-element.51.rest_0_, f32[16,256]{1,0:T(8,128)S(1)} %get-tuple-element.49.rest_1_.left_ref), custom_call_target="tpu_custom_call" | custom-call | flops 1 | bytes 1 | tf_op jit(solution)/shard_map/moments_b_keep/pallas_call | solution.py:401
  17.6 0.6 %collective-permute-done.1.away_ref = bf16[1,8,4992]{2,1,0:T(8,128)(2,1)S(1)} collective-permute-done((bf16[1,8,4992]{2,1,0:T(8,128)(2,1)S(1)}, bf16[1,8,4992]{2,1,0:T(8,128)(2,1)S(1)}, u32[]{:S(2)}, u32[]{:S(2)}) %collective-permute-start.1) | collective-permute-done | bytes 79904 | tf_op jit(solution)/shard_map/ppermute | solution.py:326
  18.2 2.9 %collective-permute-start.5 = (bf16[1,8,4992]{2,1,0:T(8,128)(2,1)S(1)}, bf16[1,8,4992]{2,1,0:T(8,128)(2,1)S(1)}, u32[]{:S(2)}, u32[]{:S(2)}) collective-permute-start(bf16[1,8,4992]{2,1,0:T(8,128)(2,1)S(1)} %get-tuple-element.58.refs_0_), channel_id=1, source_target_pairs={{0,24},{4,28},{8,16},{12,20},{16,8},{20,12},{24,0},{28,4},{1,25},{... | collective-permute-start | bytes 239624 | tf_op jit(solution)/shard_map/ppermute | solution.py:326
  21.6 0.7 %collective-permute-start.7 = (bf16[1,8,4992]{2,1,0:T(8,128)(2,1)S(1)}, bf16[1,8,4992]{2,1,0:T(8,128)(2,1)S(1)}, u32[]{:S(2)}, u32[]{:S(2)}) collective-permute-start(bf16[1,8,4992]{2,1,0:T(8,128)(2,1)S(1)} %get-tuple-element.58.refs_0_), channel_id=1, source_target_pairs={{0,8},{4,12},{8,0},{12,4},{16,24},{20,28},{24,16},{28,20},{1,9},{5... | collective-permute-start | bytes 239624 | tf_op jit(solution)/shard_map/ppermute | solution.py:326
  22.3 3.3 %collective-permute-done.3.refs_2_ = bf16[3,8,4992]{2,1,0:T(8,128)(2,1)S(1)} collective-permute-done((bf16[3,8,4992]{2,1,0:T(8,128)(2,1)S(1)}, bf16[3,8,4992]{2,1,0:T(8,128)(2,1)S(1)}, u32[]{:S(2)}, u32[]{:S(2)}) %collective-permute-start.3) | collective-permute-done | bytes 239648 | tf_op jit(solution)/shard_map/ppermute | solution.py:326
  26.0 1.4 %weights_field.1 = (bf16[3,8,4096]{2,1,0:T(8,128)(2,1)S(1)}, f32[3,1,3200]{2,1,0:T(1,128)S(1)}, f32[256,80]{1,0:T(8,128)S(1)}, f32[80,128]{1,0:T(8,128)S(1)}, f32[8,128]{1,0:T(8,128)S(1)}) custom-call(f32[16,256]{1,0:T(8,128)S(1)} %get-tuple-element.54.token_ref, f32[1,25600]{1,0:T(1,128)S(1)} %bitcast.6, f32[1,25600]{1,0:T(1,128)S(1)} %bitcast.17, ...), custom_call_target="tpu_custom_call" | custom-call | tf_op jit(solution)/shard_map/weights_field/pallas_call | solution.py:416
  27.5 1.3 %collective-permute-done.6.refs_2_ = bf16[1,8,4992]{2,1,0:T(8,128)(2,1)S(1)} collective-permute-done((bf16[1,8,4992]{2,1,0:T(8,128)(2,1)S(1)}, bf16[1,8,4992]{2,1,0:T(8,128)(2,1)S(1)}, u32[]{:S(2)}, u32[]{:S(2)}) %collective-permute-start.6) | collective-permute-done | bytes 79904 | tf_op jit(solution)/shard_map/ppermute | solution.py:326
  29.8 1.1 %field.3 = (f32[256,80]{1,0:T(8,128)S(1)}, f32[80,128]{1,0:T(8,128)S(1)}, f32[8,128]{1,0:T(8,128)S(1)}) custom-call(f32[1,25600]{1,0:T(1,128)S(1)} %bitcast.8, s32[1,25600]{1,0:T(1,128)S(1)} %bitcast.13, bf16[3,256,3200]{2,1,0:T(8,128)(2,1)S(1)} %get-tuple-element.55.kept_ref.refs_2_, bf16[1,256,3200]{2,1,0:T(8,128)(2,1)S(1)} %get-tuple-element.63.refs_3_, ...), custom_call_target="tpu_custom_call" | custom-call | tf_op jit(solution)/shard_map/field/pallas_call | solution.py:416
  30.9 1.5 %field.4 = (f32[256,80]{1,0:T(8,128)S(1)}, f32[80,128]{1,0:T(8,128)S(1)}, f32[8,128]{1,0:T(8,128)S(1)}) custom-call(f32[1,25600]{1,0:T(1,128)S(1)} %bitcast.9, s32[1,25600]{1,0:T(1,128)S(1)} %bitcast.14, bf16[3,256,3200]{2,1,0:T(8,128)(2,1)S(1)} %get-tuple-element.60.refs_2_, bf16[3,8,4096]{2,1,0:T(8,128)(2,1)S(1)} %collective-permute-done.9.refs_3_, ...), custom_call_target="tpu_custom_call" | custom-call | tf_op jit(solution)/shard_map/field/pallas_call | solution.py:416
  32.4 0.7 %field.5 = (bf16[8,2560]{1,0:T(8,128)(2,1)S(1)}, f32[8,128]{1,0:T(8,128)S(1)}) custom-call(f32[1,25600]{1,0:T(1,128)S(1)} %bitcast.10, s32[1,25600]{1,0:T(1,128)S(1)} %bitcast.15, bf16[1,256,3200]{2,1,0:T(8,128)(2,1)S(1)} %get-tuple-element.50.refs_2_, bf16[1,8,4096]{2,1,0:T(8,128)(2,1)S(1)} %collective-permute-done.8.refs_3_, ...), custom_call_target="tpu_custom_call" | custom-call | tf_op jit(solution)/shard_map/field/pallas_call | solution.py:416
  33.1 3.7 %collective-permute-start.10 = (bf16[8,2560]{1,0:T(8,128)(2,1)S(1)}, bf16[8,2560]{1,0:T(8,128)(2,1)S(1)}, u32[]{:S(2)}, u32[]{:S(2)}) collective-permute-start(bf16[8,2560]{1,0:T(8,128)(2,1)S(1)} %get-tuple-element.72.flat_ref.rest_3_), channel_id=1, source_target_pairs={{0,3},{1,2},{2,1},{3,0},{4,7},{5,6},{6,5},{7,4},{8,11},{9,10},{10,... | collective-permute-start | bytes 122888 | tf_op jit(solution)/shard_map/ppermute | solution.py:326
  36.8 0.8 %collective-permute-start.12 = (bf16[8,2560]{1,0:T(8,128)(2,1)S(1)}, bf16[8,2560]{1,0:T(8,128)(2,1)S(1)}, u32[]{:S(2)}, u32[]{:S(2)}) collective-permute-start(bf16[8,2560]{1,0:T(8,128)(2,1)S(1)} %get-tuple-element.72.flat_ref.rest_3_), channel_id=1, source_target_pairs={{0,1},{1,0},{2,3},{3,2},{4,5},{5,4},{6,7},{7,6},{8,9},{9,8},{10,11... | collective-permute-start | bytes 122888 | tf_op jit(solution)/shard_map/ppermute | solution.py:326
  37.5 0.9 %stats.1 = (f32[8,128]{1,0:T(8,128)S(1)}, bf16[10,6,256]{2,1,0:T(8,128)(2,1)}) custom-call(bf16[8,2560]{1,0:T(8,128)(2,1)S(1)} %get-tuple-element.72.flat_ref.rest_3_, f32[1,25600]{1,0:T(1,128)S(1)} %bitcast.11, f32[1,25600]{1,0:T(1,128)S(1)} %bitcast.19, s32[1,25600]{1,0:T(1,128)S(1)} %bitcast.16, f32[3,2,3200]{2,1,0:T(2,128)S(1)} %get-tuple-element.73.rest_0_, ...), custom_call_target="tpu_custom_call" | custom-call | tf_op jit(solution)/shard_map/stats/pallas_call | solution.py:416
  39.0 2.7 %collective-permute-done.11.rest_1_ = bf16[8,2560]{1,0:T(8,128)(2,1)S(1)} collective-permute-done((bf16[8,2560]{1,0:T(8,128)(2,1)S(1)}, bf16[8,2560]{1,0:T(8,128)(2,1)S(1)}, u32[]{:S(2)}, u32[]{:S(2)}) %collective-permute-start.11) | collective-permute-done | bytes 40992 | tf_op jit(solution)/shard_map/ppermute | solution.py:326
  41.9 1.7 %collective-permute-start.14 = (f32[8,128]{1,0:T(8,128)S(1)}, f32[8,128]{1,0:T(8,128)S(1)}, u32[]{:S(2)}, u32[]{:S(2)}) collective-permute-start(f32[8,128]{1,0:T(8,128)S(1)} %pair.1), channel_id=1, source_target_pairs={{0,24},{4,28},{8,16},{12,20},{16,8},{20,12},{24,0},{28,4},{1,25},{... | collective-permute-start | bytes 12296 | tf_op jit(solution)/shard_map/ppermute | solution.py:326
  43.6 1.2 %collective-permute-start.15 = (f32[8,128]{1,0:T(8,128)S(1)}, f32[8,128]{1,0:T(8,128)S(1)}, u32[]{:S(2)}, u32[]{:S(2)}) collective-permute-start(f32[8,128]{1,0:T(8,128)S(1)} %add.3.own_ref), channel_id=1, source_target_pairs={{0,8},{4,20},{8,0},{12,28},{16,24},{20,4},{24,16},{28,12},{1,9},{5... | collective-permute-start | bytes 12296 | tf_op jit(solution)/shard_map/ppermute | solution.py:330
  44.8 1.6 %collective-permute-done.14.common_ref = f32[8,128]{1,0:T(8,128)S(1)} collective-permute-done((f32[8,128]{1,0:T(8,128)S(1)}, f32[8,128]{1,0:T(8,128)S(1)}, u32[]{:S(2)}, u32[]{:S(2)}) %collective-permute-start.14) | collective-permute-done | bytes 4128 | tf_op jit(solution)/shard_map/ppermute | solution.py:326
  46.5 0.8 %collective-permute-done.15.rest_0_ = f32[8,128]{1,0:T(8,128)S(1)} collective-permute-done((f32[8,128]{1,0:T(8,128)S(1)}, f32[8,128]{1,0:T(8,128)S(1)}, u32[]{:S(2)}, u32[]{:S(2)}) %collective-permute-start.15) | collective-permute-done | bytes 4128 | tf_op jit(solution)/shard_map/ppermute | solution.py:330
  47.6 0.8 %collective-permute-done.16.rest_1_ = f32[8,128]{1,0:T(8,128)S(1)} collective-permute-done((f32[8,128]{1,0:T(8,128)S(1)}, f32[8,128]{1,0:T(8,128)S(1)}, u32[]{:S(2)}, u32[]{:S(2)}) %collective-permute-start.16) | collective-permute-done | bytes 4128 | tf_op jit(solution)/shard_map/ppermute | solution.py:326
  48.4 0.7 %final.1 = (f32[6,24]{1,0:T(8,128)}, f32[1,6]{1,0:T(1,128)}, f32[1,6]{1,0:T(1,128)}) custom-call(f32[8,128]{1,0:T(8,128)S(1)} %get-tuple-element.79.count_ref, f32[8,128]{1,0:T(8,128)S(1)} %add.3.own_ref, f32[8,128]{1,0:T(8,128)S(1)} %collective-permute-done.14.common_ref, f32[8,128]{1,0:T(8,128)S(1)} %collective-permute-done.15.rest_0_, ...), custom_call_target="tpu_custom_call" | custom-call | tf_op jit(solution)/shard_map/final/pallas_call | solution.py:416
  (34 shorter events, 4.5 us)
Async XLA Ops:
  5.5 4.6 %collective-permute-start = (bf16[3,8,4992]{2,1,0:T(8,128)(2,1)S(1)}, bf16[3,8,4992]{2,1,0:T(8,128)(2,1)S(1)}, u32[]{:S(2)}, u32[]{:S(2)}) collective-permute-start(bf16[3,8,4992]{2,1,0:T(8,128)(2,1)S(1)} %get-tuple-element.48), channel_id=1, source_target_pairs={{0,4},{4,0},{8,12},{12,8},{16,20},{20,16},{24,28},{28,24},{1,5},{5... | collective-permute-start | bytes 718856 | tf_op jit(solution)/shard_map/ppermute | solution.py:326
  10.2 11.5 %collective-permute-start.2 = (bf16[3,8,4992]{2,1,0:T(8,128)(2,1)S(1)}, bf16[3,8,4992]{2,1,0:T(8,128)(2,1)S(1)}, u32[]{:S(2)}, u32[]{:S(2)}) collective-permute-start(bf16[3,8,4992]{2,1,0:T(8,128)(2,1)S(1)} %get-tuple-element.56.refs_0_), channel_id=1, source_target_pairs={{0,24},{4,28},{8,16},{12,20},{16,8},{20,12},{24,0},{28,4},{1,25},{... | collective-permute-start | bytes 718856 | tf_op jit(solution)/shard_map/ppermute | solution.py:326
  13.7 11.9 %collective-permute-start.3 = (bf16[3,8,4992]{2,1,0:T(8,128)(2,1)S(1)}, bf16[3,8,4992]{2,1,0:T(8,128)(2,1)S(1)}, u32[]{:S(2)}, u32[]{:S(2)}) collective-permute-start(bf16[3,8,4992]{2,1,0:T(8,128)(2,1)S(1)} %get-tuple-element.56.refs_0_), channel_id=1, source_target_pairs={{0,16},{4,20},{8,24},{12,28},{16,0},{20,4},{24,8},{28,12},{1,17},{... | collective-permute-start | bytes 718856 | tf_op jit(solution)/shard_map/ppermute | solution.py:326
  14.2 11.8 %collective-permute-start.4 = (bf16[3,8,4992]{2,1,0:T(8,128)(2,1)S(1)}, bf16[3,8,4992]{2,1,0:T(8,128)(2,1)S(1)}, u32[]{:S(2)}, u32[]{:S(2)}) collective-permute-start(bf16[3,8,4992]{2,1,0:T(8,128)(2,1)S(1)} %get-tuple-element.56.refs_0_), channel_id=1, source_target_pairs={{0,8},{4,12},{8,0},{12,4},{16,24},{20,28},{24,16},{28,20},{1,9},{5... | collective-permute-start | bytes 718856 | tf_op jit(solution)/shard_map/ppermute | solution.py:326
  16.8 1.3 %collective-permute-start.1 = (bf16[1,8,4992]{2,1,0:T(8,128)(2,1)S(1)}, bf16[1,8,4992]{2,1,0:T(8,128)(2,1)S(1)}, u32[]{:S(2)}, u32[]{:S(2)}) collective-permute-start(bf16[1,8,4992]{2,1,0:T(8,128)(2,1)S(1)} %get-tuple-element.53), channel_id=1, source_target_pairs={{0,4},{4,0},{8,12},{12,8},{16,20},{20,16},{24,28},{28,24},{1,5},{5... | collective-permute-start | bytes 239624 | tf_op jit(solution)/shard_map/ppermute | solution.py:326
  16.9 9.1 %copy-start = (f32[25600]{0:T(1024)S(1)}, f32[25600]{0:T(1024)}, u32[]{:S(2)}) copy-start(f32[25600]{0:T(1024)} %param.7) | copy-start | bytes 307204
  16.9 9.1 %copy-start.1 = (s32[25600]{0:T(1024)S(1)}, s32[25600]{0:T(1024)}, u32[]{:S(2)}) copy-start(s32[25600]{0:T(1024)} %param.9) | copy-start | bytes 307204
  16.9 9.1 %copy-start.2 = (f32[25600]{0:T(1024)S(1)}, f32[25600]{0:T(1024)}, u32[]{:S(2)}) copy-start(f32[25600]{0:T(1024)} %param.8) | copy-start | bytes 307204
  18.2 9.3 %collective-permute-start.5 = (bf16[1,8,4992]{2,1,0:T(8,128)(2,1)S(1)}, bf16[1,8,4992]{2,1,0:T(8,128)(2,1)S(1)}, u32[]{:S(2)}, u32[]{:S(2)}) collective-permute-start(bf16[1,8,4992]{2,1,0:T(8,128)(2,1)S(1)} %get-tuple-element.58.refs_0_), channel_id=1, source_target_pairs={{0,24},{4,28},{8,16},{12,20},{16,8},{20,12},{24,0},{28,4},{1,25},{... | collective-permute-start | bytes 239624 | tf_op jit(solution)/shard_map/ppermute | solution.py:326
  21.1 7.6 %collective-permute-start.6 = (bf16[1,8,4992]{2,1,0:T(8,128)(2,1)S(1)}, bf16[1,8,4992]{2,1,0:T(8,128)(2,1)S(1)}, u32[]{:S(2)}, u32[]{:S(2)}) collective-permute-start(bf16[1,8,4992]{2,1,0:T(8,128)(2,1)S(1)} %get-tuple-element.58.refs_0_), channel_id=1, source_target_pairs={{0,16},{4,20},{8,24},{12,28},{16,0},{20,4},{24,8},{28,12},{1,17},{... | collective-permute-start | bytes 239624 | tf_op jit(solution)/shard_map/ppermute | solution.py:326
  21.6 7.4 %collective-permute-start.7 = (bf16[1,8,4992]{2,1,0:T(8,128)(2,1)S(1)}, bf16[1,8,4992]{2,1,0:T(8,128)(2,1)S(1)}, u32[]{:S(2)}, u32[]{:S(2)}) collective-permute-start(bf16[1,8,4992]{2,1,0:T(8,128)(2,1)S(1)} %get-tuple-element.58.refs_0_), channel_id=1, source_target_pairs={{0,8},{4,12},{8,0},{12,4},{16,24},{20,28},{24,16},{28,20},{1,9},{5... | collective-permute-start | bytes 239624 | tf_op jit(solution)/shard_map/ppermute | solution.py:326
  29.2 1.7 %collective-permute-start.9 = (bf16[3,8,4096]{2,1,0:T(8,128)(2,1)S(1)}, bf16[3,8,4096]{2,1,0:T(8,128)(2,1)S(1)}, u32[]{:S(2)}, u32[]{:S(2)}) collective-permute-start(bf16[3,8,4096]{2,1,0:T(8,128)(2,1)S(1)} %relay.1.refs_4_), channel_id=1, source_target_pairs={{0,4},{4,0},{8,12},{12,8},{16,20},{20,16},{24,28},{28,24},{1,5},{5... | collective-permute-start | bytes 589832 | tf_op jit(solution)/shard_map/ppermute | solution.py:326
  29.3 3.1 %collective-permute-start.8 = (bf16[1,8,4096]{2,1,0:T(8,128)(2,1)S(1)}, bf16[1,8,4096]{2,1,0:T(8,128)(2,1)S(1)}, u32[]{:S(2)}, u32[]{:S(2)}) collective-permute-start(bf16[1,8,4096]{2,1,0:T(8,128)(2,1)S(1)} %get-tuple-element.59.refs_5_), channel_id=1, source_target_pairs={{0,4},{4,0},{8,12},{12,8},{16,20},{20,16},{24,28},{28,24},{1,5},{5... | collective-permute-start | bytes 196616 | tf_op jit(solution)/shard_map/ppermute | solution.py:326
  33.1 5.9 %collective-permute-start.10 = (bf16[8,2560]{1,0:T(8,128)(2,1)S(1)}, bf16[8,2560]{1,0:T(8,128)(2,1)S(1)}, u32[]{:S(2)}, u32[]{:S(2)}) collective-permute-start(bf16[8,2560]{1,0:T(8,128)(2,1)S(1)} %get-tuple-element.72.flat_ref.rest_3_), channel_id=1, source_target_pairs={{0,3},{1,2},{2,1},{3,0},{4,7},{5,6},{6,5},{7,4},{8,11},{9,10},{10,... | collective-permute-start | bytes 122888 | tf_op jit(solution)/shard_map/ppermute | solution.py:326
  36.8 4.9 %collective-permute-start.11 = (bf16[8,2560]{1,0:T(8,128)(2,1)S(1)}, bf16[8,2560]{1,0:T(8,128)(2,1)S(1)}, u32[]{:S(2)}, u32[]{:S(2)}) collective-permute-start(bf16[8,2560]{1,0:T(8,128)(2,1)S(1)} %get-tuple-element.72.flat_ref.rest_3_), channel_id=1, source_target_pairs={{0,2},{1,3},{2,0},{3,1},{4,6},{5,7},{6,4},{7,5},{8,10},{9,11},{10,... | collective-permute-start | bytes 122888 | tf_op jit(solution)/shard_map/ppermute | solution.py:326
  36.8 4.9 %collective-permute-start.12 = (bf16[8,2560]{1,0:T(8,128)(2,1)S(1)}, bf16[8,2560]{1,0:T(8,128)(2,1)S(1)}, u32[]{:S(2)}, u32[]{:S(2)}) collective-permute-start(bf16[8,2560]{1,0:T(8,128)(2,1)S(1)} %get-tuple-element.72.flat_ref.rest_3_), channel_id=1, source_target_pairs={{0,1},{1,0},{2,3},{3,2},{4,5},{5,4},{6,7},{7,6},{8,9},{9,8},{10,11... | collective-permute-start | bytes 122888 | tf_op jit(solution)/shard_map/ppermute | solution.py:326
  41.8 1.8 %collective-permute-start.13 = (f32[8,128]{1,0:T(8,128)S(1)}, f32[8,128]{1,0:T(8,128)S(1)}, u32[]{:S(2)}, u32[]{:S(2)}) collective-permute-start(f32[8,128]{1,0:T(8,128)S(1)} %pair.1), channel_id=1, source_target_pairs={{0,4},{4,0},{8,12},{12,8},{16,20},{20,16},{24,28},{28,24},{1,5},{5... | collective-permute-start | bytes 12296 | tf_op jit(solution)/shard_map/ppermute | solution.py:326
  41.9 4.6 %collective-permute-start.14 = (f32[8,128]{1,0:T(8,128)S(1)}, f32[8,128]{1,0:T(8,128)S(1)}, u32[]{:S(2)}, u32[]{:S(2)}) collective-permute-start(f32[8,128]{1,0:T(8,128)S(1)} %pair.1), channel_id=1, source_target_pairs={{0,24},{4,28},{8,16},{12,20},{16,8},{20,12},{24,0},{28,4},{1,25},{... | collective-permute-start | bytes 12296 | tf_op jit(solution)/shard_map/ppermute | solution.py:326
  43.6 3.6 %collective-permute-start.15 = (f32[8,128]{1,0:T(8,128)S(1)}, f32[8,128]{1,0:T(8,128)S(1)}, u32[]{:S(2)}, u32[]{:S(2)}) collective-permute-start(f32[8,128]{1,0:T(8,128)S(1)} %add.3.own_ref), channel_id=1, source_target_pairs={{0,8},{4,20},{8,0},{12,28},{16,24},{20,4},{24,16},{28,12},{1,9},{5... | collective-permute-start | bytes 12296 | tf_op jit(solution)/shard_map/ppermute | solution.py:330
  46.5 1.2 %collective-permute-start.17 = (f32[8,128]{1,0:T(8,128)S(1)}, f32[8,128]{1,0:T(8,128)S(1)}, u32[]{:S(2)}, u32[]{:S(2)}) collective-permute-start(f32[8,128]{1,0:T(8,128)S(1)} %collective-permute-done.14.common_ref), channel_id=1, source_target_pairs={{0,4},{4,0},{8,12},{12,8},{16,20},{20,16},{24,28},{28,24},{1,5},{5... | collective-permute-start | bytes 12296 | tf_op jit(solution)/shard_map/ppermute | solution.py:326
  47.2 1.2 %collective-permute-start.16 = (f32[8,128]{1,0:T(8,128)S(1)}, f32[8,128]{1,0:T(8,128)S(1)}, u32[]{:S(2)}, u32[]{:S(2)}) collective-permute-start(f32[8,128]{1,0:T(8,128)S(1)} %collective-permute-done.15.rest_0_), channel_id=1, source_target_pairs={{0,4},{4,0},{8,12},{12,8},{16,20},{20,16},{24,28},{28,24},{1,5},{5... | collective-permute-start | bytes 12296 | tf_op jit(solution)/shard_map/ppermute | solution.py:326

commit v5 on v1

--- a/solution.py
+++ b/solution.py
@@ -86,6 +86,7 @@
             pl.when(last)(lambda: act(copy(distance, target, semaphore, tail)))
             pl.when(jnp.logical_not(last))(lambda: act(copy(distance, target, semaphore, block)))
 
+    square_ref = rest.pop(0)
     if fetched:
         buffer, arrived = rest[:2]
         rest = rest[2:]
@@ -126,20 +127,26 @@
     ends = jnp.broadcast_to(with_low(base), (ROWS, span - block))
 
     def work(slot, source):
-        squares = []
-        for at in range(0, block, PIECE):
-            lanes = slice(at, min(at + PIECE, block))
+        def piece(at, width):
+            lanes = pl.ds(at, width)
             square = 0.0
             for r in range(0, rows, 16):
                 dose = source[r : r + 16, lanes].astype(F32)
                 kept_ref[slot, r : r + 16, lanes] = dose.astype(BF16)
                 dose = dose * dose
                 square = square + (dose[:8] + dose[8:])
-            squares.append(jnp.sum(square, axis=0, keepdims=True))
+            square_ref[:, lanes] = jnp.sum(square, axis=0, keepdims=True)
+
+        @pl.loop(0, block // PIECE)
+        def _(index):
+            piece(pl.multiple_of(index * PIECE, LANES), PIECE)
+
+        if block % PIECE:
+            piece(block - block % PIECE, block % PIECE)
         total = jnp.dot(left, kept_ref[slot], preferred_element_type=F32) - base
         ones = total[ONES : ONES + 1]
         local_ref[slot, 0:1] = ones
-        local_ref[slot, 1:2] = jnp.concatenate(squares, axis=1) - 2.0 * ones - rows
+        local_ref[slot, 1:2] = square_ref[...] - 2.0 * ones - rows
         high, low = pack_sums(jnp.concatenate([with_low(total), ends], axis=1))
         sums_ref[slot, :, :span] = high.astype(BF16)
         sums_ref[slot, :, span:] = low.astype(BF16)
@@ -375,7 +382,7 @@
             out_shape.append(jax.ShapeDtypeStruct((ROWS, rows), F32))
         if given is not None:
             out_shape.append(jax.ShapeDtypeStruct((rows, block), jnp.int32))
-        scratch = []
+        scratch = [VMEM((1, block), F32)]
         if fetched:
             scratch += [VMEM((fetched, rows, block), jnp.int32), pltpu.SemaphoreType.DMA((fetched,))]
         if given is not None:
@@ -463,11 +470,13 @@
         shape = [jax.ShapeDtypeStruct(value.shape, value.dtype)]
         (value,) = plain(relay_kernel, (terms[2], value), shape, "relay")
         u_away.append(swap(value, "ind", n, 1))
-        terms = fields([kept_here], [(slot, distance)], [value], terms)
-    blocks = list(enumerate(away_order))
-    middle = (chips - 1) // 2
-    terms = fields([kept_away], blocks[:middle], u_away[:middle], terms)
-    flat, number = fields([kept_away], blocks[middle:], u_away[middle:], terms, last=True)
+        if slot < chips - 2:
+            terms = fields([kept_here], [(slot, distance)], [value], terms)
+        else:
+            blocks = [(slot, distance), (0, away_order[0])]
+            terms = fields([kept_here, kept_away], blocks, [value, u_away[0]], terms)
+    blocks = list(enumerate(away_order))[1:]
+    flat, number = fields([kept_away], blocks, u_away[1:], terms, last=True)
 
     flats = [flat] + [swap(flat, "bin", n_bin, d) for d in range(1, n_bin)]
     order = (rows, (away_order, here_order, [1], [0]))

time: 46.3 us -> 46.3 us (level)
    pallas_call x14 -> x13, Pallas kernels: 6.6 us -> 6.45 us  [plain(): pl.pallas_call(kernel, in_specs=[in_vmem()] * len(operands), out_specs=[i...]
  transfers between devices with their start and end apart: 20 -> 20, of which waited for: 9 -> 9; matrix products, arithmetic and copies ran while one was open for 0% -> 0% of each run, Pallas kernels for 25% -> 26%
where the time goes in v5:
time: 46.3 us; the launch traced here: 46 us
  Pallas kernels  18.9 us (41%)
  starting transfers between devices  16.5 us (36%)
  waiting for transfers between devices  9.82 us (21%)
  between operations  0.83 us (2%)
    ppermute x19, starting transfers between devices, swap(): return lax.ppermute(value, axis, [(i, i ^ distance) for i in range(size)])  15.9 us
    pallas_call x4, Pallas kernels, moments(): pl.pallas_call(functools.partial(moments_kernel, snps, distances, opening...  12.4 us
    ppermute x19, waiting for transfers between devices, swap(): return lax.ppermute(value, axis, [(i, i ^ distance) for i in range(size)])  8.38 us
    pallas_call x13, Pallas kernels, plain(): pl.pallas_call(kernel, in_specs=[in_vmem()] * len(operands), out_specs=[i...  6.45 us
    ppermute x1, waiting for transfers between devices, swap_mixed(): lax.ppermute(value, 'ind', [(i, i ^ pair[i % 2]) for i in range(size)])  1.44 us
  transfers between devices with their start and end apart: 20, of which 9 were waited for; matrix products, arithmetic and copies ran while one was open for 0% of the time, Pallas kernels for 26%

profile of v5, /device:TPU:0, one launch (start us, length us, event | category | flops | bytes accessed | tf_op | source)
XLA Modules:
  0.0 46.0 jit_solution(12597881594612691230)
XLA Ops:
  0.6 4.9 %moments_away.1 = (bf16[3,256,3200]{2,1,0:T(8,128)(2,1)S(1)}, bf16[3,8,4992]{2,1,0:T(8,128)(2,1)S(1)}, f32[3,2,3200]{2,1,0:T(2,128)S(1)}, f32[16,256]{1,0:T(8,128)S(1)}, s32[256,3200]{1,0:T(8,128)S(1)}) custom-call(s32[256,25600]{1,0:T(8,128)} %geno_ref.7, s32[10,256]{1,0:T(8,128)} %rest_0_.1, bf16[256]{0:T(256)(128)(2,1)} %rest_1_.1), custom_call_target="tpu_custom_call" | custom-call | flops 1 | bytes 9830400 | tf_op jit(solution)/shard_map/moments_away/pallas_call | solution.py:396
  6.0 3.7 %moments_here.1 = (bf16[3,256,3200]{2,1,0:T(8,128)(2,1)S(1)}, bf16[3,8,4992]{2,1,0:T(8,128)(2,1)S(1)}, f32[3,2,3200]{2,1,0:T(2,128)S(1)}) custom-call(s32[256,25600]{1,0:T(8,128)} %geno_ref.7, s32[256,3200]{1,0:T(8,128)S(1)} %get-tuple-element.45.rest_0_, f32[16,256]{1,0:T(8,128)S(1)} %get-tuple-element.46.rest_1_.left_ref), custom_call_target="tpu_custom_call" | custom-call | flops 1 | bytes 9830400 | tf_op jit(solution)/shard_map/moments_here/pallas_call | solution.py:396
  9.9 3.5 %collective-permute-start.2 = (bf16[8,4992]{1,0:T(8,128)(2,1)S(1)}, bf16[8,4992]{1,0:T(8,128)(2,1)S(1)}, u32[]{:S(2)}, u32[]{:S(2)}) collective-permute-start(bf16[8,4992]{1,0:T(8,128)(2,1)S(1)} %get-tuple-element.56), channel_id=1, source_target_pairs={{0,24},{4,28},{8,16},{12,20},{16,8},{20,12},{24,0},{28,4},{1,25},{... | collective-permute-start | bytes 239624 | tf_op jit(solution)/shard_map/ppermute | solution.py:320
  14.1 2.9 %moments_near.1 = (bf16[1,256,3200]{2,1,0:T(8,128)(2,1)S(1)}, bf16[1,8,4992]{2,1,0:T(8,128)(2,1)S(1)}, f32[1,2,3200]{2,1,0:T(2,128)S(1)}, s32[256,3200]{1,0:T(8,128)S(1)}) custom-call(s32[256,25600]{1,0:T(8,128)} %geno_ref.7, f32[16,256]{1,0:T(8,128)S(1)} %get-tuple-element.50.rest_0_.rest_1_), custom_call_target="tpu_custom_call" | custom-call | flops 1 | bytes 1 | tf_op jit(solution)/shard_map/moments_near/pallas_call | solution.py:396
  17.1 0.9 %moments_own.1 = (bf16[1,256,3200]{2,1,0:T(8,128)(2,1)S(1)}, bf16[1,8,4992]{2,1,0:T(8,128)(2,1)S(1)}, f32[1,2,3200]{2,1,0:T(2,128)S(1)}) custom-call(s32[256,25600]{1,0:T(8,128)} %geno_ref.7, s32[256,3200]{1,0:T(8,128)S(1)} %get-tuple-element.51.rest_0_, f32[16,256]{1,0:T(8,128)S(1)} %get-tuple-element.50.rest_0_.rest_1_), custom_call_target="tpu_custom_call" | custom-call | flops 1 | bytes 1 | tf_op jit(solution)/shard_map/moments_own/pallas_call | solution.py:396
  18.7 2.8 %collective-permute-start.6 = (bf16[8,4096]{1,0:T(8,128)(2,1)S(1)}, bf16[8,4096]{1,0:T(8,128)(2,1)S(1)}, u32[]{:S(2)}, u32[]{:S(2)}) collective-permute-start(bf16[8,4096]{1,0:T(8,128)(2,1)S(1)} %get-tuple-element.59.refs_4_), channel_id=1, source_target_pairs={{0,24},{4,28},{8,16},{12,20},{16,8},{20,12},{24,0},{28,4},{1,25},{... | collective-permute-start | bytes 196616 | tf_op jit(solution)/shard_map/ppermute | solution.py:320
  22.2 1.1 %field.5 = (f32[256,80]{1,0:T(8,128)S(1)}, f32[80,128]{1,0:T(8,128)S(1)}, f32[8,128]{1,0:T(8,128)S(1)}) custom-call(f32[1,25600]{1,0:T(1,128)S(1)} %bitcast.7, s32[1,25600]{1,0:T(1,128)S(1)} %bitcast.13, bf16[1,256,3200]{2,1,0:T(8,128)(2,1)S(1)} %get-tuple-element.52.refs_2_, bf16[1,256,3200]{2,1,0:T(8,128)(2,1)S(1)} %get-tuple-element.53.refs_3_, ...), custom_call_target="tpu_custom_call" | custom-call | flops 1 | bytes 1 | tf_op jit(solution)/shard_map/field/pallas_call | solution.py:411
  23.3 0.9 %collective-permute-done.6.value_ref = bf16[8,4096]{1,0:T(8,128)(2,1)S(1)} collective-permute-done((bf16[8,4096]{1,0:T(8,128)(2,1)S(1)}, bf16[8,4096]{1,0:T(8,128)(2,1)S(1)}, u32[]{:S(2)}, u32[]{:S(2)}) %collective-permute-start.6) | collective-permute-done | bytes 65568 | tf_op jit(solution)/shard_map/ppermute | solution.py:320
  24.2 0.6 %field.6 = (f32[256,80]{1,0:T(8,128)S(1)}, f32[80,128]{1,0:T(8,128)S(1)}, f32[8,128]{1,0:T(8,128)S(1)}) custom-call(f32[1,25600]{1,0:T(1,128)S(1)} %bitcast.8, s32[1,25600]{1,0:T(1,128)S(1)} %bitcast.14, bf16[3,256,3200]{2,1,0:T(8,128)(2,1)S(1)} %get-tuple-element.47.refs_2_, bf16[8,4096]{1,0:T(8,128)(2,1)S(1)} %relay.3.refs_3_, ...), custom_call_target="tpu_custom_call" | custom-call | flops 1 | bytes 1 | tf_op jit(solution)/shard_map/field/pallas_call | solution.py:411
  24.8 1.0 %collective-permute-done.7.value_ref = bf16[8,4096]{1,0:T(8,128)(2,1)S(1)} collective-permute-done((bf16[8,4096]{1,0:T(8,128)(2,1)S(1)}, bf16[8,4096]{1,0:T(8,128)(2,1)S(1)}, u32[]{:S(2)}, u32[]{:S(2)}) %collective-permute-start.7) | collective-permute-done | bytes 65568 | tf_op jit(solution)/shard_map/ppermute | solution.py:320
  25.9 0.6 %field.7 = (f32[256,80]{1,0:T(8,128)S(1)}, f32[80,128]{1,0:T(8,128)S(1)}, f32[8,128]{1,0:T(8,128)S(1)}) custom-call(f32[1,25600]{1,0:T(1,128)S(1)} %bitcast.9, s32[1,25600]{1,0:T(1,128)S(1)} %bitcast.15, bf16[3,256,3200]{2,1,0:T(8,128)(2,1)S(1)} %get-tuple-element.47.refs_2_, bf16[8,4096]{1,0:T(8,128)(2,1)S(1)} %relay.4.refs_3_, ...), custom_call_target="tpu_custom_call" | custom-call | flops 1 | bytes 1 | tf_op jit(solution)/shard_map/field/pallas_call | solution.py:411
  27.1 1.1 %field.8 = (f32[256,80]{1,0:T(8,128)S(1)}, f32[80,128]{1,0:T(8,128)S(1)}, f32[8,128]{1,0:T(8,128)S(1)}) custom-call(f32[1,25600]{1,0:T(1,128)S(1)} %bitcast.10, s32[1,25600]{1,0:T(1,128)S(1)} %bitcast.16, bf16[3,256,3200]{2,1,0:T(8,128)(2,1)S(1)} %get-tuple-element.47.refs_2_, bf16[3,256,3200]{2,1,0:T(8,128)(2,1)S(1)} %get-tuple-element.44.refs_3_.refs_2_, ...), custom_call_target="tpu_custom_call" | custom-call | flops 1 | bytes 1 | tf_op jit(solution)/shard_map/field/pallas_call | solution.py:411
  28.2 1.2 %field.9 = (bf16[8,2560]{1,0:T(8,128)(2,1)S(1)}, f32[8,128]{1,0:T(8,128)S(1)}) custom-call(f32[1,25600]{1,0:T(1,128)S(1)} %bitcast.11, s32[1,25600]{1,0:T(1,128)S(1)} %bitcast.17, bf16[3,256,3200]{2,1,0:T(8,128)(2,1)S(1)} %get-tuple-element.44.refs_3_.refs_2_, bf16[8,4096]{1,0:T(8,128)(2,1)S(1)} %collective-permute-done.8.refs_3_, ...), custom_call_target="tpu_custom_call" | custom-call | flops 1 | bytes 1 | tf_op jit(solution)/shard_map/field/pallas_call | solution.py:411
  29.4 3.7 %collective-permute-start.14 = (bf16[8,2560]{1,0:T(8,128)(2,1)S(1)}, bf16[8,2560]{1,0:T(8,128)(2,1)S(1)}, u32[]{:S(2)}, u32[]{:S(2)}) collective-permute-start(bf16[8,2560]{1,0:T(8,128)(2,1)S(1)} %get-tuple-element.72.flat_ref.rest_0_), channel_id=1, source_target_pairs={{0,3},{1,2},{2,1},{3,0},{4,7},{5,6},{6,5},{7,4},{8,11},{9,10},{10,... | collective-permute-start | bytes 122888 | tf_op jit(solution)/shard_map/ppermute | solution.py:320
  33.1 0.8 %collective-permute-start.12 = (bf16[8,2560]{1,0:T(8,128)(2,1)S(1)}, bf16[8,2560]{1,0:T(8,128)(2,1)S(1)}, u32[]{:S(2)}, u32[]{:S(2)}) collective-permute-start(bf16[8,2560]{1,0:T(8,128)(2,1)S(1)} %get-tuple-element.72.flat_ref.rest_0_), channel_id=1, source_target_pairs={{0,1},{1,0},{2,3},{3,2},{4,5},{5,4},{6,7},{7,6},{8,9},{9,8},{10,11... | collective-permute-start | bytes 122888 | tf_op jit(solution)/shard_map/ppermute | solution.py:320
  33.8 0.8 %stats.1 = (f32[8,128]{1,0:T(8,128)S(1)}, bf16[10,6,256]{2,1,0:T(8,128)(2,1)}) custom-call(bf16[8,2560]{1,0:T(8,128)(2,1)S(1)} %get-tuple-element.72.flat_ref.rest_0_, f32[1,25600]{1,0:T(1,128)S(1)} %bitcast.12, f32[1,25600]{1,0:T(1,128)S(1)} %bitcast.20, s32[1,25600]{1,0:T(1,128)S(1)} %bitcast.18, f32[1,3200]{1,0:T(1,128)S(1)} %get-tuple-element.73.trait_ref, ...), custom_call_target="tpu_custom_call" | custom-call | tf_op jit(solution)/shard_map/stats/pallas_call | solution.py:411
  34.7 0.6 %collective-permute-done.14.rest_3_ = bf16[8,2560]{1,0:T(8,128)(2,1)S(1)} collective-permute-done((bf16[8,2560]{1,0:T(8,128)(2,1)S(1)}, bf16[8,2560]{1,0:T(8,128)(2,1)S(1)}, u32[]{:S(2)}, u32[]{:S(2)}) %collective-permute-start.14) | collective-permute-done | bytes 40992 | tf_op jit(solution)/shard_map/ppermute | solution.py:320
  35.3 2.7 %collective-permute-done.13.rest_2_ = bf16[8,2560]{1,0:T(8,128)(2,1)S(1)} collective-permute-done((bf16[8,2560]{1,0:T(8,128)(2,1)S(1)}, bf16[8,2560]{1,0:T(8,128)(2,1)S(1)}, u32[]{:S(2)}, u32[]{:S(2)}) %collective-permute-start.13) | collective-permute-done | bytes 40992 | tf_op jit(solution)/shard_map/ppermute | solution.py:320
  38.2 2.4 %collective-permute-start.16 = (f32[8,128]{1,0:T(8,128)S(1)}, f32[8,128]{1,0:T(8,128)S(1)}, u32[]{:S(2)}, u32[]{:S(2)}) collective-permute-start(f32[8,128]{1,0:T(8,128)S(1)} %pair.1), channel_id=1, source_target_pairs={{0,24},{4,28},{8,16},{12,20},{16,8},{20,12},{24,0},{28,4},{1,25},{... | collective-permute-start | bytes 12296 | tf_op jit(solution)/shard_map/ppermute | solution.py:320
  40.6 0.6 %collective-permute-start.17 = (f32[8,128]{1,0:T(8,128)S(1)}, f32[8,128]{1,0:T(8,128)S(1)}, u32[]{:S(2)}, u32[]{:S(2)}) collective-permute-start(f32[8,128]{1,0:T(8,128)S(1)} %add.3.own_ref), channel_id=1, source_target_pairs={{0,8},{4,20},{8,0},{12,28},{16,24},{20,4},{24,16},{28,12},{1,9},{5... | collective-permute-start | bytes 12296 | tf_op jit(solution)/shard_map/ppermute | solution.py:324
  41.2 1.6 %collective-permute-done.16.common_ref = f32[8,128]{1,0:T(8,128)S(1)} collective-permute-done((f32[8,128]{1,0:T(8,128)S(1)}, f32[8,128]{1,0:T(8,128)S(1)}, u32[]{:S(2)}, u32[]{:S(2)}) %collective-permute-start.16) | collective-permute-done | bytes 4128 | tf_op jit(solution)/shard_map/ppermute | solution.py:320
  42.8 1.4 %collective-permute-done.17.rest_0_ = f32[8,128]{1,0:T(8,128)S(1)} collective-permute-done((f32[8,128]{1,0:T(8,128)S(1)}, f32[8,128]{1,0:T(8,128)S(1)}, u32[]{:S(2)}, u32[]{:S(2)}) %collective-permute-start.17) | collective-permute-done | bytes 4128 | tf_op jit(solution)/shard_map/ppermute | solution.py:324
  44.2 1.2 %collective-permute-done.18.rest_1_ = f32[8,128]{1,0:T(8,128)S(1)} collective-permute-done((f32[8,128]{1,0:T(8,128)S(1)}, f32[8,128]{1,0:T(8,128)S(1)}, u32[]{:S(2)}, u32[]{:S(2)}) %collective-permute-start.18) | collective-permute-done | bytes 4128 | tf_op jit(solution)/shard_map/ppermute | solution.py:320
  45.4 0.7 %final.1 = (f32[6,24]{1,0:T(8,128)}, f32[1,6]{1,0:T(1,128)}, f32[1,6]{1,0:T(1,128)}) custom-call(f32[8,128]{1,0:T(8,128)S(1)} %get-tuple-element.79.count_ref, f32[8,128]{1,0:T(8,128)S(1)} %add.3.own_ref, f32[8,128]{1,0:T(8,128)S(1)} %collective-permute-done.16.common_ref, f32[8,128]{1,0:T(8,128)S(1)} %collective-permute-done.17.rest_0_, ...), custom_call_target="tpu_custom_call" | custom-call | tf_op jit(solution)/shard_map/final/pallas_call | solution.py:411
  (40 shorter events, 3.5 us)
Async XLA Ops:
  5.5 4.3 %collective-permute-start = (bf16[3,8,4992]{2,1,0:T(8,128)(2,1)S(1)}, bf16[3,8,4992]{2,1,0:T(8,128)(2,1)S(1)}, u32[]{:S(2)}, u32[]{:S(2)}) collective-permute-start(bf16[3,8,4992]{2,1,0:T(8,128)(2,1)S(1)} %get-tuple-element.49), channel_id=1, source_target_pairs={{0,4},{4,0},{8,12},{12,8},{16,20},{20,16},{24,28},{28,24},{1,5},{5... | collective-permute-start | bytes 718856 | tf_op jit(solution)/shard_map/ppermute | solution.py:320
  9.9 8.1 %collective-permute-start.2 = (bf16[8,4992]{1,0:T(8,128)(2,1)S(1)}, bf16[8,4992]{1,0:T(8,128)(2,1)S(1)}, u32[]{:S(2)}, u32[]{:S(2)}) collective-permute-start(bf16[8,4992]{1,0:T(8,128)(2,1)S(1)} %get-tuple-element.56), channel_id=1, source_target_pairs={{0,24},{4,28},{8,16},{12,20},{16,8},{20,12},{24,0},{28,4},{1,25},{... | collective-permute-start | bytes 239624 | tf_op jit(solution)/shard_map/ppermute | solution.py:320
  13.4 4.8 %collective-permute-start.3 = (bf16[8,4992]{1,0:T(8,128)(2,1)S(1)}, bf16[8,4992]{1,0:T(8,128)(2,1)S(1)}, u32[]{:S(2)}, u32[]{:S(2)}) collective-permute-start(bf16[8,4992]{1,0:T(8,128)(2,1)S(1)} %get-tuple-element.57), channel_id=1, source_target_pairs={{0,16},{4,20},{8,24},{12,28},{16,0},{20,4},{24,8},{28,12},{1,17},{... | collective-permute-start | bytes 239624 | tf_op jit(solution)/shard_map/ppermute | solution.py:320
  13.9 4.5 %collective-permute-start.4 = (bf16[8,4992]{1,0:T(8,128)(2,1)S(1)}, bf16[8,4992]{1,0:T(8,128)(2,1)S(1)}, u32[]{:S(2)}, u32[]{:S(2)}) collective-permute-start(bf16[8,4992]{1,0:T(8,128)(2,1)S(1)} %get-tuple-element.58), channel_id=1, source_target_pairs={{0,8},{4,12},{8,0},{12,4},{16,24},{20,28},{24,16},{28,20},{1,9},{5... | collective-permute-start | bytes 239624 | tf_op jit(solution)/shard_map/ppermute | solution.py:320
  17.0 1.4 %collective-permute-start.1 = (bf16[1,8,4992]{2,1,0:T(8,128)(2,1)S(1)}, bf16[1,8,4992]{2,1,0:T(8,128)(2,1)S(1)}, u32[]{:S(2)}, u32[]{:S(2)}) collective-permute-start(bf16[1,8,4992]{2,1,0:T(8,128)(2,1)S(1)} %get-tuple-element.55), channel_id=1, source_target_pairs={{0,4},{4,0},{8,12},{12,8},{16,20},{20,16},{24,28},{28,24},{1,5},{5... | collective-permute-start | bytes 239624 | tf_op jit(solution)/shard_map/ppermute | solution.py:320
  17.1 1.3 %copy-start = (f32[25600]{0:T(1024)S(1)}, f32[25600]{0:T(1024)}, u32[]{:S(2)}) copy-start(f32[25600]{0:T(1024)} %param.7) | copy-start | bytes 307204
  17.1 1.3 %copy-start.2 = (f32[25600]{0:T(1024)S(1)}, f32[25600]{0:T(1024)}, u32[]{:S(2)}) copy-start(f32[25600]{0:T(1024)} %param.8) | copy-start | bytes 307204
  17.1 5.1 %copy-start.1 = (s32[25600]{0:T(1024)S(1)}, s32[25600]{0:T(1024)}, u32[]{:S(2)}) copy-start(s32[25600]{0:T(1024)} %param.9) | copy-start | bytes 307204
  18.6 3.7 %collective-permute-start.5 = (bf16[8,4096]{1,0:T(8,128)(2,1)S(1)}, bf16[8,4096]{1,0:T(8,128)(2,1)S(1)}, u32[]{:S(2)}, u32[]{:S(2)}) collective-permute-start(bf16[8,4096]{1,0:T(8,128)(2,1)S(1)} %get-tuple-element.59.refs_4_), channel_id=1, source_target_pairs={{0,4},{4,0},{8,12},{12,8},{16,20},{20,16},{24,28},{28,24},{1,5},{5... | collective-permute-start | bytes 196616 | tf_op jit(solution)/shard_map/ppermute | solution.py:320
  18.7 5.4 %collective-permute-start.6 = (bf16[8,4096]{1,0:T(8,128)(2,1)S(1)}, bf16[8,4096]{1,0:T(8,128)(2,1)S(1)}, u32[]{:S(2)}, u32[]{:S(2)}) collective-permute-start(bf16[8,4096]{1,0:T(8,128)(2,1)S(1)} %get-tuple-element.59.refs_4_), channel_id=1, source_target_pairs={{0,24},{4,28},{8,16},{12,20},{16,8},{20,12},{24,0},{28,4},{1,25},{... | collective-permute-start | bytes 196616 | tf_op jit(solution)/shard_map/ppermute | solution.py:320
  21.6 4.3 %collective-permute-start.7 = (bf16[8,4096]{1,0:T(8,128)(2,1)S(1)}, bf16[8,4096]{1,0:T(8,128)(2,1)S(1)}, u32[]{:S(2)}, u32[]{:S(2)}) collective-permute-start(bf16[8,4096]{1,0:T(8,128)(2,1)S(1)} %get-tuple-element.59.refs_4_), channel_id=1, source_target_pairs={{0,16},{4,20},{8,24},{12,28},{16,0},{20,4},{24,8},{28,12},{1,17},{... | collective-permute-start | bytes 196616 | tf_op jit(solution)/shard_map/ppermute | solution.py:320
  22.1 4.4 %collective-permute-start.9 = (bf16[8,4096]{1,0:T(8,128)(2,1)S(1)}, bf16[8,4096]{1,0:T(8,128)(2,1)S(1)}, u32[]{:S(2)}, u32[]{:S(2)}) collective-permute-start(bf16[8,4096]{1,0:T(8,128)(2,1)S(1)} %get-tuple-element.59.refs_4_), channel_id=1, source_target_pairs={{0,8},{4,12},{8,0},{12,4},{16,24},{20,28},{24,16},{28,20},{1,9},{5... | collective-permute-start | bytes 196616 | tf_op jit(solution)/shard_map/ppermute | solution.py:320
  24.2 2.9 %collective-permute-start.11 = (bf16[8,4096]{1,0:T(8,128)(2,1)S(1)}, bf16[8,4096]{1,0:T(8,128)(2,1)S(1)}, u32[]{:S(2)}, u32[]{:S(2)}) collective-permute-start(bf16[8,4096]{1,0:T(8,128)(2,1)S(1)} %relay.3.refs_3_), channel_id=1, source_target_pairs={{0,4},{4,0},{8,12},{12,8},{16,20},{20,16},{24,28},{28,24},{1,5},{5... | collective-permute-start | bytes 196616 | tf_op jit(solution)/shard_map/ppermute | solution.py:320
  26.5 1.7 %collective-permute-start.10 = (bf16[8,4096]{1,0:T(8,128)(2,1)S(1)}, bf16[8,4096]{1,0:T(8,128)(2,1)S(1)}, u32[]{:S(2)}, u32[]{:S(2)}) collective-permute-start(bf16[8,4096]{1,0:T(8,128)(2,1)S(1)} %relay.5.refs_4_), channel_id=1, source_target_pairs={{0,4},{4,0},{8,12},{12,8},{16,20},{20,16},{24,28},{28,24},{1,5},{5... | collective-permute-start | bytes 196616 | tf_op jit(solution)/shard_map/ppermute | solution.py:320
  26.6 1.6 %collective-permute-start.8 = (bf16[8,4096]{1,0:T(8,128)(2,1)S(1)}, bf16[8,4096]{1,0:T(8,128)(2,1)S(1)}, u32[]{:S(2)}, u32[]{:S(2)}) collective-permute-start(bf16[8,4096]{1,0:T(8,128)(2,1)S(1)} %relay.4.refs_3_), channel_id=1, source_target_pairs={{0,4},{4,0},{8,12},{12,8},{16,20},{20,16},{24,28},{28,24},{1,5},{5... | collective-permute-start | bytes 196616 | tf_op jit(solution)/shard_map/ppermute | solution.py:320
  29.4 5.9 %collective-permute-start.14 = (bf16[8,2560]{1,0:T(8,128)(2,1)S(1)}, bf16[8,2560]{1,0:T(8,128)(2,1)S(1)}, u32[]{:S(2)}, u32[]{:S(2)}) collective-permute-start(bf16[8,2560]{1,0:T(8,128)(2,1)S(1)} %get-tuple-element.72.flat_ref.rest_0_), channel_id=1, source_target_pairs={{0,3},{1,2},{2,1},{3,0},{4,7},{5,6},{6,5},{7,4},{8,11},{9,10},{10,... | collective-permute-start | bytes 122888 | tf_op jit(solution)/shard_map/ppermute | solution.py:320
  33.1 4.9 %collective-permute-start.13 = (bf16[8,2560]{1,0:T(8,128)(2,1)S(1)}, bf16[8,2560]{1,0:T(8,128)(2,1)S(1)}, u32[]{:S(2)}, u32[]{:S(2)}) collective-permute-start(bf16[8,2560]{1,0:T(8,128)(2,1)S(1)} %get-tuple-element.72.flat_ref.rest_0_), channel_id=1, source_target_pairs={{0,2},{1,3},{2,0},{3,1},{4,6},{5,7},{6,4},{7,5},{8,10},{9,11},{10,... | collective-permute-start | bytes 122888 | tf_op jit(solution)/shard_map/ppermute | solution.py:320
  33.1 4.9 %collective-permute-start.12 = (bf16[8,2560]{1,0:T(8,128)(2,1)S(1)}, bf16[8,2560]{1,0:T(8,128)(2,1)S(1)}, u32[]{:S(2)}, u32[]{:S(2)}) collective-permute-start(bf16[8,2560]{1,0:T(8,128)(2,1)S(1)} %get-tuple-element.72.flat_ref.rest_0_), channel_id=1, source_target_pairs={{0,1},{1,0},{2,3},{3,2},{4,5},{5,4},{6,7},{7,6},{8,9},{9,8},{10,11... | collective-permute-start | bytes 122888 | tf_op jit(solution)/shard_map/ppermute | solution.py:320
  38.1 2.5 %collective-permute-start.15 = (f32[8,128]{1,0:T(8,128)S(1)}, f32[8,128]{1,0:T(8,128)S(1)}, u32[]{:S(2)}, u32[]{:S(2)}) collective-permute-start(f32[8,128]{1,0:T(8,128)S(1)} %pair.1), channel_id=1, source_target_pairs={{0,4},{4,0},{8,12},{12,8},{16,20},{20,16},{24,28},{28,24},{1,5},{5... | collective-permute-start | bytes 12296 | tf_op jit(solution)/shard_map/ppermute | solution.py:320
  38.2 4.6 %collective-permute-start.16 = (f32[8,128]{1,0:T(8,128)S(1)}, f32[8,128]{1,0:T(8,128)S(1)}, u32[]{:S(2)}, u32[]{:S(2)}) collective-permute-start(f32[8,128]{1,0:T(8,128)S(1)} %pair.1), channel_id=1, source_target_pairs={{0,24},{4,28},{8,16},{12,20},{16,8},{20,12},{24,0},{28,4},{1,25},{... | collective-permute-start | bytes 12296 | tf_op jit(solution)/shard_map/ppermute | solution.py:320
  40.6 3.6 %collective-permute-start.17 = (f32[8,128]{1,0:T(8,128)S(1)}, f32[8,128]{1,0:T(8,128)S(1)}, u32[]{:S(2)}, u32[]{:S(2)}) collective-permute-start(f32[8,128]{1,0:T(8,128)S(1)} %add.3.own_ref), channel_id=1, source_target_pairs={{0,8},{4,20},{8,0},{12,28},{16,24},{20,4},{24,16},{28,12},{1,9},{5... | collective-permute-start | bytes 12296 | tf_op jit(solution)/shard_map/ppermute | solution.py:324
  42.7 1.5 %collective-permute-start.19 = (f32[8,128]{1,0:T(8,128)S(1)}, f32[8,128]{1,0:T(8,128)S(1)}, u32[]{:S(2)}, u32[]{:S(2)}) collective-permute-start(f32[8,128]{1,0:T(8,128)S(1)} %collective-permute-done.16.common_ref), channel_id=1, source_target_pairs={{0,4},{4,0},{8,12},{12,8},{16,20},{20,16},{24,28},{28,24},{1,5},{5... | collective-permute-start | bytes 12296 | tf_op jit(solution)/shard_map/ppermute | solution.py:320
  44.2 1.2 %collective-permute-start.18 = (f32[8,128]{1,0:T(8,128)S(1)}, f32[8,128]{1,0:T(8,128)S(1)}, u32[]{:S(2)}, u32[]{:S(2)}) collective-permute-start(f32[8,128]{1,0:T(8,128)S(1)} %collective-permute-done.17.rest_0_), channel_id=1, source_target_pairs={{0,4},{4,0},{8,12},{12,8},{16,20},{20,16},{24,28},{28,24},{1,5},{5... | collective-permute-start | bytes 12296 | tf_op jit(solution)/shard_map/ppermute | solution.py:320

commit v6 on v1

--- a/solution.py
+++ b/solution.py
@@ -15,7 +15,7 @@
 TRAIT, ONES = PROBES, PROBES + 1
 TRACE_LANE, QUAD_LANE = LANES - 2, LANES - 1
 PIECE = 640
-DOT_PIECE = 768
+DOT_PIECE = 1664
 F32 = jnp.float32
 BF16 = jnp.bfloat16
 VMEM = pltpu.VMEM
@@ -463,11 +463,13 @@
         shape = [jax.ShapeDtypeStruct(value.shape, value.dtype)]
         (value,) = plain(relay_kernel, (terms[2], value), shape, "relay")
         u_away.append(swap(value, "ind", n, 1))
-        terms = fields([kept_here], [(slot, distance)], [value], terms)
-    blocks = list(enumerate(away_order))
-    middle = (chips - 1) // 2
-    terms = fields([kept_away], blocks[:middle], u_away[:middle], terms)
-    flat, number = fields([kept_away], blocks[middle:], u_away[middle:], terms, last=True)
+        if slot < chips - 2:
+            terms = fields([kept_here], [(slot, distance)], [value], terms)
+        else:
+            blocks = [(slot, distance), (0, away_order[0])]
+            terms = fields([kept_here, kept_away], blocks, [value, u_away[0]], terms)
+    blocks = list(enumerate(away_order))[1:]
+    flat, number = fields([kept_away], blocks, u_away[1:], terms, last=True)
 
     flats = [flat] + [swap(flat, "bin", n_bin, d) for d in range(1, n_bin)]
     order = (rows, (away_order, here_order, [1], [0]))

time: 46.3 us -> 46.2 us (level)
    pallas_call x14 -> x13, Pallas kernels: 6.6 us -> 6.39 us  [plain(): pl.pallas_call(kernel, in_specs=[in_vmem()] * len(operands), out_specs=[i...]
where the time goes in v6:
time: 46.2 us; the launch traced here: 45.9 us
  Pallas kernels  18.5 us (40%)
  starting transfers between devices  16.5 us (36%)
  waiting for transfers between devices  10.1 us (22%)
  between operations  0.83 us (2%)
    ppermute x19, starting transfers between devices, swap(): return lax.ppermute(value, axis, [(i, i ^ distance) for i in range(size)])  15.9 us
    pallas_call x4, Pallas kernels, moments(): pl.pallas_call(functools.partial(moments_kernel, snps, distances, opening...  12.1 us
    ppermute x19, waiting for transfers between devices, swap(): return lax.ppermute(value, axis, [(i, i ^ distance) for i in range(size)])  8.61 us
    pallas_call x13, Pallas kernels, plain(): pl.pallas_call(kernel, in_specs=[in_vmem()] * len(operands), out_specs=[i...  6.39 us
    ppermute x1, waiting for transfers between devices, swap_mixed(): lax.ppermute(value, 'ind', [(i, i ^ pair[i % 2]) for i in range(size)])  1.47 us
  transfers between devices with their start and end apart: 20, of which 9 were waited for; matrix products, arithmetic and copies ran while one was open for 0% of the time, Pallas kernels for 25%

profile of v6, /device:TPU:0, one launch (start us, length us, event | category | flops | bytes accessed | tf_op | source)
XLA Modules:
  0.0 45.9 jit_solution(15200822963923531788)
XLA Ops:
  0.6 4.9 %moments_away.1 = (bf16[3,256,3200]{2,1,0:T(8,128)(2,1)S(1)}, bf16[3,8,4992]{2,1,0:T(8,128)(2,1)S(1)}, f32[3,2,3200]{2,1,0:T(2,128)S(1)}, f32[16,256]{1,0:T(8,128)S(1)}, s32[256,3200]{1,0:T(8,128)S(1)}) custom-call(s32[256,25600]{1,0:T(8,128)} %geno_ref.7, s32[10,256]{1,0:T(8,128)} %rest_0_.1, bf16[256]{0:T(256)(128)(2,1)} %rest_1_.1), custom_call_target="tpu_custom_call" | custom-call | flops 1 | bytes 9830400 | tf_op jit(solution)/shard_map/moments_away/pallas_call | solution.py:389
  6.0 3.6 %moments_here.1 = (bf16[3,256,3200]{2,1,0:T(8,128)(2,1)S(1)}, bf16[3,8,4992]{2,1,0:T(8,128)(2,1)S(1)}, f32[3,2,3200]{2,1,0:T(2,128)S(1)}) custom-call(s32[256,25600]{1,0:T(8,128)} %geno_ref.7, s32[256,3200]{1,0:T(8,128)S(1)} %get-tuple-element.45.rest_0_, f32[16,256]{1,0:T(8,128)S(1)} %get-tuple-element.46.rest_1_.left_ref), custom_call_target="tpu_custom_call" | custom-call | flops 1 | bytes 9830400 | tf_op jit(solution)/shard_map/moments_here/pallas_call | solution.py:389
  9.7 3.5 %collective-permute-start.2 = (bf16[8,4992]{1,0:T(8,128)(2,1)S(1)}, bf16[8,4992]{1,0:T(8,128)(2,1)S(1)}, u32[]{:S(2)}, u32[]{:S(2)}) collective-permute-start(bf16[8,4992]{1,0:T(8,128)(2,1)S(1)} %get-tuple-element.56), channel_id=1, source_target_pairs={{0,24},{4,28},{8,16},{12,20},{16,8},{20,12},{24,0},{28,4},{1,25},{... | collective-permute-start | bytes 239624 | tf_op jit(solution)/shard_map/ppermute | solution.py:313
  13.9 2.9 %moments_near.1 = (bf16[1,256,3200]{2,1,0:T(8,128)(2,1)S(1)}, bf16[1,8,4992]{2,1,0:T(8,128)(2,1)S(1)}, f32[1,2,3200]{2,1,0:T(2,128)S(1)}, s32[256,3200]{1,0:T(8,128)S(1)}) custom-call(s32[256,25600]{1,0:T(8,128)} %geno_ref.7, f32[16,256]{1,0:T(8,128)S(1)} %get-tuple-element.50.rest_0_.rest_1_), custom_call_target="tpu_custom_call" | custom-call | flops 1 | bytes 1 | tf_op jit(solution)/shard_map/moments_near/pallas_call | solution.py:389
  17.0 0.7 %moments_own.1 = (bf16[1,256,3200]{2,1,0:T(8,128)(2,1)S(1)}, bf16[1,8,4992]{2,1,0:T(8,128)(2,1)S(1)}, f32[1,2,3200]{2,1,0:T(2,128)S(1)}) custom-call(s32[256,25600]{1,0:T(8,128)} %geno_ref.7, s32[256,3200]{1,0:T(8,128)S(1)} %get-tuple-element.51.rest_0_, f32[16,256]{1,0:T(8,128)S(1)} %get-tuple-element.50.rest_0_.rest_1_), custom_call_target="tpu_custom_call" | custom-call | flops 1 | bytes 1 | tf_op jit(solution)/shard_map/moments_own/pallas_call | solution.py:389
  18.6 2.8 %collective-permute-start.6 = (bf16[8,4096]{1,0:T(8,128)(2,1)S(1)}, bf16[8,4096]{1,0:T(8,128)(2,1)S(1)}, u32[]{:S(2)}, u32[]{:S(2)}) collective-permute-start(bf16[8,4096]{1,0:T(8,128)(2,1)S(1)} %get-tuple-element.59.refs_4_), channel_id=1, source_target_pairs={{0,24},{4,28},{8,16},{12,20},{16,8},{20,12},{24,0},{28,4},{1,25},{... | collective-permute-start | bytes 196616 | tf_op jit(solution)/shard_map/ppermute | solution.py:313
  22.1 1.1 %field.5 = (f32[256,80]{1,0:T(8,128)S(1)}, f32[80,128]{1,0:T(8,128)S(1)}, f32[8,128]{1,0:T(8,128)S(1)}) custom-call(f32[1,25600]{1,0:T(1,128)S(1)} %bitcast.7, s32[1,25600]{1,0:T(1,128)S(1)} %bitcast.13, bf16[1,256,3200]{2,1,0:T(8,128)(2,1)S(1)} %get-tuple-element.52.refs_2_, bf16[1,256,3200]{2,1,0:T(8,128)(2,1)S(1)} %get-tuple-element.53.refs_3_, ...), custom_call_target="tpu_custom_call" | custom-call | flops 1 | bytes 1 | tf_op jit(solution)/shard_map/field/pallas_call | solution.py:404
  23.2 0.9 %collective-permute-done.6.value_ref = bf16[8,4096]{1,0:T(8,128)(2,1)S(1)} collective-permute-done((bf16[8,4096]{1,0:T(8,128)(2,1)S(1)}, bf16[8,4096]{1,0:T(8,128)(2,1)S(1)}, u32[]{:S(2)}, u32[]{:S(2)}) %collective-permute-start.6) | collective-permute-done | bytes 65568 | tf_op jit(solution)/shard_map/ppermute | solution.py:313
  24.1 0.6 %field.6 = (f32[256,80]{1,0:T(8,128)S(1)}, f32[80,128]{1,0:T(8,128)S(1)}, f32[8,128]{1,0:T(8,128)S(1)}) custom-call(f32[1,25600]{1,0:T(1,128)S(1)} %bitcast.8, s32[1,25600]{1,0:T(1,128)S(1)} %bitcast.14, bf16[3,256,3200]{2,1,0:T(8,128)(2,1)S(1)} %get-tuple-element.47.refs_2_, bf16[8,4096]{1,0:T(8,128)(2,1)S(1)} %relay.3.refs_3_, ...), custom_call_target="tpu_custom_call" | custom-call | flops 1 | bytes 1 | tf_op jit(solution)/shard_map/field/pallas_call | solution.py:404
  24.7 1.0 %collective-permute-done.7.value_ref = bf16[8,4096]{1,0:T(8,128)(2,1)S(1)} collective-permute-done((bf16[8,4096]{1,0:T(8,128)(2,1)S(1)}, bf16[8,4096]{1,0:T(8,128)(2,1)S(1)}, u32[]{:S(2)}, u32[]{:S(2)}) %collective-permute-start.7) | collective-permute-done | bytes 65568 | tf_op jit(solution)/shard_map/ppermute | solution.py:313
  25.7 0.6 %field.7 = (f32[256,80]{1,0:T(8,128)S(1)}, f32[80,128]{1,0:T(8,128)S(1)}, f32[8,128]{1,0:T(8,128)S(1)}) custom-call(f32[1,25600]{1,0:T(1,128)S(1)} %bitcast.9, s32[1,25600]{1,0:T(1,128)S(1)} %bitcast.15, bf16[3,256,3200]{2,1,0:T(8,128)(2,1)S(1)} %get-tuple-element.47.refs_2_, bf16[8,4096]{1,0:T(8,128)(2,1)S(1)} %relay.4.refs_3_, ...), custom_call_target="tpu_custom_call" | custom-call | flops 1 | bytes 1 | tf_op jit(solution)/shard_map/field/pallas_call | solution.py:404
  27.0 1.0 %field.8 = (f32[256,80]{1,0:T(8,128)S(1)}, f32[80,128]{1,0:T(8,128)S(1)}, f32[8,128]{1,0:T(8,128)S(1)}) custom-call(f32[1,25600]{1,0:T(1,128)S(1)} %bitcast.10, s32[1,25600]{1,0:T(1,128)S(1)} %bitcast.16, bf16[3,256,3200]{2,1,0:T(8,128)(2,1)S(1)} %get-tuple-element.47.refs_2_, bf16[3,256,3200]{2,1,0:T(8,128)(2,1)S(1)} %get-tuple-element.44.refs_3_.refs_2_, ...), custom_call_target="tpu_custom_call" | custom-call | flops 1 | bytes 1 | tf_op jit(solution)/shard_map/field/pallas_call | solution.py:404
  28.0 1.2 %field.9 = (bf16[8,2560]{1,0:T(8,128)(2,1)S(1)}, f32[8,128]{1,0:T(8,128)S(1)}) custom-call(f32[1,25600]{1,0:T(1,128)S(1)} %bitcast.11, s32[1,25600]{1,0:T(1,128)S(1)} %bitcast.17, bf16[3,256,3200]{2,1,0:T(8,128)(2,1)S(1)} %get-tuple-element.44.refs_3_.refs_2_, bf16[8,4096]{1,0:T(8,128)(2,1)S(1)} %collective-permute-done.8.refs_3_, ...), custom_call_target="tpu_custom_call" | custom-call | flops 1 | bytes 1 | tf_op jit(solution)/shard_map/field/pallas_call | solution.py:404
  29.2 3.7 %collective-permute-start.14 = (bf16[8,2560]{1,0:T(8,128)(2,1)S(1)}, bf16[8,2560]{1,0:T(8,128)(2,1)S(1)}, u32[]{:S(2)}, u32[]{:S(2)}) collective-permute-start(bf16[8,2560]{1,0:T(8,128)(2,1)S(1)} %get-tuple-element.72.flat_ref.rest_0_), channel_id=1, source_target_pairs={{0,3},{1,2},{2,1},{3,0},{4,7},{5,6},{6,5},{7,4},{8,11},{9,10},{10,... | collective-permute-start | bytes 122888 | tf_op jit(solution)/shard_map/ppermute | solution.py:313
  32.9 0.8 %collective-permute-start.12 = (bf16[8,2560]{1,0:T(8,128)(2,1)S(1)}, bf16[8,2560]{1,0:T(8,128)(2,1)S(1)}, u32[]{:S(2)}, u32[]{:S(2)}) collective-permute-start(bf16[8,2560]{1,0:T(8,128)(2,1)S(1)} %get-tuple-element.72.flat_ref.rest_0_), channel_id=1, source_target_pairs={{0,1},{1,0},{2,3},{3,2},{4,5},{5,4},{6,7},{7,6},{8,9},{9,8},{10,11... | collective-permute-start | bytes 122888 | tf_op jit(solution)/shard_map/ppermute | solution.py:313
  33.7 0.8 %stats.1 = (f32[8,128]{1,0:T(8,128)S(1)}, bf16[10,6,256]{2,1,0:T(8,128)(2,1)}) custom-call(bf16[8,2560]{1,0:T(8,128)(2,1)S(1)} %get-tuple-element.72.flat_ref.rest_0_, f32[1,25600]{1,0:T(1,128)S(1)} %bitcast.12, f32[1,25600]{1,0:T(1,128)S(1)} %bitcast.20, s32[1,25600]{1,0:T(1,128)S(1)} %bitcast.18, f32[1,3200]{1,0:T(1,128)S(1)} %get-tuple-element.73.trait_ref, ...), custom_call_target="tpu_custom_call" | custom-call | tf_op jit(solution)/shard_map/stats/pallas_call | solution.py:404
  34.5 0.6 %collective-permute-done.14.rest_3_ = bf16[8,2560]{1,0:T(8,128)(2,1)S(1)} collective-permute-done((bf16[8,2560]{1,0:T(8,128)(2,1)S(1)}, bf16[8,2560]{1,0:T(8,128)(2,1)S(1)}, u32[]{:S(2)}, u32[]{:S(2)}) %collective-permute-start.14) | collective-permute-done | bytes 40992 | tf_op jit(solution)/shard_map/ppermute | solution.py:313
  35.1 2.7 %collective-permute-done.13.rest_2_ = bf16[8,2560]{1,0:T(8,128)(2,1)S(1)} collective-permute-done((bf16[8,2560]{1,0:T(8,128)(2,1)S(1)}, bf16[8,2560]{1,0:T(8,128)(2,1)S(1)}, u32[]{:S(2)}, u32[]{:S(2)}) %collective-permute-start.13) | collective-permute-done | bytes 40992 | tf_op jit(solution)/shard_map/ppermute | solution.py:313
  38.0 2.4 %collective-permute-start.16 = (f32[8,128]{1,0:T(8,128)S(1)}, f32[8,128]{1,0:T(8,128)S(1)}, u32[]{:S(2)}, u32[]{:S(2)}) collective-permute-start(f32[8,128]{1,0:T(8,128)S(1)} %pair.1), channel_id=1, source_target_pairs={{0,24},{4,28},{8,16},{12,20},{16,8},{20,12},{24,0},{28,4},{1,25},{... | collective-permute-start | bytes 12296 | tf_op jit(solution)/shard_map/ppermute | solution.py:313
  40.4 0.5 %collective-permute-start.17 = (f32[8,128]{1,0:T(8,128)S(1)}, f32[8,128]{1,0:T(8,128)S(1)}, u32[]{:S(2)}, u32[]{:S(2)}) collective-permute-start(f32[8,128]{1,0:T(8,128)S(1)} %add.3.own_ref), channel_id=1, source_target_pairs={{0,8},{4,20},{8,0},{12,28},{16,24},{20,4},{24,16},{28,12},{1,9},{5... | collective-permute-start | bytes 12296 | tf_op jit(solution)/shard_map/ppermute | solution.py:317
  41.0 1.6 %collective-permute-done.16.common_ref = f32[8,128]{1,0:T(8,128)S(1)} collective-permute-done((f32[8,128]{1,0:T(8,128)S(1)}, f32[8,128]{1,0:T(8,128)S(1)}, u32[]{:S(2)}, u32[]{:S(2)}) %collective-permute-start.16) | collective-permute-done | bytes 4128 | tf_op jit(solution)/shard_map/ppermute | solution.py:313
  42.6 1.5 %collective-permute-done.17.rest_0_ = f32[8,128]{1,0:T(8,128)S(1)} collective-permute-done((f32[8,128]{1,0:T(8,128)S(1)}, f32[8,128]{1,0:T(8,128)S(1)}, u32[]{:S(2)}, u32[]{:S(2)}) %collective-permute-start.17) | collective-permute-done | bytes 4128 | tf_op jit(solution)/shard_map/ppermute | solution.py:317
  44.1 1.2 %collective-permute-done.18.rest_1_ = f32[8,128]{1,0:T(8,128)S(1)} collective-permute-done((f32[8,128]{1,0:T(8,128)S(1)}, f32[8,128]{1,0:T(8,128)S(1)}, u32[]{:S(2)}, u32[]{:S(2)}) %collective-permute-start.18) | collective-permute-done | bytes 4128 | tf_op jit(solution)/shard_map/ppermute | solution.py:313
  45.2 0.7 %final.1 = (f32[6,24]{1,0:T(8,128)}, f32[1,6]{1,0:T(1,128)}, f32[1,6]{1,0:T(1,128)}) custom-call(f32[8,128]{1,0:T(8,128)S(1)} %get-tuple-element.79.count_ref, f32[8,128]{1,0:T(8,128)S(1)} %add.3.own_ref, f32[8,128]{1,0:T(8,128)S(1)} %collective-permute-done.16.common_ref, f32[8,128]{1,0:T(8,128)S(1)} %collective-permute-done.17.rest_0_, ...), custom_call_target="tpu_custom_call" | custom-call | tf_op jit(solution)/shard_map/final/pallas_call | solution.py:404
  (40 shorter events, 3.7 us)
Async XLA Ops:
  5.5 4.1 %collective-permute-start = (bf16[3,8,4992]{2,1,0:T(8,128)(2,1)S(1)}, bf16[3,8,4992]{2,1,0:T(8,128)(2,1)S(1)}, u32[]{:S(2)}, u32[]{:S(2)}) collective-permute-start(bf16[3,8,4992]{2,1,0:T(8,128)(2,1)S(1)} %get-tuple-element.49), channel_id=1, source_target_pairs={{0,4},{4,0},{8,12},{12,8},{16,20},{20,16},{24,28},{28,24},{1,5},{5... | collective-permute-start | bytes 718856 | tf_op jit(solution)/shard_map/ppermute | solution.py:313
  9.7 7.9 %collective-permute-start.2 = (bf16[8,4992]{1,0:T(8,128)(2,1)S(1)}, bf16[8,4992]{1,0:T(8,128)(2,1)S(1)}, u32[]{:S(2)}, u32[]{:S(2)}) collective-permute-start(bf16[8,4992]{1,0:T(8,128)(2,1)S(1)} %get-tuple-element.56), channel_id=1, source_target_pairs={{0,24},{4,28},{8,16},{12,20},{16,8},{20,12},{24,0},{28,4},{1,25},{... | collective-permute-start | bytes 239624 | tf_op jit(solution)/shard_map/ppermute | solution.py:313
  13.3 4.8 %collective-permute-start.3 = (bf16[8,4992]{1,0:T(8,128)(2,1)S(1)}, bf16[8,4992]{1,0:T(8,128)(2,1)S(1)}, u32[]{:S(2)}, u32[]{:S(2)}) collective-permute-start(bf16[8,4992]{1,0:T(8,128)(2,1)S(1)} %get-tuple-element.57), channel_id=1, source_target_pairs={{0,16},{4,20},{8,24},{12,28},{16,0},{20,4},{24,8},{28,12},{1,17},{... | collective-permute-start | bytes 239624 | tf_op jit(solution)/shard_map/ppermute | solution.py:313
  13.8 4.5 %collective-permute-start.4 = (bf16[8,4992]{1,0:T(8,128)(2,1)S(1)}, bf16[8,4992]{1,0:T(8,128)(2,1)S(1)}, u32[]{:S(2)}, u32[]{:S(2)}) collective-permute-start(bf16[8,4992]{1,0:T(8,128)(2,1)S(1)} %get-tuple-element.58), channel_id=1, source_target_pairs={{0,8},{4,12},{8,0},{12,4},{16,24},{20,28},{24,16},{28,20},{1,9},{5... | collective-permute-start | bytes 239624 | tf_op jit(solution)/shard_map/ppermute | solution.py:313
  16.9 1.4 %collective-permute-start.1 = (bf16[1,8,4992]{2,1,0:T(8,128)(2,1)S(1)}, bf16[1,8,4992]{2,1,0:T(8,128)(2,1)S(1)}, u32[]{:S(2)}, u32[]{:S(2)}) collective-permute-start(bf16[1,8,4992]{2,1,0:T(8,128)(2,1)S(1)} %get-tuple-element.55), channel_id=1, source_target_pairs={{0,4},{4,0},{8,12},{12,8},{16,20},{20,16},{24,28},{28,24},{1,5},{5... | collective-permute-start | bytes 239624 | tf_op jit(solution)/shard_map/ppermute | solution.py:313
  17.0 1.3 %copy-start = (f32[25600]{0:T(1024)S(1)}, f32[25600]{0:T(1024)}, u32[]{:S(2)}) copy-start(f32[25600]{0:T(1024)} %param.7) | copy-start | bytes 307204
  17.0 1.3 %copy-start.2 = (f32[25600]{0:T(1024)S(1)}, f32[25600]{0:T(1024)}, u32[]{:S(2)}) copy-start(f32[25600]{0:T(1024)} %param.8) | copy-start | bytes 307204
  17.0 5.1 %copy-start.1 = (s32[25600]{0:T(1024)S(1)}, s32[25600]{0:T(1024)}, u32[]{:S(2)}) copy-start(s32[25600]{0:T(1024)} %param.9) | copy-start | bytes 307204
  18.5 3.7 %collective-permute-start.5 = (bf16[8,4096]{1,0:T(8,128)(2,1)S(1)}, bf16[8,4096]{1,0:T(8,128)(2,1)S(1)}, u32[]{:S(2)}, u32[]{:S(2)}) collective-permute-start(bf16[8,4096]{1,0:T(8,128)(2,1)S(1)} %get-tuple-element.59.refs_4_), channel_id=1, source_target_pairs={{0,4},{4,0},{8,12},{12,8},{16,20},{20,16},{24,28},{28,24},{1,5},{5... | collective-permute-start | bytes 196616 | tf_op jit(solution)/shard_map/ppermute | solution.py:313
  18.6 5.4 %collective-permute-start.6 = (bf16[8,4096]{1,0:T(8,128)(2,1)S(1)}, bf16[8,4096]{1,0:T(8,128)(2,1)S(1)}, u32[]{:S(2)}, u32[]{:S(2)}) collective-permute-start(bf16[8,4096]{1,0:T(8,128)(2,1)S(1)} %get-tuple-element.59.refs_4_), channel_id=1, source_target_pairs={{0,24},{4,28},{8,16},{12,20},{16,8},{20,12},{24,0},{28,4},{1,25},{... | collective-permute-start | bytes 196616 | tf_op jit(solution)/shard_map/ppermute | solution.py:313
  21.5 4.3 %collective-permute-start.7 = (bf16[8,4096]{1,0:T(8,128)(2,1)S(1)}, bf16[8,4096]{1,0:T(8,128)(2,1)S(1)}, u32[]{:S(2)}, u32[]{:S(2)}) collective-permute-start(bf16[8,4096]{1,0:T(8,128)(2,1)S(1)} %get-tuple-element.59.refs_4_), channel_id=1, source_target_pairs={{0,16},{4,20},{8,24},{12,28},{16,0},{20,4},{24,8},{28,12},{1,17},{... | collective-permute-start | bytes 196616 | tf_op jit(solution)/shard_map/ppermute | solution.py:313
  22.0 4.4 %collective-permute-start.9 = (bf16[8,4096]{1,0:T(8,128)(2,1)S(1)}, bf16[8,4096]{1,0:T(8,128)(2,1)S(1)}, u32[]{:S(2)}, u32[]{:S(2)}) collective-permute-start(bf16[8,4096]{1,0:T(8,128)(2,1)S(1)} %get-tuple-element.59.refs_4_), channel_id=1, source_target_pairs={{0,8},{4,12},{8,0},{12,4},{16,24},{20,28},{24,16},{28,20},{1,9},{5... | collective-permute-start | bytes 196616 | tf_op jit(solution)/shard_map/ppermute | solution.py:313
  24.1 2.9 %collective-permute-start.11 = (bf16[8,4096]{1,0:T(8,128)(2,1)S(1)}, bf16[8,4096]{1,0:T(8,128)(2,1)S(1)}, u32[]{:S(2)}, u32[]{:S(2)}) collective-permute-start(bf16[8,4096]{1,0:T(8,128)(2,1)S(1)} %relay.3.refs_3_), channel_id=1, source_target_pairs={{0,4},{4,0},{8,12},{12,8},{16,20},{20,16},{24,28},{28,24},{1,5},{5... | collective-permute-start | bytes 196616 | tf_op jit(solution)/shard_map/ppermute | solution.py:313
  26.4 1.6 %collective-permute-start.10 = (bf16[8,4096]{1,0:T(8,128)(2,1)S(1)}, bf16[8,4096]{1,0:T(8,128)(2,1)S(1)}, u32[]{:S(2)}, u32[]{:S(2)}) collective-permute-start(bf16[8,4096]{1,0:T(8,128)(2,1)S(1)} %relay.5.refs_4_), channel_id=1, source_target_pairs={{0,4},{4,0},{8,12},{12,8},{16,20},{20,16},{24,28},{28,24},{1,5},{5... | collective-permute-start | bytes 196616 | tf_op jit(solution)/shard_map/ppermute | solution.py:313
  26.5 1.6 %collective-permute-start.8 = (bf16[8,4096]{1,0:T(8,128)(2,1)S(1)}, bf16[8,4096]{1,0:T(8,128)(2,1)S(1)}, u32[]{:S(2)}, u32[]{:S(2)}) collective-permute-start(bf16[8,4096]{1,0:T(8,128)(2,1)S(1)} %relay.4.refs_3_), channel_id=1, source_target_pairs={{0,4},{4,0},{8,12},{12,8},{16,20},{20,16},{24,28},{28,24},{1,5},{5... | collective-permute-start | bytes 196616 | tf_op jit(solution)/shard_map/ppermute | solution.py:313
  29.2 5.9 %collective-permute-start.14 = (bf16[8,2560]{1,0:T(8,128)(2,1)S(1)}, bf16[8,2560]{1,0:T(8,128)(2,1)S(1)}, u32[]{:S(2)}, u32[]{:S(2)}) collective-permute-start(bf16[8,2560]{1,0:T(8,128)(2,1)S(1)} %get-tuple-element.72.flat_ref.rest_0_), channel_id=1, source_target_pairs={{0,3},{1,2},{2,1},{3,0},{4,7},{5,6},{6,5},{7,4},{8,11},{9,10},{10,... | collective-permute-start | bytes 122888 | tf_op jit(solution)/shard_map/ppermute | solution.py:313
  32.9 4.9 %collective-permute-start.13 = (bf16[8,2560]{1,0:T(8,128)(2,1)S(1)}, bf16[8,2560]{1,0:T(8,128)(2,1)S(1)}, u32[]{:S(2)}, u32[]{:S(2)}) collective-permute-start(bf16[8,2560]{1,0:T(8,128)(2,1)S(1)} %get-tuple-element.72.flat_ref.rest_0_), channel_id=1, source_target_pairs={{0,2},{1,3},{2,0},{3,1},{4,6},{5,7},{6,4},{7,5},{8,10},{9,11},{10,... | collective-permute-start | bytes 122888 | tf_op jit(solution)/shard_map/ppermute | solution.py:313
  32.9 4.9 %collective-permute-start.12 = (bf16[8,2560]{1,0:T(8,128)(2,1)S(1)}, bf16[8,2560]{1,0:T(8,128)(2,1)S(1)}, u32[]{:S(2)}, u32[]{:S(2)}) collective-permute-start(bf16[8,2560]{1,0:T(8,128)(2,1)S(1)} %get-tuple-element.72.flat_ref.rest_0_), channel_id=1, source_target_pairs={{0,1},{1,0},{2,3},{3,2},{4,5},{5,4},{6,7},{7,6},{8,9},{9,8},{10,11... | collective-permute-start | bytes 122888 | tf_op jit(solution)/shard_map/ppermute | solution.py:313
  37.9 2.5 %collective-permute-start.15 = (f32[8,128]{1,0:T(8,128)S(1)}, f32[8,128]{1,0:T(8,128)S(1)}, u32[]{:S(2)}, u32[]{:S(2)}) collective-permute-start(f32[8,128]{1,0:T(8,128)S(1)} %pair.1), channel_id=1, source_target_pairs={{0,4},{4,0},{8,12},{12,8},{16,20},{20,16},{24,28},{28,24},{1,5},{5... | collective-permute-start | bytes 12296 | tf_op jit(solution)/shard_map/ppermute | solution.py:313
  38.0 4.6 %collective-permute-start.16 = (f32[8,128]{1,0:T(8,128)S(1)}, f32[8,128]{1,0:T(8,128)S(1)}, u32[]{:S(2)}, u32[]{:S(2)}) collective-permute-start(f32[8,128]{1,0:T(8,128)S(1)} %pair.1), channel_id=1, source_target_pairs={{0,24},{4,28},{8,16},{12,20},{16,8},{20,12},{24,0},{28,4},{1,25},{... | collective-permute-start | bytes 12296 | tf_op jit(solution)/shard_map/ppermute | solution.py:313
  40.4 3.6 %collective-permute-start.17 = (f32[8,128]{1,0:T(8,128)S(1)}, f32[8,128]{1,0:T(8,128)S(1)}, u32[]{:S(2)}, u32[]{:S(2)}) collective-permute-start(f32[8,128]{1,0:T(8,128)S(1)} %add.3.own_ref), channel_id=1, source_target_pairs={{0,8},{4,20},{8,0},{12,28},{16,24},{20,4},{24,16},{28,12},{1,9},{5... | collective-permute-start | bytes 12296 | tf_op jit(solution)/shard_map/ppermute | solution.py:317
  42.6 1.5 %collective-permute-start.19 = (f32[8,128]{1,0:T(8,128)S(1)}, f32[8,128]{1,0:T(8,128)S(1)}, u32[]{:S(2)}, u32[]{:S(2)}) collective-permute-start(f32[8,128]{1,0:T(8,128)S(1)} %collective-permute-done.16.common_ref), channel_id=1, source_target_pairs={{0,4},{4,0},{8,12},{12,8},{16,20},{20,16},{24,28},{28,24},{1,5},{5... | collective-permute-start | bytes 12296 | tf_op jit(solution)/shard_map/ppermute | solution.py:313
  44.0 1.2 %collective-permute-start.18 = (f32[8,128]{1,0:T(8,128)S(1)}, f32[8,128]{1,0:T(8,128)S(1)}, u32[]{:S(2)}, u32[]{:S(2)}) collective-permute-start(f32[8,128]{1,0:T(8,128)S(1)} %collective-permute-done.17.rest_0_), channel_id=1, source_target_pairs={{0,4},{4,0},{8,12},{12,8},{16,20},{20,16},{24,28},{28,24},{1,5},{5... | collective-permute-start | bytes 12296 | tf_op jit(solution)/shard_map/ppermute | solution.py:313

commit v7 on v6

--- a/solution.py
+++ b/solution.py
@@ -91,7 +91,9 @@
         rest = rest[2:]
 
         def fetch(index, act):
-            distance = distances[0] - 2 * (index + taken)
+            distance = distances[taken]
+            for slot in range(taken + 1, slots):
+                distance = jnp.where(index + taken == slot, distances[slot], distance)
             whole_or_tail(distance, buffer.at[index], arrived.at[index], act)
 
     if raw_out is not None:
@@ -397,7 +399,7 @@
             name=name,
         )(genotype, *extra)
 
-    here_order = list(range(n - 2, 0, -2))
+    here_order = [n - 2] + list(range(2, n - 2, 2))
     away_order = [d + 1 for d in here_order]
 
     def plain(kernel, operands, out_shape, name, **options):

time: 46.2 us -> 46.2 us (level)
  transfers between devices with their start and end apart: 20 -> 20, of which waited for: 9 -> 8; matrix products, arithmetic and copies ran while one was open for 0% -> 0% of each run, Pallas kernels for 25% -> 25%
where the time goes in v7:
time: 46.2 us; the launch traced here: 45.9 us
  Pallas kernels  18.5 us (40%)
  starting transfers between devices  16.1 us (35%)
  waiting for transfers between devices  10.4 us (23%)
  between operations  0.84 us (2%)
    ppermute x19, starting transfers between devices, swap(): return lax.ppermute(value, axis, [(i, i ^ distance) for i in range(size)])  15.9 us
    pallas_call x4, Pallas kernels, moments(): pl.pallas_call(functools.partial(moments_kernel, snps, distances, opening...  12.1 us
    ppermute x19, waiting for transfers between devices, swap(): return lax.ppermute(value, axis, [(i, i ^ distance) for i in range(size)])  8.95 us
    pallas_call x13, Pallas kernels, plain(): pl.pallas_call(kernel, in_specs=[in_vmem()] * len(operands), out_specs=[i...  6.38 us
    ppermute x1, waiting for transfers between devices, swap_mixed(): lax.ppermute(value, 'ind', [(i, i ^ pair[i % 2]) for i in range(size)])  1.47 us
  transfers between devices with their start and end apart: 20, of which 8 were waited for; matrix products, arithmetic and copies ran while one was open for 0% of the time, Pallas kernels for 25%

profile of v7, /device:TPU:0, one launch (start us, length us, event | category | flops | bytes accessed | tf_op | source)
XLA Modules:
  0.0 45.9 jit_solution(9235827503379259458)
XLA Ops:
  0.6 4.9 %moments_away.1 = (bf16[3,256,3200]{2,1,0:T(8,128)(2,1)S(1)}, bf16[3,8,4992]{2,1,0:T(8,128)(2,1)S(1)}, f32[3,2,3200]{2,1,0:T(2,128)S(1)}, f32[16,256]{1,0:T(8,128)S(1)}, s32[256,3200]{1,0:T(8,128)S(1)}) custom-call(s32[256,25600]{1,0:T(8,128)} %geno_ref.7, s32[10,256]{1,0:T(8,128)} %rest_0_.1, bf16[256]{0:T(256)(128)(2,1)} %rest_1_.1), custom_call_target="tpu_custom_call" | custom-call | flops 1 | bytes 9830400 | tf_op jit(solution)/shard_map/moments_away/pallas_call | solution.py:391
  6.0 3.6 %moments_here.1 = (bf16[3,256,3200]{2,1,0:T(8,128)(2,1)S(1)}, bf16[3,8,4992]{2,1,0:T(8,128)(2,1)S(1)}, f32[3,2,3200]{2,1,0:T(2,128)S(1)}) custom-call(s32[256,25600]{1,0:T(8,128)} %geno_ref.7, s32[256,3200]{1,0:T(8,128)S(1)} %get-tuple-element.45.rest_0_, f32[16,256]{1,0:T(8,128)S(1)} %get-tuple-element.46.rest_1_.left_ref), custom_call_target="tpu_custom_call" | custom-call | flops 1 | bytes 9830400 | tf_op jit(solution)/shard_map/moments_here/pallas_call | solution.py:391
  9.7 3.5 %collective-permute-start.2 = (bf16[8,4992]{1,0:T(8,128)(2,1)S(1)}, bf16[8,4992]{1,0:T(8,128)(2,1)S(1)}, u32[]{:S(2)}, u32[]{:S(2)}) collective-permute-start(bf16[8,4992]{1,0:T(8,128)(2,1)S(1)} %get-tuple-element.56), channel_id=1, source_target_pairs={{0,24},{4,28},{8,16},{12,20},{16,8},{20,12},{24,0},{28,4},{1,25},{... | collective-permute-start | bytes 239624 | tf_op jit(solution)/shard_map/ppermute | solution.py:315
  13.9 2.9 %moments_near.1 = (bf16[1,256,3200]{2,1,0:T(8,128)(2,1)S(1)}, bf16[1,8,4992]{2,1,0:T(8,128)(2,1)S(1)}, f32[1,2,3200]{2,1,0:T(2,128)S(1)}, s32[256,3200]{1,0:T(8,128)S(1)}) custom-call(s32[256,25600]{1,0:T(8,128)} %geno_ref.7, f32[16,256]{1,0:T(8,128)S(1)} %get-tuple-element.50.rest_0_.rest_1_), custom_call_target="tpu_custom_call" | custom-call | flops 1 | bytes 1 | tf_op jit(solution)/shard_map/moments_near/pallas_call | solution.py:391
  17.0 0.7 %moments_own.1 = (bf16[1,256,3200]{2,1,0:T(8,128)(2,1)S(1)}, bf16[1,8,4992]{2,1,0:T(8,128)(2,1)S(1)}, f32[1,2,3200]{2,1,0:T(2,128)S(1)}) custom-call(s32[256,25600]{1,0:T(8,128)} %geno_ref.7, s32[256,3200]{1,0:T(8,128)S(1)} %get-tuple-element.51.rest_0_, f32[16,256]{1,0:T(8,128)S(1)} %get-tuple-element.50.rest_0_.rest_1_), custom_call_target="tpu_custom_call" | custom-call | flops 1 | bytes 1 | tf_op jit(solution)/shard_map/moments_own/pallas_call | solution.py:391
  17.7 0.6 %collective-permute-done.3.refs_1_ = bf16[8,4992]{1,0:T(8,128)(2,1)S(1)} collective-permute-done((bf16[8,4992]{1,0:T(8,128)(2,1)S(1)}, bf16[8,4992]{1,0:T(8,128)(2,1)S(1)}, u32[]{:S(2)}, u32[]{:S(2)}) %collective-permute-start.3) | collective-permute-done | bytes 79904 | tf_op jit(solution)/shard_map/ppermute | solution.py:315
  18.6 2.8 %collective-permute-start.6 = (bf16[8,4096]{1,0:T(8,128)(2,1)S(1)}, bf16[8,4096]{1,0:T(8,128)(2,1)S(1)}, u32[]{:S(2)}, u32[]{:S(2)}) collective-permute-start(bf16[8,4096]{1,0:T(8,128)(2,1)S(1)} %get-tuple-element.59.refs_4_), channel_id=1, source_target_pairs={{0,24},{4,28},{8,16},{12,20},{16,8},{20,12},{24,0},{28,4},{1,25},{... | collective-permute-start | bytes 196616 | tf_op jit(solution)/shard_map/ppermute | solution.py:315
  22.1 1.1 %field.5 = (f32[256,80]{1,0:T(8,128)S(1)}, f32[80,128]{1,0:T(8,128)S(1)}, f32[8,128]{1,0:T(8,128)S(1)}) custom-call(f32[1,25600]{1,0:T(1,128)S(1)} %bitcast.7, s32[1,25600]{1,0:T(1,128)S(1)} %bitcast.13, bf16[1,256,3200]{2,1,0:T(8,128)(2,1)S(1)} %get-tuple-element.52.refs_2_, bf16[1,256,3200]{2,1,0:T(8,128)(2,1)S(1)} %get-tuple-element.53.refs_3_, ...), custom_call_target="tpu_custom_call" | custom-call | flops 1 | bytes 1 | tf_op jit(solution)/shard_map/field/pallas_call | solution.py:406
  23.2 0.9 %collective-permute-done.6.value_ref = bf16[8,4096]{1,0:T(8,128)(2,1)S(1)} collective-permute-done((bf16[8,4096]{1,0:T(8,128)(2,1)S(1)}, bf16[8,4096]{1,0:T(8,128)(2,1)S(1)}, u32[]{:S(2)}, u32[]{:S(2)}) %collective-permute-start.6) | collective-permute-done | bytes 65568 | tf_op jit(solution)/shard_map/ppermute | solution.py:315
  24.1 0.6 %field.6 = (f32[256,80]{1,0:T(8,128)S(1)}, f32[80,128]{1,0:T(8,128)S(1)}, f32[8,128]{1,0:T(8,128)S(1)}) custom-call(f32[1,25600]{1,0:T(1,128)S(1)} %bitcast.8, s32[1,25600]{1,0:T(1,128)S(1)} %bitcast.14, bf16[3,256,3200]{2,1,0:T(8,128)(2,1)S(1)} %get-tuple-element.47.refs_2_, bf16[8,4096]{1,0:T(8,128)(2,1)S(1)} %relay.3.refs_3_, ...), custom_call_target="tpu_custom_call" | custom-call | flops 1 | bytes 1 | tf_op jit(solution)/shard_map/field/pallas_call | solution.py:406
  24.7 1.0 %collective-permute-done.7.value_ref = bf16[8,4096]{1,0:T(8,128)(2,1)S(1)} collective-permute-done((bf16[8,4096]{1,0:T(8,128)(2,1)S(1)}, bf16[8,4096]{1,0:T(8,128)(2,1)S(1)}, u32[]{:S(2)}, u32[]{:S(2)}) %collective-permute-start.7) | collective-permute-done | bytes 65568 | tf_op jit(solution)/shard_map/ppermute | solution.py:315
  25.7 0.6 %field.7 = (f32[256,80]{1,0:T(8,128)S(1)}, f32[80,128]{1,0:T(8,128)S(1)}, f32[8,128]{1,0:T(8,128)S(1)}) custom-call(f32[1,25600]{1,0:T(1,128)S(1)} %bitcast.9, s32[1,25600]{1,0:T(1,128)S(1)} %bitcast.15, bf16[3,256,3200]{2,1,0:T(8,128)(2,1)S(1)} %get-tuple-element.47.refs_2_, bf16[8,4096]{1,0:T(8,128)(2,1)S(1)} %relay.4.refs_3_, ...), custom_call_target="tpu_custom_call" | custom-call | flops 1 | bytes 1 | tf_op jit(solution)/shard_map/field/pallas_call | solution.py:406
  27.0 1.0 %field.8 = (f32[256,80]{1,0:T(8,128)S(1)}, f32[80,128]{1,0:T(8,128)S(1)}, f32[8,128]{1,0:T(8,128)S(1)}) custom-call(f32[1,25600]{1,0:T(1,128)S(1)} %bitcast.10, s32[1,25600]{1,0:T(1,128)S(1)} %bitcast.16, bf16[3,256,3200]{2,1,0:T(8,128)(2,1)S(1)} %get-tuple-element.47.refs_2_, bf16[3,256,3200]{2,1,0:T(8,128)(2,1)S(1)} %get-tuple-element.44.refs_3_.refs_2_, ...), custom_call_target="tpu_custom_call" | custom-call | flops 1 | bytes 1 | tf_op jit(solution)/shard_map/field/pallas_call | solution.py:406
  28.0 1.2 %field.9 = (bf16[8,2560]{1,0:T(8,128)(2,1)S(1)}, f32[8,128]{1,0:T(8,128)S(1)}) custom-call(f32[1,25600]{1,0:T(1,128)S(1)} %bitcast.11, s32[1,25600]{1,0:T(1,128)S(1)} %bitcast.17, bf16[3,256,3200]{2,1,0:T(8,128)(2,1)S(1)} %get-tuple-element.44.refs_3_.refs_2_, bf16[8,4096]{1,0:T(8,128)(2,1)S(1)} %collective-permute-done.8.refs_3_, ...), custom_call_target="tpu_custom_call" | custom-call | flops 1 | bytes 1 | tf_op jit(solution)/shard_map/field/pallas_call | solution.py:406
  29.2 3.7 %collective-permute-start.14 = (bf16[8,2560]{1,0:T(8,128)(2,1)S(1)}, bf16[8,2560]{1,0:T(8,128)(2,1)S(1)}, u32[]{:S(2)}, u32[]{:S(2)}) collective-permute-start(bf16[8,2560]{1,0:T(8,128)(2,1)S(1)} %get-tuple-element.72.flat_ref.rest_0_), channel_id=1, source_target_pairs={{0,3},{1,2},{2,1},{3,0},{4,7},{5,6},{6,5},{7,4},{8,11},{9,10},{10,... | collective-permute-start | bytes 122888 | tf_op jit(solution)/shard_map/ppermute | solution.py:315
  32.9 0.8 %collective-permute-start.12 = (bf16[8,2560]{1,0:T(8,128)(2,1)S(1)}, bf16[8,2560]{1,0:T(8,128)(2,1)S(1)}, u32[]{:S(2)}, u32[]{:S(2)}) collective-permute-start(bf16[8,2560]{1,0:T(8,128)(2,1)S(1)} %get-tuple-element.72.flat_ref.rest_0_), channel_id=1, source_target_pairs={{0,1},{1,0},{2,3},{3,2},{4,5},{5,4},{6,7},{7,6},{8,9},{9,8},{10,11... | collective-permute-start | bytes 122888 | tf_op jit(solution)/shard_map/ppermute | solution.py:315
  33.7 0.8 %stats.1 = (f32[8,128]{1,0:T(8,128)S(1)}, bf16[10,6,256]{2,1,0:T(8,128)(2,1)}) custom-call(bf16[8,2560]{1,0:T(8,128)(2,1)S(1)} %get-tuple-element.72.flat_ref.rest_0_, f32[1,25600]{1,0:T(1,128)S(1)} %bitcast.12, f32[1,25600]{1,0:T(1,128)S(1)} %bitcast.20, s32[1,25600]{1,0:T(1,128)S(1)} %bitcast.18, f32[1,3200]{1,0:T(1,128)S(1)} %get-tuple-element.73.trait_ref, ...), custom_call_target="tpu_custom_call" | custom-call | tf_op jit(solution)/shard_map/stats/pallas_call | solution.py:406
  34.5 0.6 %collective-permute-done.14.rest_3_ = bf16[8,2560]{1,0:T(8,128)(2,1)S(1)} collective-permute-done((bf16[8,2560]{1,0:T(8,128)(2,1)S(1)}, bf16[8,2560]{1,0:T(8,128)(2,1)S(1)}, u32[]{:S(2)}, u32[]{:S(2)}) %collective-permute-start.14) | collective-permute-done | bytes 40992 | tf_op jit(solution)/shard_map/ppermute | solution.py:315
  35.1 2.7 %collective-permute-done.13.rest_2_ = bf16[8,2560]{1,0:T(8,128)(2,1)S(1)} collective-permute-done((bf16[8,2560]{1,0:T(8,128)(2,1)S(1)}, bf16[8,2560]{1,0:T(8,128)(2,1)S(1)}, u32[]{:S(2)}, u32[]{:S(2)}) %collective-permute-start.13) | collective-permute-done | bytes 40992 | tf_op jit(solution)/shard_map/ppermute | solution.py:315
  38.0 2.4 %collective-permute-start.16 = (f32[8,128]{1,0:T(8,128)S(1)}, f32[8,128]{1,0:T(8,128)S(1)}, u32[]{:S(2)}, u32[]{:S(2)}) collective-permute-start(f32[8,128]{1,0:T(8,128)S(1)} %pair.1), channel_id=1, source_target_pairs={{0,24},{4,28},{8,16},{12,20},{16,8},{20,12},{24,0},{28,4},{1,25},{... | collective-permute-start | bytes 12296 | tf_op jit(solution)/shard_map/ppermute | solution.py:315
  40.6 1.9 %collective-permute-done.16.common_ref = f32[8,128]{1,0:T(8,128)S(1)} collective-permute-done((f32[8,128]{1,0:T(8,128)S(1)}, f32[8,128]{1,0:T(8,128)S(1)}, u32[]{:S(2)}, u32[]{:S(2)}) %collective-permute-start.16) | collective-permute-done | bytes 4128 | tf_op jit(solution)/shard_map/ppermute | solution.py:315
  42.6 1.5 %collective-permute-done.17.rest_0_ = f32[8,128]{1,0:T(8,128)S(1)} collective-permute-done((f32[8,128]{1,0:T(8,128)S(1)}, f32[8,128]{1,0:T(8,128)S(1)}, u32[]{:S(2)}, u32[]{:S(2)}) %collective-permute-start.17) | collective-permute-done | bytes 4128 | tf_op jit(solution)/shard_map/ppermute | solution.py:319
  44.1 1.2 %collective-permute-done.18.rest_1_ = f32[8,128]{1,0:T(8,128)S(1)} collective-permute-done((f32[8,128]{1,0:T(8,128)S(1)}, f32[8,128]{1,0:T(8,128)S(1)}, u32[]{:S(2)}, u32[]{:S(2)}) %collective-permute-start.18) | collective-permute-done | bytes 4128 | tf_op jit(solution)/shard_map/ppermute | solution.py:315
  45.2 0.7 %final.1 = (f32[6,24]{1,0:T(8,128)}, f32[1,6]{1,0:T(1,128)}, f32[1,6]{1,0:T(1,128)}) custom-call(f32[8,128]{1,0:T(8,128)S(1)} %get-tuple-element.79.count_ref, f32[8,128]{1,0:T(8,128)S(1)} %add.3.own_ref, f32[8,128]{1,0:T(8,128)S(1)} %collective-permute-done.16.common_ref, f32[8,128]{1,0:T(8,128)S(1)} %collective-permute-done.17.rest_0_, ...), custom_call_target="tpu_custom_call" | custom-call | tf_op jit(solution)/shard_map/final/pallas_call | solution.py:406
  (40 shorter events, 3.3 us)
Async XLA Ops:
  5.5 4.1 %collective-permute-start = (bf16[3,8,4992]{2,1,0:T(8,128)(2,1)S(1)}, bf16[3,8,4992]{2,1,0:T(8,128)(2,1)S(1)}, u32[]{:S(2)}, u32[]{:S(2)}) collective-permute-start(bf16[3,8,4992]{2,1,0:T(8,128)(2,1)S(1)} %get-tuple-element.49), channel_id=1, source_target_pairs={{0,4},{4,0},{8,12},{12,8},{16,20},{20,16},{24,28},{28,24},{1,5},{5... | collective-permute-start | bytes 718856 | tf_op jit(solution)/shard_map/ppermute | solution.py:315
  9.7 7.9 %collective-permute-start.2 = (bf16[8,4992]{1,0:T(8,128)(2,1)S(1)}, bf16[8,4992]{1,0:T(8,128)(2,1)S(1)}, u32[]{:S(2)}, u32[]{:S(2)}) collective-permute-start(bf16[8,4992]{1,0:T(8,128)(2,1)S(1)} %get-tuple-element.56), channel_id=1, source_target_pairs={{0,24},{4,28},{8,16},{12,20},{16,8},{20,12},{24,0},{28,4},{1,25},{... | collective-permute-start | bytes 239624 | tf_op jit(solution)/shard_map/ppermute | solution.py:315
  13.3 5.0 %collective-permute-start.3 = (bf16[8,4992]{1,0:T(8,128)(2,1)S(1)}, bf16[8,4992]{1,0:T(8,128)(2,1)S(1)}, u32[]{:S(2)}, u32[]{:S(2)}) collective-permute-start(bf16[8,4992]{1,0:T(8,128)(2,1)S(1)} %get-tuple-element.57), channel_id=1, source_target_pairs={{0,8},{4,12},{8,0},{12,4},{16,24},{20,28},{24,16},{28,20},{1,9},{5... | collective-permute-start | bytes 239624 | tf_op jit(solution)/shard_map/ppermute | solution.py:315
  13.8 4.5 %collective-permute-start.4 = (bf16[8,4992]{1,0:T(8,128)(2,1)S(1)}, bf16[8,4992]{1,0:T(8,128)(2,1)S(1)}, u32[]{:S(2)}, u32[]{:S(2)}) collective-permute-start(bf16[8,4992]{1,0:T(8,128)(2,1)S(1)} %get-tuple-element.58), channel_id=1, source_target_pairs={{0,16},{4,20},{8,24},{12,28},{16,0},{20,4},{24,8},{28,12},{1,17},{... | collective-permute-start | bytes 239624 | tf_op jit(solution)/shard_map/ppermute | solution.py:315
  16.9 1.4 %collective-permute-start.1 = (bf16[1,8,4992]{2,1,0:T(8,128)(2,1)S(1)}, bf16[1,8,4992]{2,1,0:T(8,128)(2,1)S(1)}, u32[]{:S(2)}, u32[]{:S(2)}) collective-permute-start(bf16[1,8,4992]{2,1,0:T(8,128)(2,1)S(1)} %get-tuple-element.55), channel_id=1, source_target_pairs={{0,4},{4,0},{8,12},{12,8},{16,20},{20,16},{24,28},{28,24},{1,5},{5... | collective-permute-start | bytes 239624 | tf_op jit(solution)/shard_map/ppermute | solution.py:315
  17.0 1.3 %copy-start = (f32[25600]{0:T(1024)S(1)}, f32[25600]{0:T(1024)}, u32[]{:S(2)}) copy-start(f32[25600]{0:T(1024)} %param.7) | copy-start | bytes 307204
  17.0 1.3 %copy-start.2 = (f32[25600]{0:T(1024)S(1)}, f32[25600]{0:T(1024)}, u32[]{:S(2)}) copy-start(f32[25600]{0:T(1024)} %param.8) | copy-start | bytes 307204
  17.0 5.1 %copy-start.1 = (s32[25600]{0:T(1024)S(1)}, s32[25600]{0:T(1024)}, u32[]{:S(2)}) copy-start(s32[25600]{0:T(1024)} %param.9) | copy-start | bytes 307204
  18.5 3.6 %collective-permute-start.5 = (bf16[8,4096]{1,0:T(8,128)(2,1)S(1)}, bf16[8,4096]{1,0:T(8,128)(2,1)S(1)}, u32[]{:S(2)}, u32[]{:S(2)}) collective-permute-start(bf16[8,4096]{1,0:T(8,128)(2,1)S(1)} %get-tuple-element.59.refs_4_), channel_id=1, source_target_pairs={{0,4},{4,0},{8,12},{12,8},{16,20},{20,16},{24,28},{28,24},{1,5},{5... | collective-permute-start | bytes 196616 | tf_op jit(solution)/shard_map/ppermute | solution.py:315
  18.6 5.4 %collective-permute-start.6 = (bf16[8,4096]{1,0:T(8,128)(2,1)S(1)}, bf16[8,4096]{1,0:T(8,128)(2,1)S(1)}, u32[]{:S(2)}, u32[]{:S(2)}) collective-permute-start(bf16[8,4096]{1,0:T(8,128)(2,1)S(1)} %get-tuple-element.59.refs_4_), channel_id=1, source_target_pairs={{0,24},{4,28},{8,16},{12,20},{16,8},{20,12},{24,0},{28,4},{1,25},{... | collective-permute-start | bytes 196616 | tf_op jit(solution)/shard_map/ppermute | solution.py:315
  21.5 4.3 %collective-permute-start.7 = (bf16[8,4096]{1,0:T(8,128)(2,1)S(1)}, bf16[8,4096]{1,0:T(8,128)(2,1)S(1)}, u32[]{:S(2)}, u32[]{:S(2)}) collective-permute-start(bf16[8,4096]{1,0:T(8,128)(2,1)S(1)} %get-tuple-element.59.refs_4_), channel_id=1, source_target_pairs={{0,8},{4,12},{8,0},{12,4},{16,24},{20,28},{24,16},{28,20},{1,9},{5... | collective-permute-start | bytes 196616 | tf_op jit(solution)/shard_map/ppermute | solution.py:315
  22.0 4.3 %collective-permute-start.9 = (bf16[8,4096]{1,0:T(8,128)(2,1)S(1)}, bf16[8,4096]{1,0:T(8,128)(2,1)S(1)}, u32[]{:S(2)}, u32[]{:S(2)}) collective-permute-start(bf16[8,4096]{1,0:T(8,128)(2,1)S(1)} %get-tuple-element.59.refs_4_), channel_id=1, source_target_pairs={{0,16},{4,20},{8,24},{12,28},{16,0},{20,4},{24,8},{28,12},{1,17},{... | collective-permute-start | bytes 196616 | tf_op jit(solution)/shard_map/ppermute | solution.py:315
  24.1 2.9 %collective-permute-start.11 = (bf16[8,4096]{1,0:T(8,128)(2,1)S(1)}, bf16[8,4096]{1,0:T(8,128)(2,1)S(1)}, u32[]{:S(2)}, u32[]{:S(2)}) collective-permute-start(bf16[8,4096]{1,0:T(8,128)(2,1)S(1)} %relay.3.refs_3_), channel_id=1, source_target_pairs={{0,4},{4,0},{8,12},{12,8},{16,20},{20,16},{24,28},{28,24},{1,5},{5... | collective-permute-start | bytes 196616 | tf_op jit(solution)/shard_map/ppermute | solution.py:315
  26.4 1.6 %collective-permute-start.10 = (bf16[8,4096]{1,0:T(8,128)(2,1)S(1)}, bf16[8,4096]{1,0:T(8,128)(2,1)S(1)}, u32[]{:S(2)}, u32[]{:S(2)}) collective-permute-start(bf16[8,4096]{1,0:T(8,128)(2,1)S(1)} %relay.5.refs_4_), channel_id=1, source_target_pairs={{0,4},{4,0},{8,12},{12,8},{16,20},{20,16},{24,28},{28,24},{1,5},{5... | collective-permute-start | bytes 196616 | tf_op jit(solution)/shard_map/ppermute | solution.py:315
  26.5 1.6 %collective-permute-start.8 = (bf16[8,4096]{1,0:T(8,128)(2,1)S(1)}, bf16[8,4096]{1,0:T(8,128)(2,1)S(1)}, u32[]{:S(2)}, u32[]{:S(2)}) collective-permute-start(bf16[8,4096]{1,0:T(8,128)(2,1)S(1)} %relay.4.refs_3_), channel_id=1, source_target_pairs={{0,4},{4,0},{8,12},{12,8},{16,20},{20,16},{24,28},{28,24},{1,5},{5... | collective-permute-start | bytes 196616 | tf_op jit(solution)/shard_map/ppermute | solution.py:315
  29.2 5.9 %collective-permute-start.14 = (bf16[8,2560]{1,0:T(8,128)(2,1)S(1)}, bf16[8,2560]{1,0:T(8,128)(2,1)S(1)}, u32[]{:S(2)}, u32[]{:S(2)}) collective-permute-start(bf16[8,2560]{1,0:T(8,128)(2,1)S(1)} %get-tuple-element.72.flat_ref.rest_0_), channel_id=1, source_target_pairs={{0,3},{1,2},{2,1},{3,0},{4,7},{5,6},{6,5},{7,4},{8,11},{9,10},{10,... | collective-permute-start | bytes 122888 | tf_op jit(solution)/shard_map/ppermute | solution.py:315
  32.9 4.9 %collective-permute-start.13 = (bf16[8,2560]{1,0:T(8,128)(2,1)S(1)}, bf16[8,2560]{1,0:T(8,128)(2,1)S(1)}, u32[]{:S(2)}, u32[]{:S(2)}) collective-permute-start(bf16[8,2560]{1,0:T(8,128)(2,1)S(1)} %get-tuple-element.72.flat_ref.rest_0_), channel_id=1, source_target_pairs={{0,2},{1,3},{2,0},{3,1},{4,6},{5,7},{6,4},{7,5},{8,10},{9,11},{10,... | collective-permute-start | bytes 122888 | tf_op jit(solution)/shard_map/ppermute | solution.py:315
  32.9 4.9 %collective-permute-start.12 = (bf16[8,2560]{1,0:T(8,128)(2,1)S(1)}, bf16[8,2560]{1,0:T(8,128)(2,1)S(1)}, u32[]{:S(2)}, u32[]{:S(2)}) collective-permute-start(bf16[8,2560]{1,0:T(8,128)(2,1)S(1)} %get-tuple-element.72.flat_ref.rest_0_), channel_id=1, source_target_pairs={{0,1},{1,0},{2,3},{3,2},{4,5},{5,4},{6,7},{7,6},{8,9},{9,8},{10,11... | collective-permute-start | bytes 122888 | tf_op jit(solution)/shard_map/ppermute | solution.py:315
  37.9 2.5 %collective-permute-start.15 = (f32[8,128]{1,0:T(8,128)S(1)}, f32[8,128]{1,0:T(8,128)S(1)}, u32[]{:S(2)}, u32[]{:S(2)}) collective-permute-start(f32[8,128]{1,0:T(8,128)S(1)} %pair.1), channel_id=1, source_target_pairs={{0,4},{4,0},{8,12},{12,8},{16,20},{20,16},{24,28},{28,24},{1,5},{5... | collective-permute-start | bytes 12296 | tf_op jit(solution)/shard_map/ppermute | solution.py:315
  38.0 4.6 %collective-permute-start.16 = (f32[8,128]{1,0:T(8,128)S(1)}, f32[8,128]{1,0:T(8,128)S(1)}, u32[]{:S(2)}, u32[]{:S(2)}) collective-permute-start(f32[8,128]{1,0:T(8,128)S(1)} %pair.1), channel_id=1, source_target_pairs={{0,24},{4,28},{8,16},{12,20},{16,8},{20,12},{24,0},{28,4},{1,25},{... | collective-permute-start | bytes 12296 | tf_op jit(solution)/shard_map/ppermute | solution.py:315
  40.4 3.6 %collective-permute-start.17 = (f32[8,128]{1,0:T(8,128)S(1)}, f32[8,128]{1,0:T(8,128)S(1)}, u32[]{:S(2)}, u32[]{:S(2)}) collective-permute-start(f32[8,128]{1,0:T(8,128)S(1)} %add.3.own_ref), channel_id=1, source_target_pairs={{0,8},{4,20},{8,0},{12,28},{16,24},{20,4},{24,16},{28,12},{1,9},{5... | collective-permute-start | bytes 12296 | tf_op jit(solution)/shard_map/ppermute | solution.py:319
  42.6 1.5 %collective-permute-start.19 = (f32[8,128]{1,0:T(8,128)S(1)}, f32[8,128]{1,0:T(8,128)S(1)}, u32[]{:S(2)}, u32[]{:S(2)}) collective-permute-start(f32[8,128]{1,0:T(8,128)S(1)} %collective-permute-done.16.common_ref), channel_id=1, source_target_pairs={{0,4},{4,0},{8,12},{12,8},{16,20},{20,16},{24,28},{28,24},{1,5},{5... | collective-permute-start | bytes 12296 | tf_op jit(solution)/shard_map/ppermute | solution.py:315
  44.0 1.2 %collective-permute-start.18 = (f32[8,128]{1,0:T(8,128)S(1)}, f32[8,128]{1,0:T(8,128)S(1)}, u32[]{:S(2)}, u32[]{:S(2)}) collective-permute-start(f32[8,128]{1,0:T(8,128)S(1)} %collective-permute-done.17.rest_0_), channel_id=1, source_target_pairs={{0,4},{4,0},{8,12},{12,8},{16,20},{20,16},{24,28},{28,24},{1,5},{5... | collective-permute-start | bytes 12296 | tf_op jit(solution)/shard_map/ppermute | solution.py:315

commit v8 on v7

--- a/solution.py
+++ b/solution.py
@@ -461,15 +461,21 @@
     u_here = [swap(u, "ind", n, d) for d in here_order]
     terms = fields([kept_own, kept_near], [(0, 0), (0, 1)], [u, u_near], [])
     u_away = []
-    for slot, (distance, value) in enumerate(zip(here_order, u_here)):
-        shape = [jax.ShapeDtypeStruct(value.shape, value.dtype)]
-        (value,) = plain(relay_kernel, (terms[2], value), shape, "relay")
-        u_away.append(swap(value, "ind", n, 1))
-        if slot < chips - 2:
-            terms = fields([kept_here], [(slot, distance)], [value], terms)
-        else:
-            blocks = [(slot, distance), (0, away_order[0])]
-            terms = fields([kept_here, kept_away], blocks, [value, u_away[0]], terms)
+    for first in range(0, chips - 1, 2):
+        slots = range(first, min(first + 2, chips - 1))
+        values = []
+        for slot in slots:
+            shape = [jax.ShapeDtypeStruct(u.shape, u.dtype)]
+            (value,) = plain(relay_kernel, (terms[2], u_here[slot]), shape, "relay")
+            u_away.append(swap(value, "ind", n, 1))
+            values.append(value)
+        blocks = [(slot, here_order[slot]) for slot in slots]
+        kept = [kept_here] * len(blocks)
+        if len(blocks) == 1:
+            blocks.append((0, away_order[0]))
+            kept.append(kept_away)
+            values.append(u_away[0])
+        terms = fields(kept, blocks, values, terms)
     blocks = list(enumerate(away_order))[1:]
     flat, number = fields([kept_away], blocks, u_away[1:], terms, last=True)
 

time: 46.2 us -> 46 us (level)
    ppermute x19, waiting for transfers between devices: 8.95 us -> 9.57 us  [swap(): return lax.ppermute(value, axis, [(i, i ^ distance) for i in range(size)])]
    ppermute x19, starting transfers between devices: 15.9 us -> 15.3 us  [swap(): return lax.ppermute(value, axis, [(i, i ^ distance) for i in range(size)])]
    ppermute x1, waiting for transfers between devices: 1.47 us -> 0.85 us  [swap_mixed(): lax.ppermute(value, 'ind', [(i, i ^ pair[i % 2]) for i in range(size)])]
    ppermute x1, starting transfers between devices: 0.21 us -> 0.81 us  [swap_mixed(): lax.ppermute(value, 'ind', [(i, i ^ pair[i % 2]) for i in range(size)])]
    pallas_call x13 -> x12, Pallas kernels: 6.38 us -> 6.21 us  [plain(): pl.pallas_call(kernel, in_specs=[in_vmem()] * len(operands), out_specs=[i...]
  transfers between devices with their start and end apart: 20 -> 20, of which waited for: 8 -> 9; matrix products, arithmetic and copies ran while one was open for 0% -> 0% of each run, Pallas kernels for 25% -> 24%
where the time goes in v8:
time: 46 us; the launch traced here: 45.7 us
  Pallas kernels  18.3 us (40%)
  starting transfers between devices  16.1 us (35%)
  waiting for transfers between devices  10.4 us (23%)
  between operations  0.83 us (2%)
    ppermute x19, starting transfers between devices, swap(): return lax.ppermute(value, axis, [(i, i ^ distance) for i in range(size)])  15.3 us
    pallas_call x4, Pallas kernels, moments(): pl.pallas_call(functools.partial(moments_kernel, snps, distances, opening...  12.1 us
    ppermute x19, waiting for transfers between devices, swap(): return lax.ppermute(value, axis, [(i, i ^ distance) for i in range(size)])  9.57 us
    pallas_call x12, Pallas kernels, plain(): pl.pallas_call(kernel, in_specs=[in_vmem()] * len(operands), out_specs=[i...  6.21 us
  transfers between devices with their start and end apart: 20, of which 9 were waited for; matrix products, arithmetic and copies ran while one was open for 0% of the time, Pallas kernels for 24%

profile of v8, /device:TPU:0, one launch (start us, length us, event | category | flops | bytes accessed | tf_op | source)
XLA Modules:
  0.0 45.7 jit_solution(16235931651986151212)
XLA Ops:
  0.6 4.9 %moments_away.1 = (bf16[3,256,3200]{2,1,0:T(8,128)(2,1)S(1)}, bf16[3,8,4992]{2,1,0:T(8,128)(2,1)S(1)}, f32[3,2,3200]{2,1,0:T(2,128)S(1)}, f32[16,256]{1,0:T(8,128)S(1)}, s32[256,3200]{1,0:T(8,128)S(1)}) custom-call(s32[256,25600]{1,0:T(8,128)} %geno_ref.7, s32[10,256]{1,0:T(8,128)} %rest_0_.1, bf16[256]{0:T(256)(128)(2,1)} %rest_1_.1), custom_call_target="tpu_custom_call" | custom-call | flops 1 | bytes 9830400 | tf_op jit(solution)/shard_map/moments_away/pallas_call | solution.py:391
  6.0 3.6 %moments_here.1 = (bf16[3,256,3200]{2,1,0:T(8,128)(2,1)S(1)}, bf16[3,8,4992]{2,1,0:T(8,128)(2,1)S(1)}, f32[3,2,3200]{2,1,0:T(2,128)S(1)}) custom-call(s32[256,25600]{1,0:T(8,128)} %geno_ref.7, s32[256,3200]{1,0:T(8,128)S(1)} %get-tuple-element.43.rest_0_, f32[16,256]{1,0:T(8,128)S(1)} %get-tuple-element.42.rest_1_.left_ref), custom_call_target="tpu_custom_call" | custom-call | flops 1 | bytes 9830400 | tf_op jit(solution)/shard_map/moments_here/pallas_call | solution.py:391
  9.7 3.5 %collective-permute-start.2 = (bf16[8,4992]{1,0:T(8,128)(2,1)S(1)}, bf16[8,4992]{1,0:T(8,128)(2,1)S(1)}, u32[]{:S(2)}, u32[]{:S(2)}) collective-permute-start(bf16[8,4992]{1,0:T(8,128)(2,1)S(1)} %get-tuple-element.52), channel_id=1, source_target_pairs={{0,24},{4,28},{8,16},{12,20},{16,8},{20,12},{24,0},{28,4},{1,25},{... | collective-permute-start | bytes 239624 | tf_op jit(solution)/shard_map/ppermute | solution.py:315
  13.9 2.9 %moments_near.1 = (bf16[1,256,3200]{2,1,0:T(8,128)(2,1)S(1)}, bf16[1,8,4992]{2,1,0:T(8,128)(2,1)S(1)}, f32[1,2,3200]{2,1,0:T(2,128)S(1)}, s32[256,3200]{1,0:T(8,128)S(1)}) custom-call(s32[256,25600]{1,0:T(8,128)} %geno_ref.7, f32[16,256]{1,0:T(8,128)S(1)} %get-tuple-element.46.rest_0_.rest_1_), custom_call_target="tpu_custom_call" | custom-call | flops 1 | bytes 1 | tf_op jit(solution)/shard_map/moments_near/pallas_call | solution.py:391
  17.0 0.7 %moments_own.1 = (bf16[1,256,3200]{2,1,0:T(8,128)(2,1)S(1)}, bf16[1,8,4992]{2,1,0:T(8,128)(2,1)S(1)}, f32[1,2,3200]{2,1,0:T(2,128)S(1)}) custom-call(s32[256,25600]{1,0:T(8,128)} %geno_ref.7, s32[256,3200]{1,0:T(8,128)S(1)} %get-tuple-element.47.rest_0_, f32[16,256]{1,0:T(8,128)S(1)} %get-tuple-element.46.rest_0_.rest_1_), custom_call_target="tpu_custom_call" | custom-call | flops 1 | bytes 1 | tf_op jit(solution)/shard_map/moments_own/pallas_call | solution.py:391
  17.7 0.6 %collective-permute-done.3.refs_1_ = bf16[8,4992]{1,0:T(8,128)(2,1)S(1)} collective-permute-done((bf16[8,4992]{1,0:T(8,128)(2,1)S(1)}, bf16[8,4992]{1,0:T(8,128)(2,1)S(1)}, u32[]{:S(2)}, u32[]{:S(2)}) %collective-permute-start.3) | collective-permute-done | bytes 79904 | tf_op jit(solution)/shard_map/ppermute | solution.py:315
  18.6 2.8 %collective-permute-start.8 = (bf16[8,4096]{1,0:T(8,128)(2,1)S(1)}, bf16[8,4096]{1,0:T(8,128)(2,1)S(1)}, u32[]{:S(2)}, u32[]{:S(2)}) collective-permute-start(bf16[8,4096]{1,0:T(8,128)(2,1)S(1)} %get-tuple-element.55.refs_4_), channel_id=1, source_target_pairs={{0,24},{4,28},{8,16},{12,20},{16,8},{20,12},{24,0},{28,4},{1,25},{... | collective-permute-start | bytes 196616 | tf_op jit(solution)/shard_map/ppermute | solution.py:315
  22.1 1.1 %field.4 = (f32[256,80]{1,0:T(8,128)S(1)}, f32[80,128]{1,0:T(8,128)S(1)}, f32[8,128]{1,0:T(8,128)S(1)}) custom-call(f32[1,25600]{1,0:T(1,128)S(1)} %bitcast.7, s32[1,25600]{1,0:T(1,128)S(1)} %bitcast.12, bf16[1,256,3200]{2,1,0:T(8,128)(2,1)S(1)} %get-tuple-element.48.refs_2_, bf16[1,256,3200]{2,1,0:T(8,128)(2,1)S(1)} %get-tuple-element.49.refs_3_, ...), custom_call_target="tpu_custom_call" | custom-call | flops 1 | bytes 1 | tf_op jit(solution)/shard_map/field/pallas_call | solution.py:406
  23.2 0.9 %collective-permute-done.8.value_ref = bf16[8,4096]{1,0:T(8,128)(2,1)S(1)} collective-permute-done((bf16[8,4096]{1,0:T(8,128)(2,1)S(1)}, bf16[8,4096]{1,0:T(8,128)(2,1)S(1)}, u32[]{:S(2)}, u32[]{:S(2)}) %collective-permute-start.8) | collective-permute-done | bytes 65568 | tf_op jit(solution)/shard_map/ppermute | solution.py:315
  24.1 1.7 %collective-permute-done.6.value_ref = bf16[8,4096]{1,0:T(8,128)(2,1)S(1)} collective-permute-done((bf16[8,4096]{1,0:T(8,128)(2,1)S(1)}, bf16[8,4096]{1,0:T(8,128)(2,1)S(1)}, u32[]{:S(2)}, u32[]{:S(2)}) %collective-permute-start.6) | collective-permute-done | bytes 65568 | tf_op jit(solution)/shard_map/ppermute | solution.py:315
  25.7 1.0 %field.5 = (f32[256,80]{1,0:T(8,128)S(1)}, f32[80,128]{1,0:T(8,128)S(1)}, f32[8,128]{1,0:T(8,128)S(1)}) custom-call(f32[1,25600]{1,0:T(1,128)S(1)} %bitcast.8, s32[1,25600]{1,0:T(1,128)S(1)} %bitcast.13, bf16[3,256,3200]{2,1,0:T(8,128)(2,1)S(1)} %get-tuple-element.57.refs_2_.refs_3_, bf16[3,256,3200]{2,1,0:T(8,128)(2,1)S(1)} %get-tuple-element.57.refs_2_.refs_3_, ...), custom_call_target="tpu_custom_call" | custom-call | flops 1 | bytes 1 | tf_op jit(solution)/shard_map/field/pallas_call | solution.py:406
  27.4 1.0 %field.6 = (f32[256,80]{1,0:T(8,128)S(1)}, f32[80,128]{1,0:T(8,128)S(1)}, f32[8,128]{1,0:T(8,128)S(1)}) custom-call(f32[1,25600]{1,0:T(1,128)S(1)} %bitcast.9, s32[1,25600]{1,0:T(1,128)S(1)} %bitcast.14, bf16[3,256,3200]{2,1,0:T(8,128)(2,1)S(1)} %get-tuple-element.57.refs_2_.refs_3_, bf16[3,256,3200]{2,1,0:T(8,128)(2,1)S(1)} %get-tuple-element.41.refs_3_.refs_2_, ...), custom_call_target="tpu_custom_call" | custom-call | flops 1 | bytes 1 | tf_op jit(solution)/shard_map/field/pallas_call | solution.py:406
  28.4 1.2 %field.7 = (bf16[8,2560]{1,0:T(8,128)(2,1)S(1)}, f32[8,128]{1,0:T(8,128)S(1)}) custom-call(f32[1,25600]{1,0:T(1,128)S(1)} %bitcast.10, s32[1,25600]{1,0:T(1,128)S(1)} %bitcast.15, bf16[3,256,3200]{2,1,0:T(8,128)(2,1)S(1)} %get-tuple-element.41.refs_3_.refs_2_, bf16[8,4096]{1,0:T(8,128)(2,1)S(1)} %collective-permute-done.7.refs_3_, ...), custom_call_target="tpu_custom_call" | custom-call | flops 1 | bytes 1 | tf_op jit(solution)/shard_map/field/pallas_call | solution.py:406
  29.6 3.7 %collective-permute-start.14 = (bf16[8,2560]{1,0:T(8,128)(2,1)S(1)}, bf16[8,2560]{1,0:T(8,128)(2,1)S(1)}, u32[]{:S(2)}, u32[]{:S(2)}) collective-permute-start(bf16[8,2560]{1,0:T(8,128)(2,1)S(1)} %get-tuple-element.66.flat_ref.rest_0_), channel_id=1, source_target_pairs={{0,3},{1,2},{2,1},{3,0},{4,7},{5,6},{6,5},{7,4},{8,11},{9,10},{10,... | collective-permute-start | bytes 122888 | tf_op jit(solution)/shard_map/ppermute | solution.py:315
  33.3 0.8 %collective-permute-start.12 = (bf16[8,2560]{1,0:T(8,128)(2,1)S(1)}, bf16[8,2560]{1,0:T(8,128)(2,1)S(1)}, u32[]{:S(2)}, u32[]{:S(2)}) collective-permute-start(bf16[8,2560]{1,0:T(8,128)(2,1)S(1)} %get-tuple-element.66.flat_ref.rest_0_), channel_id=1, source_target_pairs={{0,1},{1,0},{2,3},{3,2},{4,5},{5,4},{6,7},{7,6},{8,9},{9,8},{10,11... | collective-permute-start | bytes 122888 | tf_op jit(solution)/shard_map/ppermute | solution.py:315
  34.1 0.8 %stats.1 = (f32[8,128]{1,0:T(8,128)S(1)}, bf16[10,6,256]{2,1,0:T(8,128)(2,1)}) custom-call(bf16[8,2560]{1,0:T(8,128)(2,1)S(1)} %get-tuple-element.66.flat_ref.rest_0_, f32[1,25600]{1,0:T(1,128)S(1)} %bitcast.11, f32[1,25600]{1,0:T(1,128)S(1)} %bitcast.18, s32[1,25600]{1,0:T(1,128)S(1)} %bitcast.16, f32[1,3200]{1,0:T(1,128)S(1)} %get-tuple-element.67.trait_ref, ...), custom_call_target="tpu_custom_call" | custom-call | tf_op jit(solution)/shard_map/stats/pallas_call | solution.py:406
  34.9 0.6 %collective-permute-done.14.rest_3_ = bf16[8,2560]{1,0:T(8,128)(2,1)S(1)} collective-permute-done((bf16[8,2560]{1,0:T(8,128)(2,1)S(1)}, bf16[8,2560]{1,0:T(8,128)(2,1)S(1)}, u32[]{:S(2)}, u32[]{:S(2)}) %collective-permute-start.14) | collective-permute-done | bytes 40992 | tf_op jit(solution)/shard_map/ppermute | solution.py:315
  35.5 2.7 %collective-permute-done.13.rest_2_ = bf16[8,2560]{1,0:T(8,128)(2,1)S(1)} collective-permute-done((bf16[8,2560]{1,0:T(8,128)(2,1)S(1)}, bf16[8,2560]{1,0:T(8,128)(2,1)S(1)}, u32[]{:S(2)}, u32[]{:S(2)}) %collective-permute-start.13) | collective-permute-done | bytes 40992 | tf_op jit(solution)/shard_map/ppermute | solution.py:315
  38.4 1.8 %collective-permute-start.16 = (f32[8,128]{1,0:T(8,128)S(1)}, f32[8,128]{1,0:T(8,128)S(1)}, u32[]{:S(2)}, u32[]{:S(2)}) collective-permute-start(f32[8,128]{1,0:T(8,128)S(1)} %pair.1), channel_id=1, source_target_pairs={{0,24},{4,28},{8,16},{12,20},{16,8},{20,12},{24,0},{28,4},{1,25},{... | collective-permute-start | bytes 12296 | tf_op jit(solution)/shard_map/ppermute | solution.py:315
  40.3 0.8 %collective-permute-start.17 = (f32[8,128]{1,0:T(8,128)S(1)}, f32[8,128]{1,0:T(8,128)S(1)}, u32[]{:S(2)}, u32[]{:S(2)}) collective-permute-start(f32[8,128]{1,0:T(8,128)S(1)} %add.3.own_ref), channel_id=1, source_target_pairs={{0,8},{4,20},{8,0},{12,28},{16,24},{20,4},{24,16},{28,12},{1,9},{5... | collective-permute-start | bytes 12296 | tf_op jit(solution)/shard_map/ppermute | solution.py:319
  41.1 1.9 %collective-permute-done.16.common_ref = f32[8,128]{1,0:T(8,128)S(1)} collective-permute-done((f32[8,128]{1,0:T(8,128)S(1)}, f32[8,128]{1,0:T(8,128)S(1)}, u32[]{:S(2)}, u32[]{:S(2)}) %collective-permute-start.16) | collective-permute-done | bytes 4128 | tf_op jit(solution)/shard_map/ppermute | solution.py:315
  43.0 0.9 %collective-permute-done.17.rest_0_ = f32[8,128]{1,0:T(8,128)S(1)} collective-permute-done((f32[8,128]{1,0:T(8,128)S(1)}, f32[8,128]{1,0:T(8,128)S(1)}, u32[]{:S(2)}, u32[]{:S(2)}) %collective-permute-start.17) | collective-permute-done | bytes 4128 | tf_op jit(solution)/shard_map/ppermute | solution.py:319
  44.2 0.9 %collective-permute-done.18.rest_1_ = f32[8,128]{1,0:T(8,128)S(1)} collective-permute-done((f32[8,128]{1,0:T(8,128)S(1)}, f32[8,128]{1,0:T(8,128)S(1)}, u32[]{:S(2)}, u32[]{:S(2)}) %collective-permute-start.18) | collective-permute-done | bytes 4128 | tf_op jit(solution)/shard_map/ppermute | solution.py:315
  45.0 0.7 %final.1 = (f32[6,24]{1,0:T(8,128)}, f32[1,6]{1,0:T(1,128)}, f32[1,6]{1,0:T(1,128)}) custom-call(f32[8,128]{1,0:T(8,128)S(1)} %get-tuple-element.73.count_ref, f32[8,128]{1,0:T(8,128)S(1)} %add.3.own_ref, f32[8,128]{1,0:T(8,128)S(1)} %collective-permute-done.16.common_ref, f32[8,128]{1,0:T(8,128)S(1)} %collective-permute-done.17.rest_0_, ...), custom_call_target="tpu_custom_call" | custom-call | tf_op jit(solution)/shard_map/final/pallas_call | solution.py:406
  (39 shorter events, 3.4 us)
Async XLA Ops:
  5.5 4.1 %collective-permute-start = (bf16[3,8,4992]{2,1,0:T(8,128)(2,1)S(1)}, bf16[3,8,4992]{2,1,0:T(8,128)(2,1)S(1)}, u32[]{:S(2)}, u32[]{:S(2)}) collective-permute-start(bf16[3,8,4992]{2,1,0:T(8,128)(2,1)S(1)} %get-tuple-element.45), channel_id=1, source_target_pairs={{0,4},{4,0},{8,12},{12,8},{16,20},{20,16},{24,28},{28,24},{1,5},{5... | collective-permute-start | bytes 718856 | tf_op jit(solution)/shard_map/ppermute | solution.py:315
  9.7 7.9 %collective-permute-start.2 = (bf16[8,4992]{1,0:T(8,128)(2,1)S(1)}, bf16[8,4992]{1,0:T(8,128)(2,1)S(1)}, u32[]{:S(2)}, u32[]{:S(2)}) collective-permute-start(bf16[8,4992]{1,0:T(8,128)(2,1)S(1)} %get-tuple-element.52), channel_id=1, source_target_pairs={{0,24},{4,28},{8,16},{12,20},{16,8},{20,12},{24,0},{28,4},{1,25},{... | collective-permute-start | bytes 239624 | tf_op jit(solution)/shard_map/ppermute | solution.py:315
  13.3 5.0 %collective-permute-start.3 = (bf16[8,4992]{1,0:T(8,128)(2,1)S(1)}, bf16[8,4992]{1,0:T(8,128)(2,1)S(1)}, u32[]{:S(2)}, u32[]{:S(2)}) collective-permute-start(bf16[8,4992]{1,0:T(8,128)(2,1)S(1)} %get-tuple-element.53), channel_id=1, source_target_pairs={{0,8},{4,12},{8,0},{12,4},{16,24},{20,28},{24,16},{28,20},{1,9},{5... | collective-permute-start | bytes 239624 | tf_op jit(solution)/shard_map/ppermute | solution.py:315
  13.8 4.5 %collective-permute-start.4 = (bf16[8,4992]{1,0:T(8,128)(2,1)S(1)}, bf16[8,4992]{1,0:T(8,128)(2,1)S(1)}, u32[]{:S(2)}, u32[]{:S(2)}) collective-permute-start(bf16[8,4992]{1,0:T(8,128)(2,1)S(1)} %get-tuple-element.54), channel_id=1, source_target_pairs={{0,16},{4,20},{8,24},{12,28},{16,0},{20,4},{24,8},{28,12},{1,17},{... | collective-permute-start | bytes 239624 | tf_op jit(solution)/shard_map/ppermute | solution.py:315
  16.9 1.4 %collective-permute-start.1 = (bf16[1,8,4992]{2,1,0:T(8,128)(2,1)S(1)}, bf16[1,8,4992]{2,1,0:T(8,128)(2,1)S(1)}, u32[]{:S(2)}, u32[]{:S(2)}) collective-permute-start(bf16[1,8,4992]{2,1,0:T(8,128)(2,1)S(1)} %get-tuple-element.51), channel_id=1, source_target_pairs={{0,4},{4,0},{8,12},{12,8},{16,20},{20,16},{24,28},{28,24},{1,5},{5... | collective-permute-start | bytes 239624 | tf_op jit(solution)/shard_map/ppermute | solution.py:315
  17.0 1.3 %copy-start = (f32[25600]{0:T(1024)S(1)}, f32[25600]{0:T(1024)}, u32[]{:S(2)}) copy-start(f32[25600]{0:T(1024)} %param.7) | copy-start | bytes 307204
  17.0 1.3 %copy-start.2 = (f32[25600]{0:T(1024)S(1)}, f32[25600]{0:T(1024)}, u32[]{:S(2)}) copy-start(f32[25600]{0:T(1024)} %param.8) | copy-start | bytes 307204
  17.0 5.1 %copy-start.1 = (s32[25600]{0:T(1024)S(1)}, s32[25600]{0:T(1024)}, u32[]{:S(2)}) copy-start(s32[25600]{0:T(1024)} %param.9) | copy-start | bytes 307204
  18.5 3.6 %collective-permute-start.5 = (bf16[8,4096]{1,0:T(8,128)(2,1)S(1)}, bf16[8,4096]{1,0:T(8,128)(2,1)S(1)}, u32[]{:S(2)}, u32[]{:S(2)}) collective-permute-start(bf16[8,4096]{1,0:T(8,128)(2,1)S(1)} %get-tuple-element.55.refs_4_), channel_id=1, source_target_pairs={{0,4},{4,0},{8,12},{12,8},{16,20},{20,16},{24,28},{28,24},{1,5},{5... | collective-permute-start | bytes 196616 | tf_op jit(solution)/shard_map/ppermute | solution.py:315
  18.6 5.4 %collective-permute-start.8 = (bf16[8,4096]{1,0:T(8,128)(2,1)S(1)}, bf16[8,4096]{1,0:T(8,128)(2,1)S(1)}, u32[]{:S(2)}, u32[]{:S(2)}) collective-permute-start(bf16[8,4096]{1,0:T(8,128)(2,1)S(1)} %get-tuple-element.55.refs_4_), channel_id=1, source_target_pairs={{0,24},{4,28},{8,16},{12,20},{16,8},{20,12},{24,0},{28,4},{1,25},{... | collective-permute-start | bytes 196616 | tf_op jit(solution)/shard_map/ppermute | solution.py:315
  21.5 4.3 %collective-permute-start.6 = (bf16[8,4096]{1,0:T(8,128)(2,1)S(1)}, bf16[8,4096]{1,0:T(8,128)(2,1)S(1)}, u32[]{:S(2)}, u32[]{:S(2)}) collective-permute-start(bf16[8,4096]{1,0:T(8,128)(2,1)S(1)} %get-tuple-element.55.refs_4_), channel_id=1, source_target_pairs={{0,8},{4,12},{8,0},{12,4},{16,24},{20,28},{24,16},{28,20},{1,9},{5... | collective-permute-start | bytes 196616 | tf_op jit(solution)/shard_map/ppermute | solution.py:315
  22.0 4.8 %collective-permute-start.9 = (bf16[8,4096]{1,0:T(8,128)(2,1)S(1)}, bf16[8,4096]{1,0:T(8,128)(2,1)S(1)}, u32[]{:S(2)}, u32[]{:S(2)}) collective-permute-start(bf16[8,4096]{1,0:T(8,128)(2,1)S(1)} %get-tuple-element.55.refs_4_), channel_id=1, source_target_pairs={{0,16},{4,20},{8,24},{12,28},{16,0},{20,4},{24,8},{28,12},{1,17},{... | collective-permute-start | bytes 196616 | tf_op jit(solution)/shard_map/ppermute | solution.py:315
  24.1 3.3 %collective-permute-start.11 = (bf16[8,4096]{1,0:T(8,128)(2,1)S(1)}, bf16[8,4096]{1,0:T(8,128)(2,1)S(1)}, u32[]{:S(2)}, u32[]{:S(2)}) collective-permute-start(bf16[8,4096]{1,0:T(8,128)(2,1)S(1)} %relay.4.refs_4_), channel_id=1, source_target_pairs={{0,4},{4,0},{8,12},{12,8},{16,20},{20,16},{24,28},{28,24},{1,5},{5... | collective-permute-start | bytes 196616 | tf_op jit(solution)/shard_map/ppermute | solution.py:315
  26.8 1.6 %collective-permute-start.10 = (bf16[8,4096]{1,0:T(8,128)(2,1)S(1)}, bf16[8,4096]{1,0:T(8,128)(2,1)S(1)}, u32[]{:S(2)}, u32[]{:S(2)}) collective-permute-start(bf16[8,4096]{1,0:T(8,128)(2,1)S(1)} %relay.5.refs_4_), channel_id=1, source_target_pairs={{0,4},{4,0},{8,12},{12,8},{16,20},{20,16},{24,28},{28,24},{1,5},{5... | collective-permute-start | bytes 196616 | tf_op jit(solution)/shard_map/ppermute | solution.py:315
  26.9 1.6 %collective-permute-start.7 = (bf16[8,4096]{1,0:T(8,128)(2,1)S(1)}, bf16[8,4096]{1,0:T(8,128)(2,1)S(1)}, u32[]{:S(2)}, u32[]{:S(2)}) collective-permute-start(bf16[8,4096]{1,0:T(8,128)(2,1)S(1)} %relay.3.refs_5_), channel_id=1, source_target_pairs={{0,4},{4,0},{8,12},{12,8},{16,20},{20,16},{24,28},{28,24},{1,5},{5... | collective-permute-start | bytes 196616 | tf_op jit(solution)/shard_map/ppermute | solution.py:315
  29.6 5.9 %collective-permute-start.14 = (bf16[8,2560]{1,0:T(8,128)(2,1)S(1)}, bf16[8,2560]{1,0:T(8,128)(2,1)S(1)}, u32[]{:S(2)}, u32[]{:S(2)}) collective-permute-start(bf16[8,2560]{1,0:T(8,128)(2,1)S(1)} %get-tuple-element.66.flat_ref.rest_0_), channel_id=1, source_target_pairs={{0,3},{1,2},{2,1},{3,0},{4,7},{5,6},{6,5},{7,4},{8,11},{9,10},{10,... | collective-permute-start | bytes 122888 | tf_op jit(solution)/shard_map/ppermute | solution.py:315
  33.3 4.9 %collective-permute-start.13 = (bf16[8,2560]{1,0:T(8,128)(2,1)S(1)}, bf16[8,2560]{1,0:T(8,128)(2,1)S(1)}, u32[]{:S(2)}, u32[]{:S(2)}) collective-permute-start(bf16[8,2560]{1,0:T(8,128)(2,1)S(1)} %get-tuple-element.66.flat_ref.rest_0_), channel_id=1, source_target_pairs={{0,2},{1,3},{2,0},{3,1},{4,6},{5,7},{6,4},{7,5},{8,10},{9,11},{10,... | collective-permute-start | bytes 122888 | tf_op jit(solution)/shard_map/ppermute | solution.py:315
  33.3 4.9 %collective-permute-start.12 = (bf16[8,2560]{1,0:T(8,128)(2,1)S(1)}, bf16[8,2560]{1,0:T(8,128)(2,1)S(1)}, u32[]{:S(2)}, u32[]{:S(2)}) collective-permute-start(bf16[8,2560]{1,0:T(8,128)(2,1)S(1)} %get-tuple-element.66.flat_ref.rest_0_), channel_id=1, source_target_pairs={{0,1},{1,0},{2,3},{3,2},{4,5},{5,4},{6,7},{7,6},{8,9},{9,8},{10,11... | collective-permute-start | bytes 122888 | tf_op jit(solution)/shard_map/ppermute | solution.py:315
  38.4 1.9 %collective-permute-start.15 = (f32[8,128]{1,0:T(8,128)S(1)}, f32[8,128]{1,0:T(8,128)S(1)}, u32[]{:S(2)}, u32[]{:S(2)}) collective-permute-start(f32[8,128]{1,0:T(8,128)S(1)} %pair.1), channel_id=1, source_target_pairs={{0,4},{4,0},{8,12},{12,8},{16,20},{20,16},{24,28},{28,24},{1,5},{5... | collective-permute-start | bytes 12296 | tf_op jit(solution)/shard_map/ppermute | solution.py:315
  38.4 4.6 %collective-permute-start.16 = (f32[8,128]{1,0:T(8,128)S(1)}, f32[8,128]{1,0:T(8,128)S(1)}, u32[]{:S(2)}, u32[]{:S(2)}) collective-permute-start(f32[8,128]{1,0:T(8,128)S(1)} %pair.1), channel_id=1, source_target_pairs={{0,24},{4,28},{8,16},{12,20},{16,8},{20,12},{24,0},{28,4},{1,25},{... | collective-permute-start | bytes 12296 | tf_op jit(solution)/shard_map/ppermute | solution.py:315
  40.3 3.6 %collective-permute-start.17 = (f32[8,128]{1,0:T(8,128)S(1)}, f32[8,128]{1,0:T(8,128)S(1)}, u32[]{:S(2)}, u32[]{:S(2)}) collective-permute-start(f32[8,128]{1,0:T(8,128)S(1)} %add.3.own_ref), channel_id=1, source_target_pairs={{0,8},{4,20},{8,0},{12,28},{16,24},{20,4},{24,16},{28,12},{1,9},{5... | collective-permute-start | bytes 12296 | tf_op jit(solution)/shard_map/ppermute | solution.py:319
  43.0 1.2 %collective-permute-start.19 = (f32[8,128]{1,0:T(8,128)S(1)}, f32[8,128]{1,0:T(8,128)S(1)}, u32[]{:S(2)}, u32[]{:S(2)}) collective-permute-start(f32[8,128]{1,0:T(8,128)S(1)} %collective-permute-done.16.common_ref), channel_id=1, source_target_pairs={{0,4},{4,0},{8,12},{12,8},{16,20},{20,16},{24,28},{28,24},{1,5},{5... | collective-permute-start | bytes 12296 | tf_op jit(solution)/shard_map/ppermute | solution.py:315
  43.9 1.2 %collective-permute-start.18 = (f32[8,128]{1,0:T(8,128)S(1)}, f32[8,128]{1,0:T(8,128)S(1)}, u32[]{:S(2)}, u32[]{:S(2)}) collective-permute-start(f32[8,128]{1,0:T(8,128)S(1)} %collective-permute-done.17.rest_0_), channel_id=1, source_target_pairs={{0,4},{4,0},{8,12},{12,8},{16,20},{20,16},{24,28},{28,24},{1,5},{5... | collective-permute-start | bytes 12296 | tf_op jit(solution)/shard_map/ppermute | solution.py:315

commit v9 on v8

--- a/solution.py
+++ b/solution.py
@@ -20,6 +20,36 @@
 BF16 = jnp.bfloat16
 VMEM = pltpu.VMEM
 MIB = 1 << 20
+
+
+def folds(rows, width):
+    return rows == 6 and width % (4 * LANES) == 0
+
+
+def fold_rows(value, rows):
+    width = value.shape[1]
+    if not folds(rows, width):
+        return value
+    main = width * 3 // 4
+    tail = value[:, main:]
+    row = rows_iota(SUBLANES)
+    result = value[:, :main]
+    for at in range(2):
+        line = jnp.concatenate([tail[3 * at + i : 3 * at + i + 1] for i in range(3)], axis=1)
+        result = jnp.where(row == 6 + at, line, result)
+    return result
+
+
+def unfold_rows(value, rows, width):
+    if not folds(rows, width):
+        return value
+    main, part = width * 3 // 4, width // 4
+    row = rows_iota(SUBLANES)
+    tail = jnp.zeros((SUBLANES, part), F32)
+    for i in range(6):
+        line = value[6 + i // 3 : 7 + i // 3, i % 3 * part : (i % 3 + 1) * part]
+        tail = jnp.where(row == i, line, tail)
+    return jnp.concatenate([jnp.where(row < 6, value, 0.0), tail], axis=1)
 
 
 def core():
@@ -219,7 +249,7 @@
     quad = jnp.sum(jnp.where(member, trait * trait, 0.0), axis=1, keepdims=True)
     lane = lax.broadcasted_iota(jnp.int32, (SUBLANES, LANES), 1)
     out_ref[...] = jnp.where(lane == TRACE_LANE, trace, jnp.where(lane == QUAD_LANE, quad, 0.0))
-    flat = flat_ref[...].astype(F32)
+    flat = unfold_rows(flat_ref[...].astype(F32), own_bins, PROBES * rows)
     for b in range(PROBES):
         field_ref[b] = flat[:own_bins, b * rows : (b + 1) * rows].astype(BF16)
 
@@ -271,15 +301,16 @@
     count_ref[...] = jnp.broadcast_to(number, count_ref.shape)
     inverse = 1.0 / jnp.maximum(number, 1.0)
     flat = [acc[b * SUBLANES : (b + 1) * SUBLANES] * inverse for b in range(PROBES)]
-    flat_ref[...] = jnp.concatenate(flat, axis=1).astype(BF16)
-
-
-def pair_kernel(stats_ref, *rest):
+    flat_ref[...] = fold_rows(jnp.concatenate(flat, axis=1), own_bins).astype(BF16)
+
+
+def pair_kernel(own_bins, width, stats_ref, *rest):
     flats, out_ref = rest[:-1], rest[-1]
-    everyone = [flat[...].astype(F32) for flat in flats]
+    everyone = [unfold_rows(flat[...].astype(F32), own_bins, width) for flat in flats]
+    own = everyone[0].astype(BF16)
     everyone += [jnp.zeros_like(everyone[0])] * (LANES // SUBLANES - len(flats))
     out_ref[...] = stats_ref[...] + lax.dot_general(
-        flats[0][...],
+        own,
         jnp.concatenate(everyone, axis=0).astype(BF16),
         (((1,), (1,)), ((), ())),
         preferred_element_type=F32,
@@ -446,7 +477,10 @@
         jax.ShapeDtypeStruct((PROBES * SUBLANES, LANES), F32),
         number_shape,
     ]
-    end_shape = [jax.ShapeDtypeStruct((SUBLANES, PROBES * rows), BF16), number_shape]
+    wide = PROBES * rows
+    if folds(own_bins, wide):
+        wide = wide * 3 // 4
+    end_shape = [jax.ShapeDtypeStruct((SUBLANES, wide), BF16), number_shape]
 
     def fields(kept, blocks, us, terms, last=False):
         return plain(
@@ -487,7 +521,12 @@
         [number_shape, jax.ShapeDtypeStruct((PROBES, own_bins, rows), BF16)],
         "stats",
     )
-    (part,) = plain(pair_kernel, (stats, *flats), [number_shape], "pair")
+    (part,) = plain(
+        functools.partial(pair_kernel, own_bins, PROBES * rows),
+        (stats, *flats),
+        [number_shape],
+        "pair",
+    )
     pairs, common = chosen_pairs(list(range(2, n, 2)))
     part_common = swap(part, "ind", n, common)
     part = part + swap(part, "ind", n, 1)

time: 46 us -> 45.9 us (level)
  transfers between devices with their start and end apart: 20 -> 20, of which waited for: 9 -> 9; matrix products, arithmetic and copies ran while one was open for 0% -> 0% of each run, Pallas kernels for 24% -> 25%
where the time goes in v9:
time: 45.9 us; the launch traced here: 45.6 us
  Pallas kernels  18.4 us (40%)
  starting transfers between devices  16.1 us (35%)
  waiting for transfers between devices  10.3 us (22%)
  between operations  0.83 us (2%)
    ppermute x19, starting transfers between devices, swap(): return lax.ppermute(value, axis, [(i, i ^ distance) for i in range(size)])  15.3 us
    pallas_call x4, Pallas kernels, moments(): pl.pallas_call(functools.partial(moments_kernel, snps, distances, opening...  12.1 us
    ppermute x19, waiting for transfers between devices, swap(): return lax.ppermute(value, axis, [(i, i ^ distance) for i in range(size)])  9.44 us
    pallas_call x12, Pallas kernels, plain(): pl.pallas_call(kernel, in_specs=[in_vmem()] * len(operands), out_specs=[i...  6.27 us
  transfers between devices with their start and end apart: 20, of which 9 were waited for; matrix products, arithmetic and copies ran while one was open for 0% of the time, Pallas kernels for 25%

profile of v9, /device:TPU:0, one launch (start us, length us, event | category | flops | bytes accessed | tf_op | source)
XLA Modules:
  0.0 45.6 jit_solution(182924650310974775)
XLA Ops:
  0.6 4.9 %moments_away.1 = (bf16[3,256,3200]{2,1,0:T(8,128)(2,1)S(1)}, bf16[3,8,4992]{2,1,0:T(8,128)(2,1)S(1)}, f32[3,2,3200]{2,1,0:T(2,128)S(1)}, f32[16,256]{1,0:T(8,128)S(1)}, s32[256,3200]{1,0:T(8,128)S(1)}) custom-call(s32[256,25600]{1,0:T(8,128)} %geno_ref.7, s32[10,256]{1,0:T(8,128)} %rest_0_.1, bf16[256]{0:T(256)(128)(2,1)} %rest_1_.1), custom_call_target="tpu_custom_call" | custom-call | flops 1 | bytes 9830400 | tf_op jit(solution)/shard_map/moments_away/pallas_call | solution.py:422
  6.0 3.6 %moments_here.1 = (bf16[3,256,3200]{2,1,0:T(8,128)(2,1)S(1)}, bf16[3,8,4992]{2,1,0:T(8,128)(2,1)S(1)}, f32[3,2,3200]{2,1,0:T(2,128)S(1)}) custom-call(s32[256,25600]{1,0:T(8,128)} %geno_ref.7, s32[256,3200]{1,0:T(8,128)S(1)} %get-tuple-element.43.rest_0_, f32[16,256]{1,0:T(8,128)S(1)} %get-tuple-element.42.rest_1_.left_ref), custom_call_target="tpu_custom_call" | custom-call | flops 1 | bytes 9830400 | tf_op jit(solution)/shard_map/moments_here/pallas_call | solution.py:422
  9.7 3.5 %collective-permute-start.2 = (bf16[8,4992]{1,0:T(8,128)(2,1)S(1)}, bf16[8,4992]{1,0:T(8,128)(2,1)S(1)}, u32[]{:S(2)}, u32[]{:S(2)}) collective-permute-start(bf16[8,4992]{1,0:T(8,128)(2,1)S(1)} %get-tuple-element.52), channel_id=1, source_target_pairs={{0,24},{4,28},{8,16},{12,20},{16,8},{20,12},{24,0},{28,4},{1,25},{... | collective-permute-start | bytes 239624 | tf_op jit(solution)/shard_map/ppermute | solution.py:346
  13.9 2.9 %moments_near.1 = (bf16[1,256,3200]{2,1,0:T(8,128)(2,1)S(1)}, bf16[1,8,4992]{2,1,0:T(8,128)(2,1)S(1)}, f32[1,2,3200]{2,1,0:T(2,128)S(1)}, s32[256,3200]{1,0:T(8,128)S(1)}) custom-call(s32[256,25600]{1,0:T(8,128)} %geno_ref.7, f32[16,256]{1,0:T(8,128)S(1)} %get-tuple-element.46.rest_0_.rest_1_), custom_call_target="tpu_custom_call" | custom-call | flops 1 | bytes 1 | tf_op jit(solution)/shard_map/moments_near/pallas_call | solution.py:422
  17.0 0.7 %moments_own.1 = (bf16[1,256,3200]{2,1,0:T(8,128)(2,1)S(1)}, bf16[1,8,4992]{2,1,0:T(8,128)(2,1)S(1)}, f32[1,2,3200]{2,1,0:T(2,128)S(1)}) custom-call(s32[256,25600]{1,0:T(8,128)} %geno_ref.7, s32[256,3200]{1,0:T(8,128)S(1)} %get-tuple-element.47.rest_0_, f32[16,256]{1,0:T(8,128)S(1)} %get-tuple-element.46.rest_0_.rest_1_), custom_call_target="tpu_custom_call" | custom-call | flops 1 | bytes 1 | tf_op jit(solution)/shard_map/moments_own/pallas_call | solution.py:422
  17.7 0.6 %collective-permute-done.3.refs_1_ = bf16[8,4992]{1,0:T(8,128)(2,1)S(1)} collective-permute-done((bf16[8,4992]{1,0:T(8,128)(2,1)S(1)}, bf16[8,4992]{1,0:T(8,128)(2,1)S(1)}, u32[]{:S(2)}, u32[]{:S(2)}) %collective-permute-start.3) | collective-permute-done | bytes 79904 | tf_op jit(solution)/shard_map/ppermute | solution.py:346
  18.6 2.8 %collective-permute-start.8 = (bf16[8,4096]{1,0:T(8,128)(2,1)S(1)}, bf16[8,4096]{1,0:T(8,128)(2,1)S(1)}, u32[]{:S(2)}, u32[]{:S(2)}) collective-permute-start(bf16[8,4096]{1,0:T(8,128)(2,1)S(1)} %get-tuple-element.55.refs_4_), channel_id=1, source_target_pairs={{0,24},{4,28},{8,16},{12,20},{16,8},{20,12},{24,0},{28,4},{1,25},{... | collective-permute-start | bytes 196616 | tf_op jit(solution)/shard_map/ppermute | solution.py:346
  21.5 0.5 %collective-permute-start.6 = (bf16[8,4096]{1,0:T(8,128)(2,1)S(1)}, bf16[8,4096]{1,0:T(8,128)(2,1)S(1)}, u32[]{:S(2)}, u32[]{:S(2)}) collective-permute-start(bf16[8,4096]{1,0:T(8,128)(2,1)S(1)} %get-tuple-element.55.refs_4_), channel_id=1, source_target_pairs={{0,8},{4,12},{8,0},{12,4},{16,24},{20,28},{24,16},{28,20},{1,9},{5... | collective-permute-start | bytes 196616 | tf_op jit(solution)/shard_map/ppermute | solution.py:346
  22.1 1.1 %field.4 = (f32[256,80]{1,0:T(8,128)S(1)}, f32[80,128]{1,0:T(8,128)S(1)}, f32[8,128]{1,0:T(8,128)S(1)}) custom-call(f32[1,25600]{1,0:T(1,128)S(1)} %bitcast.7, s32[1,25600]{1,0:T(1,128)S(1)} %bitcast.12, bf16[1,256,3200]{2,1,0:T(8,128)(2,1)S(1)} %get-tuple-element.48.refs_2_, bf16[1,256,3200]{2,1,0:T(8,128)(2,1)S(1)} %get-tuple-element.49.refs_3_, ...), custom_call_target="tpu_custom_call" | custom-call | flops 1 | bytes 1 | tf_op jit(solution)/shard_map/field/pallas_call | solution.py:437
  23.2 0.9 %collective-permute-done.8.value_ref = bf16[8,4096]{1,0:T(8,128)(2,1)S(1)} collective-permute-done((bf16[8,4096]{1,0:T(8,128)(2,1)S(1)}, bf16[8,4096]{1,0:T(8,128)(2,1)S(1)}, u32[]{:S(2)}, u32[]{:S(2)}) %collective-permute-start.8) | collective-permute-done | bytes 65568 | tf_op jit(solution)/shard_map/ppermute | solution.py:346
  24.1 1.7 %collective-permute-done.6.value_ref = bf16[8,4096]{1,0:T(8,128)(2,1)S(1)} collective-permute-done((bf16[8,4096]{1,0:T(8,128)(2,1)S(1)}, bf16[8,4096]{1,0:T(8,128)(2,1)S(1)}, u32[]{:S(2)}, u32[]{:S(2)}) %collective-permute-start.6) | collective-permute-done | bytes 65568 | tf_op jit(solution)/shard_map/ppermute | solution.py:346
  25.7 1.0 %field.5 = (f32[256,80]{1,0:T(8,128)S(1)}, f32[80,128]{1,0:T(8,128)S(1)}, f32[8,128]{1,0:T(8,128)S(1)}) custom-call(f32[1,25600]{1,0:T(1,128)S(1)} %bitcast.8, s32[1,25600]{1,0:T(1,128)S(1)} %bitcast.13, bf16[3,256,3200]{2,1,0:T(8,128)(2,1)S(1)} %get-tuple-element.57.refs_2_.refs_3_, bf16[3,256,3200]{2,1,0:T(8,128)(2,1)S(1)} %get-tuple-element.57.refs_2_.refs_3_, ...), custom_call_target="tpu_custom_call" | custom-call | flops 1 | bytes 1 | tf_op jit(solution)/shard_map/field/pallas_call | solution.py:437
  27.4 1.0 %field.6 = (f32[256,80]{1,0:T(8,128)S(1)}, f32[80,128]{1,0:T(8,128)S(1)}, f32[8,128]{1,0:T(8,128)S(1)}) custom-call(f32[1,25600]{1,0:T(1,128)S(1)} %bitcast.9, s32[1,25600]{1,0:T(1,128)S(1)} %bitcast.14, bf16[3,256,3200]{2,1,0:T(8,128)(2,1)S(1)} %get-tuple-element.57.refs_2_.refs_3_, bf16[3,256,3200]{2,1,0:T(8,128)(2,1)S(1)} %get-tuple-element.41.refs_3_.refs_2_, ...), custom_call_target="tpu_custom_call" | custom-call | flops 1 | bytes 1 | tf_op jit(solution)/shard_map/field/pallas_call | solution.py:437
  28.4 1.2 %field.7 = (bf16[8,1920]{1,0:T(8,128)(2,1)S(1)}, f32[8,128]{1,0:T(8,128)S(1)}) custom-call(f32[1,25600]{1,0:T(1,128)S(1)} %bitcast.10, s32[1,25600]{1,0:T(1,128)S(1)} %bitcast.15, bf16[3,256,3200]{2,1,0:T(8,128)(2,1)S(1)} %get-tuple-element.41.refs_3_.refs_2_, bf16[8,4096]{1,0:T(8,128)(2,1)S(1)} %collective-permute-done.7.refs_3_, ...), custom_call_target="tpu_custom_call" | custom-call | flops 1 | bytes 1 | tf_op jit(solution)/shard_map/field/pallas_call | solution.py:437
  29.6 3.7 %collective-permute-start.14 = (bf16[8,1920]{1,0:T(8,128)(2,1)S(1)}, bf16[8,1920]{1,0:T(8,128)(2,1)S(1)}, u32[]{:S(2)}, u32[]{:S(2)}) collective-permute-start(bf16[8,1920]{1,0:T(8,128)(2,1)S(1)} %get-tuple-element.66.flat_ref.rest_0_), channel_id=1, source_target_pairs={{0,3},{1,2},{2,1},{3,0},{4,7},{5,6},{6,5},{7,4},{8,11},{9,10},{10,... | collective-permute-start | bytes 92168 | tf_op jit(solution)/shard_map/ppermute | solution.py:346
  33.3 0.8 %collective-permute-start.12 = (bf16[8,1920]{1,0:T(8,128)(2,1)S(1)}, bf16[8,1920]{1,0:T(8,128)(2,1)S(1)}, u32[]{:S(2)}, u32[]{:S(2)}) collective-permute-start(bf16[8,1920]{1,0:T(8,128)(2,1)S(1)} %get-tuple-element.66.flat_ref.rest_0_), channel_id=1, source_target_pairs={{0,1},{1,0},{2,3},{3,2},{4,5},{5,4},{6,7},{7,6},{8,9},{9,8},{10,11... | collective-permute-start | bytes 92168 | tf_op jit(solution)/shard_map/ppermute | solution.py:346
  34.1 0.8 %stats.1 = (f32[8,128]{1,0:T(8,128)S(1)}, bf16[10,6,256]{2,1,0:T(8,128)(2,1)}) custom-call(bf16[8,1920]{1,0:T(8,128)(2,1)S(1)} %get-tuple-element.66.flat_ref.rest_0_, f32[1,25600]{1,0:T(1,128)S(1)} %bitcast.11, f32[1,25600]{1,0:T(1,128)S(1)} %bitcast.18, s32[1,25600]{1,0:T(1,128)S(1)} %bitcast.16, f32[1,3200]{1,0:T(1,128)S(1)} %get-tuple-element.67.trait_ref, ...), custom_call_target="tpu_custom_call" | custom-call | tf_op jit(solution)/shard_map/stats/pallas_call | solution.py:437
  35.4 2.7 %collective-permute-done.13.rest_2_ = bf16[8,1920]{1,0:T(8,128)(2,1)S(1)} collective-permute-done((bf16[8,1920]{1,0:T(8,128)(2,1)S(1)}, bf16[8,1920]{1,0:T(8,128)(2,1)S(1)}, u32[]{:S(2)}, u32[]{:S(2)}) %collective-permute-start.13) | collective-permute-done | bytes 30752 | tf_op jit(solution)/shard_map/ppermute | solution.py:346
  38.3 1.8 %collective-permute-start.16 = (f32[8,128]{1,0:T(8,128)S(1)}, f32[8,128]{1,0:T(8,128)S(1)}, u32[]{:S(2)}, u32[]{:S(2)}) collective-permute-start(f32[8,128]{1,0:T(8,128)S(1)} %pair.1), channel_id=1, source_target_pairs={{0,24},{4,28},{8,16},{12,20},{16,8},{20,12},{24,0},{28,4},{1,25},{... | collective-permute-start | bytes 12296 | tf_op jit(solution)/shard_map/ppermute | solution.py:346
  40.2 0.8 %collective-permute-start.17 = (f32[8,128]{1,0:T(8,128)S(1)}, f32[8,128]{1,0:T(8,128)S(1)}, u32[]{:S(2)}, u32[]{:S(2)}) collective-permute-start(f32[8,128]{1,0:T(8,128)S(1)} %add.3.own_ref), channel_id=1, source_target_pairs={{0,8},{4,20},{8,0},{12,28},{16,24},{20,4},{24,16},{28,12},{1,9},{5... | collective-permute-start | bytes 12296 | tf_op jit(solution)/shard_map/ppermute | solution.py:350
  41.0 1.9 %collective-permute-done.16.common_ref = f32[8,128]{1,0:T(8,128)S(1)} collective-permute-done((f32[8,128]{1,0:T(8,128)S(1)}, f32[8,128]{1,0:T(8,128)S(1)}, u32[]{:S(2)}, u32[]{:S(2)}) %collective-permute-start.16) | collective-permute-done | bytes 4128 | tf_op jit(solution)/shard_map/ppermute | solution.py:346
  42.9 0.9 %collective-permute-done.17.rest_0_ = f32[8,128]{1,0:T(8,128)S(1)} collective-permute-done((f32[8,128]{1,0:T(8,128)S(1)}, f32[8,128]{1,0:T(8,128)S(1)}, u32[]{:S(2)}, u32[]{:S(2)}) %collective-permute-start.17) | collective-permute-done | bytes 4128 | tf_op jit(solution)/shard_map/ppermute | solution.py:350
  44.1 0.9 %collective-permute-done.18.rest_1_ = f32[8,128]{1,0:T(8,128)S(1)} collective-permute-done((f32[8,128]{1,0:T(8,128)S(1)}, f32[8,128]{1,0:T(8,128)S(1)}, u32[]{:S(2)}, u32[]{:S(2)}) %collective-permute-start.18) | collective-permute-done | bytes 4128 | tf_op jit(solution)/shard_map/ppermute | solution.py:346
  44.9 0.7 %final.1 = (f32[6,24]{1,0:T(8,128)}, f32[1,6]{1,0:T(1,128)}, f32[1,6]{1,0:T(1,128)}) custom-call(f32[8,128]{1,0:T(8,128)S(1)} %get-tuple-element.73.count_ref, f32[8,128]{1,0:T(8,128)S(1)} %add.3.own_ref, f32[8,128]{1,0:T(8,128)S(1)} %collective-permute-done.16.common_ref, f32[8,128]{1,0:T(8,128)S(1)} %collective-permute-done.17.rest_0_, ...), custom_call_target="tpu_custom_call" | custom-call | tf_op jit(solution)/shard_map/final/pallas_call | solution.py:437
  (39 shorter events, 3.3 us)
Async XLA Ops:
  5.5 4.1 %collective-permute-start = (bf16[3,8,4992]{2,1,0:T(8,128)(2,1)S(1)}, bf16[3,8,4992]{2,1,0:T(8,128)(2,1)S(1)}, u32[]{:S(2)}, u32[]{:S(2)}) collective-permute-start(bf16[3,8,4992]{2,1,0:T(8,128)(2,1)S(1)} %get-tuple-element.45), channel_id=1, source_target_pairs={{0,4},{4,0},{8,12},{12,8},{16,20},{20,16},{24,28},{28,24},{1,5},{5... | collective-permute-start | bytes 718856 | tf_op jit(solution)/shard_map/ppermute | solution.py:346
  9.7 7.9 %collective-permute-start.2 = (bf16[8,4992]{1,0:T(8,128)(2,1)S(1)}, bf16[8,4992]{1,0:T(8,128)(2,1)S(1)}, u32[]{:S(2)}, u32[]{:S(2)}) collective-permute-start(bf16[8,4992]{1,0:T(8,128)(2,1)S(1)} %get-tuple-element.52), channel_id=1, source_target_pairs={{0,24},{4,28},{8,16},{12,20},{16,8},{20,12},{24,0},{28,4},{1,25},{... | collective-permute-start | bytes 239624 | tf_op jit(solution)/shard_map/ppermute | solution.py:346
  13.3 5.0 %collective-permute-start.3 = (bf16[8,4992]{1,0:T(8,128)(2,1)S(1)}, bf16[8,4992]{1,0:T(8,128)(2,1)S(1)}, u32[]{:S(2)}, u32[]{:S(2)}) collective-permute-start(bf16[8,4992]{1,0:T(8,128)(2,1)S(1)} %get-tuple-element.53), channel_id=1, source_target_pairs={{0,8},{4,12},{8,0},{12,4},{16,24},{20,28},{24,16},{28,20},{1,9},{5... | collective-permute-start | bytes 239624 | tf_op jit(solution)/shard_map/ppermute | solution.py:346
  13.8 4.5 %collective-permute-start.4 = (bf16[8,4992]{1,0:T(8,128)(2,1)S(1)}, bf16[8,4992]{1,0:T(8,128)(2,1)S(1)}, u32[]{:S(2)}, u32[]{:S(2)}) collective-permute-start(bf16[8,4992]{1,0:T(8,128)(2,1)S(1)} %get-tuple-element.54), channel_id=1, source_target_pairs={{0,16},{4,20},{8,24},{12,28},{16,0},{20,4},{24,8},{28,12},{1,17},{... | collective-permute-start | bytes 239624 | tf_op jit(solution)/shard_map/ppermute | solution.py:346
  16.9 1.4 %collective-permute-start.1 = (bf16[1,8,4992]{2,1,0:T(8,128)(2,1)S(1)}, bf16[1,8,4992]{2,1,0:T(8,128)(2,1)S(1)}, u32[]{:S(2)}, u32[]{:S(2)}) collective-permute-start(bf16[1,8,4992]{2,1,0:T(8,128)(2,1)S(1)} %get-tuple-element.51), channel_id=1, source_target_pairs={{0,4},{4,0},{8,12},{12,8},{16,20},{20,16},{24,28},{28,24},{1,5},{5... | collective-permute-start | bytes 239624 | tf_op jit(solution)/shard_map/ppermute | solution.py:346
  17.0 1.3 %copy-start = (f32[25600]{0:T(1024)S(1)}, f32[25600]{0:T(1024)}, u32[]{:S(2)}) copy-start(f32[25600]{0:T(1024)} %param.7) | copy-start | bytes 307204
  17.0 1.3 %copy-start.2 = (f32[25600]{0:T(1024)S(1)}, f32[25600]{0:T(1024)}, u32[]{:S(2)}) copy-start(f32[25600]{0:T(1024)} %param.8) | copy-start | bytes 307204
  17.0 5.1 %copy-start.1 = (s32[25600]{0:T(1024)S(1)}, s32[25600]{0:T(1024)}, u32[]{:S(2)}) copy-start(s32[25600]{0:T(1024)} %param.9) | copy-start | bytes 307204
  18.5 3.6 %collective-permute-start.5 = (bf16[8,4096]{1,0:T(8,128)(2,1)S(1)}, bf16[8,4096]{1,0:T(8,128)(2,1)S(1)}, u32[]{:S(2)}, u32[]{:S(2)}) collective-permute-start(bf16[8,4096]{1,0:T(8,128)(2,1)S(1)} %get-tuple-element.55.refs_4_), channel_id=1, source_target_pairs={{0,4},{4,0},{8,12},{12,8},{16,20},{20,16},{24,28},{28,24},{1,5},{5... | collective-permute-start | bytes 196616 | tf_op jit(solution)/shard_map/ppermute | solution.py:346
  18.6 5.4 %collective-permute-start.8 = (bf16[8,4096]{1,0:T(8,128)(2,1)S(1)}, bf16[8,4096]{1,0:T(8,128)(2,1)S(1)}, u32[]{:S(2)}, u32[]{:S(2)}) collective-permute-start(bf16[8,4096]{1,0:T(8,128)(2,1)S(1)} %get-tuple-element.55.refs_4_), channel_id=1, source_target_pairs={{0,24},{4,28},{8,16},{12,20},{16,8},{20,12},{24,0},{28,4},{1,25},{... | collective-permute-start | bytes 196616 | tf_op jit(solution)/shard_map/ppermute | solution.py:346
  21.5 4.3 %collective-permute-start.6 = (bf16[8,4096]{1,0:T(8,128)(2,1)S(1)}, bf16[8,4096]{1,0:T(8,128)(2,1)S(1)}, u32[]{:S(2)}, u32[]{:S(2)}) collective-permute-start(bf16[8,4096]{1,0:T(8,128)(2,1)S(1)} %get-tuple-element.55.refs_4_), channel_id=1, source_target_pairs={{0,8},{4,12},{8,0},{12,4},{16,24},{20,28},{24,16},{28,20},{1,9},{5... | collective-permute-start | bytes 196616 | tf_op jit(solution)/shard_map/ppermute | solution.py:346
  22.0 4.8 %collective-permute-start.9 = (bf16[8,4096]{1,0:T(8,128)(2,1)S(1)}, bf16[8,4096]{1,0:T(8,128)(2,1)S(1)}, u32[]{:S(2)}, u32[]{:S(2)}) collective-permute-start(bf16[8,4096]{1,0:T(8,128)(2,1)S(1)} %get-tuple-element.55.refs_4_), channel_id=1, source_target_pairs={{0,16},{4,20},{8,24},{12,28},{16,0},{20,4},{24,8},{28,12},{1,17},{... | collective-permute-start | bytes 196616 | tf_op jit(solution)/shard_map/ppermute | solution.py:346
  24.1 3.3 %collective-permute-start.11 = (bf16[8,4096]{1,0:T(8,128)(2,1)S(1)}, bf16[8,4096]{1,0:T(8,128)(2,1)S(1)}, u32[]{:S(2)}, u32[]{:S(2)}) collective-permute-start(bf16[8,4096]{1,0:T(8,128)(2,1)S(1)} %relay.4.refs_4_), channel_id=1, source_target_pairs={{0,4},{4,0},{8,12},{12,8},{16,20},{20,16},{24,28},{28,24},{1,5},{5... | collective-permute-start | bytes 196616 | tf_op jit(solution)/shard_map/ppermute | solution.py:346
  26.8 1.6 %collective-permute-start.10 = (bf16[8,4096]{1,0:T(8,128)(2,1)S(1)}, bf16[8,4096]{1,0:T(8,128)(2,1)S(1)}, u32[]{:S(2)}, u32[]{:S(2)}) collective-permute-start(bf16[8,4096]{1,0:T(8,128)(2,1)S(1)} %relay.5.refs_4_), channel_id=1, source_target_pairs={{0,4},{4,0},{8,12},{12,8},{16,20},{20,16},{24,28},{28,24},{1,5},{5... | collective-permute-start | bytes 196616 | tf_op jit(solution)/shard_map/ppermute | solution.py:346
  26.9 1.6 %collective-permute-start.7 = (bf16[8,4096]{1,0:T(8,128)(2,1)S(1)}, bf16[8,4096]{1,0:T(8,128)(2,1)S(1)}, u32[]{:S(2)}, u32[]{:S(2)}) collective-permute-start(bf16[8,4096]{1,0:T(8,128)(2,1)S(1)} %relay.3.refs_5_), channel_id=1, source_target_pairs={{0,4},{4,0},{8,12},{12,8},{16,20},{20,16},{24,28},{28,24},{1,5},{5... | collective-permute-start | bytes 196616 | tf_op jit(solution)/shard_map/ppermute | solution.py:346
  29.6 5.8 %collective-permute-start.14 = (bf16[8,1920]{1,0:T(8,128)(2,1)S(1)}, bf16[8,1920]{1,0:T(8,128)(2,1)S(1)}, u32[]{:S(2)}, u32[]{:S(2)}) collective-permute-start(bf16[8,1920]{1,0:T(8,128)(2,1)S(1)} %get-tuple-element.66.flat_ref.rest_0_), channel_id=1, source_target_pairs={{0,3},{1,2},{2,1},{3,0},{4,7},{5,6},{6,5},{7,4},{8,11},{9,10},{10,... | collective-permute-start | bytes 92168 | tf_op jit(solution)/shard_map/ppermute | solution.py:346
  33.3 4.8 %collective-permute-start.13 = (bf16[8,1920]{1,0:T(8,128)(2,1)S(1)}, bf16[8,1920]{1,0:T(8,128)(2,1)S(1)}, u32[]{:S(2)}, u32[]{:S(2)}) collective-permute-start(bf16[8,1920]{1,0:T(8,128)(2,1)S(1)} %get-tuple-element.66.flat_ref.rest_0_), channel_id=1, source_target_pairs={{0,2},{1,3},{2,0},{3,1},{4,6},{5,7},{6,4},{7,5},{8,10},{9,11},{10,... | collective-permute-start | bytes 92168 | tf_op jit(solution)/shard_map/ppermute | solution.py:346
  33.3 4.8 %collective-permute-start.12 = (bf16[8,1920]{1,0:T(8,128)(2,1)S(1)}, bf16[8,1920]{1,0:T(8,128)(2,1)S(1)}, u32[]{:S(2)}, u32[]{:S(2)}) collective-permute-start(bf16[8,1920]{1,0:T(8,128)(2,1)S(1)} %get-tuple-element.66.flat_ref.rest_0_), channel_id=1, source_target_pairs={{0,1},{1,0},{2,3},{3,2},{4,5},{5,4},{6,7},{7,6},{8,9},{9,8},{10,11... | collective-permute-start | bytes 92168 | tf_op jit(solution)/shard_map/ppermute | solution.py:346
  38.3 1.9 %collective-permute-start.15 = (f32[8,128]{1,0:T(8,128)S(1)}, f32[8,128]{1,0:T(8,128)S(1)}, u32[]{:S(2)}, u32[]{:S(2)}) collective-permute-start(f32[8,128]{1,0:T(8,128)S(1)} %pair.1), channel_id=1, source_target_pairs={{0,4},{4,0},{8,12},{12,8},{16,20},{20,16},{24,28},{28,24},{1,5},{5... | collective-permute-start | bytes 12296 | tf_op jit(solution)/shard_map/ppermute | solution.py:346
  38.3 4.6 %collective-permute-start.16 = (f32[8,128]{1,0:T(8,128)S(1)}, f32[8,128]{1,0:T(8,128)S(1)}, u32[]{:S(2)}, u32[]{:S(2)}) collective-permute-start(f32[8,128]{1,0:T(8,128)S(1)} %pair.1), channel_id=1, source_target_pairs={{0,24},{4,28},{8,16},{12,20},{16,8},{20,12},{24,0},{28,4},{1,25},{... | collective-permute-start | bytes 12296 | tf_op jit(solution)/shard_map/ppermute | solution.py:346
  40.2 3.6 %collective-permute-start.17 = (f32[8,128]{1,0:T(8,128)S(1)}, f32[8,128]{1,0:T(8,128)S(1)}, u32[]{:S(2)}, u32[]{:S(2)}) collective-permute-start(f32[8,128]{1,0:T(8,128)S(1)} %add.3.own_ref), channel_id=1, source_target_pairs={{0,8},{4,20},{8,0},{12,28},{16,24},{20,4},{24,16},{28,12},{1,9},{5... | collective-permute-start | bytes 12296 | tf_op jit(solution)/shard_map/ppermute | solution.py:350
  42.9 1.2 %collective-permute-start.19 = (f32[8,128]{1,0:T(8,128)S(1)}, f32[8,128]{1,0:T(8,128)S(1)}, u32[]{:S(2)}, u32[]{:S(2)}) collective-permute-start(f32[8,128]{1,0:T(8,128)S(1)} %collective-permute-done.16.common_ref), channel_id=1, source_target_pairs={{0,4},{4,0},{8,12},{12,8},{16,20},{20,16},{24,28},{28,24},{1,5},{5... | collective-permute-start | bytes 12296 | tf_op jit(solution)/shard_map/ppermute | solution.py:346
  43.8 1.2 %collective-permute-start.18 = (f32[8,128]{1,0:T(8,128)S(1)}, f32[8,128]{1,0:T(8,128)S(1)}, u32[]{:S(2)}, u32[]{:S(2)}) collective-permute-start(f32[8,128]{1,0:T(8,128)S(1)} %collective-permute-done.17.rest_0_), channel_id=1, source_target_pairs={{0,4},{4,0},{8,12},{12,8},{16,20},{20,16},{24,28},{28,24},{1,5},{5... | collective-permute-start | bytes 12296 | tf_op jit(solution)/shard_map/ppermute | solution.py:346

commit v10 on v9

--- a/solution.py
+++ b/solution.py
@@ -304,10 +304,11 @@
     flat_ref[...] = fold_rows(jnp.concatenate(flat, axis=1), own_bins).astype(BF16)
 
 
-def pair_kernel(own_bins, width, stats_ref, *rest):
+def pair_kernel(own_bins, width, distances, stats_ref, *rest):
     flats, out_ref = rest[:-1], rest[-1]
     everyone = [unfold_rows(flat[...].astype(F32), own_bins, width) for flat in flats]
     own = everyone[0].astype(BF16)
+    everyone = [everyone[distances.index(d)] for d in range(len(distances))]
     everyone += [jnp.zeros_like(everyone[0])] * (LANES // SUBLANES - len(flats))
     out_ref[...] = stats_ref[...] + lax.dot_general(
         own,
@@ -513,7 +514,9 @@
     blocks = list(enumerate(away_order))[1:]
     flat, number = fields([kept_away], blocks, u_away[1:], terms, last=True)
 
-    flats = [flat] + [swap(flat, "bin", n_bin, d) for d in range(1, n_bin)]
+    middle = n_bin // 2
+    distances = [0] + [d for d in range(1, n_bin) if d != middle] + [middle]
+    flats = [flat] + [swap(flat, "bin", n_bin, d) for d in distances[1:]]
     order = (rows, (away_order, here_order, [1], [0]))
     stats, field = plain(
         functools.partial(stats_kernel, own_bins, order),
@@ -522,7 +525,7 @@
         "stats",
     )
     (part,) = plain(
-        functools.partial(pair_kernel, own_bins, PROBES * rows),
+        functools.partial(pair_kernel, own_bins, PROBES * rows, distances),
         (stats, *flats),
         [number_shape],
         "pair",

time: 45.9 us -> 45.8 us (level)
  transfers between devices with their start and end apart: 20 -> 20, of which waited for: 9 -> 8; matrix products, arithmetic and copies ran while one was open for 0% -> 0% of each run, Pallas kernels for 25% -> 25%
where the time goes in v10:
time: 45.8 us; the launch traced here: 45.5 us
  Pallas kernels  18.4 us (40%)
  starting transfers between devices  15.9 us (35%)
  waiting for transfers between devices  10.4 us (23%)
  between operations  0.83 us (2%)
    ppermute x19, starting transfers between devices, swap(): return lax.ppermute(value, axis, [(i, i ^ distance) for i in range(size)])  15.1 us
    pallas_call x4, Pallas kernels, moments(): pl.pallas_call(functools.partial(moments_kernel, snps, distances, opening...  12.1 us
    ppermute x19, waiting for transfers between devices, swap(): return lax.ppermute(value, axis, [(i, i ^ distance) for i in range(size)])  9.55 us
    pallas_call x12, Pallas kernels, plain(): pl.pallas_call(kernel, in_specs=[in_vmem()] * len(operands), out_specs=[i...  6.27 us
  transfers between devices with their start and end apart: 20, of which 8 were waited for; matrix products, arithmetic and copies ran while one was open for 0% of the time, Pallas kernels for 25%

profile of v10, /device:TPU:0, one launch (start us, length us, event | category | flops | bytes accessed | tf_op | source)
XLA Modules:
  0.0 45.5 jit_solution(8359461893271993999)
XLA Ops:
  0.6 4.9 %moments_away.1 = (bf16[3,256,3200]{2,1,0:T(8,128)(2,1)S(1)}, bf16[3,8,4992]{2,1,0:T(8,128)(2,1)S(1)}, f32[3,2,3200]{2,1,0:T(2,128)S(1)}, f32[16,256]{1,0:T(8,128)S(1)}, s32[256,3200]{1,0:T(8,128)S(1)}) custom-call(s32[256,25600]{1,0:T(8,128)} %geno_ref.7, s32[10,256]{1,0:T(8,128)} %rest_0_.1, bf16[256]{0:T(256)(128)(2,1)} %rest_1_.1), custom_call_target="tpu_custom_call" | custom-call | flops 1 | bytes 9830400 | tf_op jit(solution)/shard_map/moments_away/pallas_call | solution.py:423
  6.0 3.6 %moments_here.1 = (bf16[3,256,3200]{2,1,0:T(8,128)(2,1)S(1)}, bf16[3,8,4992]{2,1,0:T(8,128)(2,1)S(1)}, f32[3,2,3200]{2,1,0:T(2,128)S(1)}) custom-call(s32[256,25600]{1,0:T(8,128)} %geno_ref.7, s32[256,3200]{1,0:T(8,128)S(1)} %get-tuple-element.43.rest_0_, f32[16,256]{1,0:T(8,128)S(1)} %get-tuple-element.42.rest_1_.left_ref), custom_call_target="tpu_custom_call" | custom-call | flops 1 | bytes 9830400 | tf_op jit(solution)/shard_map/moments_here/pallas_call | solution.py:423
  9.7 3.5 %collective-permute-start.2 = (bf16[8,4992]{1,0:T(8,128)(2,1)S(1)}, bf16[8,4992]{1,0:T(8,128)(2,1)S(1)}, u32[]{:S(2)}, u32[]{:S(2)}) collective-permute-start(bf16[8,4992]{1,0:T(8,128)(2,1)S(1)} %get-tuple-element.52), channel_id=1, source_target_pairs={{0,24},{4,28},{8,16},{12,20},{16,8},{20,12},{24,0},{28,4},{1,25},{... | collective-permute-start | bytes 239624 | tf_op jit(solution)/shard_map/ppermute | solution.py:347
  13.9 2.9 %moments_near.1 = (bf16[1,256,3200]{2,1,0:T(8,128)(2,1)S(1)}, bf16[1,8,4992]{2,1,0:T(8,128)(2,1)S(1)}, f32[1,2,3200]{2,1,0:T(2,128)S(1)}, s32[256,3200]{1,0:T(8,128)S(1)}) custom-call(s32[256,25600]{1,0:T(8,128)} %geno_ref.7, f32[16,256]{1,0:T(8,128)S(1)} %get-tuple-element.46.rest_0_.rest_1_), custom_call_target="tpu_custom_call" | custom-call | flops 1 | bytes 1 | tf_op jit(solution)/shard_map/moments_near/pallas_call | solution.py:423
  17.0 0.7 %moments_own.1 = (bf16[1,256,3200]{2,1,0:T(8,128)(2,1)S(1)}, bf16[1,8,4992]{2,1,0:T(8,128)(2,1)S(1)}, f32[1,2,3200]{2,1,0:T(2,128)S(1)}) custom-call(s32[256,25600]{1,0:T(8,128)} %geno_ref.7, s32[256,3200]{1,0:T(8,128)S(1)} %get-tuple-element.47.rest_0_, f32[16,256]{1,0:T(8,128)S(1)} %get-tuple-element.46.rest_0_.rest_1_), custom_call_target="tpu_custom_call" | custom-call | flops 1 | bytes 1 | tf_op jit(solution)/shard_map/moments_own/pallas_call | solution.py:423
  17.7 0.6 %collective-permute-done.3.refs_1_ = bf16[8,4992]{1,0:T(8,128)(2,1)S(1)} collective-permute-done((bf16[8,4992]{1,0:T(8,128)(2,1)S(1)}, bf16[8,4992]{1,0:T(8,128)(2,1)S(1)}, u32[]{:S(2)}, u32[]{:S(2)}) %collective-permute-start.3) | collective-permute-done | bytes 79904 | tf_op jit(solution)/shard_map/ppermute | solution.py:347
  18.6 2.8 %collective-permute-start.8 = (bf16[8,4096]{1,0:T(8,128)(2,1)S(1)}, bf16[8,4096]{1,0:T(8,128)(2,1)S(1)}, u32[]{:S(2)}, u32[]{:S(2)}) collective-permute-start(bf16[8,4096]{1,0:T(8,128)(2,1)S(1)} %get-tuple-element.55.refs_4_), channel_id=1, source_target_pairs={{0,24},{4,28},{8,16},{12,20},{16,8},{20,12},{24,0},{28,4},{1,25},{... | collective-permute-start | bytes 196616 | tf_op jit(solution)/shard_map/ppermute | solution.py:347
  21.5 0.5 %collective-permute-start.6 = (bf16[8,4096]{1,0:T(8,128)(2,1)S(1)}, bf16[8,4096]{1,0:T(8,128)(2,1)S(1)}, u32[]{:S(2)}, u32[]{:S(2)}) collective-permute-start(bf16[8,4096]{1,0:T(8,128)(2,1)S(1)} %get-tuple-element.55.refs_4_), channel_id=1, source_target_pairs={{0,8},{4,12},{8,0},{12,4},{16,24},{20,28},{24,16},{28,20},{1,9},{5... | collective-permute-start | bytes 196616 | tf_op jit(solution)/shard_map/ppermute | solution.py:347
  22.1 1.1 %field.4 = (f32[256,80]{1,0:T(8,128)S(1)}, f32[80,128]{1,0:T(8,128)S(1)}, f32[8,128]{1,0:T(8,128)S(1)}) custom-call(f32[1,25600]{1,0:T(1,128)S(1)} %bitcast.7, s32[1,25600]{1,0:T(1,128)S(1)} %bitcast.12, bf16[1,256,3200]{2,1,0:T(8,128)(2,1)S(1)} %get-tuple-element.48.refs_2_, bf16[1,256,3200]{2,1,0:T(8,128)(2,1)S(1)} %get-tuple-element.49.refs_3_, ...), custom_call_target="tpu_custom_call" | custom-call | flops 1 | bytes 1 | tf_op jit(solution)/shard_map/field/pallas_call | solution.py:438
  23.2 0.9 %collective-permute-done.8.value_ref = bf16[8,4096]{1,0:T(8,128)(2,1)S(1)} collective-permute-done((bf16[8,4096]{1,0:T(8,128)(2,1)S(1)}, bf16[8,4096]{1,0:T(8,128)(2,1)S(1)}, u32[]{:S(2)}, u32[]{:S(2)}) %collective-permute-start.8) | collective-permute-done | bytes 65568 | tf_op jit(solution)/shard_map/ppermute | solution.py:347
  24.1 1.7 %collective-permute-done.6.value_ref = bf16[8,4096]{1,0:T(8,128)(2,1)S(1)} collective-permute-done((bf16[8,4096]{1,0:T(8,128)(2,1)S(1)}, bf16[8,4096]{1,0:T(8,128)(2,1)S(1)}, u32[]{:S(2)}, u32[]{:S(2)}) %collective-permute-start.6) | collective-permute-done | bytes 65568 | tf_op jit(solution)/shard_map/ppermute | solution.py:347
  25.7 1.0 %field.5 = (f32[256,80]{1,0:T(8,128)S(1)}, f32[80,128]{1,0:T(8,128)S(1)}, f32[8,128]{1,0:T(8,128)S(1)}) custom-call(f32[1,25600]{1,0:T(1,128)S(1)} %bitcast.8, s32[1,25600]{1,0:T(1,128)S(1)} %bitcast.13, bf16[3,256,3200]{2,1,0:T(8,128)(2,1)S(1)} %get-tuple-element.57.refs_2_.refs_3_, bf16[3,256,3200]{2,1,0:T(8,128)(2,1)S(1)} %get-tuple-element.57.refs_2_.refs_3_, ...), custom_call_target="tpu_custom_call" | custom-call | flops 1 | bytes 1 | tf_op jit(solution)/shard_map/field/pallas_call | solution.py:438
  27.4 1.0 %field.6 = (f32[256,80]{1,0:T(8,128)S(1)}, f32[80,128]{1,0:T(8,128)S(1)}, f32[8,128]{1,0:T(8,128)S(1)}) custom-call(f32[1,25600]{1,0:T(1,128)S(1)} %bitcast.9, s32[1,25600]{1,0:T(1,128)S(1)} %bitcast.14, bf16[3,256,3200]{2,1,0:T(8,128)(2,1)S(1)} %get-tuple-element.57.refs_2_.refs_3_, bf16[3,256,3200]{2,1,0:T(8,128)(2,1)S(1)} %get-tuple-element.41.refs_3_.refs_2_, ...), custom_call_target="tpu_custom_call" | custom-call | flops 1 | bytes 1 | tf_op jit(solution)/shard_map/field/pallas_call | solution.py:438
  28.4 1.2 %field.7 = (bf16[8,1920]{1,0:T(8,128)(2,1)S(1)}, f32[8,128]{1,0:T(8,128)S(1)}) custom-call(f32[1,25600]{1,0:T(1,128)S(1)} %bitcast.10, s32[1,25600]{1,0:T(1,128)S(1)} %bitcast.15, bf16[3,256,3200]{2,1,0:T(8,128)(2,1)S(1)} %get-tuple-element.41.refs_3_.refs_2_, bf16[8,4096]{1,0:T(8,128)(2,1)S(1)} %collective-permute-done.7.refs_3_, ...), custom_call_target="tpu_custom_call" | custom-call | flops 1 | bytes 1 | tf_op jit(solution)/shard_map/field/pallas_call | solution.py:438
  29.6 2.7 %collective-permute-start.14 = (bf16[8,1920]{1,0:T(8,128)(2,1)S(1)}, bf16[8,1920]{1,0:T(8,128)(2,1)S(1)}, u32[]{:S(2)}, u32[]{:S(2)}) collective-permute-start(bf16[8,1920]{1,0:T(8,128)(2,1)S(1)} %get-tuple-element.66.flat_ref.rest_0_), channel_id=1, source_target_pairs={{0,2},{1,3},{2,0},{3,1},{4,6},{5,7},{6,4},{7,5},{8,10},{9,11},{10,... | collective-permute-start | bytes 92168 | tf_op jit(solution)/shard_map/ppermute | solution.py:347
  32.3 1.3 %collective-permute-start.13 = (bf16[8,1920]{1,0:T(8,128)(2,1)S(1)}, bf16[8,1920]{1,0:T(8,128)(2,1)S(1)}, u32[]{:S(2)}, u32[]{:S(2)}) collective-permute-start(bf16[8,1920]{1,0:T(8,128)(2,1)S(1)} %get-tuple-element.66.flat_ref.rest_0_), channel_id=1, source_target_pairs={{0,3},{1,2},{2,1},{3,0},{4,7},{5,6},{6,5},{7,4},{8,11},{9,10},{10,... | collective-permute-start | bytes 92168 | tf_op jit(solution)/shard_map/ppermute | solution.py:347
  33.9 0.8 %stats.1 = (f32[8,128]{1,0:T(8,128)S(1)}, bf16[10,6,256]{2,1,0:T(8,128)(2,1)}) custom-call(bf16[8,1920]{1,0:T(8,128)(2,1)S(1)} %get-tuple-element.66.flat_ref.rest_0_, f32[1,25600]{1,0:T(1,128)S(1)} %bitcast.11, f32[1,25600]{1,0:T(1,128)S(1)} %bitcast.18, s32[1,25600]{1,0:T(1,128)S(1)} %bitcast.16, f32[1,3200]{1,0:T(1,128)S(1)} %get-tuple-element.67.trait_ref, ...), custom_call_target="tpu_custom_call" | custom-call | tf_op jit(solution)/shard_map/stats/pallas_call | solution.py:438
  34.7 3.3 %collective-permute-done.13.rest_2_ = bf16[8,1920]{1,0:T(8,128)(2,1)S(1)} collective-permute-done((bf16[8,1920]{1,0:T(8,128)(2,1)S(1)}, bf16[8,1920]{1,0:T(8,128)(2,1)S(1)}, u32[]{:S(2)}, u32[]{:S(2)}) %collective-permute-start.13) | collective-permute-done | bytes 30752 | tf_op jit(solution)/shard_map/ppermute | solution.py:347
  38.2 1.8 %collective-permute-start.16 = (f32[8,128]{1,0:T(8,128)S(1)}, f32[8,128]{1,0:T(8,128)S(1)}, u32[]{:S(2)}, u32[]{:S(2)}) collective-permute-start(f32[8,128]{1,0:T(8,128)S(1)} %pair.1), channel_id=1, source_target_pairs={{0,24},{4,28},{8,16},{12,20},{16,8},{20,12},{24,0},{28,4},{1,25},{... | collective-permute-start | bytes 12296 | tf_op jit(solution)/shard_map/ppermute | solution.py:347
  40.1 0.8 %collective-permute-start.17 = (f32[8,128]{1,0:T(8,128)S(1)}, f32[8,128]{1,0:T(8,128)S(1)}, u32[]{:S(2)}, u32[]{:S(2)}) collective-permute-start(f32[8,128]{1,0:T(8,128)S(1)} %add.3.own_ref), channel_id=1, source_target_pairs={{0,8},{4,20},{8,0},{12,28},{16,24},{20,4},{24,16},{28,12},{1,9},{5... | collective-permute-start | bytes 12296 | tf_op jit(solution)/shard_map/ppermute | solution.py:351
  40.9 1.9 %collective-permute-done.16.common_ref = f32[8,128]{1,0:T(8,128)S(1)} collective-permute-done((f32[8,128]{1,0:T(8,128)S(1)}, f32[8,128]{1,0:T(8,128)S(1)}, u32[]{:S(2)}, u32[]{:S(2)}) %collective-permute-start.16) | collective-permute-done | bytes 4128 | tf_op jit(solution)/shard_map/ppermute | solution.py:347
  42.8 0.9 %collective-permute-done.17.rest_0_ = f32[8,128]{1,0:T(8,128)S(1)} collective-permute-done((f32[8,128]{1,0:T(8,128)S(1)}, f32[8,128]{1,0:T(8,128)S(1)}, u32[]{:S(2)}, u32[]{:S(2)}) %collective-permute-start.17) | collective-permute-done | bytes 4128 | tf_op jit(solution)/shard_map/ppermute | solution.py:351
  44.0 0.9 %collective-permute-done.18.rest_1_ = f32[8,128]{1,0:T(8,128)S(1)} collective-permute-done((f32[8,128]{1,0:T(8,128)S(1)}, f32[8,128]{1,0:T(8,128)S(1)}, u32[]{:S(2)}, u32[]{:S(2)}) %collective-permute-start.18) | collective-permute-done | bytes 4128 | tf_op jit(solution)/shard_map/ppermute | solution.py:347
  44.8 0.7 %final.1 = (f32[6,24]{1,0:T(8,128)}, f32[1,6]{1,0:T(1,128)}, f32[1,6]{1,0:T(1,128)}) custom-call(f32[8,128]{1,0:T(8,128)S(1)} %get-tuple-element.73.count_ref, f32[8,128]{1,0:T(8,128)S(1)} %add.3.own_ref, f32[8,128]{1,0:T(8,128)S(1)} %collective-permute-done.16.common_ref, f32[8,128]{1,0:T(8,128)S(1)} %collective-permute-done.17.rest_0_, ...), custom_call_target="tpu_custom_call" | custom-call | tf_op jit(solution)/shard_map/final/pallas_call | solution.py:438
  (39 shorter events, 3.1 us)
Async XLA Ops:
  5.5 4.1 %collective-permute-start = (bf16[3,8,4992]{2,1,0:T(8,128)(2,1)S(1)}, bf16[3,8,4992]{2,1,0:T(8,128)(2,1)S(1)}, u32[]{:S(2)}, u32[]{:S(2)}) collective-permute-start(bf16[3,8,4992]{2,1,0:T(8,128)(2,1)S(1)} %get-tuple-element.45), channel_id=1, source_target_pairs={{0,4},{4,0},{8,12},{12,8},{16,20},{20,16},{24,28},{28,24},{1,5},{5... | collective-permute-start | bytes 718856 | tf_op jit(solution)/shard_map/ppermute | solution.py:347
  9.7 7.9 %collective-permute-start.2 = (bf16[8,4992]{1,0:T(8,128)(2,1)S(1)}, bf16[8,4992]{1,0:T(8,128)(2,1)S(1)}, u32[]{:S(2)}, u32[]{:S(2)}) collective-permute-start(bf16[8,4992]{1,0:T(8,128)(2,1)S(1)} %get-tuple-element.52), channel_id=1, source_target_pairs={{0,24},{4,28},{8,16},{12,20},{16,8},{20,12},{24,0},{28,4},{1,25},{... | collective-permute-start | bytes 239624 | tf_op jit(solution)/shard_map/ppermute | solution.py:347
  13.3 5.0 %collective-permute-start.3 = (bf16[8,4992]{1,0:T(8,128)(2,1)S(1)}, bf16[8,4992]{1,0:T(8,128)(2,1)S(1)}, u32[]{:S(2)}, u32[]{:S(2)}) collective-permute-start(bf16[8,4992]{1,0:T(8,128)(2,1)S(1)} %get-tuple-element.53), channel_id=1, source_target_pairs={{0,8},{4,12},{8,0},{12,4},{16,24},{20,28},{24,16},{28,20},{1,9},{5... | collective-permute-start | bytes 239624 | tf_op jit(solution)/shard_map/ppermute | solution.py:347
  13.8 4.5 %collective-permute-start.4 = (bf16[8,4992]{1,0:T(8,128)(2,1)S(1)}, bf16[8,4992]{1,0:T(8,128)(2,1)S(1)}, u32[]{:S(2)}, u32[]{:S(2)}) collective-permute-start(bf16[8,4992]{1,0:T(8,128)(2,1)S(1)} %get-tuple-element.54), channel_id=1, source_target_pairs={{0,16},{4,20},{8,24},{12,28},{16,0},{20,4},{24,8},{28,12},{1,17},{... | collective-permute-start | bytes 239624 | tf_op jit(solution)/shard_map/ppermute | solution.py:347
  16.9 1.4 %collective-permute-start.1 = (bf16[1,8,4992]{2,1,0:T(8,128)(2,1)S(1)}, bf16[1,8,4992]{2,1,0:T(8,128)(2,1)S(1)}, u32[]{:S(2)}, u32[]{:S(2)}) collective-permute-start(bf16[1,8,4992]{2,1,0:T(8,128)(2,1)S(1)} %get-tuple-element.51), channel_id=1, source_target_pairs={{0,4},{4,0},{8,12},{12,8},{16,20},{20,16},{24,28},{28,24},{1,5},{5... | collective-permute-start | bytes 239624 | tf_op jit(solution)/shard_map/ppermute | solution.py:347
  17.0 1.3 %copy-start = (f32[25600]{0:T(1024)S(1)}, f32[25600]{0:T(1024)}, u32[]{:S(2)}) copy-start(f32[25600]{0:T(1024)} %param.7) | copy-start | bytes 307204
  17.0 1.3 %copy-start.2 = (f32[25600]{0:T(1024)S(1)}, f32[25600]{0:T(1024)}, u32[]{:S(2)}) copy-start(f32[25600]{0:T(1024)} %param.8) | copy-start | bytes 307204
  17.0 5.1 %copy-start.1 = (s32[25600]{0:T(1024)S(1)}, s32[25600]{0:T(1024)}, u32[]{:S(2)}) copy-start(s32[25600]{0:T(1024)} %param.9) | copy-start | bytes 307204
  18.5 3.6 %collective-permute-start.5 = (bf16[8,4096]{1,0:T(8,128)(2,1)S(1)}, bf16[8,4096]{1,0:T(8,128)(2,1)S(1)}, u32[]{:S(2)}, u32[]{:S(2)}) collective-permute-start(bf16[8,4096]{1,0:T(8,128)(2,1)S(1)} %get-tuple-element.55.refs_4_), channel_id=1, source_target_pairs={{0,4},{4,0},{8,12},{12,8},{16,20},{20,16},{24,28},{28,24},{1,5},{5... | collective-permute-start | bytes 196616 | tf_op jit(solution)/shard_map/ppermute | solution.py:347
  18.6 5.4 %collective-permute-start.8 = (bf16[8,4096]{1,0:T(8,128)(2,1)S(1)}, bf16[8,4096]{1,0:T(8,128)(2,1)S(1)}, u32[]{:S(2)}, u32[]{:S(2)}) collective-permute-start(bf16[8,4096]{1,0:T(8,128)(2,1)S(1)} %get-tuple-element.55.refs_4_), channel_id=1, source_target_pairs={{0,24},{4,28},{8,16},{12,20},{16,8},{20,12},{24,0},{28,4},{1,25},{... | collective-permute-start | bytes 196616 | tf_op jit(solution)/shard_map/ppermute | solution.py:347
  21.5 4.3 %collective-permute-start.6 = (bf16[8,4096]{1,0:T(8,128)(2,1)S(1)}, bf16[8,4096]{1,0:T(8,128)(2,1)S(1)}, u32[]{:S(2)}, u32[]{:S(2)}) collective-permute-start(bf16[8,4096]{1,0:T(8,128)(2,1)S(1)} %get-tuple-element.55.refs_4_), channel_id=1, source_target_pairs={{0,8},{4,12},{8,0},{12,4},{16,24},{20,28},{24,16},{28,20},{1,9},{5... | collective-permute-start | bytes 196616 | tf_op jit(solution)/shard_map/ppermute | solution.py:347
  22.0 4.8 %collective-permute-start.9 = (bf16[8,4096]{1,0:T(8,128)(2,1)S(1)}, bf16[8,4096]{1,0:T(8,128)(2,1)S(1)}, u32[]{:S(2)}, u32[]{:S(2)}) collective-permute-start(bf16[8,4096]{1,0:T(8,128)(2,1)S(1)} %get-tuple-element.55.refs_4_), channel_id=1, source_target_pairs={{0,16},{4,20},{8,24},{12,28},{16,0},{20,4},{24,8},{28,12},{1,17},{... | collective-permute-start | bytes 196616 | tf_op jit(solution)/shard_map/ppermute | solution.py:347
  24.1 3.3 %collective-permute-start.11 = (bf16[8,4096]{1,0:T(8,128)(2,1)S(1)}, bf16[8,4096]{1,0:T(8,128)(2,1)S(1)}, u32[]{:S(2)}, u32[]{:S(2)}) collective-permute-start(bf16[8,4096]{1,0:T(8,128)(2,1)S(1)} %relay.4.refs_4_), channel_id=1, source_target_pairs={{0,4},{4,0},{8,12},{12,8},{16,20},{20,16},{24,28},{28,24},{1,5},{5... | collective-permute-start | bytes 196616 | tf_op jit(solution)/shard_map/ppermute | solution.py:347
  26.8 1.6 %collective-permute-start.10 = (bf16[8,4096]{1,0:T(8,128)(2,1)S(1)}, bf16[8,4096]{1,0:T(8,128)(2,1)S(1)}, u32[]{:S(2)}, u32[]{:S(2)}) collective-permute-start(bf16[8,4096]{1,0:T(8,128)(2,1)S(1)} %relay.5.refs_4_), channel_id=1, source_target_pairs={{0,4},{4,0},{8,12},{12,8},{16,20},{20,16},{24,28},{28,24},{1,5},{5... | collective-permute-start | bytes 196616 | tf_op jit(solution)/shard_map/ppermute | solution.py:347
  26.9 1.6 %collective-permute-start.7 = (bf16[8,4096]{1,0:T(8,128)(2,1)S(1)}, bf16[8,4096]{1,0:T(8,128)(2,1)S(1)}, u32[]{:S(2)}, u32[]{:S(2)}) collective-permute-start(bf16[8,4096]{1,0:T(8,128)(2,1)S(1)} %relay.3.refs_5_), channel_id=1, source_target_pairs={{0,4},{4,0},{8,12},{12,8},{16,20},{20,16},{24,28},{28,24},{1,5},{5... | collective-permute-start | bytes 196616 | tf_op jit(solution)/shard_map/ppermute | solution.py:347
  29.6 5.1 %collective-permute-start.14 = (bf16[8,1920]{1,0:T(8,128)(2,1)S(1)}, bf16[8,1920]{1,0:T(8,128)(2,1)S(1)}, u32[]{:S(2)}, u32[]{:S(2)}) collective-permute-start(bf16[8,1920]{1,0:T(8,128)(2,1)S(1)} %get-tuple-element.66.flat_ref.rest_0_), channel_id=1, source_target_pairs={{0,2},{1,3},{2,0},{3,1},{4,6},{5,7},{6,4},{7,5},{8,10},{9,11},{10,... | collective-permute-start | bytes 92168 | tf_op jit(solution)/shard_map/ppermute | solution.py:347
  32.3 5.7 %collective-permute-start.13 = (bf16[8,1920]{1,0:T(8,128)(2,1)S(1)}, bf16[8,1920]{1,0:T(8,128)(2,1)S(1)}, u32[]{:S(2)}, u32[]{:S(2)}) collective-permute-start(bf16[8,1920]{1,0:T(8,128)(2,1)S(1)} %get-tuple-element.66.flat_ref.rest_0_), channel_id=1, source_target_pairs={{0,3},{1,2},{2,1},{3,0},{4,7},{5,6},{6,5},{7,4},{8,11},{9,10},{10,... | collective-permute-start | bytes 92168 | tf_op jit(solution)/shard_map/ppermute | solution.py:347
  33.7 4.3 %collective-permute-start.12 = (bf16[8,1920]{1,0:T(8,128)(2,1)S(1)}, bf16[8,1920]{1,0:T(8,128)(2,1)S(1)}, u32[]{:S(2)}, u32[]{:S(2)}) collective-permute-start(bf16[8,1920]{1,0:T(8,128)(2,1)S(1)} %get-tuple-element.66.flat_ref.rest_0_), channel_id=1, source_target_pairs={{0,1},{1,0},{2,3},{3,2},{4,5},{5,4},{6,7},{7,6},{8,9},{9,8},{10,11... | collective-permute-start | bytes 92168 | tf_op jit(solution)/shard_map/ppermute | solution.py:347
  38.2 1.9 %collective-permute-start.15 = (f32[8,128]{1,0:T(8,128)S(1)}, f32[8,128]{1,0:T(8,128)S(1)}, u32[]{:S(2)}, u32[]{:S(2)}) collective-permute-start(f32[8,128]{1,0:T(8,128)S(1)} %pair.1), channel_id=1, source_target_pairs={{0,4},{4,0},{8,12},{12,8},{16,20},{20,16},{24,28},{28,24},{1,5},{5... | collective-permute-start | bytes 12296 | tf_op jit(solution)/shard_map/ppermute | solution.py:347
  38.2 4.6 %collective-permute-start.16 = (f32[8,128]{1,0:T(8,128)S(1)}, f32[8,128]{1,0:T(8,128)S(1)}, u32[]{:S(2)}, u32[]{:S(2)}) collective-permute-start(f32[8,128]{1,0:T(8,128)S(1)} %pair.1), channel_id=1, source_target_pairs={{0,24},{4,28},{8,16},{12,20},{16,8},{20,12},{24,0},{28,4},{1,25},{... | collective-permute-start | bytes 12296 | tf_op jit(solution)/shard_map/ppermute | solution.py:347
  40.1 3.6 %collective-permute-start.17 = (f32[8,128]{1,0:T(8,128)S(1)}, f32[8,128]{1,0:T(8,128)S(1)}, u32[]{:S(2)}, u32[]{:S(2)}) collective-permute-start(f32[8,128]{1,0:T(8,128)S(1)} %add.3.own_ref), channel_id=1, source_target_pairs={{0,8},{4,20},{8,0},{12,28},{16,24},{20,4},{24,16},{28,12},{1,9},{5... | collective-permute-start | bytes 12296 | tf_op jit(solution)/shard_map/ppermute | solution.py:351
  42.8 1.2 %collective-permute-start.19 = (f32[8,128]{1,0:T(8,128)S(1)}, f32[8,128]{1,0:T(8,128)S(1)}, u32[]{:S(2)}, u32[]{:S(2)}) collective-permute-start(f32[8,128]{1,0:T(8,128)S(1)} %collective-permute-done.16.common_ref), channel_id=1, source_target_pairs={{0,4},{4,0},{8,12},{12,8},{16,20},{20,16},{24,28},{28,24},{1,5},{5... | collective-permute-start | bytes 12296 | tf_op jit(solution)/shard_map/ppermute | solution.py:347
  43.7 1.2 %collective-permute-start.18 = (f32[8,128]{1,0:T(8,128)S(1)}, f32[8,128]{1,0:T(8,128)S(1)}, u32[]{:S(2)}, u32[]{:S(2)}) collective-permute-start(f32[8,128]{1,0:T(8,128)S(1)} %collective-permute-done.17.rest_0_), channel_id=1, source_target_pairs={{0,4},{4,0},{8,12},{12,8},{16,20},{20,16},{24,28},{28,24},{1,5},{5... | collective-permute-start | bytes 12296 | tf_op jit(solution)/shard_map/ppermute | solution.py:347

commit v11 on v10

--- a/solution.py
+++ b/solution.py
@@ -161,13 +161,11 @@
         squares = []
         for at in range(0, block, PIECE):
             lanes = slice(at, min(at + PIECE, block))
-            square = 0.0
             for r in range(0, rows, 16):
-                dose = source[r : r + 16, lanes].astype(F32)
-                kept_ref[slot, r : r + 16, lanes] = dose.astype(BF16)
-                dose = dose * dose
-                square = square + (dose[:8] + dose[8:])
-            squares.append(jnp.sum(square, axis=0, keepdims=True))
+                dose = source[r : r + 16, lanes].astype(F32).astype(BF16)
+                kept_ref[slot, r : r + 16, lanes] = dose
+                square = dose * dose if r == 0 else square + dose * dose
+            squares.append(jnp.sum(square.astype(F32), axis=0, keepdims=True))
         total = jnp.dot(left, kept_ref[slot], preferred_element_type=F32) - base
         ones = total[ONES : ONES + 1]
         local_ref[slot, 0:1] = ones

time: 45.8 us -> 45.7 us (level)
  transfers between devices with their start and end apart: 20 -> 20, of which waited for: 8 -> 9; matrix products, arithmetic and copies ran while one was open for 0% -> 0% of each run, Pallas kernels for 25% -> 24%
where the time goes in v11:
time: 45.7 us; the launch traced here: 45.4 us
  Pallas kernels  18.2 us (40%)
  starting transfers between devices  15.9 us (35%)
  waiting for transfers between devices  10.5 us (23%)
  between operations  0.83 us (2%)
    ppermute x19, starting transfers between devices, swap(): return lax.ppermute(value, axis, [(i, i ^ distance) for i in range(size)])  15.1 us
    pallas_call x4, Pallas kernels, moments(): pl.pallas_call(functools.partial(moments_kernel, snps, distances, opening...  12 us
    ppermute x19, waiting for transfers between devices, swap(): return lax.ppermute(value, axis, [(i, i ^ distance) for i in range(size)])  9.62 us
    pallas_call x12, Pallas kernels, plain(): pl.pallas_call(kernel, in_specs=[in_vmem()] * len(operands), out_specs=[i...  6.28 us
  transfers between devices with their start and end apart: 20, of which 9 were waited for; matrix products, arithmetic and copies ran while one was open for 0% of the time, Pallas kernels for 24%

profile of v11, /device:TPU:0, one launch (start us, length us, event | category | flops | bytes accessed | tf_op | source)
XLA Modules:
  0.0 45.4 jit_solution(8548673647654205530)
XLA Ops:
  0.6 4.9 %moments_away.1 = (bf16[3,256,3200]{2,1,0:T(8,128)(2,1)S(1)}, bf16[3,8,4992]{2,1,0:T(8,128)(2,1)S(1)}, f32[3,2,3200]{2,1,0:T(2,128)S(1)}, f32[16,256]{1,0:T(8,128)S(1)}, s32[256,3200]{1,0:T(8,128)S(1)}) custom-call(s32[256,25600]{1,0:T(8,128)} %geno_ref.7, s32[10,256]{1,0:T(8,128)} %rest_0_.1, bf16[256]{0:T(256)(128)(2,1)} %rest_1_.1), custom_call_target="tpu_custom_call" | custom-call | flops 1 | bytes 9830400 | tf_op jit(solution)/shard_map/moments_away/pallas_call | solution.py:421
  6.0 3.5 %moments_here.1 = (bf16[3,256,3200]{2,1,0:T(8,128)(2,1)S(1)}, bf16[3,8,4992]{2,1,0:T(8,128)(2,1)S(1)}, f32[3,2,3200]{2,1,0:T(2,128)S(1)}) custom-call(s32[256,25600]{1,0:T(8,128)} %geno_ref.7, s32[256,3200]{1,0:T(8,128)S(1)} %get-tuple-element.43.rest_0_, f32[16,256]{1,0:T(8,128)S(1)} %get-tuple-element.42.rest_1_.left_ref), custom_call_target="tpu_custom_call" | custom-call | flops 1 | bytes 9830400 | tf_op jit(solution)/shard_map/moments_here/pallas_call | solution.py:421
  9.7 3.5 %collective-permute-start.2 = (bf16[8,4992]{1,0:T(8,128)(2,1)S(1)}, bf16[8,4992]{1,0:T(8,128)(2,1)S(1)}, u32[]{:S(2)}, u32[]{:S(2)}) collective-permute-start(bf16[8,4992]{1,0:T(8,128)(2,1)S(1)} %get-tuple-element.52), channel_id=1, source_target_pairs={{0,24},{4,28},{8,16},{12,20},{16,8},{20,12},{24,0},{28,4},{1,25},{... | collective-permute-start | bytes 239624 | tf_op jit(solution)/shard_map/ppermute | solution.py:345
  13.8 2.9 %moments_near.1 = (bf16[1,256,3200]{2,1,0:T(8,128)(2,1)S(1)}, bf16[1,8,4992]{2,1,0:T(8,128)(2,1)S(1)}, f32[1,2,3200]{2,1,0:T(2,128)S(1)}, s32[256,3200]{1,0:T(8,128)S(1)}) custom-call(s32[256,25600]{1,0:T(8,128)} %geno_ref.7, f32[16,256]{1,0:T(8,128)S(1)} %get-tuple-element.46.rest_0_.rest_1_), custom_call_target="tpu_custom_call" | custom-call | flops 1 | bytes 1 | tf_op jit(solution)/shard_map/moments_near/pallas_call | solution.py:421
  16.9 0.6 %moments_own.1 = (bf16[1,256,3200]{2,1,0:T(8,128)(2,1)S(1)}, bf16[1,8,4992]{2,1,0:T(8,128)(2,1)S(1)}, f32[1,2,3200]{2,1,0:T(2,128)S(1)}) custom-call(s32[256,25600]{1,0:T(8,128)} %geno_ref.7, s32[256,3200]{1,0:T(8,128)S(1)} %get-tuple-element.47.rest_0_, f32[16,256]{1,0:T(8,128)S(1)} %get-tuple-element.46.rest_0_.rest_1_), custom_call_target="tpu_custom_call" | custom-call | flops 1 | bytes 1 | tf_op jit(solution)/shard_map/moments_own/pallas_call | solution.py:421
  17.5 0.7 %collective-permute-done.3.refs_1_ = bf16[8,4992]{1,0:T(8,128)(2,1)S(1)} collective-permute-done((bf16[8,4992]{1,0:T(8,128)(2,1)S(1)}, bf16[8,4992]{1,0:T(8,128)(2,1)S(1)}, u32[]{:S(2)}, u32[]{:S(2)}) %collective-permute-start.3) | collective-permute-done | bytes 79904 | tf_op jit(solution)/shard_map/ppermute | solution.py:345
  18.5 2.8 %collective-permute-start.8 = (bf16[8,4096]{1,0:T(8,128)(2,1)S(1)}, bf16[8,4096]{1,0:T(8,128)(2,1)S(1)}, u32[]{:S(2)}, u32[]{:S(2)}) collective-permute-start(bf16[8,4096]{1,0:T(8,128)(2,1)S(1)} %get-tuple-element.55.refs_4_), channel_id=1, source_target_pairs={{0,24},{4,28},{8,16},{12,20},{16,8},{20,12},{24,0},{28,4},{1,25},{... | collective-permute-start | bytes 196616 | tf_op jit(solution)/shard_map/ppermute | solution.py:345
  21.4 0.5 %collective-permute-start.6 = (bf16[8,4096]{1,0:T(8,128)(2,1)S(1)}, bf16[8,4096]{1,0:T(8,128)(2,1)S(1)}, u32[]{:S(2)}, u32[]{:S(2)}) collective-permute-start(bf16[8,4096]{1,0:T(8,128)(2,1)S(1)} %get-tuple-element.55.refs_4_), channel_id=1, source_target_pairs={{0,8},{4,12},{8,0},{12,4},{16,24},{20,28},{24,16},{28,20},{1,9},{5... | collective-permute-start | bytes 196616 | tf_op jit(solution)/shard_map/ppermute | solution.py:345
  22.0 1.1 %field.4 = (f32[256,80]{1,0:T(8,128)S(1)}, f32[80,128]{1,0:T(8,128)S(1)}, f32[8,128]{1,0:T(8,128)S(1)}) custom-call(f32[1,25600]{1,0:T(1,128)S(1)} %bitcast.7, s32[1,25600]{1,0:T(1,128)S(1)} %bitcast.12, bf16[1,256,3200]{2,1,0:T(8,128)(2,1)S(1)} %get-tuple-element.48.refs_2_, bf16[1,256,3200]{2,1,0:T(8,128)(2,1)S(1)} %get-tuple-element.49.refs_3_, ...), custom_call_target="tpu_custom_call" | custom-call | flops 1 | bytes 1 | tf_op jit(solution)/shard_map/field/pallas_call | solution.py:436
  23.1 0.9 %collective-permute-done.8.value_ref = bf16[8,4096]{1,0:T(8,128)(2,1)S(1)} collective-permute-done((bf16[8,4096]{1,0:T(8,128)(2,1)S(1)}, bf16[8,4096]{1,0:T(8,128)(2,1)S(1)}, u32[]{:S(2)}, u32[]{:S(2)}) %collective-permute-start.8) | collective-permute-done | bytes 65568 | tf_op jit(solution)/shard_map/ppermute | solution.py:345
  24.0 1.7 %collective-permute-done.6.value_ref = bf16[8,4096]{1,0:T(8,128)(2,1)S(1)} collective-permute-done((bf16[8,4096]{1,0:T(8,128)(2,1)S(1)}, bf16[8,4096]{1,0:T(8,128)(2,1)S(1)}, u32[]{:S(2)}, u32[]{:S(2)}) %collective-permute-start.6) | collective-permute-done | bytes 65568 | tf_op jit(solution)/shard_map/ppermute | solution.py:345
  25.7 1.0 %field.5 = (f32[256,80]{1,0:T(8,128)S(1)}, f32[80,128]{1,0:T(8,128)S(1)}, f32[8,128]{1,0:T(8,128)S(1)}) custom-call(f32[1,25600]{1,0:T(1,128)S(1)} %bitcast.8, s32[1,25600]{1,0:T(1,128)S(1)} %bitcast.13, bf16[3,256,3200]{2,1,0:T(8,128)(2,1)S(1)} %get-tuple-element.57.refs_2_.refs_3_, bf16[3,256,3200]{2,1,0:T(8,128)(2,1)S(1)} %get-tuple-element.57.refs_2_.refs_3_, ...), custom_call_target="tpu_custom_call" | custom-call | flops 1 | bytes 1 | tf_op jit(solution)/shard_map/field/pallas_call | solution.py:436
  27.3 1.0 %field.6 = (f32[256,80]{1,0:T(8,128)S(1)}, f32[80,128]{1,0:T(8,128)S(1)}, f32[8,128]{1,0:T(8,128)S(1)}) custom-call(f32[1,25600]{1,0:T(1,128)S(1)} %bitcast.9, s32[1,25600]{1,0:T(1,128)S(1)} %bitcast.14, bf16[3,256,3200]{2,1,0:T(8,128)(2,1)S(1)} %get-tuple-element.57.refs_2_.refs_3_, bf16[3,256,3200]{2,1,0:T(8,128)(2,1)S(1)} %get-tuple-element.41.refs_3_.refs_2_, ...), custom_call_target="tpu_custom_call" | custom-call | flops 1 | bytes 1 | tf_op jit(solution)/shard_map/field/pallas_call | solution.py:436
  28.4 1.2 %field.7 = (bf16[8,1920]{1,0:T(8,128)(2,1)S(1)}, f32[8,128]{1,0:T(8,128)S(1)}) custom-call(f32[1,25600]{1,0:T(1,128)S(1)} %bitcast.10, s32[1,25600]{1,0:T(1,128)S(1)} %bitcast.15, bf16[3,256,3200]{2,1,0:T(8,128)(2,1)S(1)} %get-tuple-element.41.refs_3_.refs_2_, bf16[8,4096]{1,0:T(8,128)(2,1)S(1)} %collective-permute-done.7.refs_3_, ...), custom_call_target="tpu_custom_call" | custom-call | flops 1 | bytes 1 | tf_op jit(solution)/shard_map/field/pallas_call | solution.py:436
  29.6 2.7 %collective-permute-start.14 = (bf16[8,1920]{1,0:T(8,128)(2,1)S(1)}, bf16[8,1920]{1,0:T(8,128)(2,1)S(1)}, u32[]{:S(2)}, u32[]{:S(2)}) collective-permute-start(bf16[8,1920]{1,0:T(8,128)(2,1)S(1)} %get-tuple-element.66.flat_ref.rest_0_), channel_id=1, source_target_pairs={{0,2},{1,3},{2,0},{3,1},{4,6},{5,7},{6,4},{7,5},{8,10},{9,11},{10,... | collective-permute-start | bytes 92168 | tf_op jit(solution)/shard_map/ppermute | solution.py:345
  32.2 1.3 %collective-permute-start.13 = (bf16[8,1920]{1,0:T(8,128)(2,1)S(1)}, bf16[8,1920]{1,0:T(8,128)(2,1)S(1)}, u32[]{:S(2)}, u32[]{:S(2)}) collective-permute-start(bf16[8,1920]{1,0:T(8,128)(2,1)S(1)} %get-tuple-element.66.flat_ref.rest_0_), channel_id=1, source_target_pairs={{0,3},{1,2},{2,1},{3,0},{4,7},{5,6},{6,5},{7,4},{8,11},{9,10},{10,... | collective-permute-start | bytes 92168 | tf_op jit(solution)/shard_map/ppermute | solution.py:345
  33.8 0.8 %stats.1 = (f32[8,128]{1,0:T(8,128)S(1)}, bf16[10,6,256]{2,1,0:T(8,128)(2,1)}) custom-call(bf16[8,1920]{1,0:T(8,128)(2,1)S(1)} %get-tuple-element.66.flat_ref.rest_0_, f32[1,25600]{1,0:T(1,128)S(1)} %bitcast.11, f32[1,25600]{1,0:T(1,128)S(1)} %bitcast.18, s32[1,25600]{1,0:T(1,128)S(1)} %bitcast.16, f32[1,3200]{1,0:T(1,128)S(1)} %get-tuple-element.67.trait_ref, ...), custom_call_target="tpu_custom_call" | custom-call | tf_op jit(solution)/shard_map/stats/pallas_call | solution.py:436
  34.8 3.2 %collective-permute-done.13.rest_2_ = bf16[8,1920]{1,0:T(8,128)(2,1)S(1)} collective-permute-done((bf16[8,1920]{1,0:T(8,128)(2,1)S(1)}, bf16[8,1920]{1,0:T(8,128)(2,1)S(1)}, u32[]{:S(2)}, u32[]{:S(2)}) %collective-permute-start.13) | collective-permute-done | bytes 30752 | tf_op jit(solution)/shard_map/ppermute | solution.py:345
  38.2 1.8 %collective-permute-start.16 = (f32[8,128]{1,0:T(8,128)S(1)}, f32[8,128]{1,0:T(8,128)S(1)}, u32[]{:S(2)}, u32[]{:S(2)}) collective-permute-start(f32[8,128]{1,0:T(8,128)S(1)} %pair.1), channel_id=1, source_target_pairs={{0,24},{4,28},{8,16},{12,20},{16,8},{20,12},{24,0},{28,4},{1,25},{... | collective-permute-start | bytes 12296 | tf_op jit(solution)/shard_map/ppermute | solution.py:345
  40.0 0.8 %collective-permute-start.17 = (f32[8,128]{1,0:T(8,128)S(1)}, f32[8,128]{1,0:T(8,128)S(1)}, u32[]{:S(2)}, u32[]{:S(2)}) collective-permute-start(f32[8,128]{1,0:T(8,128)S(1)} %add.3.own_ref), channel_id=1, source_target_pairs={{0,8},{4,20},{8,0},{12,28},{16,24},{20,4},{24,16},{28,12},{1,9},{5... | collective-permute-start | bytes 12296 | tf_op jit(solution)/shard_map/ppermute | solution.py:349
  40.8 1.9 %collective-permute-done.16.common_ref = f32[8,128]{1,0:T(8,128)S(1)} collective-permute-done((f32[8,128]{1,0:T(8,128)S(1)}, f32[8,128]{1,0:T(8,128)S(1)}, u32[]{:S(2)}, u32[]{:S(2)}) %collective-permute-start.16) | collective-permute-done | bytes 4128 | tf_op jit(solution)/shard_map/ppermute | solution.py:345
  42.7 0.8 %collective-permute-done.17.rest_0_ = f32[8,128]{1,0:T(8,128)S(1)} collective-permute-done((f32[8,128]{1,0:T(8,128)S(1)}, f32[8,128]{1,0:T(8,128)S(1)}, u32[]{:S(2)}, u32[]{:S(2)}) %collective-permute-start.17) | collective-permute-done | bytes 4128 | tf_op jit(solution)/shard_map/ppermute | solution.py:349
  43.9 0.8 %collective-permute-done.18.rest_1_ = f32[8,128]{1,0:T(8,128)S(1)} collective-permute-done((f32[8,128]{1,0:T(8,128)S(1)}, f32[8,128]{1,0:T(8,128)S(1)}, u32[]{:S(2)}, u32[]{:S(2)}) %collective-permute-start.18) | collective-permute-done | bytes 4128 | tf_op jit(solution)/shard_map/ppermute | solution.py:345
  44.7 0.7 %final.1 = (f32[6,24]{1,0:T(8,128)}, f32[1,6]{1,0:T(1,128)}, f32[1,6]{1,0:T(1,128)}) custom-call(f32[8,128]{1,0:T(8,128)S(1)} %get-tuple-element.73.count_ref, f32[8,128]{1,0:T(8,128)S(1)} %add.3.own_ref, f32[8,128]{1,0:T(8,128)S(1)} %collective-permute-done.16.common_ref, f32[8,128]{1,0:T(8,128)S(1)} %collective-permute-done.17.rest_0_, ...), custom_call_target="tpu_custom_call" | custom-call | tf_op jit(solution)/shard_map/final/pallas_call | solution.py:436
  (39 shorter events, 3.2 us)
Async XLA Ops:
  5.5 4.1 %collective-permute-start = (bf16[3,8,4992]{2,1,0:T(8,128)(2,1)S(1)}, bf16[3,8,4992]{2,1,0:T(8,128)(2,1)S(1)}, u32[]{:S(2)}, u32[]{:S(2)}) collective-permute-start(bf16[3,8,4992]{2,1,0:T(8,128)(2,1)S(1)} %get-tuple-element.45), channel_id=1, source_target_pairs={{0,4},{4,0},{8,12},{12,8},{16,20},{20,16},{24,28},{28,24},{1,5},{5... | collective-permute-start | bytes 718856 | tf_op jit(solution)/shard_map/ppermute | solution.py:345
  9.7 7.9 %collective-permute-start.2 = (bf16[8,4992]{1,0:T(8,128)(2,1)S(1)}, bf16[8,4992]{1,0:T(8,128)(2,1)S(1)}, u32[]{:S(2)}, u32[]{:S(2)}) collective-permute-start(bf16[8,4992]{1,0:T(8,128)(2,1)S(1)} %get-tuple-element.52), channel_id=1, source_target_pairs={{0,24},{4,28},{8,16},{12,20},{16,8},{20,12},{24,0},{28,4},{1,25},{... | collective-permute-start | bytes 239624 | tf_op jit(solution)/shard_map/ppermute | solution.py:345
  13.2 5.0 %collective-permute-start.3 = (bf16[8,4992]{1,0:T(8,128)(2,1)S(1)}, bf16[8,4992]{1,0:T(8,128)(2,1)S(1)}, u32[]{:S(2)}, u32[]{:S(2)}) collective-permute-start(bf16[8,4992]{1,0:T(8,128)(2,1)S(1)} %get-tuple-element.53), channel_id=1, source_target_pairs={{0,8},{4,12},{8,0},{12,4},{16,24},{20,28},{24,16},{28,20},{1,9},{5... | collective-permute-start | bytes 239624 | tf_op jit(solution)/shard_map/ppermute | solution.py:345
  13.7 4.5 %collective-permute-start.4 = (bf16[8,4992]{1,0:T(8,128)(2,1)S(1)}, bf16[8,4992]{1,0:T(8,128)(2,1)S(1)}, u32[]{:S(2)}, u32[]{:S(2)}) collective-permute-start(bf16[8,4992]{1,0:T(8,128)(2,1)S(1)} %get-tuple-element.54), channel_id=1, source_target_pairs={{0,16},{4,20},{8,24},{12,28},{16,0},{20,4},{24,8},{28,12},{1,17},{... | collective-permute-start | bytes 239624 | tf_op jit(solution)/shard_map/ppermute | solution.py:345
  16.8 1.4 %collective-permute-start.1 = (bf16[1,8,4992]{2,1,0:T(8,128)(2,1)S(1)}, bf16[1,8,4992]{2,1,0:T(8,128)(2,1)S(1)}, u32[]{:S(2)}, u32[]{:S(2)}) collective-permute-start(bf16[1,8,4992]{2,1,0:T(8,128)(2,1)S(1)} %get-tuple-element.51), channel_id=1, source_target_pairs={{0,4},{4,0},{8,12},{12,8},{16,20},{20,16},{24,28},{28,24},{1,5},{5... | collective-permute-start | bytes 239624 | tf_op jit(solution)/shard_map/ppermute | solution.py:345
  16.9 1.3 %copy-start = (f32[25600]{0:T(1024)S(1)}, f32[25600]{0:T(1024)}, u32[]{:S(2)}) copy-start(f32[25600]{0:T(1024)} %param.7) | copy-start | bytes 307204
  16.9 1.3 %copy-start.2 = (f32[25600]{0:T(1024)S(1)}, f32[25600]{0:T(1024)}, u32[]{:S(2)}) copy-start(f32[25600]{0:T(1024)} %param.8) | copy-start | bytes 307204
  16.9 5.1 %copy-start.1 = (s32[25600]{0:T(1024)S(1)}, s32[25600]{0:T(1024)}, u32[]{:S(2)}) copy-start(s32[25600]{0:T(1024)} %param.9) | copy-start | bytes 307204
  18.4 3.6 %collective-permute-start.5 = (bf16[8,4096]{1,0:T(8,128)(2,1)S(1)}, bf16[8,4096]{1,0:T(8,128)(2,1)S(1)}, u32[]{:S(2)}, u32[]{:S(2)}) collective-permute-start(bf16[8,4096]{1,0:T(8,128)(2,1)S(1)} %get-tuple-element.55.refs_4_), channel_id=1, source_target_pairs={{0,4},{4,0},{8,12},{12,8},{16,20},{20,16},{24,28},{28,24},{1,5},{5... | collective-permute-start | bytes 196616 | tf_op jit(solution)/shard_map/ppermute | solution.py:345
  18.5 5.4 %collective-permute-start.8 = (bf16[8,4096]{1,0:T(8,128)(2,1)S(1)}, bf16[8,4096]{1,0:T(8,128)(2,1)S(1)}, u32[]{:S(2)}, u32[]{:S(2)}) collective-permute-start(bf16[8,4096]{1,0:T(8,128)(2,1)S(1)} %get-tuple-element.55.refs_4_), channel_id=1, source_target_pairs={{0,24},{4,28},{8,16},{12,20},{16,8},{20,12},{24,0},{28,4},{1,25},{... | collective-permute-start | bytes 196616 | tf_op jit(solution)/shard_map/ppermute | solution.py:345
  21.4 4.3 %collective-permute-start.6 = (bf16[8,4096]{1,0:T(8,128)(2,1)S(1)}, bf16[8,4096]{1,0:T(8,128)(2,1)S(1)}, u32[]{:S(2)}, u32[]{:S(2)}) collective-permute-start(bf16[8,4096]{1,0:T(8,128)(2,1)S(1)} %get-tuple-element.55.refs_4_), channel_id=1, source_target_pairs={{0,8},{4,12},{8,0},{12,4},{16,24},{20,28},{24,16},{28,20},{1,9},{5... | collective-permute-start | bytes 196616 | tf_op jit(solution)/shard_map/ppermute | solution.py:345
  21.9 4.8 %collective-permute-start.9 = (bf16[8,4096]{1,0:T(8,128)(2,1)S(1)}, bf16[8,4096]{1,0:T(8,128)(2,1)S(1)}, u32[]{:S(2)}, u32[]{:S(2)}) collective-permute-start(bf16[8,4096]{1,0:T(8,128)(2,1)S(1)} %get-tuple-element.55.refs_4_), channel_id=1, source_target_pairs={{0,16},{4,20},{8,24},{12,28},{16,0},{20,4},{24,8},{28,12},{1,17},{... | collective-permute-start | bytes 196616 | tf_op jit(solution)/shard_map/ppermute | solution.py:345
  24.0 3.3 %collective-permute-start.11 = (bf16[8,4096]{1,0:T(8,128)(2,1)S(1)}, bf16[8,4096]{1,0:T(8,128)(2,1)S(1)}, u32[]{:S(2)}, u32[]{:S(2)}) collective-permute-start(bf16[8,4096]{1,0:T(8,128)(2,1)S(1)} %relay.4.refs_4_), channel_id=1, source_target_pairs={{0,4},{4,0},{8,12},{12,8},{16,20},{20,16},{24,28},{28,24},{1,5},{5... | collective-permute-start | bytes 196616 | tf_op jit(solution)/shard_map/ppermute | solution.py:345
  26.7 1.6 %collective-permute-start.10 = (bf16[8,4096]{1,0:T(8,128)(2,1)S(1)}, bf16[8,4096]{1,0:T(8,128)(2,1)S(1)}, u32[]{:S(2)}, u32[]{:S(2)}) collective-permute-start(bf16[8,4096]{1,0:T(8,128)(2,1)S(1)} %relay.5.refs_4_), channel_id=1, source_target_pairs={{0,4},{4,0},{8,12},{12,8},{16,20},{20,16},{24,28},{28,24},{1,5},{5... | collective-permute-start | bytes 196616 | tf_op jit(solution)/shard_map/ppermute | solution.py:345
  26.8 1.6 %collective-permute-start.7 = (bf16[8,4096]{1,0:T(8,128)(2,1)S(1)}, bf16[8,4096]{1,0:T(8,128)(2,1)S(1)}, u32[]{:S(2)}, u32[]{:S(2)}) collective-permute-start(bf16[8,4096]{1,0:T(8,128)(2,1)S(1)} %relay.3.refs_5_), channel_id=1, source_target_pairs={{0,4},{4,0},{8,12},{12,8},{16,20},{20,16},{24,28},{28,24},{1,5},{5... | collective-permute-start | bytes 196616 | tf_op jit(solution)/shard_map/ppermute | solution.py:345
  29.6 5.2 %collective-permute-start.14 = (bf16[8,1920]{1,0:T(8,128)(2,1)S(1)}, bf16[8,1920]{1,0:T(8,128)(2,1)S(1)}, u32[]{:S(2)}, u32[]{:S(2)}) collective-permute-start(bf16[8,1920]{1,0:T(8,128)(2,1)S(1)} %get-tuple-element.66.flat_ref.rest_0_), channel_id=1, source_target_pairs={{0,2},{1,3},{2,0},{3,1},{4,6},{5,7},{6,4},{7,5},{8,10},{9,11},{10,... | collective-permute-start | bytes 92168 | tf_op jit(solution)/shard_map/ppermute | solution.py:345
  32.2 5.7 %collective-permute-start.13 = (bf16[8,1920]{1,0:T(8,128)(2,1)S(1)}, bf16[8,1920]{1,0:T(8,128)(2,1)S(1)}, u32[]{:S(2)}, u32[]{:S(2)}) collective-permute-start(bf16[8,1920]{1,0:T(8,128)(2,1)S(1)} %get-tuple-element.66.flat_ref.rest_0_), channel_id=1, source_target_pairs={{0,3},{1,2},{2,1},{3,0},{4,7},{5,6},{6,5},{7,4},{8,11},{9,10},{10,... | collective-permute-start | bytes 92168 | tf_op jit(solution)/shard_map/ppermute | solution.py:345
  33.6 4.3 %collective-permute-start.12 = (bf16[8,1920]{1,0:T(8,128)(2,1)S(1)}, bf16[8,1920]{1,0:T(8,128)(2,1)S(1)}, u32[]{:S(2)}, u32[]{:S(2)}) collective-permute-start(bf16[8,1920]{1,0:T(8,128)(2,1)S(1)} %get-tuple-element.66.flat_ref.rest_0_), channel_id=1, source_target_pairs={{0,1},{1,0},{2,3},{3,2},{4,5},{5,4},{6,7},{7,6},{8,9},{9,8},{10,11... | collective-permute-start | bytes 92168 | tf_op jit(solution)/shard_map/ppermute | solution.py:345
  38.1 1.9 %collective-permute-start.15 = (f32[8,128]{1,0:T(8,128)S(1)}, f32[8,128]{1,0:T(8,128)S(1)}, u32[]{:S(2)}, u32[]{:S(2)}) collective-permute-start(f32[8,128]{1,0:T(8,128)S(1)} %pair.1), channel_id=1, source_target_pairs={{0,4},{4,0},{8,12},{12,8},{16,20},{20,16},{24,28},{28,24},{1,5},{5... | collective-permute-start | bytes 12296 | tf_op jit(solution)/shard_map/ppermute | solution.py:345
  38.2 4.6 %collective-permute-start.16 = (f32[8,128]{1,0:T(8,128)S(1)}, f32[8,128]{1,0:T(8,128)S(1)}, u32[]{:S(2)}, u32[]{:S(2)}) collective-permute-start(f32[8,128]{1,0:T(8,128)S(1)} %pair.1), channel_id=1, source_target_pairs={{0,24},{4,28},{8,16},{12,20},{16,8},{20,12},{24,0},{28,4},{1,25},{... | collective-permute-start | bytes 12296 | tf_op jit(solution)/shard_map/ppermute | solution.py:345
  40.0 3.6 %collective-permute-start.17 = (f32[8,128]{1,0:T(8,128)S(1)}, f32[8,128]{1,0:T(8,128)S(1)}, u32[]{:S(2)}, u32[]{:S(2)}) collective-permute-start(f32[8,128]{1,0:T(8,128)S(1)} %add.3.own_ref), channel_id=1, source_target_pairs={{0,8},{4,20},{8,0},{12,28},{16,24},{20,4},{24,16},{28,12},{1,9},{5... | collective-permute-start | bytes 12296 | tf_op jit(solution)/shard_map/ppermute | solution.py:349
  42.7 1.2 %collective-permute-start.19 = (f32[8,128]{1,0:T(8,128)S(1)}, f32[8,128]{1,0:T(8,128)S(1)}, u32[]{:S(2)}, u32[]{:S(2)}) collective-permute-start(f32[8,128]{1,0:T(8,128)S(1)} %collective-permute-done.16.common_ref), channel_id=1, source_target_pairs={{0,4},{4,0},{8,12},{12,8},{16,20},{20,16},{24,28},{28,24},{1,5},{5... | collective-permute-start | bytes 12296 | tf_op jit(solution)/shard_map/ppermute | solution.py:345
  43.6 1.2 %collective-permute-start.18 = (f32[8,128]{1,0:T(8,128)S(1)}, f32[8,128]{1,0:T(8,128)S(1)}, u32[]{:S(2)}, u32[]{:S(2)}) collective-permute-start(f32[8,128]{1,0:T(8,128)S(1)} %collective-permute-done.17.rest_0_), channel_id=1, source_target_pairs={{0,4},{4,0},{8,12},{12,8},{16,20},{20,16},{24,28},{28,24},{1,5},{5... | collective-permute-start | bytes 12296 | tf_op jit(solution)/shard_map/ppermute | solution.py:345

commit v12 on v11

--- a/solution.py
+++ b/solution.py
@@ -14,7 +14,7 @@
 ROWS = 16
 TRAIT, ONES = PROBES, PROBES + 1
 TRACE_LANE, QUAD_LANE = LANES - 2, LANES - 1
-PIECE = 640
+PIECE = 1664
 DOT_PIECE = 1664
 F32 = jnp.float32
 BF16 = jnp.bfloat16

time: 45.7 us -> 45.7 us (level)
  transfers between devices with their start and end apart: 20 -> 20, of which waited for: 9 -> 8; matrix products, arithmetic and copies ran while one was open for 0% -> 0% of each run, Pallas kernels for 24% -> 24%
where the time goes in v12:
time: 45.7 us; the launch traced here: 45.4 us
  Pallas kernels  18.2 us (40%)
  starting transfers between devices  15.9 us (35%)
  waiting for transfers between devices  10.5 us (23%)
  between operations  0.83 us (2%)
    ppermute x19, starting transfers between devices, swap(): return lax.ppermute(value, axis, [(i, i ^ distance) for i in range(size)])  15.1 us
    pallas_call x4, Pallas kernels, moments(): pl.pallas_call(functools.partial(moments_kernel, snps, distances, opening...  11.9 us
    ppermute x19, waiting for transfers between devices, swap(): return lax.ppermute(value, axis, [(i, i ^ distance) for i in range(size)])  9.64 us
    pallas_call x12, Pallas kernels, plain(): pl.pallas_call(kernel, in_specs=[in_vmem()] * len(operands), out_specs=[i...  6.27 us
  transfers between devices with their start and end apart: 20, of which 8 were waited for; matrix products, arithmetic and copies ran while one was open for 0% of the time, Pallas kernels for 24%

profile of v12, /device:TPU:0, one launch (start us, length us, event | category | flops | bytes accessed | tf_op | source)
XLA Modules:
  0.0 45.4 jit_solution(11779045313175198415)
XLA Ops:
  0.6 4.9 %moments_away.1 = (bf16[3,256,3200]{2,1,0:T(8,128)(2,1)S(1)}, bf16[3,8,4992]{2,1,0:T(8,128)(2,1)S(1)}, f32[3,2,3200]{2,1,0:T(2,128)S(1)}, f32[16,256]{1,0:T(8,128)S(1)}, s32[256,3200]{1,0:T(8,128)S(1)}) custom-call(s32[256,25600]{1,0:T(8,128)} %geno_ref.7, s32[10,256]{1,0:T(8,128)} %rest_0_.1, bf16[256]{0:T(256)(128)(2,1)} %rest_1_.1), custom_call_target="tpu_custom_call" | custom-call | flops 1 | bytes 9830400 | tf_op jit(solution)/shard_map/moments_away/pallas_call | solution.py:421
  6.0 3.5 %moments_here.1 = (bf16[3,256,3200]{2,1,0:T(8,128)(2,1)S(1)}, bf16[3,8,4992]{2,1,0:T(8,128)(2,1)S(1)}, f32[3,2,3200]{2,1,0:T(2,128)S(1)}) custom-call(s32[256,25600]{1,0:T(8,128)} %geno_ref.7, s32[256,3200]{1,0:T(8,128)S(1)} %get-tuple-element.43.rest_0_, f32[16,256]{1,0:T(8,128)S(1)} %get-tuple-element.42.rest_1_.left_ref), custom_call_target="tpu_custom_call" | custom-call | flops 1 | bytes 9830400 | tf_op jit(solution)/shard_map/moments_here/pallas_call | solution.py:421
  9.6 3.5 %collective-permute-start.2 = (bf16[8,4992]{1,0:T(8,128)(2,1)S(1)}, bf16[8,4992]{1,0:T(8,128)(2,1)S(1)}, u32[]{:S(2)}, u32[]{:S(2)}) collective-permute-start(bf16[8,4992]{1,0:T(8,128)(2,1)S(1)} %get-tuple-element.52), channel_id=1, source_target_pairs={{0,24},{4,28},{8,16},{12,20},{16,8},{20,12},{24,0},{28,4},{1,25},{... | collective-permute-start | bytes 239624 | tf_op jit(solution)/shard_map/ppermute | solution.py:345
  13.8 2.9 %moments_near.1 = (bf16[1,256,3200]{2,1,0:T(8,128)(2,1)S(1)}, bf16[1,8,4992]{2,1,0:T(8,128)(2,1)S(1)}, f32[1,2,3200]{2,1,0:T(2,128)S(1)}, s32[256,3200]{1,0:T(8,128)S(1)}) custom-call(s32[256,25600]{1,0:T(8,128)} %geno_ref.7, f32[16,256]{1,0:T(8,128)S(1)} %get-tuple-element.46.rest_0_.rest_1_), custom_call_target="tpu_custom_call" | custom-call | flops 1 | bytes 1 | tf_op jit(solution)/shard_map/moments_near/pallas_call | solution.py:421
  16.9 0.6 %moments_own.1 = (bf16[1,256,3200]{2,1,0:T(8,128)(2,1)S(1)}, bf16[1,8,4992]{2,1,0:T(8,128)(2,1)S(1)}, f32[1,2,3200]{2,1,0:T(2,128)S(1)}) custom-call(s32[256,25600]{1,0:T(8,128)} %geno_ref.7, s32[256,3200]{1,0:T(8,128)S(1)} %get-tuple-element.47.rest_0_, f32[16,256]{1,0:T(8,128)S(1)} %get-tuple-element.46.rest_0_.rest_1_), custom_call_target="tpu_custom_call" | custom-call | flops 1 | bytes 1 | tf_op jit(solution)/shard_map/moments_own/pallas_call | solution.py:421
  17.5 0.7 %collective-permute-done.3.refs_1_ = bf16[8,4992]{1,0:T(8,128)(2,1)S(1)} collective-permute-done((bf16[8,4992]{1,0:T(8,128)(2,1)S(1)}, bf16[8,4992]{1,0:T(8,128)(2,1)S(1)}, u32[]{:S(2)}, u32[]{:S(2)}) %collective-permute-start.3) | collective-permute-done | bytes 79904 | tf_op jit(solution)/shard_map/ppermute | solution.py:345
  18.5 2.8 %collective-permute-start.8 = (bf16[8,4096]{1,0:T(8,128)(2,1)S(1)}, bf16[8,4096]{1,0:T(8,128)(2,1)S(1)}, u32[]{:S(2)}, u32[]{:S(2)}) collective-permute-start(bf16[8,4096]{1,0:T(8,128)(2,1)S(1)} %get-tuple-element.55.refs_4_), channel_id=1, source_target_pairs={{0,24},{4,28},{8,16},{12,20},{16,8},{20,12},{24,0},{28,4},{1,25},{... | collective-permute-start | bytes 196616 | tf_op jit(solution)/shard_map/ppermute | solution.py:345
  21.4 0.5 %collective-permute-start.6 = (bf16[8,4096]{1,0:T(8,128)(2,1)S(1)}, bf16[8,4096]{1,0:T(8,128)(2,1)S(1)}, u32[]{:S(2)}, u32[]{:S(2)}) collective-permute-start(bf16[8,4096]{1,0:T(8,128)(2,1)S(1)} %get-tuple-element.55.refs_4_), channel_id=1, source_target_pairs={{0,8},{4,12},{8,0},{12,4},{16,24},{20,28},{24,16},{28,20},{1,9},{5... | collective-permute-start | bytes 196616 | tf_op jit(solution)/shard_map/ppermute | solution.py:345
  22.0 1.1 %field.4 = (f32[256,80]{1,0:T(8,128)S(1)}, f32[80,128]{1,0:T(8,128)S(1)}, f32[8,128]{1,0:T(8,128)S(1)}) custom-call(f32[1,25600]{1,0:T(1,128)S(1)} %bitcast.7, s32[1,25600]{1,0:T(1,128)S(1)} %bitcast.12, bf16[1,256,3200]{2,1,0:T(8,128)(2,1)S(1)} %get-tuple-element.48.refs_2_, bf16[1,256,3200]{2,1,0:T(8,128)(2,1)S(1)} %get-tuple-element.49.refs_3_, ...), custom_call_target="tpu_custom_call" | custom-call | flops 1 | bytes 1 | tf_op jit(solution)/shard_map/field/pallas_call | solution.py:436
  23.1 0.9 %collective-permute-done.8.value_ref = bf16[8,4096]{1,0:T(8,128)(2,1)S(1)} collective-permute-done((bf16[8,4096]{1,0:T(8,128)(2,1)S(1)}, bf16[8,4096]{1,0:T(8,128)(2,1)S(1)}, u32[]{:S(2)}, u32[]{:S(2)}) %collective-permute-start.8) | collective-permute-done | bytes 65568 | tf_op jit(solution)/shard_map/ppermute | solution.py:345
  24.0 1.7 %collective-permute-done.6.value_ref = bf16[8,4096]{1,0:T(8,128)(2,1)S(1)} collective-permute-done((bf16[8,4096]{1,0:T(8,128)(2,1)S(1)}, bf16[8,4096]{1,0:T(8,128)(2,1)S(1)}, u32[]{:S(2)}, u32[]{:S(2)}) %collective-permute-start.6) | collective-permute-done | bytes 65568 | tf_op jit(solution)/shard_map/ppermute | solution.py:345
  25.6 1.0 %field.5 = (f32[256,80]{1,0:T(8,128)S(1)}, f32[80,128]{1,0:T(8,128)S(1)}, f32[8,128]{1,0:T(8,128)S(1)}) custom-call(f32[1,25600]{1,0:T(1,128)S(1)} %bitcast.8, s32[1,25600]{1,0:T(1,128)S(1)} %bitcast.13, bf16[3,256,3200]{2,1,0:T(8,128)(2,1)S(1)} %get-tuple-element.57.refs_2_.refs_3_, bf16[3,256,3200]{2,1,0:T(8,128)(2,1)S(1)} %get-tuple-element.57.refs_2_.refs_3_, ...), custom_call_target="tpu_custom_call" | custom-call | flops 1 | bytes 1 | tf_op jit(solution)/shard_map/field/pallas_call | solution.py:436
  27.3 1.0 %field.6 = (f32[256,80]{1,0:T(8,128)S(1)}, f32[80,128]{1,0:T(8,128)S(1)}, f32[8,128]{1,0:T(8,128)S(1)}) custom-call(f32[1,25600]{1,0:T(1,128)S(1)} %bitcast.9, s32[1,25600]{1,0:T(1,128)S(1)} %bitcast.14, bf16[3,256,3200]{2,1,0:T(8,128)(2,1)S(1)} %get-tuple-element.57.refs_2_.refs_3_, bf16[3,256,3200]{2,1,0:T(8,128)(2,1)S(1)} %get-tuple-element.41.refs_3_.refs_2_, ...), custom_call_target="tpu_custom_call" | custom-call | flops 1 | bytes 1 | tf_op jit(solution)/shard_map/field/pallas_call | solution.py:436
  28.3 1.2 %field.7 = (bf16[8,1920]{1,0:T(8,128)(2,1)S(1)}, f32[8,128]{1,0:T(8,128)S(1)}) custom-call(f32[1,25600]{1,0:T(1,128)S(1)} %bitcast.10, s32[1,25600]{1,0:T(1,128)S(1)} %bitcast.15, bf16[3,256,3200]{2,1,0:T(8,128)(2,1)S(1)} %get-tuple-element.41.refs_3_.refs_2_, bf16[8,4096]{1,0:T(8,128)(2,1)S(1)} %collective-permute-done.7.refs_3_, ...), custom_call_target="tpu_custom_call" | custom-call | flops 1 | bytes 1 | tf_op jit(solution)/shard_map/field/pallas_call | solution.py:436
  29.5 2.7 %collective-permute-start.14 = (bf16[8,1920]{1,0:T(8,128)(2,1)S(1)}, bf16[8,1920]{1,0:T(8,128)(2,1)S(1)}, u32[]{:S(2)}, u32[]{:S(2)}) collective-permute-start(bf16[8,1920]{1,0:T(8,128)(2,1)S(1)} %get-tuple-element.66.flat_ref.rest_0_), channel_id=1, source_target_pairs={{0,2},{1,3},{2,0},{3,1},{4,6},{5,7},{6,4},{7,5},{8,10},{9,11},{10,... | collective-permute-start | bytes 92168 | tf_op jit(solution)/shard_map/ppermute | solution.py:345
  32.2 1.3 %collective-permute-start.13 = (bf16[8,1920]{1,0:T(8,128)(2,1)S(1)}, bf16[8,1920]{1,0:T(8,128)(2,1)S(1)}, u32[]{:S(2)}, u32[]{:S(2)}) collective-permute-start(bf16[8,1920]{1,0:T(8,128)(2,1)S(1)} %get-tuple-element.66.flat_ref.rest_0_), channel_id=1, source_target_pairs={{0,3},{1,2},{2,1},{3,0},{4,7},{5,6},{6,5},{7,4},{8,11},{9,10},{10,... | collective-permute-start | bytes 92168 | tf_op jit(solution)/shard_map/ppermute | solution.py:345
  33.8 0.8 %stats.1 = (f32[8,128]{1,0:T(8,128)S(1)}, bf16[10,6,256]{2,1,0:T(8,128)(2,1)}) custom-call(bf16[8,1920]{1,0:T(8,128)(2,1)S(1)} %get-tuple-element.66.flat_ref.rest_0_, f32[1,25600]{1,0:T(1,128)S(1)} %bitcast.11, f32[1,25600]{1,0:T(1,128)S(1)} %bitcast.18, s32[1,25600]{1,0:T(1,128)S(1)} %bitcast.16, f32[1,3200]{1,0:T(1,128)S(1)} %get-tuple-element.67.trait_ref, ...), custom_call_target="tpu_custom_call" | custom-call | tf_op jit(solution)/shard_map/stats/pallas_call | solution.py:436
  34.6 3.2 %collective-permute-done.13.rest_2_ = bf16[8,1920]{1,0:T(8,128)(2,1)S(1)} collective-permute-done((bf16[8,1920]{1,0:T(8,128)(2,1)S(1)}, bf16[8,1920]{1,0:T(8,128)(2,1)S(1)}, u32[]{:S(2)}, u32[]{:S(2)}) %collective-permute-start.13) | collective-permute-done | bytes 30752 | tf_op jit(solution)/shard_map/ppermute | solution.py:345
  38.1 1.8 %collective-permute-start.16 = (f32[8,128]{1,0:T(8,128)S(1)}, f32[8,128]{1,0:T(8,128)S(1)}, u32[]{:S(2)}, u32[]{:S(2)}) collective-permute-start(f32[8,128]{1,0:T(8,128)S(1)} %pair.1), channel_id=1, source_target_pairs={{0,24},{4,28},{8,16},{12,20},{16,8},{20,12},{24,0},{28,4},{1,25},{... | collective-permute-start | bytes 12296 | tf_op jit(solution)/shard_map/ppermute | solution.py:345
  39.9 0.8 %collective-permute-start.17 = (f32[8,128]{1,0:T(8,128)S(1)}, f32[8,128]{1,0:T(8,128)S(1)}, u32[]{:S(2)}, u32[]{:S(2)}) collective-permute-start(f32[8,128]{1,0:T(8,128)S(1)} %add.3.own_ref), channel_id=1, source_target_pairs={{0,8},{4,20},{8,0},{12,28},{16,24},{20,4},{24,16},{28,12},{1,9},{5... | collective-permute-start | bytes 12296 | tf_op jit(solution)/shard_map/ppermute | solution.py:349
  40.7 1.9 %collective-permute-done.16.common_ref = f32[8,128]{1,0:T(8,128)S(1)} collective-permute-done((f32[8,128]{1,0:T(8,128)S(1)}, f32[8,128]{1,0:T(8,128)S(1)}, u32[]{:S(2)}, u32[]{:S(2)}) %collective-permute-start.16) | collective-permute-done | bytes 4128 | tf_op jit(solution)/shard_map/ppermute | solution.py:345
  42.7 0.9 %collective-permute-done.17.rest_0_ = f32[8,128]{1,0:T(8,128)S(1)} collective-permute-done((f32[8,128]{1,0:T(8,128)S(1)}, f32[8,128]{1,0:T(8,128)S(1)}, u32[]{:S(2)}, u32[]{:S(2)}) %collective-permute-start.17) | collective-permute-done | bytes 4128 | tf_op jit(solution)/shard_map/ppermute | solution.py:349
  43.9 0.9 %collective-permute-done.18.rest_1_ = f32[8,128]{1,0:T(8,128)S(1)} collective-permute-done((f32[8,128]{1,0:T(8,128)S(1)}, f32[8,128]{1,0:T(8,128)S(1)}, u32[]{:S(2)}, u32[]{:S(2)}) %collective-permute-start.18) | collective-permute-done | bytes 4128 | tf_op jit(solution)/shard_map/ppermute | solution.py:345
  44.7 0.7 %final.1 = (f32[6,24]{1,0:T(8,128)}, f32[1,6]{1,0:T(1,128)}, f32[1,6]{1,0:T(1,128)}) custom-call(f32[8,128]{1,0:T(8,128)S(1)} %get-tuple-element.73.count_ref, f32[8,128]{1,0:T(8,128)S(1)} %add.3.own_ref, f32[8,128]{1,0:T(8,128)S(1)} %collective-permute-done.16.common_ref, f32[8,128]{1,0:T(8,128)S(1)} %collective-permute-done.17.rest_0_, ...), custom_call_target="tpu_custom_call" | custom-call | tf_op jit(solution)/shard_map/final/pallas_call | solution.py:436
  (39 shorter events, 3.1 us)
Async XLA Ops:
  5.5 4.0 %collective-permute-start = (bf16[3,8,4992]{2,1,0:T(8,128)(2,1)S(1)}, bf16[3,8,4992]{2,1,0:T(8,128)(2,1)S(1)}, u32[]{:S(2)}, u32[]{:S(2)}) collective-permute-start(bf16[3,8,4992]{2,1,0:T(8,128)(2,1)S(1)} %get-tuple-element.45), channel_id=1, source_target_pairs={{0,4},{4,0},{8,12},{12,8},{16,20},{20,16},{24,28},{28,24},{1,5},{5... | collective-permute-start | bytes 718856 | tf_op jit(solution)/shard_map/ppermute | solution.py:345
  9.6 7.8 %collective-permute-start.2 = (bf16[8,4992]{1,0:T(8,128)(2,1)S(1)}, bf16[8,4992]{1,0:T(8,128)(2,1)S(1)}, u32[]{:S(2)}, u32[]{:S(2)}) collective-permute-start(bf16[8,4992]{1,0:T(8,128)(2,1)S(1)} %get-tuple-element.52), channel_id=1, source_target_pairs={{0,24},{4,28},{8,16},{12,20},{16,8},{20,12},{24,0},{28,4},{1,25},{... | collective-permute-start | bytes 239624 | tf_op jit(solution)/shard_map/ppermute | solution.py:345
  13.2 5.0 %collective-permute-start.3 = (bf16[8,4992]{1,0:T(8,128)(2,1)S(1)}, bf16[8,4992]{1,0:T(8,128)(2,1)S(1)}, u32[]{:S(2)}, u32[]{:S(2)}) collective-permute-start(bf16[8,4992]{1,0:T(8,128)(2,1)S(1)} %get-tuple-element.53), channel_id=1, source_target_pairs={{0,8},{4,12},{8,0},{12,4},{16,24},{20,28},{24,16},{28,20},{1,9},{5... | collective-permute-start | bytes 239624 | tf_op jit(solution)/shard_map/ppermute | solution.py:345
  13.7 4.5 %collective-permute-start.4 = (bf16[8,4992]{1,0:T(8,128)(2,1)S(1)}, bf16[8,4992]{1,0:T(8,128)(2,1)S(1)}, u32[]{:S(2)}, u32[]{:S(2)}) collective-permute-start(bf16[8,4992]{1,0:T(8,128)(2,1)S(1)} %get-tuple-element.54), channel_id=1, source_target_pairs={{0,16},{4,20},{8,24},{12,28},{16,0},{20,4},{24,8},{28,12},{1,17},{... | collective-permute-start | bytes 239624 | tf_op jit(solution)/shard_map/ppermute | solution.py:345
  16.8 1.4 %collective-permute-start.1 = (bf16[1,8,4992]{2,1,0:T(8,128)(2,1)S(1)}, bf16[1,8,4992]{2,1,0:T(8,128)(2,1)S(1)}, u32[]{:S(2)}, u32[]{:S(2)}) collective-permute-start(bf16[1,8,4992]{2,1,0:T(8,128)(2,1)S(1)} %get-tuple-element.51), channel_id=1, source_target_pairs={{0,4},{4,0},{8,12},{12,8},{16,20},{20,16},{24,28},{28,24},{1,5},{5... | collective-permute-start | bytes 239624 | tf_op jit(solution)/shard_map/ppermute | solution.py:345
  16.8 1.3 %copy-start = (f32[25600]{0:T(1024)S(1)}, f32[25600]{0:T(1024)}, u32[]{:S(2)}) copy-start(f32[25600]{0:T(1024)} %param.7) | copy-start | bytes 307204
  16.9 1.3 %copy-start.2 = (f32[25600]{0:T(1024)S(1)}, f32[25600]{0:T(1024)}, u32[]{:S(2)}) copy-start(f32[25600]{0:T(1024)} %param.8) | copy-start | bytes 307204
  16.9 5.1 %copy-start.1 = (s32[25600]{0:T(1024)S(1)}, s32[25600]{0:T(1024)}, u32[]{:S(2)}) copy-start(s32[25600]{0:T(1024)} %param.9) | copy-start | bytes 307204
  18.4 3.6 %collective-permute-start.5 = (bf16[8,4096]{1,0:T(8,128)(2,1)S(1)}, bf16[8,4096]{1,0:T(8,128)(2,1)S(1)}, u32[]{:S(2)}, u32[]{:S(2)}) collective-permute-start(bf16[8,4096]{1,0:T(8,128)(2,1)S(1)} %get-tuple-element.55.refs_4_), channel_id=1, source_target_pairs={{0,4},{4,0},{8,12},{12,8},{16,20},{20,16},{24,28},{28,24},{1,5},{5... | collective-permute-start | bytes 196616 | tf_op jit(solution)/shard_map/ppermute | solution.py:345
  18.5 5.4 %collective-permute-start.8 = (bf16[8,4096]{1,0:T(8,128)(2,1)S(1)}, bf16[8,4096]{1,0:T(8,128)(2,1)S(1)}, u32[]{:S(2)}, u32[]{:S(2)}) collective-permute-start(bf16[8,4096]{1,0:T(8,128)(2,1)S(1)} %get-tuple-element.55.refs_4_), channel_id=1, source_target_pairs={{0,24},{4,28},{8,16},{12,20},{16,8},{20,12},{24,0},{28,4},{1,25},{... | collective-permute-start | bytes 196616 | tf_op jit(solution)/shard_map/ppermute | solution.py:345
  21.4 4.3 %collective-permute-start.6 = (bf16[8,4096]{1,0:T(8,128)(2,1)S(1)}, bf16[8,4096]{1,0:T(8,128)(2,1)S(1)}, u32[]{:S(2)}, u32[]{:S(2)}) collective-permute-start(bf16[8,4096]{1,0:T(8,128)(2,1)S(1)} %get-tuple-element.55.refs_4_), channel_id=1, source_target_pairs={{0,8},{4,12},{8,0},{12,4},{16,24},{20,28},{24,16},{28,20},{1,9},{5... | collective-permute-start | bytes 196616 | tf_op jit(solution)/shard_map/ppermute | solution.py:345
  21.9 4.8 %collective-permute-start.9 = (bf16[8,4096]{1,0:T(8,128)(2,1)S(1)}, bf16[8,4096]{1,0:T(8,128)(2,1)S(1)}, u32[]{:S(2)}, u32[]{:S(2)}) collective-permute-start(bf16[8,4096]{1,0:T(8,128)(2,1)S(1)} %get-tuple-element.55.refs_4_), channel_id=1, source_target_pairs={{0,16},{4,20},{8,24},{12,28},{16,0},{20,4},{24,8},{28,12},{1,17},{... | collective-permute-start | bytes 196616 | tf_op jit(solution)/shard_map/ppermute | solution.py:345
  23.9 3.3 %collective-permute-start.11 = (bf16[8,4096]{1,0:T(8,128)(2,1)S(1)}, bf16[8,4096]{1,0:T(8,128)(2,1)S(1)}, u32[]{:S(2)}, u32[]{:S(2)}) collective-permute-start(bf16[8,4096]{1,0:T(8,128)(2,1)S(1)} %relay.4.refs_4_), channel_id=1, source_target_pairs={{0,4},{4,0},{8,12},{12,8},{16,20},{20,16},{24,28},{28,24},{1,5},{5... | collective-permute-start | bytes 196616 | tf_op jit(solution)/shard_map/ppermute | solution.py:345
  26.7 1.6 %collective-permute-start.10 = (bf16[8,4096]{1,0:T(8,128)(2,1)S(1)}, bf16[8,4096]{1,0:T(8,128)(2,1)S(1)}, u32[]{:S(2)}, u32[]{:S(2)}) collective-permute-start(bf16[8,4096]{1,0:T(8,128)(2,1)S(1)} %relay.5.refs_4_), channel_id=1, source_target_pairs={{0,4},{4,0},{8,12},{12,8},{16,20},{20,16},{24,28},{28,24},{1,5},{5... | collective-permute-start | bytes 196616 | tf_op jit(solution)/shard_map/ppermute | solution.py:345
  26.8 1.6 %collective-permute-start.7 = (bf16[8,4096]{1,0:T(8,128)(2,1)S(1)}, bf16[8,4096]{1,0:T(8,128)(2,1)S(1)}, u32[]{:S(2)}, u32[]{:S(2)}) collective-permute-start(bf16[8,4096]{1,0:T(8,128)(2,1)S(1)} %relay.3.refs_5_), channel_id=1, source_target_pairs={{0,4},{4,0},{8,12},{12,8},{16,20},{20,16},{24,28},{28,24},{1,5},{5... | collective-permute-start | bytes 196616 | tf_op jit(solution)/shard_map/ppermute | solution.py:345
  29.5 5.1 %collective-permute-start.14 = (bf16[8,1920]{1,0:T(8,128)(2,1)S(1)}, bf16[8,1920]{1,0:T(8,128)(2,1)S(1)}, u32[]{:S(2)}, u32[]{:S(2)}) collective-permute-start(bf16[8,1920]{1,0:T(8,128)(2,1)S(1)} %get-tuple-element.66.flat_ref.rest_0_), channel_id=1, source_target_pairs={{0,2},{1,3},{2,0},{3,1},{4,6},{5,7},{6,4},{7,5},{8,10},{9,11},{10,... | collective-permute-start | bytes 92168 | tf_op jit(solution)/shard_map/ppermute | solution.py:345
  32.2 5.7 %collective-permute-start.13 = (bf16[8,1920]{1,0:T(8,128)(2,1)S(1)}, bf16[8,1920]{1,0:T(8,128)(2,1)S(1)}, u32[]{:S(2)}, u32[]{:S(2)}) collective-permute-start(bf16[8,1920]{1,0:T(8,128)(2,1)S(1)} %get-tuple-element.66.flat_ref.rest_0_), channel_id=1, source_target_pairs={{0,3},{1,2},{2,1},{3,0},{4,7},{5,6},{6,5},{7,4},{8,11},{9,10},{10,... | collective-permute-start | bytes 92168 | tf_op jit(solution)/shard_map/ppermute | solution.py:345
  33.5 4.3 %collective-permute-start.12 = (bf16[8,1920]{1,0:T(8,128)(2,1)S(1)}, bf16[8,1920]{1,0:T(8,128)(2,1)S(1)}, u32[]{:S(2)}, u32[]{:S(2)}) collective-permute-start(bf16[8,1920]{1,0:T(8,128)(2,1)S(1)} %get-tuple-element.66.flat_ref.rest_0_), channel_id=1, source_target_pairs={{0,1},{1,0},{2,3},{3,2},{4,5},{5,4},{6,7},{7,6},{8,9},{9,8},{10,11... | collective-permute-start | bytes 92168 | tf_op jit(solution)/shard_map/ppermute | solution.py:345
  38.1 1.9 %collective-permute-start.15 = (f32[8,128]{1,0:T(8,128)S(1)}, f32[8,128]{1,0:T(8,128)S(1)}, u32[]{:S(2)}, u32[]{:S(2)}) collective-permute-start(f32[8,128]{1,0:T(8,128)S(1)} %pair.1), channel_id=1, source_target_pairs={{0,4},{4,0},{8,12},{12,8},{16,20},{20,16},{24,28},{28,24},{1,5},{5... | collective-permute-start | bytes 12296 | tf_op jit(solution)/shard_map/ppermute | solution.py:345
  38.1 4.6 %collective-permute-start.16 = (f32[8,128]{1,0:T(8,128)S(1)}, f32[8,128]{1,0:T(8,128)S(1)}, u32[]{:S(2)}, u32[]{:S(2)}) collective-permute-start(f32[8,128]{1,0:T(8,128)S(1)} %pair.1), channel_id=1, source_target_pairs={{0,24},{4,28},{8,16},{12,20},{16,8},{20,12},{24,0},{28,4},{1,25},{... | collective-permute-start | bytes 12296 | tf_op jit(solution)/shard_map/ppermute | solution.py:345
  39.9 3.6 %collective-permute-start.17 = (f32[8,128]{1,0:T(8,128)S(1)}, f32[8,128]{1,0:T(8,128)S(1)}, u32[]{:S(2)}, u32[]{:S(2)}) collective-permute-start(f32[8,128]{1,0:T(8,128)S(1)} %add.3.own_ref), channel_id=1, source_target_pairs={{0,8},{4,20},{8,0},{12,28},{16,24},{20,4},{24,16},{28,12},{1,9},{5... | collective-permute-start | bytes 12296 | tf_op jit(solution)/shard_map/ppermute | solution.py:349
  42.7 1.2 %collective-permute-start.19 = (f32[8,128]{1,0:T(8,128)S(1)}, f32[8,128]{1,0:T(8,128)S(1)}, u32[]{:S(2)}, u32[]{:S(2)}) collective-permute-start(f32[8,128]{1,0:T(8,128)S(1)} %collective-permute-done.16.common_ref), channel_id=1, source_target_pairs={{0,4},{4,0},{8,12},{12,8},{16,20},{20,16},{24,28},{28,24},{1,5},{5... | collective-permute-start | bytes 12296 | tf_op jit(solution)/shard_map/ppermute | solution.py:345
  43.5 1.2 %collective-permute-start.18 = (f32[8,128]{1,0:T(8,128)S(1)}, f32[8,128]{1,0:T(8,128)S(1)}, u32[]{:S(2)}, u32[]{:S(2)}) collective-permute-start(f32[8,128]{1,0:T(8,128)S(1)} %collective-permute-done.17.rest_0_), channel_id=1, source_target_pairs={{0,4},{4,0},{8,12},{12,8},{16,20},{20,16},{24,28},{28,24},{1,5},{5... | collective-permute-start | bytes 12296 | tf_op jit(solution)/shard_map/ppermute | solution.py:345
